TPU v7x, 32 devices: a whole 2x2x4 slice. The times are simulated.
32 devices in a mesh: dp: 4 (over y, x), ctx: 8 (over z, core).
Axes of the slice: x: 2, y: 2, z: 4, core: 2. Of those that a mesh axis runs over, the one named last changes fastest.
Arguments:
- context: bfloat16 [4096, 4096], P('ctx'), may hold values from -6 to 6
- w_key: bfloat16 [4096, 1024], P('ctx', 'dp'), may hold values from -0.09375 to 0.09375
- w_value: bfloat16 [4096, 1024], P('ctx', 'dp'), may hold values from -0.09375 to 0.09375
- queries: bfloat16 [512, 1024], P('ctx', 'dp'), may hold values from -300 to 300
- offsets: int32 [512], replicated, may hold values from 3072 to 4095, as said below
- head_gain: bfloat16 [1024], P('dp'), may hold values from 0.099609375 to 1.8984375
- w_out: bfloat16 [1024, 4096], P('dp', 'ctx'), may hold values from -0.1875 to 0.1875
Outputs:
- mixed: bfloat16 [512, 4096], P('ctx', 'dp')
Inputs may be any that keep to these rules, and one draw needn't show every extreme that they name: `offsets`: strictly increasing along the latents; latent l's offset is 4096 - 2 * 512 + 2 * l or one more, the last latent's offset is 4095.
All inputs are finite; a program needn't handle non-finite values.
Results may differ from a plain program's by a relative error of at most 0.012.
Values may be sent and summed in bfloat16 or wider, within the bound.
No kernel may reach another device: no remote copies, remote signals or barrier semaphores. Data moves between devices by JAX's collectives and lax.ppermute only.
A program may use at most 64 MiB of HBM per device.

v0:
```python
import math

import jax
import jax.numpy as jnp
from jax import lax
from jax.sharding import PartitionSpec as P

DH = 128


NEGATIVE = -1e30


def local_scores(query_block, key_block, offset_block, head_count):
    block_len = key_block.shape[0]
    score_scale = 1.0 / math.sqrt(DH)
    query_heads = query_block.reshape(query_block.shape[0], head_count, DH)
    key_heads = key_block.reshape(block_len, head_count, DH)
    scores = (
        jnp.einsum("lhd,khd->lhk", query_heads, key_heads, preferred_element_type=jnp.float32)
        * score_scale
    )
    positions = jnp.arange(block_len, dtype=jnp.int32)
    is_live = positions[None, None, :] <= offset_block[:, None, None]
    return (jnp.where(is_live, scores, NEGATIVE), is_live)


def weigh_values(masked, is_live, row_peak, value_block, head_count):
    weights = jnp.where(is_live, jnp.exp(masked - row_peak[:, :, None]), 0.0).astype(jnp.bfloat16)
    value_heads = value_block.reshape(value_block.shape[0], head_count, DH)
    numerator = jnp.einsum("lhk,khd->lhd", weights, value_heads, preferred_element_type=jnp.float32)
    row_total = jnp.sum(weights.astype(jnp.float32), axis=2)
    return (row_total, numerator)


def on_device(context, w_key, w_value, queries, offsets, head_gain, w_out):
    panel_width = w_key.shape[1]
    head_count = panel_width // DH
    lat_count = queries.shape[0]
    pieces = (
        lax.all_gather(w_key, "ctx", axis=0, tiled=True),
        lax.all_gather(w_value, "ctx", axis=0, tiled=True),
    )
    key_sum = jnp.dot(context, pieces[0], preferred_element_type=jnp.float32)
    value_sum = jnp.dot(context, pieces[1], preferred_element_type=jnp.float32)
    key_rows = key_sum.astype(jnp.bfloat16)
    value_rows = value_sum.astype(jnp.bfloat16)
    lat_first = lax.axis_index("ctx") * lat_count
    my_offsets = lax.dynamic_slice_in_dim(offsets, lat_first, lat_count, 0)
    furthest = jnp.max(my_offsets)
    start_state = (
        jnp.full((lat_count, head_count), NEGATIVE, jnp.float32),
        jnp.zeros((lat_count, head_count), jnp.float32),
        jnp.zeros((lat_count, head_count, DH), jnp.float32),
    )
    pieces = (
        lax.all_gather(key_rows, "ctx", axis=0, tiled=True),
        lax.all_gather(value_rows, "ctx", axis=0, tiled=True),
    )

    def update(state):
        masked, is_live = local_scores(queries, pieces[0], my_offsets, head_count)
        row_peak = jnp.maximum(state[0], jnp.max(masked, axis=2))
        block_total, block_num = weigh_values(masked, is_live, row_peak, pieces[1], head_count)
        return (row_peak, block_total, block_num)

    row_peak, row_total, numerator = lax.cond(
        jnp.int32(0) <= furthest, update, lambda state: state, start_state
    )
    attended = numerator / row_total[:, :, None]
    gain_rows = head_gain.astype(jnp.float32).reshape(head_count, DH)
    mean_square = jnp.mean(attended * attended, axis=2, keepdims=True)
    normed = (attended * lax.rsqrt(mean_square + 1e-05) * gain_rows[None, :, :]).astype(
        jnp.bfloat16
    )
    normed = normed.reshape(lat_count, panel_width)
    out_terms = jnp.dot(
        normed, lax.all_gather(w_out, "ctx", axis=1, tiled=True), preferred_element_type=jnp.float32
    )
    return lax.psum_scatter(out_terms.astype(jnp.bfloat16), "dp", scatter_dimension=1, tiled=True)


def solution(mesh):
    placed = (
        P("ctx", None),
        P("ctx", "dp"),
        P("ctx", "dp"),
        P("ctx", "dp"),
        P(),
        P("dp"),
        P("dp", "ctx"),
    )
    return jax.shard_map(
        on_device, mesh=mesh, in_specs=placed, out_specs=P("ctx", "dp"), check_vma=False
    )
```

profile of v0, /device:TPU:0, one launch (start us, length us, event | category | flops | bytes accessed | tf_op | source)
XLA Modules:
  0.0 195.6 jit_solution(2940788018163822666)
XLA Ops:
  6.5 0.0 all-gather.10.cloned.1.call-start
  6.5 0.7 all-gather.10.cloned.1.call-update
  7.3 0.0 all-gather.6.cloned.1.call-start
  7.3 0.7 all-gather.6.cloned.1.call-update
  8.0 0.0 all-gather.12.cloned.1.call-start
  8.1 32.7 %all-gather.10.cloned.1.call-done = bf16[4096,256]{1,0:T(8,128)(2,1)} async-done(((bf16[512,256]{1,0:T(8,128)(2,1)}), bf16[4096,256]{1,0:T(8,128)(2,1)}) %all-gather.10.cloned.1.call-update) | async-done | bytes 2097168 | tf_op jit(solution)/shard_map/all_gather | solution.py:42
  40.8 4.8 %convolution_convert_fusion.1 = bf16[512,256]{1,0:T(8,128)(2,1)} fusion(bf16[512,4096]{1,0:T(8,128)(2,1)} %param.9, bf16[4096,256]{1,0:T(8,128)(2,1)} %all-gather.10.cloned.1.call-done), kind=kOutput, calls=%fused_computation.17 | convolution fusion | flops 1073872896 | bytes 6553600 | tf_op jit(solution)/shard_map/dot_general | solution.py:45
  45.6 0.0 all-gather.12.cloned.1.call-update
  45.6 0.0 copy-start.2
  45.6 0.0 copy-start.1
  45.7 0.0 all-gather.8.cloned.1.call-start
  45.7 25.3 %all-gather.6.cloned.1.call-done = bf16[4096,256]{1,0:T(8,128)(2,1)} async-done(((bf16[512,256]{1,0:T(8,128)(2,1)}), bf16[4096,256]{1,0:T(8,128)(2,1)}) %all-gather.6.cloned.1.call-update) | async-done | bytes 2097168 | tf_op jit(solution)/shard_map/all_gather | solution.py:41
  71.0 4.8 %convolution_convert_fusion.2 = bf16[512,256]{1,0:T(8,128)(2,1)} fusion(bf16[512,4096]{1,0:T(8,128)(2,1)} %param.9, bf16[4096,256]{1,0:T(8,128)(2,1)} %all-gather.6.cloned.1.call-done), kind=kOutput, calls=%fused_computation.18 | convolution fusion | flops 1073872896 | bytes 6553600 | tf_op jit(solution)/shard_map/dot_general | solution.py:44
  75.8 0.0 all-gather.8.cloned.1.call-update
  75.9 0.0 all-gather.14.cloned.1.call-start
  75.9 0.5 all-gather.14.cloned.1.call-update
  76.5 0.0 reduce-scatter.2.cloned.1.call-start
  76.5 1.4 fusion.16
  78.6 0.0 copy-done.2
  78.6 22.7 %all-gather.12.cloned.1.call-done = bf16[4096,256]{1,0:T(8,128)(2,1)} async-done(((bf16[512,256]{1,0:T(8,128)(2,1)}), bf16[4096,256]{1,0:T(8,128)(2,1)}) %all-gather.12.cloned.1.call-update) | async-done | bytes 2097168 | tf_op jit(solution)/shard_map/all_gather | solution.py:58
  101.3 30.1 %all-gather.8.cloned.1.call-done = bf16[4096,256]{1,0:T(8,128)(2,1)} async-done(((bf16[512,256]{1,0:T(8,128)(2,1)}), bf16[4096,256]{1,0:T(8,128)(2,1)}) %all-gather.8.cloned.1.call-update) | async-done | bytes 2097168 | tf_op jit(solution)/shard_map/all_gather | solution.py:57
  131.3 0.0 copy-done.1
  131.3 4.3 %conditional.1 = (f32[64,2]{0,1:T(2,128)S(1)}, f32[64,2,128]{2,0,1:T(8,128)S(1)}) conditional(s32[]{:T(128)} %convert_element_type.22, () %tuple.13, (s32[64]{0:T(128)S(1)}, bf16[4096,256]{1,0:T(8,128)(2,1)}, bf16[64,256]{1,0:T(8,128)(2,1)S(1)}, bf16[4096,256]{1,0:T(8,128)(2,1)}) %tuple.31), branch_computations={%region_1.0_spmd, %region_2.5_spmd} | conditional | flops 274464640 | bytes 20024620 | solution.py:67
  131.3 0.2 iota_compare_fusion
  131.6 0.0 copy-start
  131.6 2.7 %fusion.17 = (f32[64,2]{0,1:T(2,128)S(1)}, f32[64,2,4096]{2,0,1:T(8,128)S(1)}) fusion(pred[64,4096]{1,0:T(8,128)(4,1)S(1)} %iota_compare_fusion, bf16[4096,256]{1,0:T(8,128)(2,1)} %get-tuple-element.14, bf16[64,256]{1,0:T(8,128)(2,1)S(1)} %get-tuple-element.22), kind=kOutput, calls=%fused_computation.28 | convolution fusion | flops 135790464 | bytes 4489728 | tf_op jit(solution)/shard_map/cond/branch_1_fun/lhd,khd->lhk/dot_general | solution.py:20
  134.3 0.0 copy-done
  134.3 0.7 fusion.7
  135.0 0.7 convert_reduce_fusion
  135.6 0.2 multiply_reduce_fusion
  135.8 25.6 %all-gather.14.cloned.1.call-done = bf16[256,4096]{1,0:T(8,128)(2,1)} async-done(((bf16[256,512]{1,0:T(8,128)(2,1)}), bf16[256,4096]{1,0:T(8,128)(2,1)}) %all-gather.14.cloned.1.call-update) | async-done | bytes 2097168 | tf_op jit(solution)/shard_map/all_gather | solution.py:78
  161.4 2.9 %convolution_convert_fusion = bf16[64,4096]{1,0:T(8,128)(2,1)} fusion(bf16[256,4096]{1,0:T(8,128)(2,1)} %all-gather.14.cloned.1.call-done, f32[2,128]{1,0:T(2,128)S(1)} %bitcast_convert_fusion, f32[64,2]{0,1:T(2,128)S(1)} %add_rsqrt_fusion, f32[64,2,128]{2,0,1:T(8,128)S(1)} %get-tuple-element.19, f32[64,2]{0,1:T(2,128)S(1)} %get-tuple-element.20), kind=kOutput, calls=%fused_computation.16 | convolution fusion | flops 134545408 | bytes 2689024 | tf_op jit(solution)/shard_map/dot_general | solution.py:77
  164.3 0.0 reduce-scatter.2.cloned.1.call-update
  164.4 24.4 %reduce-scatter.2.cloned.1.call-done = bf16[64,1024]{1,0:T(8,128)(2,1)} async-done(((bf16[64,4096]{1,0:T(8,128)(2,1)}), bf16[64,1024]{1,0:T(8,128)(2,1)}) %reduce-scatter.2.cloned.1.call-update) | async-done | bytes 131088 | tf_op jit(solution)/shard_map/reduce_scatter | solution.py:80
  (3 shorter events, 0.0 us)
Async XLA Ops:
  6.5 34.3 %all-gather.10.cloned.1.call-start = ((), (), s32[]{:S(2)}) async-start(), calls=%async_computation.3 | async-start | bytes 2359296 | tf_op jit(solution)/shard_map/all_gather | solution.py:42
  7.3 63.8 %all-gather.6.cloned.1.call-start = ((), (), s32[]{:S(2)}) async-start(), calls=%async_computation.1 | async-start | bytes 2359296 | tf_op jit(solution)/shard_map/all_gather | solution.py:41
  8.0 93.2 %all-gather.12.cloned.1.call-start = ((), (), s32[]{:S(2)}) async-start(), calls=%async_computation.4 | async-start | bytes 2359296 | tf_op jit(solution)/shard_map/all_gather | solution.py:58
  45.6 32.9 %copy-start.2 = (bf16[256]{0:T(256)(128)(2,1)S(1)}, bf16[256]{0:T(256)(128)(2,1)}, u32[]{:S(2)}) copy-start(bf16[256]{0:T(256)(128)(2,1)} %param.14) | copy-start | bytes 1540
  45.6 85.7 %copy-start.1 = (bf16[64,256]{1,0:T(8,128)(2,1)S(1)}, bf16[64,256]{1,0:T(8,128)(2,1)}, u32[]{:S(2)}) copy-start(bf16[64,256]{1,0:T(8,128)(2,1)} %param.12) | copy-start | bytes 98308
  45.7 85.7 %all-gather.8.cloned.1.call-start = ((), (), s32[]{:S(2)}) async-start(), calls=%async_computation.2 | async-start | bytes 2359296 | tf_op jit(solution)/shard_map/all_gather | solution.py:57
  75.9 85.5 %all-gather.14.cloned.1.call-start = ((), (), s32[]{:S(2)}) async-start(), calls=%async_computation.5 | async-start | bytes 2359296 | tf_op jit(solution)/shard_map/all_gather | solution.py:78
  76.5 112.3 %reduce-scatter.2.cloned.1.call-start = ((), (), s32[]{:S(2)}) async-start(), calls=%async_computation.6 | async-start | bytes 655360 | tf_op jit(solution)/shard_map/reduce_scatter | solution.py:80
  131.6 2.7 %copy-start = (bf16[4096,256]{1,0:T(8,128)(2,1)S(1)}, bf16[4096,256]{1,0:T(8,128)(2,1)}, u32[]{:S(2)}) copy-start(bf16[4096,256]{1,0:T(8,128)(2,1)} %get-tuple-element.16) | copy-start | bytes 6291460 | tf_op jit(solution)/shard_map/cond
Sparse Core Ops, SparseCore 0:
  9.0 31.7 all-gather.9
  42.4 28.5 all-gather.5
  72.6 28.5 all-gather.11
  102.7 28.5 all-gather.7
  132.8 28.5 all-gather.13
  164.5 24.2 reduce-scatter.1
where the time goes:
time: 196 us
  waiting for transfers between devices  163 us (83%)
  matrix products  16 us (8%)
  between operations  14.2 us (7%)
  other arithmetic  2.45 us (1%)
    all_gather x1, waiting for transfers between devices, on_device(): lax.all_gather(w_value, 'ctx', axis=0, tiled=True)  32.7 us
    all_gather x1, waiting for transfers between devices, on_device(): lax.all_gather(key_rows, 'ctx', axis=0, tiled=True)  30.1 us
    all_gather x1, waiting for transfers between devices, on_device(): lax.all_gather(w_out, 'ctx', axis=1, tiled=True)  25.6 us
    all_gather x1, waiting for transfers between devices, on_device(): lax.all_gather(w_key, 'ctx', axis=0, tiled=True)  25.3 us
    reduce_scatter x1, waiting for transfers between devices, on_device(): lax.psum_scatter(out_terms.astype(jnp.bfloat16), 'dp', scatter_dimension=...  24.4 us
    all_gather x1, waiting for transfers between devices, on_device(): lax.all_gather(value_rows, 'ctx', axis=0, tiled=True)  22.7 us
    dot_general x1, matrix products, on_device(): key_sum = jnp.dot(context, pieces[0], preferred_element_type=jnp.float32)  4.83 us
    dot_general x1, matrix products, on_device(): value_sum = jnp.dot(context, pieces[1], preferred_element_type=jnp.float32)  4.82 us
  transfers between devices with their start and end apart: 6, of which 6 were waited for; matrix products, arithmetic and copies ran while one was open for 8% of the time, Pallas kernels for 0%

commit v1 on v0

v1 whole, which is shorter than its diff:
```python
import math

import jax
import jax.numpy as jnp
from jax import lax
from jax.sharding import PartitionSpec as P

DH = 128
NEGATIVE = -1e30
CORES = 2


def three_parts(value):
    high = value.astype(jnp.bfloat16)
    rest = value - high.astype(jnp.float32)
    middle = rest.astype(jnp.bfloat16)
    low = (rest - middle.astype(jnp.float32)).astype(jnp.bfloat16)
    return [high, middle, low]


def on_device(n_dp, n_ctx, context, w_key, w_value, queries, offsets, head_gain, w_out):
    chips = n_ctx // CORES
    rows, model = context.shape
    depth, panel = w_key.shape
    half = panel // CORES
    heads = half // DH
    lat_count = queries.shape[0]
    latents = offsets.shape[0]
    me = lax.axis_index("ctx")
    chip = me // CORES
    core = lax.rem(me, CORES)

    swap = [(i, i ^ 1) for i in range(n_ctx)]

    def line(shift, first, last):
        return [
            (z * CORES + k, (z + shift) * CORES + k)
            for z in range(first, last + 1)
            for k in range(CORES)
        ]

    def columns(array, which):
        return lax.dynamic_slice_in_dim(array, which * half, half, 1)

    def along_line(block):
        found = [[(chip, block)]]
        up = down = block
        for step in range(1, chips):
            up = lax.ppermute(up, "ctx", line(1, step - 1, chips - 2))
            down = lax.ppermute(down, "ctx", line(-1, 1, chips - step))
            if 2 * step < chips:
                found.append([(jnp.maximum(chip - step, 0), up), (jnp.minimum(chip + step, chips - 1), down)])
            else:
                below = chip >= step
                source = jnp.where(below, chip - step, jnp.minimum(chip + step, chips - 1))
                found.append([(source, jnp.where(below, up, down))])
        return found

    mine = jnp.concatenate([columns(w_key, core), columns(w_value, core)], axis=1)
    other = jnp.concatenate([columns(w_key, 1 - core), columns(w_value, 1 - core)], axis=1)
    sibling = lax.ppermute(other, "ctx", swap)
    context_sibling = lax.ppermute(context, "ctx", swap)
    query_rows = lax.all_gather(queries, "ctx", axis=0, tiled=True)
    query_rows = columns(query_rows, core)
    first_half = along_line(mine)
    second_half = along_line(sibling)

    own_sum = jnp.zeros((rows, 2 * half), jnp.float32)
    sibling_sum = jnp.zeros((rows, 2 * half), jnp.float32)
    for step in range(chips):
        for found, who in ((first_half, core), (second_half, 1 - core)):
            for source, block in found[step]:
                start = (source * CORES + who) * depth
                own_sum += jnp.dot(
                    lax.dynamic_slice_in_dim(context, start, depth, 1), block,
                    preferred_element_type=jnp.float32,
                )
                sibling_sum += jnp.dot(
                    lax.dynamic_slice_in_dim(context_sibling, start, depth, 1), block,
                    preferred_element_type=jnp.float32,
                )
    pairs = jnp.concatenate([own_sum, sibling_sum], axis=0).astype(jnp.bfloat16)
    own_first = me * rows
    sibling_first = (me + 1 - 2 * core) * rows
    within = jnp.arange(rows, dtype=jnp.int32)
    positions = jnp.concatenate([own_first + within, sibling_first + within])
    live = positions[:, None] <= offsets[None, :]

    w_all = lax.all_gather(w_out, "ctx", axis=1, tiled=True)

    score_scale = 1.0 / math.sqrt(DH)
    messages = []
    for h in range(heads):
        keys = pairs[:, h * DH : (h + 1) * DH]
        values = pairs[:, half + h * DH : half + (h + 1) * DH]
        query = query_rows[:, h * DH : (h + 1) * DH]
        scores = lax.dot_general(
            keys, query, (((1,), (1,)), ((), ())), preferred_element_type=jnp.float32
        ) * score_scale
        masked = jnp.where(live, scores, NEGATIVE)
        peak = jnp.max(masked, axis=0)
        weights = jnp.where(live, jnp.exp(masked - peak[None, :]), 0.0).astype(jnp.bfloat16)
        total = jnp.sum(weights.astype(jnp.float32), axis=0)
        numerator = lax.dot_general(
            values, weights, (((0,), (0,)), ((), ())), preferred_element_type=jnp.float32
        )
        stats = jnp.stack(three_parts(peak) + three_parts(total), axis=0)
        stats = jnp.concatenate([stats, jnp.zeros((10, latents), jnp.bfloat16)], axis=0)
        messages.append(jnp.concatenate([numerator.astype(jnp.bfloat16), stats], axis=0))
    message = jnp.stack(messages)
    message = message.reshape(heads, DH + 16, n_ctx, lat_count).transpose(2, 0, 1, 3)
    arrived = lax.all_to_all(message, "ctx", 0, 0, tiled=False)
    arrived = arrived.reshape(chips, CORES, heads, DH + 16, lat_count).astype(jnp.float32)
    peaks = jnp.sum(arrived[:, :, :, DH : DH + 3, :], axis=3)
    totals = jnp.sum(arrived[:, :, :, DH + 3 : DH + 6, :], axis=3)
    top = jnp.max(peaks, axis=0)
    scale = jnp.exp(peaks - top[None])
    total = jnp.sum(totals * scale, axis=0)
    attended = jnp.sum(arrived[:, :, :, :DH, :] * scale[:, :, :, None, :], axis=0) / total[:, :, None, :]
    mean_square = jnp.mean(attended * attended, axis=2, keepdims=True)
    gain = head_gain.astype(jnp.float32).reshape(CORES, heads, DH, 1)
    normed = (attended * lax.rsqrt(mean_square + 1e-05) * gain).astype(jnp.bfloat16)
    normed = normed.reshape(panel, lat_count)

    terms = lax.dot_general(
        normed, w_all, (((0,), (0,)), ((), ())), preferred_element_type=jnp.float32
    ).astype(jnp.bfloat16)
    wide = terms.shape[1] // n_dp
    terms = terms.reshape(lat_count, n_dp, wide).transpose(1, 0, 2)
    terms = lax.all_to_all(terms, "dp", 0, 0, tiled=False)
    return jnp.sum(terms.astype(jnp.float32), axis=0).astype(jnp.bfloat16)


def solution(mesh):
    n_dp, n_ctx = mesh.shape["dp"], mesh.shape["ctx"]
    placed = (
        P("ctx", None),
        P("ctx", "dp"),
        P("ctx", "dp"),
        P("ctx", "dp"),
        P(),
        P("dp"),
        P("dp", "ctx"),
    )

    def body(*args):
        return on_device(n_dp, n_ctx, *args)

    return jax.shard_map(
        body, mesh=mesh, in_specs=placed, out_specs=P("ctx", "dp"), check_vma=False
    )
```

time: 196 us -> 135 us (0.69)
  waiting for transfers between devices: 163 us -> 38.8 us
  blocking collectives: 0 us -> 27.8 us
  starting transfers between devices: 0.2 us -> 24.3 us
  matrix products: 16 us -> 22.5 us
  local copies, waits for them, and re-layouts: 0.02 us -> 4.06 us
    all_gather x5 -> x1, waiting for transfers between devices: 136 us -> 0.01 us  [on_device(): w_all = lax.all_gather(w_out, 'ctx', axis=1, tiled=True)]
    ppermute x0 -> x14, waiting for transfers between devices: none -> 29.1 us  [the longest x6 29.1 us: along_line(): down = lax.ppermute(down, 'ctx', line(-1, 1, chips - step))]
    reduce_scatter x1 -> x0, waiting for transfers between devices: 24.4 us -> none  [on_device(): lax.psum_scatter(out_terms.astype(jnp.bfloat16), 'dp', scatter_dimension=...]
    ppermute x0 -> x14, starting transfers between devices: none -> 20.9 us  [the longest x6 12.4 us: along_line(): up = lax.ppermute(up, 'ctx', line(1, step - 1, chips - 2))]
    all_gather x0 -> x1, blocking collectives: none -> 16.2 us  [on_device(): query_rows = lax.all_gather(queries, 'ctx', axis=0, tiled=True)]
    all_to_all x0 -> x1, blocking collectives: none -> 11.6 us  [on_device(): terms = lax.all_to_all(terms, 'dp', 0, 0, tiled=False)]
    all_to_all x0 -> x1, waiting for transfers between devices: none -> 9.64 us  [on_device(): arrived = lax.all_to_all(message, 'ctx', 0, 0, tiled=False)]
    dot_general x5 -> x23, matrix products: 16 us -> 22.5 us  [the longest x10 13.4 us: on_device(): jnp.dot(lax.dynamic_slice_in_dim(context_sibling, start, depth, 1), block...]
  transfers between devices with their start and end apart: 6 -> 16, of which waited for: 6 -> 4; matrix products, arithmetic and copies ran while one was open for 8% -> 19% of each run, Pallas kernels for 0% -> 0%
where the time goes in v1:
time: 135 us; the launch traced here: 134 us
  waiting for transfers between devices  38.8 us (29%)
  blocking collectives  27.8 us (21%)
  starting transfers between devices  24.3 us (18%)
  matrix products  22.5 us (17%)
  between operations  14 us (10%)
  local copies, waits for them, and re-layouts  4.06 us (3%)
  other arithmetic  2.23 us (2%)
    ppermute x6, waiting for transfers between devices, along_line(): down = lax.ppermute(down, 'ctx', line(-1, 1, chips - step))  29.1 us
    all_gather x1, blocking collectives, on_device(): query_rows = lax.all_gather(queries, 'ctx', axis=0, tiled=True)  16.2 us
    dot_general x10, matrix products, on_device(): jnp.dot(lax.dynamic_slice_in_dim(context_sibling, start, depth, 1), block...  13.4 us
    ppermute x6, starting transfers between devices, along_line(): up = lax.ppermute(up, 'ctx', line(1, step - 1, chips - 2))  12.4 us
    all_to_all x1, blocking collectives, on_device(): terms = lax.all_to_all(terms, 'dp', 0, 0, tiled=False)  11.6 us
    all_to_all x1, waiting for transfers between devices, on_device(): arrived = lax.all_to_all(message, 'ctx', 0, 0, tiled=False)  9.64 us
    ppermute x6, starting transfers between devices, along_line(): down = lax.ppermute(down, 'ctx', line(-1, 1, chips - step))  7.73 us
    dot_general x10, matrix products, on_device(): jnp.dot(lax.dynamic_slice_in_dim(context, start, depth, 1), block, prefer...  6.16 us
  transfers between devices with their start and end apart: 16, of which 4 were waited for; matrix products, arithmetic and copies ran while one was open for 19% of the time, Pallas kernels for 0%

profile of v1, /device:TPU:0, one launch (start us, length us, event | category | flops | bytes accessed | tf_op | source)
XLA Modules:
  0.0 133.7 jit_solution(7173668300238546618)
XLA Ops:
  6.5 0.5 collective-permute-start.13
  7.0 1.1 constant_dynamic-slice_fusion
  8.2 1.3 collective-permute-start.2
  9.5 5.1 %collective-permute-start.1 = (bf16[512,256]{1,0:T(8,128)(2,1)S(1)}, bf16[512,256]{1,0:T(8,128)(2,1)S(1)}, u32[]{:S(2)}, u32[]{:S(2)}) collective-permute-start(bf16[512,256]{1,0:T(8,128)(2,1)S(1)} %pad_maximum_fusion.2), channel_id=1, source_target_pairs={{0,2},{1,3},{2,4},{3,5},{4,6},{5,7},{8,10},{9,11},{10,12},{11,13},... | collective-permute-start | bytes 786440 | tf_op jit(solution)/shard_map/ppermute | solution.py:49
  14.6 0.3 collective-permute-start
  15.1 16.2 %all_gather.6 = bf16[512,256]{1,0:T(8,128)(2,1)S(1)} all-gather(bf16[64,256]{1,0:T(8,128)(2,1)} %param.10), channel_id=1, replica_groups=mesh['dp'=4,'ctx'=8] {'ctx'}, dimensions={0}, use_global_device_ids=true | all-gather | bytes 294912 | tf_op jit(solution)/shard_map/all_gather | solution.py:63
  31.3 1.3 %fusion.42 = f32[512,256]{1,0:T(8,128)S(1)} fusion(bf16[512,4096]{1,0:T(8,128)(2,1)} %param.7, s32[]{:T(128)S(6)} %select_n.92, bf16[512,128]{1,0:T(8,128)(2,1)S(1)} %get-tuple-element.14, bf16[512,128]{1,0:T(8,128)(2,1)S(1)} %get-tuple-element.25), kind=kOutput, calls=%fused_computation.59 | convolution fusion | flops 134742016 | bytes 1310724 | tf_op jit(solution)/shard_map/dot_general | solution.py:74
  32.6 1.3 collective-permute-start.4
  33.9 4.6 %collective-permute-start.3 = (bf16[512,256]{1,0:T(8,128)(2,1)S(1)}, bf16[512,256]{1,0:T(8,128)(2,1)S(1)}, u32[]{:S(2)}, u32[]{:S(2)}) collective-permute-start(bf16[512,256]{1,0:T(8,128)(2,1)S(1)} %collective-permute-done), channel_id=1, source_target_pairs={{0,2},{1,3},{2,4},{3,5},{4,6},{5,7},{8,10},{9,11},{10,12},{11,13},... | collective-permute-start | bytes 786440 | tf_op jit(solution)/shard_map/ppermute | solution.py:49
  38.5 0.7 collective-permute-start.5
  39.2 1.3 collective-permute-start.6
  40.5 1.4 %fusion.38 = f32[512,256]{1,0:T(8,128)S(1)} fusion(bf16[512,256]{1,0:T(8,128)(2,1)S(1)} %collective-permute-done.2, bf16[512,4096]{1,0:T(8,128)(2,1)} %param.7, s32[]{:T(128)S(6)} %select_n.97), kind=kOutput, calls=%fused_computation.55 | convolution fusion | flops 134217728 | bytes 1310724 | tf_op jit(solution)/shard_map/dot_general | solution.py:74
  41.9 1.3 %convolution_add_fusion.8 = f32[512,256]{1,0:T(8,128)S(1)} fusion(f32[512,256]{1,0:T(8,128)S(1)} %fusion.42, bf16[512,256]{1,0:T(8,128)(2,1)S(1)} %collective-permute-done, bf16[512,4096]{1,0:T(8,128)(2,1)} %param.7, s32[]{:T(128)S(6)} %select_n.94), kind=kOutput, calls=%fused_computation.23 | convolution fusion | flops 134348800 | bytes 1835012 | tf_op jit(solution)/shard_map/dot_general | solution.py:74
  43.2 0.3 fusion.10
  43.5 11.5 %collective-permute-done.6 = bf16[512,256]{1,0:T(8,128)(2,1)S(1)} collective-permute-done((bf16[512,256]{1,0:T(8,128)(2,1)S(1)}, bf16[512,256]{1,0:T(8,128)(2,1)S(1)}, u32[]{:S(2)}, u32[]{:S(2)}) %collective-permute-start.6) | collective-permute-done | bytes 262176 | tf_op jit(solution)/shard_map/ppermute | solution.py:50
  55.0 1.3 collective-permute-start.10
  56.3 0.7 collective-permute-start.9
  57.0 0.7 collective-permute-start.7
  57.7 1.3 collective-permute-start.8
  59.0 0.3 fusion.35
  59.3 0.3 fusion.33
  59.6 0.3 fusion.9
  59.9 0.7 collective-permute-start.11
  60.6 10.1 %collective-permute-done.8 = bf16[512,256]{1,0:T(8,128)(2,1)S(1)} collective-permute-done((bf16[512,256]{1,0:T(8,128)(2,1)S(1)}, bf16[512,256]{1,0:T(8,128)(2,1)S(1)}, u32[]{:S(2)}, u32[]{:S(2)}) %collective-permute-start.8) | collective-permute-done | bytes 262176 | tf_op jit(solution)/shard_map/ppermute | solution.py:50
  70.7 1.3 collective-permute-start.12
  72.0 0.3 fusion.30
  72.3 0.3 fusion.7
  72.6 7.5 %collective-permute-done.12 = bf16[512,256]{1,0:T(8,128)(2,1)S(1)} collective-permute-done((bf16[512,256]{1,0:T(8,128)(2,1)S(1)}, bf16[512,256]{1,0:T(8,128)(2,1)S(1)}, u32[]{:S(2)}, u32[]{:S(2)}) %collective-permute-start.12) | collective-permute-done | bytes 262176 | tf_op jit(solution)/shard_map/ppermute | solution.py:50
  80.2 0.3 fusion.11
  80.5 1.3 %fusion.22 = f32[512,256]{1,0:T(8,128)S(1)} fusion(bf16[512,256]{1,0:T(8,128)(2,1)S(1)} %collective-permute-done.2, bf16[512,4096]{1,0:T(8,128)(2,1)} %collective-permute-done.13, s32[]{:T(128)S(6)} %select_n.97), kind=kOutput, calls=%fused_computation.39 | convolution fusion | flops 134217728 | bytes 1310724 | tf_op jit(solution)/shard_map/dot_general | solution.py:78
  81.9 1.3 %fusion.24 = f32[512,256]{1,0:T(8,128)S(1)} fusion(bf16[512,256]{1,0:T(8,128)(2,1)S(1)} %collective-permute-done.1, bf16[512,4096]{1,0:T(8,128)(2,1)} %collective-permute-done.13, s32[]{:T(128)S(6)} %select_n.96), kind=kOutput, calls=%fused_computation.41 | convolution fusion | flops 134217728 | bytes 1310724 | tf_op jit(solution)/shard_map/dot_general | solution.py:78
  83.2 1.3 %fusion.26 = f32[512,256]{1,0:T(8,128)S(1)} fusion(bf16[512,256]{1,0:T(8,128)(2,1)S(1)} %collective-permute-done, bf16[512,4096]{1,0:T(8,128)(2,1)} %collective-permute-done.13, s32[]{:T(128)S(6)} %select_n.94), kind=kOutput, calls=%fused_computation.43 | convolution fusion | flops 134217728 | bytes 1310724 | tf_op jit(solution)/shard_map/dot_general | solution.py:78
  84.6 1.3 %fusion.17 = f32[512,256]{1,0:T(8,128)S(1)} fusion(bf16[512,4096]{1,0:T(8,128)(2,1)} %collective-permute-done.13, s32[]{:T(128)S(6)} %select_n.101, bf16[512,256]{1,0:T(8,128)(2,1)S(1)} %collective-permute-done.5, bf16[512,256]{1,0:T(8,128)(2,1)S(1)} %collective-permute-done.6, pred[]{:T(512)S(6)} %ge.8), kind=kOutput, calls=%fused_computation.34 | convolution fusion | flops 134348800 | bytes 1572869 | tf_op jit(solution)/shard_map/dot_general | solution.py:78
  85.9 1.3 %fusion.14 = f32[512,256]{1,0:T(8,128)S(1)} fusion(bf16[512,4096]{1,0:T(8,128)(2,1)} %collective-permute-done.13, s32[]{:T(128)S(6)} %select_n.107, bf16[512,256]{1,0:T(8,128)(2,1)S(1)} %collective-permute-done.9, bf16[512,256]{1,0:T(8,128)(2,1)S(1)} %collective-permute-done.10, pred[]{:T(512)S(6)} %ge.9), kind=kOutput, calls=%fused_computation.31 | convolution fusion | flops 134348800 | bytes 1572869 | tf_op jit(solution)/shard_map/dot_general | solution.py:78
  87.3 1.3 %fusion.19 = f32[512,256]{1,0:T(8,128)S(1)} fusion(bf16[512,256]{1,0:T(8,128)(2,1)S(1)} %collective-permute-done.4, bf16[512,4096]{1,0:T(8,128)(2,1)} %collective-permute-done.13, s32[]{:T(128)S(6)} %select_n.99), kind=kOutput, calls=%fused_computation.36 | convolution fusion | flops 134217728 | bytes 1310724 | tf_op jit(solution)/shard_map/dot_general | solution.py:78
  88.6 1.3 %fusion.6 = f32[512,256]{1,0:T(8,128)S(1)} fusion(f32[512,256]{1,0:T(8,128)S(1)} %fusion.22, f32[512,256]{1,0:T(8,128)S(1)} %fusion.24, f32[512,256]{1,0:T(8,128)S(1)} %fusion.26, bf16[512,4096]{1,0:T(8,128)(2,1)} %collective-permute-done.13, s32[]{:T(128)S(6)} %select_n.92, bf16[512,128]{1,0:T(8,128)(2,1)S(1)} %get-tuple-element.14, ...), kind=kOutput, calls=%fused_computation.14 | convolution fusion | flops 135135232 | bytes 2883588 | tf_op jit(solution)/shard_map/dot_general | solution.py:78
  90.0 1.3 %fusion.4 = f32[512,256]{1,0:T(8,128)S(1)} fusion(f32[512,256]{1,0:T(8,128)S(1)} %fusion.17, f32[512,256]{1,0:T(8,128)S(1)} %fusion.19, f32[512,256]{1,0:T(8,128)S(1)} %fusion.6, bf16[512,256]{1,0:T(8,128)(2,1)S(1)} %collective-permute-done.3, bf16[512,4096]{1,0:T(8,128)(2,1)} %collective-permute-done.13, s32[]{:T(128)S(6)} %select_n.98), kind=kOutput, calls=%fused_computation.11 | convolution fusion | flops 134610944 | bytes 2883588 | tf_op jit(solution)/shard_map/dot_general | solution.py:78
  91.3 1.3 %fusion.2 = f32[512,256]{1,0:T(8,128)S(1)} fusion(f32[512,256]{1,0:T(8,128)S(1)} %fusion.14, f32[512,256]{1,0:T(8,128)S(1)} %fusion.4, bf16[512,4096]{1,0:T(8,128)(2,1)} %collective-permute-done.13, s32[]{:T(128)S(6)} %select_n.104, bf16[512,256]{1,0:T(8,128)(2,1)S(1)} %collective-permute-done.7, bf16[512,256]{1,0:T(8,128)(2,1)S(1)} %collective-permute-done.8, ...), kind=kOutput, calls=%fused_computation.8 | convolution fusion | flops 134610944 | bytes 2621445 | tf_op jit(solution)/shard_map/dot_general | solution.py:78
  92.7 1.4 %fusion.12 = bf16[512,256]{1,0:T(8,128)(2,1)S(1)} fusion(f32[512,256]{1,0:T(8,128)S(1)} %fusion.2, bf16[512,4096]{1,0:T(8,128)(2,1)} %collective-permute-done.13, s32[]{:T(128)S(6)} %select_n.110, bf16[512,256]{1,0:T(8,128)(2,1)S(1)} %collective-permute-done.11, bf16[512,256]{1,0:T(8,128)(2,1)S(1)} %collective-permute-done.12, pred[]{:T(512)S(6)} %ge.9), kind=kOutput, calls=%fused_computation.25 | convolution fusion | flops 134610944 | bytes 1835013 | tf_op jit(solution)/shard_map/dot_general | solution.py:78
  94.1 0.5 fusion.1
  94.5 0.1 reduce_max.21
  94.6 0.7 convert_reduce_fusion
  95.3 0.3 convolution_convert_fusion.1
  95.6 0.1 copy.40
  95.7 0.1 reduce_sum.71
  95.8 0.2 copy.44
  96.0 0.2 copy.45
  96.2 0.2 copy.46
  96.3 0.2 copy.41
  96.5 0.2 copy.42
  96.7 0.2 copy.43
  96.9 1.1 concatenate.24
  98.0 3.4 %all-to-all-start = ((bf16[8,1,144,64]{2,3,1,0:T(8,128)(2,1)}), bf16[8,1,144,64]{2,3,1,0:T(8,128)(2,1)S(1)}, u32[]{:S(2)}, u32[]{:S(2)}) async-start(bf16[8,1,144,64]{2,3,1,0:T(8,128)(2,1)} %bitcast.2), calls=%async_computation | async-start | bytes 524288 | tf_op jit(solution)/shard_map/all_to_all | solution.py:112
  101.5 9.6 %all-to-all-done = bf16[8,1,144,64]{2,3,1,0:T(8,128)(2,1)S(1)} async-done(((bf16[8,1,144,64]{2,3,1,0:T(8,128)(2,1)}), bf16[8,1,144,64]{2,3,1,0:T(8,128)(2,1)S(1)}, u32[]{:S(2)}, u32[]{:S(2)}) %all-to-all-start) | async-done | bytes 147488 | tf_op jit(solution)/shard_map/all_to_all | solution.py:112
  111.1 0.3 slice_reduce_fusion
  111.5 0.1 copy.49
  111.6 0.1 fusion.46
  111.8 0.2 multiply_reduce_fusion
  112.0 0.1 copy.50
  112.1 0.1 mul.148
  112.2 0.1 div.38
  112.3 2.1 %convolution_convert_fusion = bf16[64,4096]{1,0:T(8,128)(2,1)S(1)} fusion(bf16[256,4096]{1,0:T(8,128)(2,1)} %all-gather.2.cloned.1.call-done, f32[8,8,2,128]{3,2,1,0:T(2,128)S(1)} %bitcast.56, f32[8,8,2,128]{3,2,1,0:T(2,128)S(1)} %bitcast.57, f32[256]{0:T(256)S(1)} %convert_element_type.203, f32[2,128,64]{1,2,0:T(8,128)S(1)} %fusion.46), kind=kOutput, calls=%fused_computation | convolution fusion | flops 134545408 | bytes 2819072 | tf_op jit(solution)/shard_map/dot_general | solution.py:125
  114.5 11.6 %all_to_all.10 = bf16[4,64,1024]{2,1,0:T(8,128)(2,1)S(1)} all-to-all(bf16[4,64,1024]{2,1,0:T(8,128)(2,1)S(1)} %bitcast.53), channel_id=1, replica_groups=mesh['dp'=4,'ctx'=8] {'dp'}, dimensions={0} | all-to-all | bytes 1048576 | tf_op jit(solution)/shard_map/all_to_all | solution.py:130
  126.1 0.7 reduce_sum.78
  (33 shorter events, 0.3 us)
Async XLA Ops:
  6.5 105.5 %all-gather.2.cloned.1.call-start = ((), (), s32[]{:S(2)}) async-start(), calls=%async_computation.2 | async-start | bytes 2359296 | tf_op jit(solution)/shard_map/all_gather | solution.py:89
  6.5 74.0 %collective-permute-start.13 = (bf16[512,4096]{1,0:T(8,128)(2,1)}, bf16[512,4096]{1,0:T(8,128)(2,1)}, u32[]{:S(2)}, u32[]{:S(2)}) collective-permute-start(bf16[512,4096]{1,0:T(8,128)(2,1)} %param.7), channel_id=1, source_target_pairs={{0,1},{1,0},{2,3},{3,2},{4,5},{5,4},{6,7},{7,6},{8,9},{9,8},{10,11... | collective-permute-start | bytes 12582920 | tf_op jit(solution)/shard_map/ppermute | solution.py:62
  8.2 31.0 %collective-permute-start.2 = (bf16[512,256]{1,0:T(8,128)(2,1)S(1)}, bf16[512,256]{1,0:T(8,128)(2,1)S(1)}, u32[]{:S(2)}, u32[]{:S(2)}) collective-permute-start(bf16[512,256]{1,0:T(8,128)(2,1)S(1)} %pad_maximum_fusion.2), channel_id=1, source_target_pairs={{2,0},{3,1},{4,2},{5,3},{6,4},{7,5},{10,8},{11,9},{12,10},{13,11},... | collective-permute-start | bytes 786440 | tf_op jit(solution)/shard_map/ppermute | solution.py:50
  9.5 29.0 %collective-permute-start.1 = (bf16[512,256]{1,0:T(8,128)(2,1)S(1)}, bf16[512,256]{1,0:T(8,128)(2,1)S(1)}, u32[]{:S(2)}, u32[]{:S(2)}) collective-permute-start(bf16[512,256]{1,0:T(8,128)(2,1)S(1)} %pad_maximum_fusion.2), channel_id=1, source_target_pairs={{0,2},{1,3},{2,4},{3,5},{4,6},{5,7},{8,10},{9,11},{10,12},{11,13},... | collective-permute-start | bytes 786440 | tf_op jit(solution)/shard_map/ppermute | solution.py:49
  14.6 18.0 %collective-permute-start = (bf16[512,256]{1,0:T(8,128)(2,1)S(1)}, bf16[512,256]{1,0:T(8,128)(2,1)S(1)}, u32[]{:S(2)}, u32[]{:S(2)}) collective-permute-start(bf16[512,256]{1,0:T(8,128)(2,1)S(1)} %pad_maximum_fusion.3), channel_id=1, source_target_pairs={{0,1},{1,0},{2,3},{3,2},{4,5},{5,4},{6,7},{7,6},{8,9},{9,8},{10,11... | collective-permute-start | bytes 786440 | tf_op jit(solution)/shard_map/ppermute | solution.py:61
  15.1 28.1 %copy-start = (bf16[512,4096]{1,0:T(8,128)(2,1)S(1)}, bf16[512,4096]{1,0:T(8,128)(2,1)}, u32[]{:S(2)}) copy-start(bf16[512,4096]{1,0:T(8,128)(2,1)} %param.7) | copy-start | bytes 12582916
  32.6 25.1 %collective-permute-start.4 = (bf16[512,256]{1,0:T(8,128)(2,1)S(1)}, bf16[512,256]{1,0:T(8,128)(2,1)S(1)}, u32[]{:S(2)}, u32[]{:S(2)}) collective-permute-start(bf16[512,256]{1,0:T(8,128)(2,1)S(1)} %collective-permute-done), channel_id=1, source_target_pairs={{2,0},{3,1},{4,2},{5,3},{6,4},{7,5},{10,8},{11,9},{12,10},{13,11},... | collective-permute-start | bytes 786440 | tf_op jit(solution)/shard_map/ppermute | solution.py:50
  33.9 23.1 %collective-permute-start.3 = (bf16[512,256]{1,0:T(8,128)(2,1)S(1)}, bf16[512,256]{1,0:T(8,128)(2,1)S(1)}, u32[]{:S(2)}, u32[]{:S(2)}) collective-permute-start(bf16[512,256]{1,0:T(8,128)(2,1)S(1)} %collective-permute-done), channel_id=1, source_target_pairs={{0,2},{1,3},{2,4},{3,5},{4,6},{5,7},{8,10},{9,11},{10,12},{11,13},... | collective-permute-start | bytes 786440 | tf_op jit(solution)/shard_map/ppermute | solution.py:49
  38.5 17.8 %collective-permute-start.5 = (bf16[512,256]{1,0:T(8,128)(2,1)S(1)}, bf16[512,256]{1,0:T(8,128)(2,1)S(1)}, u32[]{:S(2)}, u32[]{:S(2)}) collective-permute-start(bf16[512,256]{1,0:T(8,128)(2,1)S(1)} %collective-permute-done.1), channel_id=1, source_target_pairs={{2,4},{3,5},{4,6},{5,7},{10,12},{11,13},{12,14},{13,15},{18,20},{1... | collective-permute-start | bytes 786440 | tf_op jit(solution)/shard_map/ppermute | solution.py:49
  39.2 15.8 %collective-permute-start.6 = (bf16[512,256]{1,0:T(8,128)(2,1)S(1)}, bf16[512,256]{1,0:T(8,128)(2,1)S(1)}, u32[]{:S(2)}, u32[]{:S(2)}) collective-permute-start(bf16[512,256]{1,0:T(8,128)(2,1)S(1)} %collective-permute-done.2), channel_id=1, source_target_pairs={{2,0},{3,1},{4,2},{5,3},{10,8},{11,9},{12,10},{13,11},{18,16},{19,... | collective-permute-start | bytes 786440 | tf_op jit(solution)/shard_map/ppermute | solution.py:50
  55.0 17.0 %collective-permute-start.10 = (bf16[512,256]{1,0:T(8,128)(2,1)S(1)}, bf16[512,256]{1,0:T(8,128)(2,1)S(1)}, u32[]{:S(2)}, u32[]{:S(2)}) collective-permute-start(bf16[512,256]{1,0:T(8,128)(2,1)S(1)} %collective-permute-done.6), channel_id=1, source_target_pairs={{2,0},{3,1},{10,8},{11,9},{18,16},{19,17},{26,24},{27,25}} | collective-permute-start | bytes 786440 | tf_op jit(solution)/shard_map/ppermute | solution.py:50
  56.3 15.7 %collective-permute-start.9 = (bf16[512,256]{1,0:T(8,128)(2,1)S(1)}, bf16[512,256]{1,0:T(8,128)(2,1)S(1)}, u32[]{:S(2)}, u32[]{:S(2)}) collective-permute-start(bf16[512,256]{1,0:T(8,128)(2,1)S(1)} %collective-permute-done.5), channel_id=1, source_target_pairs={{4,6},{5,7},{12,14},{13,15},{20,22},{21,23},{28,30},{29,31}} | collective-permute-start | bytes 786440 | tf_op jit(solution)/shard_map/ppermute | solution.py:49
  57.0 2.9 %collective-permute-start.7 = (bf16[512,256]{1,0:T(8,128)(2,1)S(1)}, bf16[512,256]{1,0:T(8,128)(2,1)S(1)}, u32[]{:S(2)}, u32[]{:S(2)}) collective-permute-start(bf16[512,256]{1,0:T(8,128)(2,1)S(1)} %collective-permute-done.3), channel_id=1, source_target_pairs={{2,4},{3,5},{4,6},{5,7},{10,12},{11,13},{12,14},{13,15},{18,20},{1... | collective-permute-start | bytes 786440 | tf_op jit(solution)/shard_map/ppermute | solution.py:49
  57.7 13.0 %collective-permute-start.8 = (bf16[512,256]{1,0:T(8,128)(2,1)S(1)}, bf16[512,256]{1,0:T(8,128)(2,1)S(1)}, u32[]{:S(2)}, u32[]{:S(2)}) collective-permute-start(bf16[512,256]{1,0:T(8,128)(2,1)S(1)} %collective-permute-done.4), channel_id=1, source_target_pairs={{2,0},{3,1},{4,2},{5,3},{10,8},{11,9},{12,10},{13,11},{18,16},{19,... | collective-permute-start | bytes 786440 | tf_op jit(solution)/shard_map/ppermute | solution.py:50
  59.9 12.7 %collective-permute-start.11 = (bf16[512,256]{1,0:T(8,128)(2,1)S(1)}, bf16[512,256]{1,0:T(8,128)(2,1)S(1)}, u32[]{:S(2)}, u32[]{:S(2)}) collective-permute-start(bf16[512,256]{1,0:T(8,128)(2,1)S(1)} %collective-permute-done.7), channel_id=1, source_target_pairs={{4,6},{5,7},{12,14},{13,15},{20,22},{21,23},{28,30},{29,31}} | collective-permute-start | bytes 786440 | tf_op jit(solution)/shard_map/ppermute | solution.py:49
  70.7 9.5 %collective-permute-start.12 = (bf16[512,256]{1,0:T(8,128)(2,1)S(1)}, bf16[512,256]{1,0:T(8,128)(2,1)S(1)}, u32[]{:S(2)}, u32[]{:S(2)}) collective-permute-start(bf16[512,256]{1,0:T(8,128)(2,1)S(1)} %collective-permute-done.8), channel_id=1, source_target_pairs={{2,0},{3,1},{10,8},{11,9},{18,16},{19,17},{26,24},{27,25}} | collective-permute-start | bytes 786440 | tf_op jit(solution)/shard_map/ppermute | solution.py:50
  90.0 4.1 %copy-start.1 = (s32[512]{0:T(512)S(1)}, s32[512]{0:T(512)}, u32[]{:S(2)}) copy-start(s32[512]{0:T(512)} %param.11) | copy-start | bytes 6148
  94.5 6.9 %copy-start.2 = (bf16[256]{0:T(256)(128)(2,1)S(1)}, bf16[256]{0:T(256)(128)(2,1)}, u32[]{:S(2)}) copy-start(bf16[256]{0:T(256)(128)(2,1)} %param.12) | copy-start | bytes 1540
  98.0 13.1 %all-to-all-start = ((bf16[8,1,144,64]{2,3,1,0:T(8,128)(2,1)}), bf16[8,1,144,64]{2,3,1,0:T(8,128)(2,1)S(1)}, u32[]{:S(2)}, u32[]{:S(2)}) async-start(bf16[8,1,144,64]{2,3,1,0:T(8,128)(2,1)} %bitcast.2), calls=%async_computation | async-start | bytes 524288 | tf_op jit(solution)/shard_map/all_to_all | solution.py:112
Sparse Core Ops, SparseCore 0:
  15.1 33.0 all-gather.1

commit v2 on v0

v2 whole, which is shorter than its diff:
```python
import functools
import math

import jax
import jax.numpy as jnp
from jax import lax
from jax.experimental import pallas as pl
from jax.experimental.pallas import tpu as pltpu
from jax.sharding import PartitionSpec as P

DH = 128
NEGATIVE = -1e30
CORES = 2
STATS = 16
VMEM = pl.BlockSpec(memory_space=pltpu.VMEM)
SMEM = pl.BlockSpec(memory_space=pltpu.SMEM)
ANY = pl.BlockSpec(memory_space=pl.ANY)
PARAMS = pltpu.CompilerParams(vmem_limit_bytes=40 * 2**20)


def three_parts(value):
    high = value.astype(jnp.bfloat16).astype(jnp.float32)
    rest = value - high
    middle = rest.astype(jnp.bfloat16).astype(jnp.float32)
    low = (rest - middle).astype(jnp.bfloat16).astype(jnp.float32)
    return [high, middle, low]


def start_slices(starts_ref, contexts, buffer, sems, count, depth):
    copies = []
    for b in range(count):
        for part in range(CORES):
            first = pl.multiple_of(starts_ref[b * CORES + part], DH)
            for which in range(CORES):
                slot = (b * CORES + part) * CORES + which
                copies.append(
                    pltpu.make_async_copy(
                        contexts[which].at[:, pl.ds(first, depth)], buffer.at[slot], sems.at[slot]
                    )
                )
    for copy in copies:
        copy.start()
    return copies


def add_products(copies, buffer, blocks, acc_ref, rows, depth, piece, fresh):
    for b, block in enumerate(blocks):
        for part in range(CORES):
            weight = block[part * piece : part * piece + depth, :]
            for which in range(CORES):
                slot = (b * CORES + part) * CORES + which
                copies[slot].wait()
                product = jnp.dot(buffer[slot], weight, preferred_element_type=jnp.float32)
                place = slice(which * rows, (which + 1) * rows)
                if fresh and b == 0 and part == 0:
                    acc_ref[place, :] = product
                else:
                    acc_ref[place, :] += product


def project_kernel(count, has_acc, depth, piece, *refs):
    starts_ref, own_ref, sibling_ref = refs[:3]
    blocks = refs[3 : 3 + count]
    acc_in = refs[3 + count] if has_acc else None
    acc_ref, buffer, sems = refs[-3:]
    rows = own_ref.shape[0]
    copies = start_slices(starts_ref, (own_ref, sibling_ref), buffer, sems, count, depth)
    if has_acc:
        acc_ref[...] = acc_in[...]
    add_products(copies, buffer, blocks, acc_ref, rows, depth, piece, not has_acc)


def project(starts, own, sibling, blocks, acc, depth, piece):
    count = len(blocks)
    rows = own.shape[0]
    width = blocks[0].shape[1]
    operands = [starts, own, sibling, *blocks] + ([acc] if acc is not None else [])
    return pl.pallas_call(
        functools.partial(project_kernel, count, acc is not None, depth, piece),
        out_shape=jax.ShapeDtypeStruct((CORES * rows, width), jnp.float32),
        in_specs=[SMEM, ANY, ANY] + [VMEM] * (len(operands) - 3),
        out_specs=VMEM,
        scratch_shapes=[
            pltpu.VMEM((count * CORES * CORES, rows, depth), own.dtype),
            pltpu.SemaphoreType.DMA((count * CORES * CORES,)),
        ],
        compiler_params=PARAMS,
        cost_estimate=pl.CostEstimate(
            flops=2 * count * CORES * CORES * rows * depth * width,
            bytes_accessed=2 * count * CORES * CORES * rows * depth,
            transcendentals=0,
        ),
    )(*operands)


def attend_kernel(chips, heads, depth, piece, *refs):
    starts_ref, firsts_ref, own_ref, sibling_ref = refs[:4]
    blocks = refs[4 : 4 + chips]
    acc_in, offsets_ref = refs[4 + chips : 6 + chips]
    messages = refs[6 + chips : 6 + 2 * chips]
    acc_ref, buffer, sems = refs[6 + 2 * chips :]
    rows = own_ref.shape[0]
    half = heads * DH
    copies = start_slices(starts_ref, (own_ref, sibling_ref), buffer, sems, 1, depth)
    acc_ref[...] = acc_in[...]
    add_products(copies, buffer, blocks[-1:], acc_ref, rows, depth, piece, False)
    score_scale = 1.0 / math.sqrt(DH)
    line = lax.broadcasted_iota(jnp.int32, (CORES * rows, 1), 0)
    positions = jnp.where(line < rows, firsts_ref[0] + line, firsts_ref[1] + line - rows)
    for h in range(heads):
        keys = acc_ref[:, h * DH : (h + 1) * DH].astype(jnp.bfloat16)
        values = acc_ref[:, half + h * DH : half + (h + 1) * DH].T.astype(jnp.bfloat16)
        for j in range(chips):
            parts = []
            for part in range(CORES):
                lines = slice(part * piece + depth, (part + 1) * piece)
                parts.append(blocks[j][lines, h * DH : (h + 1) * DH])
                parts.append(blocks[j][lines, half + h * DH : half + (h + 1) * DH])
            query = jnp.concatenate(parts, axis=0)
            scores = lax.dot_general(
                keys, query, (((1,), (1,)), ((), ())), preferred_element_type=jnp.float32
            ) * score_scale
            live = positions <= offsets_ref[j : j + 1, :]
            masked = jnp.where(live, scores, NEGATIVE)
            peak = jnp.max(masked, axis=0, keepdims=True)
            weights = jnp.where(live, jnp.exp(masked - peak), 0.0).astype(jnp.bfloat16)
            total = jnp.sum(weights.astype(jnp.float32), axis=0, keepdims=True)
            numerator = jnp.dot(values, weights, preferred_element_type=jnp.float32)
            stats = three_parts(peak) + three_parts(total)
            stats.append(jnp.zeros((STATS - len(stats), peak.shape[1]), jnp.float32))
            base = h * (DH + STATS)
            messages[j][base : base + DH, :] = numerator.astype(jnp.bfloat16)
            messages[j][base + DH : base + DH + STATS, :] = jnp.concatenate(stats, axis=0).astype(
                jnp.bfloat16
            )


def attend(starts, firsts, own, sibling, blocks, acc, offset_groups, heads, depth, piece):
    chips = len(blocks)
    rows, width = own.shape[0], blocks[0].shape[1]
    group = offset_groups.shape[1]
    message = jax.ShapeDtypeStruct((heads * (DH + STATS), group), jnp.bfloat16)
    return pl.pallas_call(
        functools.partial(attend_kernel, chips, heads, depth, piece),
        out_shape=[message] * chips,
        in_specs=[SMEM, SMEM, ANY, ANY] + [VMEM] * (chips + 2),
        out_specs=[VMEM] * chips,
        scratch_shapes=[
            pltpu.VMEM((CORES * rows, width), jnp.float32),
            pltpu.VMEM((CORES * CORES, rows, depth), own.dtype),
            pltpu.SemaphoreType.DMA((CORES * CORES,)),
        ],
        compiler_params=PARAMS,
        cost_estimate=pl.CostEstimate(
            flops=8 * CORES * rows * group * chips * heads * DH,
            bytes_accessed=2 * CORES * CORES * rows * depth,
            transcendentals=CORES * rows * group * chips * heads,
        ),
    )(starts, firsts, own, sibling, *blocks, acc, offset_groups)


def combine_kernel(chips, heads, count, *refs):
    messages, gain_ref = refs[:chips], refs[chips]
    own_ref, other_ref = refs[chips + 1 :]
    for h in range(heads):
        base = h * (DH + STATS)
        peaks, totals = [], []
        for j in range(chips):
            stats = messages[j][base + DH : base + DH + STATS, :].astype(jnp.float32)
            peaks.append(stats[0:1] + stats[1:2] + stats[2:3])
            totals.append(stats[3:4] + stats[4:5] + stats[5:6])
        top = functools.reduce(jnp.maximum, peaks)
        total, numerator = 0.0, 0.0
        for j in range(chips):
            scale = jnp.exp(peaks[j] - top)
            total += totals[j] * scale
            numerator += messages[j][base : base + DH, :].astype(jnp.float32) * scale
        attended = numerator / total
        mean_square = jnp.mean(attended * attended, axis=0, keepdims=True)
        normed = (attended * lax.rsqrt(mean_square + 1e-05)).T
        normed = (normed * gain_ref[:, h * DH : (h + 1) * DH].astype(jnp.float32)).astype(jnp.bfloat16)
        own_ref[:, h * DH : (h + 1) * DH] = normed[:count]
        other_ref[:, h * DH : (h + 1) * DH] = normed[count:]


def combine(messages, gain, heads, count):
    chips = len(messages)
    out = jax.ShapeDtypeStruct((count, heads * DH), jnp.bfloat16)
    return pl.pallas_call(
        functools.partial(combine_kernel, chips, heads, count),
        out_shape=[out, out],
        in_specs=[VMEM] * (chips + 1),
        out_specs=[VMEM, VMEM],
        compiler_params=PARAMS,
    )(*messages, gain)


def output_kernel(n_dp, wide, place_ref, own_ref, sibling_ref, w_ref, *refs):
    terms, (buffer, sems) = refs[:n_dp], refs[n_dp:]
    half = own_ref.shape[1]
    copies = []
    for i in range(n_dp):
        first = pl.multiple_of((place_ref[0] ^ i) * wide, DH)
        copies.append(
            pltpu.make_async_copy(w_ref.at[:, pl.ds(first, wide)], buffer.at[i], sems.at[i])
        )
        copies[-1].start()
    mine = pl.multiple_of(place_ref[1] * half, DH)
    other = pl.multiple_of((1 - place_ref[1]) * half, DH)
    for i in range(n_dp):
        copies[i].wait()
        total = jnp.dot(own_ref[...], buffer[i, pl.ds(mine, half), :], preferred_element_type=jnp.float32)
        total += jnp.dot(
            sibling_ref[...], buffer[i, pl.ds(other, half), :], preferred_element_type=jnp.float32
        )
        terms[i][...] = total.astype(jnp.bfloat16)


def output_terms(place, own, sibling, w_all, n_dp):
    wide = w_all.shape[1] // n_dp
    term = jax.ShapeDtypeStruct((own.shape[0], wide), jnp.bfloat16)
    return pl.pallas_call(
        functools.partial(output_kernel, n_dp, wide),
        out_shape=[term] * n_dp,
        in_specs=[SMEM, VMEM, VMEM, ANY],
        out_specs=[VMEM] * n_dp,
        scratch_shapes=[
            pltpu.VMEM((n_dp, w_all.shape[0], wide), w_all.dtype),
            pltpu.SemaphoreType.DMA((n_dp,)),
        ],
        compiler_params=PARAMS,
    )(place, own, sibling, w_all)


def on_device(n_dp, n_ctx, context, w_key, w_value, queries, offsets, head_gain, w_out):
    chips = n_ctx // CORES
    rows = context.shape[0]
    depth, panel = w_key.shape
    half = panel // CORES
    heads = half // DH
    lat_count = queries.shape[0]
    me = lax.axis_index("ctx")
    chip, core = me // CORES, lax.rem(me, CORES)

    def swap(array):
        return lax.ppermute(array, "ctx", [(i, i ^ 1) for i in range(n_ctx)])

    def across(array, bits):
        return lax.ppermute(array, "ctx", [(i, i ^ (bits * CORES)) for i in range(n_ctx)])

    def columns(array, which):
        return lax.dynamic_slice_in_dim(array, which * half, half, 1)

    def half_block(which):
        query = columns(queries, which)
        return jnp.concatenate(
            [
                jnp.concatenate([columns(w_key, which), columns(w_value, which)], axis=1),
                jnp.concatenate([query[: lat_count // 2], query[lat_count // 2 :]], axis=1),
            ],
            axis=0,
        )

    piece = depth + lat_count // 2
    sibling_part = swap(half_block(1 - core))
    context_sibling = swap(context)
    blocks = [jnp.concatenate([half_block(core), sibling_part], axis=0)]
    for j in range(1, chips):
        low = j & -j
        blocks.append(across(blocks[j ^ low], low))
    w_all = lax.all_gather(w_out, "ctx", axis=1, tiled=True)

    sources = [chip ^ j for j in range(chips)]
    starts = [
        (source * CORES + who) * depth for source in sources for who in (core, 1 - core)
    ]

    def starts_of(first, last):
        return jnp.stack(starts[first * CORES : last * CORES]).astype(jnp.int32)

    acc = project(starts_of(0, 1), context, context_sibling, blocks[:1], None, depth, piece)
    acc = project(
        starts_of(1, chips - 1), context, context_sibling, blocks[1:-1], acc, depth, piece
    )
    offset_groups = jnp.stack(
        [
            jnp.concatenate(
                [
                    lax.dynamic_slice_in_dim(offsets, (source * CORES + who) * lat_count, lat_count)
                    for who in (core, 1 - core)
                ]
            )
            for source in sources
        ]
    )
    firsts = jnp.stack([me * rows, (me + 1 - 2 * core) * rows]).astype(jnp.int32)
    messages = attend(
        starts_of(chips - 1, chips), firsts, context, context_sibling, blocks, acc, offset_groups,
        heads, depth, piece,
    )
    arrived = [messages[0]] + [across(messages[j], j) for j in range(1, chips)]
    gain = lax.dynamic_slice_in_dim(head_gain, core * half, half).reshape(1, half)
    normed_own, normed_other = combine(arrived, gain, heads, lat_count)
    normed_sibling = swap(normed_other)
    mine_dp = lax.axis_index("dp")
    terms = output_terms(
        jnp.stack([mine_dp, core]).astype(jnp.int32), normed_own, normed_sibling, w_all, n_dp
    )
    total = terms[0].astype(jnp.float32)
    for i in range(1, n_dp):
        total += lax.ppermute(terms[i], "dp", [(d, d ^ i) for d in range(n_dp)]).astype(jnp.float32)
    return total.astype(jnp.bfloat16)


def solution(mesh):
    n_dp, n_ctx = mesh.shape["dp"], mesh.shape["ctx"]
    placed = (
        P("ctx", None),
        P("ctx", "dp"),
        P("ctx", "dp"),
        P("ctx", "dp"),
        P(),
        P("dp"),
        P("dp", "ctx"),
    )

    def body(*args):
        return on_device(n_dp, n_ctx, *args)

    return jax.shard_map(
        body, mesh=mesh, in_specs=placed, out_specs=P("ctx", "dp"), check_vma=False
    )
```

time: 196 us -> 111 us (0.57)
  waiting for transfers between devices: 163 us -> 61.6 us
  matrix products: 16 us -> 0 us
  starting transfers between devices: 0.2 us -> 15.4 us
  Pallas kernels: 0 us -> 13.1 us
  local copies, waits for them, and re-layouts: 0.02 us -> 5.84 us
    all_gather x5 -> x1, waiting for transfers between devices: 136 us -> 0.01 us  [on_device(): w_all = lax.all_gather(w_out, 'ctx', axis=1, tiled=True)]
    ppermute x0 -> x12, waiting for transfers between devices: none -> 61.3 us  [the longest x6 49.7 us: across(): lax.ppermute(array, 'ctx', [(i, i ^ bits * CORES) for i in range(n_ctx)])]
    reduce_scatter x1 -> x0, waiting for transfers between devices: 24.4 us -> none  [on_device(): lax.psum_scatter(out_terms.astype(jnp.bfloat16), 'dp', scatter_dimension=...]
    dot_general x5 -> x0, matrix products: 16 us -> none  [the longest x1 4.83 us: on_device(): key_sum = jnp.dot(context, pieces[0], preferred_element_type=jnp.float32)]
    ppermute x0 -> x12, starting transfers between devices: none -> 15.4 us  [the longest x6 10.8 us: across(): lax.ppermute(array, 'ctx', [(i, i ^ bits * CORES) for i in range(n_ctx)])]
    pallas_call x0 -> x5, Pallas kernels: none -> 13.1 us  [the longest x2 6.94 us: project(): pl.pallas_call(functools.partial(project_kernel, count, acc is not None,...]
    unnamed x4 -> x8, local copies, waits for them, and re-layouts: 0.01 us -> 3.78 us
  transfers between devices with their start and end apart: 6 -> 13, of which waited for: 6 -> 9; matrix products, arithmetic and copies ran while one was open for 8% -> 2% of each run, Pallas kernels for 0% -> 10%
where the time goes in v2:
time: 111 us
  waiting for transfers between devices  61.6 us (55%)
  starting transfers between devices  15.4 us (14%)
  between operations  13.5 us (12%)
  Pallas kernels  13.1 us (12%)
  local copies, waits for them, and re-layouts  5.84 us (5%)
  other arithmetic  1.28 us (1%)
    ppermute x6, waiting for transfers between devices, across(): lax.ppermute(array, 'ctx', [(i, i ^ bits * CORES) for i in range(n_ctx)])  49.7 us
    ppermute x6, starting transfers between devices, across(): lax.ppermute(array, 'ctx', [(i, i ^ bits * CORES) for i in range(n_ctx)])  10.8 us
    pallas_call x2, Pallas kernels, project(): pl.pallas_call(functools.partial(project_kernel, count, acc is not None,...  6.94 us
    ppermute x3, waiting for transfers between devices, on_device(): lax.ppermute(terms[i], 'dp', [(d, d ^ i) for d in range(n_dp)])  6.11 us
    ppermute x3, waiting for transfers between devices, swap(): return lax.ppermute(array, 'ctx', [(i, i ^ 1) for i in range(n_ctx)])  5.53 us
    pallas_call x1, Pallas kernels, attend(): pl.pallas_call(functools.partial(attend_kernel, chips, heads, depth, piec...  4.33 us
    unnamed x8, local copies, waits for them, and re-layouts  3.78 us
    ppermute x3, starting transfers between devices, on_device(): lax.ppermute(terms[i], 'dp', [(d, d ^ i) for d in range(n_dp)])  3.55 us
  transfers between devices with their start and end apart: 13, of which 9 were waited for; matrix products, arithmetic and copies ran while one was open for 2% of the time, Pallas kernels for 10%

profile of v2, /device:TPU:0, one launch (start us, length us, event | category | flops | bytes accessed | tf_op | source)
XLA Modules:
  0.0 110.7 jit_solution(12670826847741820911)
XLA Ops:
  6.5 0.0 copy-start
  6.5 0.0 all-gather.2.cloned.1.call-start
  6.5 0.5 collective-permute-start
  7.0 0.3 all-gather.2.cloned.1.call-update
  7.3 0.8 constant_dynamic-slice_fusion
  8.0 1.1 %constant_dynamic-slice_fusion.4 = (bf16[512,128]{1,0:T(8,128)(2,1)S(1)}, bf16[512,128]{1,0:T(8,128)(2,1)S(1)}, bf16[512,128]{1,0:T(8,128)(2,1)S(1)}, bf16[512,128]{1,0:T(8,128)(2,1)S(1)}) fusion(bf16[512,256]{1,0:T(8,128)(2,1)} %param.9, s32[]{:T(128)S(6)} %select_n.41, s32[]{:T(128)S(6)} %select_n.42, bf16[512,256]{1,0:T(8,128)(2,1)} %param.8), kind=kLoop, calls=%fused_computation.8 | loop fusion | bytes 1048584 | tf_op jit(solution)/shard_map/dynamic_slice | solution.py:252
  9.2 0.0 copy-start.3
  9.2 0.5 collective-permute-start.1
  9.7 4.4 %collective-permute-done.1 = bf16[544,256]{1,0:T(8,128)(2,1)S(1)} collective-permute-done((bf16[544,256]{1,0:T(8,128)(2,1)S(1)}, bf16[544,256]{1,0:T(8,128)(2,1)S(1)}, u32[]{:S(2)}, u32[]{:S(2)}) %collective-permute-start.1) | collective-permute-done | bytes 278560 | tf_op jit(solution)/shard_map/ppermute | solution.py:246
  14.2 4.0 %collective-permute-start.3 = (bf16[1088,256]{1,0:T(8,128)(2,1)S(1)}, bf16[1088,256]{1,0:T(8,128)(2,1)S(1)}, u32[]{:S(2)}, u32[]{:S(2)}) collective-permute-start(bf16[1088,256]{1,0:T(8,128)(2,1)S(1)} %pad_maximum_fusion.refs_3_.refs_4_), channel_id=1, source_target_pairs={{0,4},{1,5},{2,6},{3,7},{4,0},{5,1},{6,2},{7,3},{8,12},{9,13},{10,... | collective-permute-start | bytes 1671176 | tf_op jit(solution)/shard_map/ppermute | solution.py:249
  18.3 0.0 copy-done.3
  18.3 0.1 fusion
  18.3 0.1 add_bitcast_fusion
  18.4 1.6 %collective-permute-start.2 = (bf16[1088,256]{1,0:T(8,128)(2,1)S(1)}, bf16[1088,256]{1,0:T(8,128)(2,1)S(1)}, u32[]{:S(2)}, u32[]{:S(2)}) collective-permute-start(bf16[1088,256]{1,0:T(8,128)(2,1)S(1)} %pad_maximum_fusion.refs_3_.refs_4_), channel_id=1, source_target_pairs={{0,2},{1,3},{2,0},{3,1},{4,6},{5,7},{6,4},{7,5},{8,10},{9,11},{10,... | collective-permute-start | bytes 1671176 | tf_op jit(solution)/shard_map/ppermute | solution.py:249
  20.0 0.1 pad_add_fusion.5.refs_0_
  20.1 40.0 %collective-permute-done.3.refs_4_.refs_6_ = bf16[1088,256]{1,0:T(8,128)(2,1)S(1)} collective-permute-done((bf16[1088,256]{1,0:T(8,128)(2,1)S(1)}, bf16[1088,256]{1,0:T(8,128)(2,1)S(1)}, u32[]{:S(2)}, u32[]{:S(2)}) %collective-permute-start.3) | collective-permute-done | bytes 557088 | tf_op jit(solution)/shard_map/ppermute | solution.py:249
  60.0 0.7 collective-permute-start.4
  60.7 0.1 pad_add_fusion.4.refs_0_
  60.8 0.1 add_bitcast_fusion.2
  60.8 0.1 pad_add_fusion.2
  60.9 0.0 collective-permute-done.refs_2_.refs_3_
  60.9 0.0 copy-start.1
  61.0 2.2 %copy-done.1 = bf16[512,4096]{1,0:T(8,128)(2,1)S(1)} copy-done((bf16[512,4096]{1,0:T(8,128)(2,1)S(1)}, bf16[512,4096]{1,0:T(8,128)(2,1)}, u32[]{:S(2)}) %copy-start.1) | copy-done | bytes 4194328
  63.1 2.8 %shard_map.73.refs_5_ = f32[1024,256]{1,0:T(8,128)S(1)} custom-call(s32[2]{0:T(128)S(1)} %pad_add_fusion.5.refs_0_, bf16[512,4096]{1,0:T(8,128)(2,1)S(1)} %copy-done.1, bf16[512,4096]{1,0:T(8,128)(2,1)} %collective-permute-done.refs_2_.refs_3_, bf16[1088,256]{1,0:T(8,128)(2,1)S(1)} %pad_maximum_fusion.refs_3_.refs_4_), custom_call_target="tpu_custom_call" | custom-call | flops 536870912 | bytes 2097152 | tf_op jit(solution)/shard_map/pallas_call | solution.py:78
  66.0 0.0 collective-permute-done.2.refs_3_.refs_5_
  66.0 4.1 %shard_map.74.refs_8_ = f32[1024,256]{1,0:T(8,128)S(1)} custom-call(s32[4]{0:T(128)S(1)} %pad_add_fusion.4.refs_0_, bf16[512,4096]{1,0:T(8,128)(2,1)S(1)} %copy-done.1, bf16[512,4096]{1,0:T(8,128)(2,1)} %collective-permute-done.refs_2_.refs_3_, bf16[1088,256]{1,0:T(8,128)(2,1)S(1)} %collective-permute-done.2.refs_3_.refs_5_, ...), custom_call_target="tpu_custom_call" | custom-call | flops 1073741824 | bytes 4194304 | tf_op jit(solution)/shard_map/pallas_call | solution.py:78
  70.1 4.0 %collective-permute-done.4.refs_7_ = bf16[1088,256]{1,0:T(8,128)(2,1)S(1)} collective-permute-done((bf16[1088,256]{1,0:T(8,128)(2,1)S(1)}, bf16[1088,256]{1,0:T(8,128)(2,1)S(1)}, u32[]{:S(2)}, u32[]{:S(2)}) %collective-permute-start.4) | collective-permute-done | bytes 557088 | tf_op jit(solution)/shard_map/ppermute | solution.py:249
  74.1 4.3 %shard_map.75 = (bf16[144,128]{1,0:T(8,128)(2,1)S(1)}, bf16[144,128]{1,0:T(8,128)(2,1)S(1)}, bf16[144,128]{1,0:T(8,128)(2,1)S(1)}, bf16[144,128]{1,0:T(8,128)(2,1)S(1)}) custom-call(s32[2]{0:T(128)S(1)} %get-tuple-element.41.refs_0_, s32[2]{0:T(128)S(1)} %get-tuple-element.42.refs_1_, bf16[512,4096]{1,0:T(8,128)(2,1)S(1)} %copy-done.1, ...), custom_call_target="tpu_custom_call" | custom-call | flops 536870912 | bytes 2097152 | tf_op jit(solution)/shard_map/pallas_call | solution.py:143
  78.5 1.2 %collective-permute-start.5 = (bf16[144,128]{1,0:T(8,128)(2,1)S(1)}, bf16[144,128]{1,0:T(8,128)(2,1)S(1)}, u32[]{:S(2)}, u32[]{:S(2)}) collective-permute-start(bf16[144,128]{1,0:T(8,128)(2,1)S(1)} %get-tuple-element.16), channel_id=1, source_target_pairs={{0,2},{1,3},{2,0},{3,1},{4,6},{5,7},{6,4},{7,5},{8,10},{9,11},{10,... | collective-permute-start | bytes 110600 | tf_op jit(solution)/shard_map/ppermute | solution.py:249
  79.7 3.4 %collective-permute-start.6 = (bf16[144,128]{1,0:T(8,128)(2,1)S(1)}, bf16[144,128]{1,0:T(8,128)(2,1)S(1)}, u32[]{:S(2)}, u32[]{:S(2)}) collective-permute-start(bf16[144,128]{1,0:T(8,128)(2,1)S(1)} %get-tuple-element.17), channel_id=1, source_target_pairs={{0,4},{1,5},{2,6},{3,7},{4,0},{5,1},{6,2},{7,3},{8,12},{9,13},{10,... | collective-permute-start | bytes 110600 | tf_op jit(solution)/shard_map/ppermute | solution.py:249
  83.0 0.0 collective-permute-start.7
  83.0 0.0 copy-done
  83.0 0.1 dynamic-slice_bitcast_fusion.refs_4_
  83.1 0.0 collective-permute-done.5.refs_1_
  83.1 2.4 %collective-permute-done.6.refs_2_ = bf16[144,128]{1,0:T(8,128)(2,1)S(1)} collective-permute-done((bf16[144,128]{1,0:T(8,128)(2,1)S(1)}, bf16[144,128]{1,0:T(8,128)(2,1)S(1)}, u32[]{:S(2)}, u32[]{:S(2)}) %collective-permute-start.6) | collective-permute-done | bytes 36896 | tf_op jit(solution)/shard_map/ppermute | solution.py:249
  85.5 3.3 %collective-permute-done.7.refs_3_ = bf16[144,128]{1,0:T(8,128)(2,1)S(1)} collective-permute-done((bf16[144,128]{1,0:T(8,128)(2,1)S(1)}, bf16[144,128]{1,0:T(8,128)(2,1)S(1)}, u32[]{:S(2)}, u32[]{:S(2)}) %collective-permute-start.7) | collective-permute-done | bytes 36896 | tf_op jit(solution)/shard_map/ppermute | solution.py:249
  88.8 0.2 shard_map.76
  89.0 0.1 collective-permute-start.8
  89.0 0.1 pad_add_fusion.1.place_ref
  89.1 0.0 all-gather.2.cloned.1.call-done.w_ref
  89.1 1.1 collective-permute-done.8.sibling_ref
  90.2 0.0 copy-start.2
  90.2 1.6 %copy-done.2 = bf16[256,4096]{1,0:T(8,128)(2,1)S(1)} copy-done((bf16[256,4096]{1,0:T(8,128)(2,1)S(1)}, bf16[256,4096]{1,0:T(8,128)(2,1)}, u32[]{:S(2)}) %copy-start.2) | copy-done | bytes 2097176
  91.8 1.6 %shard_map.77 = (bf16[64,1024]{1,0:T(8,128)(2,1)S(1)}, bf16[64,1024]{1,0:T(8,128)(2,1)S(1)}, bf16[64,1024]{1,0:T(8,128)(2,1)S(1)}, bf16[64,1024]{1,0:T(8,128)(2,1)S(1)}) custom-call(s32[2]{0:T(128)S(1)} %pad_add_fusion.1.place_ref, bf16[64,128]{1,0:T(8,128)(2,1)S(1)} %get-tuple-element.19.own_ref, bf16[64,128]{1,0:T(8,128)(2,1)S(1)} %collective-permute-done.8.sibling_ref, ...), custom_call_target="tpu_custom_call" | custom-call | tf_op jit(solution)/shard_map/pallas_call | solution.py:222
  93.5 1.6 %collective-permute-start.10 = (bf16[64,1024]{1,0:T(8,128)(2,1)S(1)}, bf16[64,1024]{1,0:T(8,128)(2,1)S(1)}, u32[]{:S(2)}, u32[]{:S(2)}) collective-permute-start(bf16[64,1024]{1,0:T(8,128)(2,1)S(1)} %get-tuple-element.23), channel_id=1, source_target_pairs={{0,16},{8,24},{16,0},{24,8},{1,17},{9,25},{17,1},{25,9},{2,18},{10... | collective-permute-start | bytes 393224 | tf_op jit(solution)/shard_map/ppermute | solution.py:311
  95.0 1.4 %collective-permute-start.11 = (bf16[64,1024]{1,0:T(8,128)(2,1)S(1)}, bf16[64,1024]{1,0:T(8,128)(2,1)S(1)}, u32[]{:S(2)}, u32[]{:S(2)}) collective-permute-start(bf16[64,1024]{1,0:T(8,128)(2,1)S(1)} %get-tuple-element.24), channel_id=1, source_target_pairs={{0,24},{8,16},{16,8},{24,0},{1,25},{9,17},{17,9},{25,1},{2,26},{10... | collective-permute-start | bytes 393224 | tf_op jit(solution)/shard_map/ppermute | solution.py:311
  96.5 0.5 collective-permute-start.9
  97.0 4.5 %collective-permute-done.10 = bf16[64,1024]{1,0:T(8,128)(2,1)S(1)} collective-permute-done((bf16[64,1024]{1,0:T(8,128)(2,1)S(1)}, bf16[64,1024]{1,0:T(8,128)(2,1)S(1)}, u32[]{:S(2)}, u32[]{:S(2)}) %collective-permute-start.10) | collective-permute-done | bytes 131104 | tf_op jit(solution)/shard_map/ppermute | solution.py:311
  101.5 0.8 collective-permute-done.11
  102.3 0.8 collective-permute-done.9
  103.1 0.7 add_convert_fusion
  (3 shorter events, 0.1 us)
Async XLA Ops:
  6.5 76.5 %copy-start = (bf16[256]{0:T(256)(128)(2,1)S(1)}, bf16[256]{0:T(256)(128)(2,1)}, u32[]{:S(2)}) copy-start(bf16[256]{0:T(256)(128)(2,1)} %param.12) | copy-start | bytes 1540
  6.5 82.6 %all-gather.2.cloned.1.call-start = ((), (), s32[]{:S(2)}) async-start(), calls=%async_computation | async-start | bytes 2359296 | tf_op jit(solution)/shard_map/all_gather | solution.py:271
  6.5 54.4 %collective-permute-start = (bf16[512,4096]{1,0:T(8,128)(2,1)}, bf16[512,4096]{1,0:T(8,128)(2,1)}, u32[]{:S(2)}, u32[]{:S(2)}) collective-permute-start(bf16[512,4096]{1,0:T(8,128)(2,1)} %refs_2_.1), channel_id=1, source_target_pairs={{0,1},{1,0},{2,3},{3,2},{4,5},{5,4},{6,7},{7,6},{8,9},{9,8},{10,11... | collective-permute-start | bytes 12582920 | tf_op jit(solution)/shard_map/ppermute | solution.py:246
  9.2 9.1 %copy-start.3 = (s32[512]{0:T(512)S(1)}, s32[512]{0:T(512)}, u32[]{:S(2)}) copy-start(s32[512]{0:T(512)} %param.11) | copy-start | bytes 6148
  9.2 5.0 %collective-permute-start.1 = (bf16[544,256]{1,0:T(8,128)(2,1)S(1)}, bf16[544,256]{1,0:T(8,128)(2,1)S(1)}, u32[]{:S(2)}, u32[]{:S(2)}) collective-permute-start(bf16[544,256]{1,0:T(8,128)(2,1)S(1)} %maximum_maximum_fusion), channel_id=1, source_target_pairs={{0,1},{1,0},{2,3},{3,2},{4,5},{5,4},{6,7},{7,6},{8,9},{9,8},{10,11... | collective-permute-start | bytes 835592 | tf_op jit(solution)/shard_map/ppermute | solution.py:246
  14.2 45.8 %collective-permute-start.3 = (bf16[1088,256]{1,0:T(8,128)(2,1)S(1)}, bf16[1088,256]{1,0:T(8,128)(2,1)S(1)}, u32[]{:S(2)}, u32[]{:S(2)}) collective-permute-start(bf16[1088,256]{1,0:T(8,128)(2,1)S(1)} %pad_maximum_fusion.refs_3_.refs_4_), channel_id=1, source_target_pairs={{0,4},{1,5},{2,6},{3,7},{4,0},{5,1},{6,2},{7,3},{8,12},{9,13},{10,... | collective-permute-start | bytes 1671176 | tf_op jit(solution)/shard_map/ppermute | solution.py:249
  18.4 47.6 %collective-permute-start.2 = (bf16[1088,256]{1,0:T(8,128)(2,1)S(1)}, bf16[1088,256]{1,0:T(8,128)(2,1)S(1)}, u32[]{:S(2)}, u32[]{:S(2)}) collective-permute-start(bf16[1088,256]{1,0:T(8,128)(2,1)S(1)} %pad_maximum_fusion.refs_3_.refs_4_), channel_id=1, source_target_pairs={{0,2},{1,3},{2,0},{3,1},{4,6},{5,7},{6,4},{7,5},{8,10},{9,11},{10,... | collective-permute-start | bytes 1671176 | tf_op jit(solution)/shard_map/ppermute | solution.py:249
  60.0 14.1 %collective-permute-start.4 = (bf16[1088,256]{1,0:T(8,128)(2,1)S(1)}, bf16[1088,256]{1,0:T(8,128)(2,1)S(1)}, u32[]{:S(2)}, u32[]{:S(2)}) collective-permute-start(bf16[1088,256]{1,0:T(8,128)(2,1)S(1)} %collective-permute-done.3.refs_4_.refs_6_), channel_id=1, source_target_pairs={{0,2},{1,3},{2,0},{3,1},{4,6},{5,7},{6,4},{7,5},{8,10},{9,11},{10,... | collective-permute-start | bytes 1671176 | tf_op jit(solution)/shard_map/ppermute | solution.py:249
  60.9 2.2 %copy-start.1 = (bf16[512,4096]{1,0:T(8,128)(2,1)S(1)}, bf16[512,4096]{1,0:T(8,128)(2,1)}, u32[]{:S(2)}) copy-start(bf16[512,4096]{1,0:T(8,128)(2,1)} %refs_2_.1) | copy-start | bytes 12582916
  78.5 4.7 %collective-permute-start.5 = (bf16[144,128]{1,0:T(8,128)(2,1)S(1)}, bf16[144,128]{1,0:T(8,128)(2,1)S(1)}, u32[]{:S(2)}, u32[]{:S(2)}) collective-permute-start(bf16[144,128]{1,0:T(8,128)(2,1)S(1)} %get-tuple-element.16), channel_id=1, source_target_pairs={{0,2},{1,3},{2,0},{3,1},{4,6},{5,7},{6,4},{7,5},{8,10},{9,11},{10,... | collective-permute-start | bytes 110600 | tf_op jit(solution)/shard_map/ppermute | solution.py:249
  79.7 5.8 %collective-permute-start.6 = (bf16[144,128]{1,0:T(8,128)(2,1)S(1)}, bf16[144,128]{1,0:T(8,128)(2,1)S(1)}, u32[]{:S(2)}, u32[]{:S(2)}) collective-permute-start(bf16[144,128]{1,0:T(8,128)(2,1)S(1)} %get-tuple-element.17), channel_id=1, source_target_pairs={{0,4},{1,5},{2,6},{3,7},{4,0},{5,1},{6,2},{7,3},{8,12},{9,13},{10,... | collective-permute-start | bytes 110600 | tf_op jit(solution)/shard_map/ppermute | solution.py:249
  83.0 5.8 %collective-permute-start.7 = (bf16[144,128]{1,0:T(8,128)(2,1)S(1)}, bf16[144,128]{1,0:T(8,128)(2,1)S(1)}, u32[]{:S(2)}, u32[]{:S(2)}) collective-permute-start(bf16[144,128]{1,0:T(8,128)(2,1)S(1)} %get-tuple-element.18), channel_id=1, source_target_pairs={{0,6},{1,7},{2,4},{3,5},{4,2},{5,3},{6,0},{7,1},{8,14},{9,15},{10,... | collective-permute-start | bytes 110600 | tf_op jit(solution)/shard_map/ppermute | solution.py:249
  89.0 1.2 %collective-permute-start.8 = (bf16[64,128]{1,0:T(8,128)(2,1)S(1)}, bf16[64,128]{1,0:T(8,128)(2,1)S(1)}, u32[]{:S(2)}, u32[]{:S(2)}) collective-permute-start(bf16[64,128]{1,0:T(8,128)(2,1)S(1)} %get-tuple-element.20), channel_id=1, source_target_pairs={{0,1},{1,0},{2,3},{3,2},{4,5},{5,4},{6,7},{7,6},{8,9},{9,8},{10,11... | collective-permute-start | bytes 49160 | tf_op jit(solution)/shard_map/ppermute | solution.py:246
  90.2 1.6 %copy-start.2 = (bf16[256,4096]{1,0:T(8,128)(2,1)S(1)}, bf16[256,4096]{1,0:T(8,128)(2,1)}, u32[]{:S(2)}) copy-start(bf16[256,4096]{1,0:T(8,128)(2,1)} %all-gather.2.cloned.1.call-done.w_ref) | copy-start | bytes 6291460
  93.5 8.0 %collective-permute-start.10 = (bf16[64,1024]{1,0:T(8,128)(2,1)S(1)}, bf16[64,1024]{1,0:T(8,128)(2,1)S(1)}, u32[]{:S(2)}, u32[]{:S(2)}) collective-permute-start(bf16[64,1024]{1,0:T(8,128)(2,1)S(1)} %get-tuple-element.23), channel_id=1, source_target_pairs={{0,16},{8,24},{16,0},{24,8},{1,17},{9,25},{17,1},{25,9},{2,18},{10... | collective-permute-start | bytes 393224 | tf_op jit(solution)/shard_map/ppermute | solution.py:311
  95.0 7.3 %collective-permute-start.11 = (bf16[64,1024]{1,0:T(8,128)(2,1)S(1)}, bf16[64,1024]{1,0:T(8,128)(2,1)S(1)}, u32[]{:S(2)}, u32[]{:S(2)}) collective-permute-start(bf16[64,1024]{1,0:T(8,128)(2,1)S(1)} %get-tuple-element.24), channel_id=1, source_target_pairs={{0,24},{8,16},{16,8},{24,0},{1,25},{9,17},{17,9},{25,1},{2,26},{10... | collective-permute-start | bytes 393224 | tf_op jit(solution)/shard_map/ppermute | solution.py:311
  96.5 6.7 %collective-permute-start.9 = (bf16[64,1024]{1,0:T(8,128)(2,1)S(1)}, bf16[64,1024]{1,0:T(8,128)(2,1)S(1)}, u32[]{:S(2)}, u32[]{:S(2)}) collective-permute-start(bf16[64,1024]{1,0:T(8,128)(2,1)S(1)} %get-tuple-element.22), channel_id=1, source_target_pairs={{0,8},{8,0},{16,24},{24,16},{1,9},{9,1},{17,25},{25,17},{2,10},{10... | collective-permute-start | bytes 393224 | tf_op jit(solution)/shard_map/ppermute | solution.py:311
Sparse Core Ops, SparseCore 0:
  9.0 50.4 all-gather.1

commit v3 on v2

v3 whole, which is shorter than its diff:
```python
import functools
import math

import jax
import jax.numpy as jnp
from jax import lax
from jax.experimental import pallas as pl
from jax.experimental.pallas import tpu as pltpu
from jax.sharding import PartitionSpec as P

DH = 128
NEGATIVE = -1e30
CORES = 2
STATS = 16
VMEM = pl.BlockSpec(memory_space=pltpu.VMEM)
SMEM = pl.BlockSpec(memory_space=pltpu.SMEM)
ANY = pl.BlockSpec(memory_space=pl.ANY)
PARAMS = pltpu.CompilerParams(vmem_limit_bytes=40 * 2**20)


def three_parts(value):
    high = value.astype(jnp.bfloat16).astype(jnp.float32)
    rest = value - high
    middle = rest.astype(jnp.bfloat16).astype(jnp.float32)
    low = (rest - middle).astype(jnp.bfloat16).astype(jnp.float32)
    return [high, middle, low]


def start_slices(starts_ref, contexts, buffer, sems, count, depth):
    copies = []
    for b in range(count):
        first = pl.multiple_of(starts_ref[b], DH)
        for which in range(CORES):
            slot = b * CORES + which
            copies.append(
                pltpu.make_async_copy(
                    contexts[which].at[:, pl.ds(first, depth)], buffer.at[slot], sems.at[slot]
                )
            )
    for copy in copies:
        copy.start()
    return copies


def add_products(copies, buffer, blocks, acc_ref, rows, depth, fresh):
    for b, block in enumerate(blocks):
        for which in range(CORES):
            slot = b * CORES + which
            copies[slot].wait()
            product = jnp.dot(buffer[slot], block[:depth, :], preferred_element_type=jnp.float32)
            place = slice(which * rows, (which + 1) * rows)
            if fresh and b == 0:
                acc_ref[place, :] = product
            else:
                acc_ref[place, :] += product


def project_kernel(count, has_acc, depth, *refs):
    starts_ref, own_ref, sibling_ref = refs[:3]
    blocks = refs[3 : 3 + count]
    acc_in = refs[3 + count] if has_acc else None
    acc_ref, buffer, sems = refs[-3:]
    copies = start_slices(starts_ref, (own_ref, sibling_ref), buffer, sems, count, depth)
    if has_acc:
        acc_ref[...] = acc_in[...]
    add_products(copies, buffer, blocks, acc_ref, own_ref.shape[0], depth, not has_acc)


def project(starts, own, sibling, blocks, acc, depth):
    count = len(blocks)
    rows = own.shape[0]
    width = blocks[0].shape[1]
    operands = [starts, own, sibling, *blocks] + ([acc] if acc is not None else [])
    return pl.pallas_call(
        functools.partial(project_kernel, count, acc is not None, depth),
        out_shape=jax.ShapeDtypeStruct((CORES * rows, width), jnp.float32),
        in_specs=[SMEM, ANY, ANY] + [VMEM] * (len(operands) - 3),
        out_specs=VMEM,
        scratch_shapes=[
            pltpu.VMEM((count * CORES, rows, depth), own.dtype),
            pltpu.SemaphoreType.DMA((count * CORES,)),
        ],
        compiler_params=PARAMS,
        cost_estimate=pl.CostEstimate(
            flops=2 * count * CORES * rows * depth * width,
            bytes_accessed=2 * count * CORES * rows * depth,
            transcendentals=0,
        ),
    )(*operands)


def attend_kernel(count, heads, depth, groups, slots, *refs):
    starts_ref, firsts_ref, slots_ref, places_ref, own_ref, sibling_ref = refs[:6]
    blocks = refs[6 : 6 + count]
    acc_in, offsets_ref = refs[6 + count : 8 + count]
    messages = refs[8 + count : 8 + count + slots]
    acc_ref, query_ref, group_ref, buffer, sems = refs[8 + count + slots :]
    rows = own_ref.shape[0]
    half = heads * DH
    lines = blocks[0].shape[0] - depth
    copies = start_slices(starts_ref, (own_ref, sibling_ref), buffer, sems, CORES, depth)
    acc_ref[...] = acc_in[...]
    for b, block in enumerate(blocks):
        query_ref[places_ref[b], :lines, :] = block[depth:, :half]
        query_ref[places_ref[b], lines:, :] = block[depth:, half:]
    add_products(copies, buffer, blocks[-CORES:], acc_ref, rows, depth, False)
    score_scale = 1.0 / math.sqrt(DH)
    line = lax.broadcasted_iota(jnp.int32, (CORES * rows, 1), 0)
    positions = jnp.where(line < rows, firsts_ref[0] + line, firsts_ref[1] + line - rows)
    for h in range(heads):
        keys = acc_ref[:, h * DH : (h + 1) * DH].astype(jnp.bfloat16)
        values = acc_ref[:, half + h * DH : half + (h + 1) * DH].T.astype(jnp.bfloat16)
        for g, members in enumerate(groups):
            query = jnp.concatenate(
                [query_ref[c, :, h * DH : (h + 1) * DH] for c in members], axis=0
            )
            scores = lax.dot_general(
                keys, query, (((1,), (1,)), ((), ())), preferred_element_type=jnp.float32
            ) * score_scale
            live = positions <= offsets_ref[g : g + 1, :]
            masked = jnp.where(live, scores, NEGATIVE)
            peak = jnp.max(masked, axis=0, keepdims=True)
            weights = jnp.where(live, jnp.exp(masked - peak), 0.0).astype(jnp.bfloat16)
            total = jnp.sum(weights.astype(jnp.float32), axis=0, keepdims=True)
            numerator = jnp.dot(values, weights, preferred_element_type=jnp.float32)
            stats = three_parts(peak) + three_parts(total)
            stats.append(jnp.zeros((STATS - len(stats), peak.shape[1]), jnp.float32))
            base = h * (DH + STATS)
            group_ref[g, base : base + DH, :] = numerator.astype(jnp.bfloat16)
            group_ref[g, base + DH : base + DH + STATS, :] = jnp.concatenate(
                stats, axis=0
            ).astype(jnp.bfloat16)
    for m in range(slots):
        messages[m][...] = group_ref[slots_ref[m]]


def attend(starts, firsts, slot_groups, places, own, sibling, blocks, acc, offsets, groups, heads, depth):
    count, slots = len(blocks), slot_groups.shape[0]
    rows, width = own.shape[0], blocks[0].shape[1]
    lat_count = 2 * (blocks[0].shape[0] - depth)
    group = lat_count * len(groups[0])
    length = heads * (DH + STATS)
    group_offsets = jnp.stack(
        [
            jnp.concatenate([offsets[c * lat_count : (c + 1) * lat_count] for c in members])
            for members in groups
        ]
    )
    return pl.pallas_call(
        functools.partial(attend_kernel, count, heads, depth, groups, slots),
        out_shape=[jax.ShapeDtypeStruct((length, group), jnp.bfloat16)] * slots,
        in_specs=[SMEM] * 4 + [ANY, ANY] + [VMEM] * (count + 2),
        out_specs=[VMEM] * slots,
        scratch_shapes=[
            pltpu.VMEM((CORES * rows, width), jnp.float32),
            pltpu.VMEM((count, lat_count, heads * DH), jnp.bfloat16),
            pltpu.VMEM((len(groups), length, group), jnp.bfloat16),
            pltpu.VMEM((CORES * CORES, rows, depth), own.dtype),
            pltpu.SemaphoreType.DMA((CORES * CORES,)),
        ],
        compiler_params=PARAMS,
        cost_estimate=pl.CostEstimate(
            flops=8 * CORES * rows * group * len(groups) * heads * DH,
            bytes_accessed=2 * CORES * CORES * rows * depth,
            transcendentals=CORES * rows * group * len(groups) * heads,
        ),
    )(starts, firsts, slot_groups, places, own, sibling, *blocks, acc, group_offsets)


def normed_head(messages, base):
    peaks, totals = [], []
    for message in messages:
        stats = message[base + DH : base + DH + STATS, :].astype(jnp.float32)
        peaks.append(stats[0:1] + stats[1:2] + stats[2:3])
        totals.append(stats[3:4] + stats[4:5] + stats[5:6])
    top = functools.reduce(jnp.maximum, peaks)
    total, numerator = 0.0, 0.0
    for message, peak, part in zip(messages, peaks, totals):
        scale = jnp.exp(peak - top)
        total += part * scale
        numerator += message[base : base + DH, :].astype(jnp.float32) * scale
    attended = numerator / total
    mean_square = jnp.mean(attended * attended, axis=0, keepdims=True)
    return (attended * lax.rsqrt(mean_square + 1e-05)).T


def combine_kernel(heads, lanes, core_ref, *refs):
    messages, gain_ref, out_ref = refs[:-2], refs[-2], refs[-1]
    half = heads * DH
    for lane in range(lanes):
        who = core_ref[0] if lane == 0 else 1 - core_ref[0]
        for h in range(heads):
            normed = normed_head(messages[lane::lanes], h * (DH + STATS))
            place = pl.ds(pl.multiple_of(who * half, DH) + h * DH, DH)
            normed = normed * gain_ref[:, place].astype(jnp.float32)
            if lanes == 1:
                place = slice(h * DH, (h + 1) * DH)
            out_ref[:, place] = normed.astype(jnp.bfloat16)


def combine(core, messages, gain, heads, lanes):
    return pl.pallas_call(
        functools.partial(combine_kernel, heads, lanes),
        out_shape=jax.ShapeDtypeStruct((messages[0].shape[1], lanes * heads * DH), jnp.bfloat16),
        in_specs=[SMEM] + [VMEM] * (len(messages) + 1),
        out_specs=VMEM,
        compiler_params=PARAMS,
    )(core, *messages, gain)


def pack_kernel(core_ref, key_ref, value_ref, query_ref, own_ref, other_ref):
    depth, half = key_ref.shape[0], key_ref.shape[1] // CORES
    lines = query_ref.shape[0] // 2
    for out_ref, who in ((own_ref, core_ref[0]), (other_ref, 1 - core_ref[0])):
        place = pl.ds(pl.multiple_of(who * half, DH), half)
        out_ref[:depth, :half] = key_ref[:, place]
        out_ref[:depth, half:] = value_ref[:, place]
        out_ref[depth:, :half] = query_ref[:lines, place]
        out_ref[depth:, half:] = query_ref[lines:, place]


def pack(core, w_key, w_value, queries):
    depth, panel = w_key.shape
    out = jax.ShapeDtypeStruct((depth + queries.shape[0] // 2, panel), w_key.dtype)
    return pl.pallas_call(
        pack_kernel,
        out_shape=[out, out],
        in_specs=[SMEM, VMEM, VMEM, VMEM],
        out_specs=[VMEM, VMEM],
        compiler_params=PARAMS,
    )(core, w_key, w_value, queries)


def finish_kernel(n_dp, core_ref, *refs):
    normed, own_w, sibling_w = refs[:n_dp], refs[n_dp : 2 * n_dp], refs[2 * n_dp : 3 * n_dp]
    own_ref, other_ref = refs[3 * n_dp :]
    rows, width = own_ref.shape[0], own_w[0].shape[1]
    for weights, who in ((own_w, core_ref[0]), (sibling_w, 1 - core_ref[0])):
        total = jnp.dot(normed[0][...], weights[0][...], preferred_element_type=jnp.float32)
        for i in range(1, n_dp):
            total += jnp.dot(normed[i][...], weights[i][...], preferred_element_type=jnp.float32)
        total = total.astype(jnp.bfloat16)
        place = pl.ds(pl.multiple_of(who * width, DH), width)
        own_ref[:, place] = total[:rows]
        other_ref[:, place] = total[rows:]


def finish(core, normed, own_w, sibling_w):
    rows, width = normed[0].shape[0] // 2, own_w[0].shape[1]
    out = jax.ShapeDtypeStruct((rows, CORES * width), jnp.bfloat16)
    return pl.pallas_call(
        functools.partial(finish_kernel, len(normed)),
        out_shape=[out, out],
        in_specs=[SMEM] + [VMEM] * (3 * len(normed)),
        out_specs=[VMEM, VMEM],
        compiler_params=PARAMS,
    )(core, *normed, *own_w, *sibling_w)


def output_kernel(n_dp, wide, place_ref, own_ref, sibling_ref, w_ref, *refs):
    terms, (buffer, sems) = refs[:n_dp], refs[n_dp:]
    half = own_ref.shape[1]
    copies = []
    for i in range(n_dp):
        first = pl.multiple_of((place_ref[0] ^ i) * wide, DH)
        copies.append(
            pltpu.make_async_copy(w_ref.at[:, pl.ds(first, wide)], buffer.at[i], sems.at[i])
        )
        copies[-1].start()
    mine = pl.multiple_of(place_ref[1] * half, DH)
    other = pl.multiple_of((1 - place_ref[1]) * half, DH)
    for i in range(n_dp):
        copies[i].wait()
        total = jnp.dot(own_ref[...], buffer[i, pl.ds(mine, half), :], preferred_element_type=jnp.float32)
        total += jnp.dot(
            sibling_ref[...], buffer[i, pl.ds(other, half), :], preferred_element_type=jnp.float32
        )
        terms[i][...] = total.astype(jnp.bfloat16)


def output_terms(place, own, sibling, w_all, n_dp):
    wide = w_all.shape[1] // n_dp
    term = jax.ShapeDtypeStruct((own.shape[0], wide), jnp.bfloat16)
    return pl.pallas_call(
        functools.partial(output_kernel, n_dp, wide),
        out_shape=[term] * n_dp,
        in_specs=[SMEM, VMEM, VMEM, ANY],
        out_specs=[VMEM] * n_dp,
        scratch_shapes=[
            pltpu.VMEM((n_dp, w_all.shape[0], wide), w_all.dtype),
            pltpu.SemaphoreType.DMA((n_dp,)),
        ],
        compiler_params=PARAMS,
    )(place, own, sibling, w_all)


def on_device(n_dp, n_ctx, context, w_key, w_value, queries, offsets, head_gain, w_out):
    chips = n_ctx // CORES
    rows = context.shape[0]
    depth, panel = w_key.shape
    heads = panel // CORES // DH
    lat_count = queries.shape[0]
    me, mine_dp = lax.axis_index("ctx"), lax.axis_index("dp")
    chip, core = me // CORES, lax.rem(me, CORES)
    core_only = core.reshape(1)

    def across(array, bits):
        return lax.ppermute(array, "ctx", [(i, i ^ bits) for i in range(n_ctx)])

    def over_dp(array, bits):
        return lax.ppermute(array, "dp", [(d, d ^ bits) for d in range(n_dp)])

    own_part, other_part = pack(core_only, w_key, w_value, queries)
    pairs = [None] * chips
    for j in sorted(range(1, chips), key=lambda j: (j.bit_count(), -j)):
        low = j & -j
        if j == low:
            pairs[j] = (across(own_part, CORES * j), across(other_part, CORES * j + 1))
        else:
            pairs[j] = tuple(across(part, CORES * low) for part in pairs[j ^ low])
    pairs[0] = (own_part, across(other_part, 1))
    context_sibling = across(context, 1)

    places = jnp.stack(
        [(chip ^ j) * CORES + who for j in range(chips) for who in (core, 1 - core)]
    ).astype(jnp.int32)
    starts = places * depth
    blocks = [part for pair in pairs for part in pair]
    last = CORES * (chips - 1)
    acc = project(starts[:CORES], context, context_sibling, blocks[:CORES], None, depth)
    acc = project(starts[CORES:last], context, context_sibling, blocks[CORES:last], acc, depth)
    firsts = jnp.stack([me * rows, (me ^ 1) * rows]).astype(jnp.int32)
    gain = head_gain.reshape(1, panel)

    def messages_to(groups, slot_groups):
        return attend(
            starts[last:], firsts, slot_groups.astype(jnp.int32), places, context, context_sibling,
            blocks, acc, offsets, groups, heads, depth,
        )

    if chips == 4 and n_dp == chips:
        first, count = CORES, 2 * CORES
        middle = list(range(first, first + count))
        groups = tuple((c, c ^ CORES) for c in middle)
        slot_groups = jnp.clip((me ^ jnp.arange(n_ctx)) - first, 0, count - 1)
        messages = messages_to(groups, slot_groups)

        between = [(c, c ^ (3 * CORES)) for c in middle]
        ready, _ = lax.optimization_barrier((w_out, pairs[2]))
        outer = lax.ppermute(w_out, "ctx", [(c ^ CORES, c) for c in middle])
        shards = [w_out, outer, lax.ppermute(outer, "ctx", between), lax.ppermute(ready, "ctx", between)]
        own_w = []
        for i in range(n_dp):
            wanted = chip ^ mine_dp ^ i
            part = shards[0]
            for j in range(1, chips):
                part = jnp.where(wanted == j, shards[j], part)
            own_w.append(over_dp(part, i) if i else part)
        sibling_w = [across(part, 1) for part in own_w]

        arrived = [messages[0]] + [
            lax.ppermute(messages[m], "ctx", [(c ^ m, c) for c in middle]) for m in range(1, n_ctx)
        ]
        normed = combine(core_only, arrived, gain, heads, CORES)
        normed = [normed] + [over_dp(normed, i) for i in range(1, n_dp)]
        own_rows, outer_rows = finish(core_only, normed, own_w, sibling_w)
        outer_rows = lax.ppermute(outer_rows, "ctx", [(c, c ^ CORES) for c in middle])
        return jnp.where((chip == 1) | (chip == 2), own_rows, outer_rows)

    groups = tuple((CORES * z, CORES * z + 1) for z in range(chips))
    messages = messages_to(groups, chip ^ jnp.arange(chips))
    arrived = [messages[0]] + [across(messages[j], CORES * j) for j in range(1, chips)]
    normed = combine(core_only, arrived, gain, heads, 1)
    normed_own = lax.dynamic_slice_in_dim(normed, core * lat_count, lat_count)
    normed_other = lax.dynamic_slice_in_dim(normed, (1 - core) * lat_count, lat_count)
    w_all = lax.all_gather(w_out, "ctx", axis=1, tiled=True)
    terms = output_terms(
        jnp.stack([mine_dp, core]).astype(jnp.int32), normed_own, across(normed_other, 1), w_all, n_dp
    )
    total = terms[0].astype(jnp.float32)
    for i in range(1, n_dp):
        total += over_dp(terms[i], i).astype(jnp.float32)
    return total.astype(jnp.bfloat16)


def solution(mesh):
    n_dp, n_ctx = mesh.shape["dp"], mesh.shape["ctx"]
    placed = (
        P("ctx", None),
        P("ctx", "dp"),
        P("ctx", "dp"),
        P("ctx", "dp"),
        P(),
        P("dp"),
        P("dp", "ctx"),
    )

    def body(*args):
        return on_device(n_dp, n_ctx, *args)

    return jax.shard_map(
        body, mesh=mesh, in_specs=placed, out_specs=P("ctx", "dp"), check_vma=False
    )
```

time: 111 us -> 117 us (1.054)
  starting transfers between devices: 15.4 us -> 63.4 us
  waiting for transfers between devices: 61.6 us -> 32.5 us
  between operations: 13.5 us -> 0.3 us
    ppermute x12 -> x29, starting transfers between devices: 15.4 us -> 63.4 us  [the longest x7 26.8 us: on_device(): lax.ppermute(messages[m], 'ctx', [(c ^ m, c) for c in middle])]
    ppermute x12 -> x29, waiting for transfers between devices: 61.3 us -> 32.5 us  [the longest x1 13.4 us: on_device(): outer = lax.ppermute(w_out, 'ctx', [(c ^ CORES, c) for c in middle])]
    select_n x0 -> x2, other arithmetic: none -> 1.75 us  [the longest x1 1.08 us: on_device(): part = jnp.where(wanted == j, shards[j], part)]
    dynamic_slice x2 -> x0, local copies, waits for them, and re-layouts: 1.22 us -> none  [the longest x1 1.13 us: columns(): return lax.dynamic_slice_in_dim(array, which * half, half, 1)]
    unnamed x8 -> x12, local copies, waits for them, and re-layouts: 3.78 us -> 4.85 us
    pallas_call x3 -> x4, Pallas kernels: 6.13 us -> 5.1 us  [the longest x1 4.36 us: attend(): pl.pallas_call(functools.partial(attend_kernel, count, heads, depth, grou...]
  transfers between devices with their start and end apart: 13 -> 29, of which waited for: 9 -> 9; matrix products, arithmetic and copies ran while one was open for 2% -> 2% of each run, Pallas kernels for 10% -> 10%
where the time goes in v3:
time: 117 us
  starting transfers between devices  63.4 us (54%)
  waiting for transfers between devices  32.5 us (28%)
  Pallas kernels  12.3 us (11%)
  local copies, waits for them, and re-layouts  6.06 us (5%)
  other arithmetic  2 us (2%)
    ppermute x7, starting transfers between devices, on_device(): lax.ppermute(messages[m], 'ctx', [(c ^ m, c) for c in middle])  26.8 us
    ppermute x12, starting transfers between devices, across(): return lax.ppermute(array, 'ctx', [(i, i ^ bits) for i in range(n_ctx)])  23.4 us
    ppermute x1, waiting for transfers between devices, on_device(): outer = lax.ppermute(w_out, 'ctx', [(c ^ CORES, c) for c in middle])  13.4 us
    pallas_call x2, Pallas kernels, project(): pl.pallas_call(functools.partial(project_kernel, count, acc is not None,...  7.23 us
    ppermute x6, starting transfers between devices, over_dp(): return lax.ppermute(array, 'dp', [(d, d ^ bits) for d in range(n_dp)])  7.11 us
    ppermute x1, waiting for transfers between devices, on_device(): lax.ppermute(outer_rows, 'ctx', [(c, c ^ CORES) for c in middle])  5.55 us
    unnamed x12, local copies, waits for them, and re-layouts  4.85 us
    ppermute x6, waiting for transfers between devices, over_dp(): return lax.ppermute(array, 'dp', [(d, d ^ bits) for d in range(n_dp)])  4.69 us
  transfers between devices with their start and end apart: 29, of which 9 were waited for; matrix products, arithmetic and copies ran while one was open for 2% of the time, Pallas kernels for 10%

profile of v3, /device:TPU:0, one launch (start us, length us, event | category | flops | bytes accessed | tf_op | source)
XLA Modules:
  0.0 116.6 jit_solution(15534144529670036262)
XLA Ops:
  0.0 0.5 collective-permute-start
  0.5 0.9 copy-done.2
  1.4 0.9 copy-done.3
  2.4 0.8 copy-done.4
  3.1 0.1 shard_map.73
  3.2 0.1 collective-permute-start.1
  3.3 3.7 %collective-permute-start.5 = (bf16[544,256]{1,0:T(8,128)(2,1)S(1)}, bf16[544,256]{1,0:T(8,128)(2,1)S(1)}, u32[]{:S(2)}, u32[]{:S(2)}) collective-permute-start(bf16[544,256]{1,0:T(8,128)(2,1)S(1)} %get-tuple-element.19), channel_id=1, source_target_pairs={{0,5},{1,4},{2,7},{3,6},{4,1},{5,0},{6,3},{7,2},{8,13},{9,12},{10,... | collective-permute-start | bytes 835592 | tf_op jit(solution)/shard_map/ppermute | solution.py:308
  7.1 0.3 collective-permute-start.4
  7.4 3.5 %collective-permute-start.19 = (bf16[256,512]{1,0:T(8,128)(2,1)}, bf16[256,512]{1,0:T(8,128)(2,1)S(1)}, u32[]{:S(2)}, u32[]{:S(2)}) collective-permute-start(bf16[256,512]{1,0:T(8,128)(2,1)} %param.13), channel_id=1, source_target_pairs={{0,2},{1,3},{6,4},{7,5},{8,10},{9,11},{14,12},{15,13},{16,18},{17,... | collective-permute-start | bytes 786440 | tf_op jit(solution)/shard_map/ppermute | solution.py:350
  10.9 0.1 stack.59.refs_3_
  11.0 1.1 fusion
  12.1 0.1 fusion.1
  12.1 13.4 %collective-permute-done.19 = bf16[256,512]{1,0:T(8,128)(2,1)S(1)} collective-permute-done((bf16[256,512]{1,0:T(8,128)(2,1)}, bf16[256,512]{1,0:T(8,128)(2,1)S(1)}, u32[]{:S(2)}, u32[]{:S(2)}) %collective-permute-start.19) | collective-permute-done | bytes 262176 | tf_op jit(solution)/shard_map/ppermute | solution.py:350
  25.6 2.4 %collective-permute-start.2 = (bf16[544,256]{1,0:T(8,128)(2,1)S(1)}, bf16[544,256]{1,0:T(8,128)(2,1)S(1)}, u32[]{:S(2)}, u32[]{:S(2)}) collective-permute-start(bf16[544,256]{1,0:T(8,128)(2,1)S(1)} %get-tuple-element.18.refs_3_.refs_6_), channel_id=1, source_target_pairs={{0,2},{1,3},{2,0},{3,1},{4,6},{5,7},{6,4},{7,5},{8,10},{9,11},{10,... | collective-permute-start | bytes 835592 | tf_op jit(solution)/shard_map/ppermute | solution.py:308
  28.0 4.3 %collective-permute-done.4.refs_5_.refs_10_ = bf16[544,256]{1,0:T(8,128)(2,1)S(1)} collective-permute-done((bf16[544,256]{1,0:T(8,128)(2,1)S(1)}, bf16[544,256]{1,0:T(8,128)(2,1)S(1)}, u32[]{:S(2)}, u32[]{:S(2)}) %collective-permute-start.4) | collective-permute-done | bytes 278560 | tf_op jit(solution)/shard_map/ppermute | solution.py:308
  32.3 0.7 collective-permute-start.20
  33.0 0.7 collective-permute-start.18
  33.7 0.1 add_bitcast_fusion
  33.7 0.1 add_bitcast_fusion.2
  33.8 0.0 collective-permute-done.1.refs_4_.refs_7_
  33.8 4.6 %collective-permute-start.3 = (bf16[544,256]{1,0:T(8,128)(2,1)S(1)}, bf16[544,256]{1,0:T(8,128)(2,1)S(1)}, u32[]{:S(2)}, u32[]{:S(2)}) collective-permute-start(bf16[544,256]{1,0:T(8,128)(2,1)S(1)} %get-tuple-element.19), channel_id=1, source_target_pairs={{0,3},{1,2},{2,1},{3,0},{4,7},{5,6},{6,5},{7,4},{8,11},{9,10},{10,... | collective-permute-start | bytes 835592 | tf_op jit(solution)/shard_map/ppermute | solution.py:308
  38.4 0.0 collective-permute-done.20
  38.4 5.9 %collective-permute-start.6 = (bf16[544,256]{1,0:T(8,128)(2,1)S(1)}, bf16[544,256]{1,0:T(8,128)(2,1)S(1)}, u32[]{:S(2)}, u32[]{:S(2)}) collective-permute-start(bf16[544,256]{1,0:T(8,128)(2,1)S(1)} %collective-permute-done.4.refs_5_.refs_10_), channel_id=1, source_target_pairs={{0,2},{1,3},{2,0},{3,1},{4,6},{5,7},{6,4},{7,5},{8,10},{9,11},{10,... | collective-permute-start | bytes 835592 | tf_op jit(solution)/shard_map/ppermute | solution.py:308
  44.3 0.0 collective-permute-done.18
  44.3 4.7 %collective-permute-start.7 = (bf16[544,256]{1,0:T(8,128)(2,1)S(1)}, bf16[544,256]{1,0:T(8,128)(2,1)S(1)}, u32[]{:S(2)}, u32[]{:S(2)}) collective-permute-start(bf16[544,256]{1,0:T(8,128)(2,1)S(1)} %collective-permute-done.5.refs_6_.refs_11_), channel_id=1, source_target_pairs={{0,2},{1,3},{2,0},{3,1},{4,6},{5,7},{6,4},{7,5},{8,10},{9,11},{10,... | collective-permute-start | bytes 835592 | tf_op jit(solution)/shard_map/ppermute | solution.py:308
  49.1 1.1 select_select_fusion
  50.1 0.0 collective-permute-done.2.refs_3_.refs_8_
  50.2 1.6 %collective-permute-start.21 = (bf16[256,512]{1,0:T(8,128)(2,1)S(1)}, bf16[256,512]{1,0:T(8,128)(2,1)S(1)}, u32[]{:S(2)}, u32[]{:S(2)}) collective-permute-start(bf16[256,512]{1,0:T(8,128)(2,1)S(1)} %get-tuple-element.33), channel_id=1, source_target_pairs={{0,8},{8,0},{16,24},{24,16},{1,9},{9,1},{17,25},{25,17},{2,10},{10... | collective-permute-start | bytes 786440 | tf_op jit(solution)/shard_map/ppermute | solution.py:311
  51.7 1.5 %collective-permute-start.22 = (bf16[256,512]{1,0:T(8,128)(2,1)S(1)}, bf16[256,512]{1,0:T(8,128)(2,1)S(1)}, u32[]{:S(2)}, u32[]{:S(2)}) collective-permute-start(bf16[256,512]{1,0:T(8,128)(2,1)S(1)} %get-tuple-element.32), channel_id=1, source_target_pairs={{0,16},{8,24},{16,0},{24,8},{1,17},{9,25},{17,1},{25,9},{2,18},{10... | collective-permute-start | bytes 786440 | tf_op jit(solution)/shard_map/ppermute | solution.py:311
  53.2 0.0 collective-permute-done.refs_2_.refs_5_
  53.2 0.5 collective-permute-start.23
  53.7 0.1 slice.34.refs_0_
  53.8 2.2 %copy-done = bf16[512,4096]{1,0:T(8,128)(2,1)S(1)} copy-done((bf16[512,4096]{1,0:T(8,128)(2,1)S(1)}, bf16[512,4096]{1,0:T(8,128)(2,1)}, u32[]{:S(2)}) %copy-start) | copy-done | bytes 4194328
  56.0 3.1 %shard_map.74.refs_7_ = f32[1024,256]{1,0:T(8,128)S(1)} custom-call(s32[2]{0:T(128)S(1)} %get-tuple-element.43.refs_0_, bf16[512,4096]{1,0:T(8,128)(2,1)S(1)} %copy-done, bf16[512,4096]{1,0:T(8,128)(2,1)} %collective-permute-done.refs_2_.refs_5_, bf16[544,256]{1,0:T(8,128)(2,1)S(1)} %get-tuple-element.18.refs_3_.refs_6_, ...), custom_call_target="tpu_custom_call" | custom-call | flops 536870912 | bytes 2097152 | tf_op jit(solution)/shard_map/pallas_call | solution.py:74
  59.1 4.1 %shard_map.75.refs_14_ = f32[1024,256]{1,0:T(8,128)S(1)} custom-call(s32[4]{0:T(128)S(1)} %slice.34.refs_0_, bf16[512,4096]{1,0:T(8,128)(2,1)S(1)} %copy-done.1, bf16[512,4096]{1,0:T(8,128)(2,1)} %collective-permute-done.refs_2_.refs_5_, bf16[544,256]{1,0:T(8,128)(2,1)S(1)} %collective-permute-done.2.refs_3_.refs_8_, ...), custom_call_target="tpu_custom_call" | custom-call | flops 1073741824 | bytes 4194304 | tf_op jit(solution)/shard_map/pallas_call | solution.py:74
  63.3 0.1 collective-permute-start.24
  63.3 0.0 collective-permute-done.21.refs_5_
  63.3 0.5 collective-permute-start.25
  63.8 0.0 collective-permute-done.7.refs_13_
  63.8 4.4 %shard_map.76 = (bf16[144,128]{1,0:T(8,128)(2,1)S(1)}, bf16[144,128]{1,0:T(8,128)(2,1)S(1)}, bf16[144,128]{1,0:T(8,128)(2,1)S(1)}, bf16[144,128]{1,0:T(8,128)(2,...) custom-call(s32[2]{0:T(128)S(1)} %get-tuple-element.44.refs_0_, ...), custom_call_target="tpu_custom_call" | custom-call | flops 536870912 | bytes 2097152 | tf_op jit(solution)/shard_map/pallas_call | solution.py:149
  68.2 1.6 %collective-permute-start.10 = (bf16[144,128]{1,0:T(8,128)(2,1)S(1)}, bf16[144,128]{1,0:T(8,128)(2,1)S(1)}, u32[]{:S(2)}, u32[]{:S(2)}) collective-permute-start(bf16[144,128]{1,0:T(8,128)(2,1)S(1)} %get-tuple-element.23), channel_id=1, source_target_pairs={{1,2},{0,3},{7,4},{6,5},{9,10},{8,11},{15,12},{14,13},{17,18},{16,... | collective-permute-start | bytes 110600 | tf_op jit(solution)/shard_map/ppermute | solution.py:362
  69.8 1.3 %collective-permute-start.11 = (bf16[144,128]{1,0:T(8,128)(2,1)S(1)}, bf16[144,128]{1,0:T(8,128)(2,1)S(1)}, u32[]{:S(2)}, u32[]{:S(2)}) collective-permute-start(bf16[144,128]{1,0:T(8,128)(2,1)S(1)} %get-tuple-element.24), channel_id=1, source_target_pairs={{6,2},{7,3},{0,4},{1,5},{14,10},{15,11},{8,12},{9,13},{22,18},{23,... | collective-permute-start | bytes 110600 | tf_op jit(solution)/shard_map/ppermute | solution.py:362
  71.2 0.0 collective-permute-done.23.refs_7_
  71.2 0.5 collective-permute-start.26
  71.6 0.1 collective-permute-start.27
  71.8 1.0 collective-permute-done.11.refs_4_
  72.8 4.6 %collective-permute-start.12 = (bf16[144,128]{1,0:T(8,128)(2,1)S(1)}, bf16[144,128]{1,0:T(8,128)(2,1)S(1)}, u32[]{:S(2)}, u32[]{:S(2)}) collective-permute-start(bf16[144,128]{1,0:T(8,128)(2,1)S(1)} %get-tuple-element.25), channel_id=1, source_target_pairs={{7,2},{6,3},{1,4},{0,5},{15,10},{14,11},{9,12},{8,13},{23,18},{22,... | collective-permute-start | bytes 110600 | tf_op jit(solution)/shard_map/ppermute | solution.py:362
  77.4 1.8 %collective-permute-done.12.refs_5_ = bf16[144,128]{1,0:T(8,128)(2,1)S(1)} collective-permute-done((bf16[144,128]{1,0:T(8,128)(2,1)S(1)}, bf16[144,128]{1,0:T(8,128)(2,1)S(1)}, u32[]{:S(2)}, u32[]{:S(2)}) %collective-permute-start.12) | collective-permute-done | bytes 36896 | tf_op jit(solution)/shard_map/ppermute | solution.py:362
  79.3 0.7 collective-permute-start.13
  79.9 0.7 collective-permute-start.14
  80.6 0.7 collective-permute-start.8
  81.3 17.2 %collective-permute-start.9 = (bf16[144,128]{1,0:T(8,128)(2,1)S(1)}, bf16[144,128]{1,0:T(8,128)(2,1)S(1)}, u32[]{:S(2)}, u32[]{:S(2)}) collective-permute-start(bf16[144,128]{1,0:T(8,128)(2,1)S(1)} %get-tuple-element.22), channel_id=1, source_target_pairs={{0,2},{1,3},{6,4},{7,5},{8,10},{9,11},{14,12},{15,13},{16,18},{17,... | collective-permute-start | bytes 110600 | tf_op jit(solution)/shard_map/ppermute | solution.py:362
  98.6 1.6 %collective-permute-done.9.refs_2_ = bf16[144,128]{1,0:T(8,128)(2,1)S(1)} collective-permute-done((bf16[144,128]{1,0:T(8,128)(2,1)S(1)}, bf16[144,128]{1,0:T(8,128)(2,1)S(1)}, u32[]{:S(2)}, u32[]{:S(2)}) %collective-permute-start.9) | collective-permute-done | bytes 36896 | tf_op jit(solution)/shard_map/ppermute | solution.py:362
  100.2 0.2 shard_map.77.refs_0_
  100.4 1.6 %collective-permute-start.15 = (bf16[128,256]{1,0:T(8,128)(2,1)S(1)}, bf16[128,256]{1,0:T(8,128)(2,1)S(1)}, u32[]{:S(2)}, u32[]{:S(2)}) collective-permute-start(bf16[128,256]{1,0:T(8,128)(2,1)S(1)} %shard_map.77.refs_0_), channel_id=1, source_target_pairs={{0,8},{8,0},{16,24},{24,16},{1,9},{9,1},{17,25},{25,17},{2,10},{10... | collective-permute-start | bytes 196616 | tf_op jit(solution)/shard_map/ppermute | solution.py:311
  101.9 1.5 %collective-permute-start.16 = (bf16[128,256]{1,0:T(8,128)(2,1)S(1)}, bf16[128,256]{1,0:T(8,128)(2,1)S(1)}, u32[]{:S(2)}, u32[]{:S(2)}) collective-permute-start(bf16[128,256]{1,0:T(8,128)(2,1)S(1)} %shard_map.77.refs_0_), channel_id=1, source_target_pairs={{0,16},{8,24},{16,0},{24,8},{1,17},{9,25},{17,1},{25,9},{2,18},{10... | collective-permute-start | bytes 196616 | tf_op jit(solution)/shard_map/ppermute | solution.py:311
  103.5 0.5 collective-permute-start.17
  103.9 0.8 collective-permute-done.15.refs_1_
  104.7 2.2 %collective-permute-done.16.refs_2_ = bf16[128,256]{1,0:T(8,128)(2,1)S(1)} collective-permute-done((bf16[128,256]{1,0:T(8,128)(2,1)S(1)}, bf16[128,256]{1,0:T(8,128)(2,1)S(1)}, u32[]{:S(2)}, u32[]{:S(2)}) %collective-permute-start.16) | collective-permute-done | bytes 65568 | tf_op jit(solution)/shard_map/ppermute | solution.py:311
  106.9 1.7 %collective-permute-done.17.refs_3_ = bf16[128,256]{1,0:T(8,128)(2,1)S(1)} collective-permute-done((bf16[128,256]{1,0:T(8,128)(2,1)S(1)}, bf16[128,256]{1,0:T(8,128)(2,1)S(1)}, u32[]{:S(2)}, u32[]{:S(2)}) %collective-permute-start.17) | collective-permute-done | bytes 65568 | tf_op jit(solution)/shard_map/ppermute | solution.py:311
  108.6 0.4 shard_map.78
  109.1 1.3 %collective-permute-start.28 = (bf16[64,1024]{1,0:T(8,128)(2,1)S(1)}, bf16[64,1024]{1,0:T(8,128)(2,1)S(1)}, u32[]{:S(2)}, u32[]{:S(2)}) collective-permute-start(bf16[64,1024]{1,0:T(8,128)(2,1)S(1)} %get-tuple-element.30), channel_id=1, source_target_pairs={{2,0},{3,1},{4,6},{5,7},{10,8},{11,9},{12,14},{13,15},{18,16},{19,... | collective-permute-start | bytes 393224 | tf_op jit(solution)/shard_map/ppermute | solution.py:367
  110.4 5.6 %collective-permute-done.28 = bf16[64,1024]{1,0:T(8,128)(2,1)S(1)} collective-permute-done((bf16[64,1024]{1,0:T(8,128)(2,1)S(1)}, bf16[64,1024]{1,0:T(8,128)(2,1)S(1)}, u32[]{:S(2)}, u32[]{:S(2)}) %collective-permute-start.28) | collective-permute-done | bytes 131104 | tf_op jit(solution)/shard_map/ppermute | solution.py:367
  115.9 0.7 broadcast_select_fusion
  (24 shorter events, 0.1 us)
Async XLA Ops:
  0.0 53.2 %collective-permute-start = (bf16[512,4096]{1,0:T(8,128)(2,1)}, bf16[512,4096]{1,0:T(8,128)(2,1)}, u32[]{:S(2)}, u32[]{:S(2)}) collective-permute-start(bf16[512,4096]{1,0:T(8,128)(2,1)} %refs_4_.1), channel_id=1, source_target_pairs={{0,1},{1,0},{2,3},{3,2},{4,5},{5,4},{6,7},{7,6},{8,9},{9,8},{10,11... | collective-permute-start | bytes 12582920 | tf_op jit(solution)/shard_map/ppermute | solution.py:308
  0.5 0.9 copy-start.2
  1.4 0.9 copy-start.3
  2.4 0.8 copy-start.4
  3.2 30.6 %collective-permute-start.1 = (bf16[544,256]{1,0:T(8,128)(2,1)S(1)}, bf16[544,256]{1,0:T(8,128)(2,1)S(1)}, u32[]{:S(2)}, u32[]{:S(2)}) collective-permute-start(bf16[544,256]{1,0:T(8,128)(2,1)S(1)} %get-tuple-element.19), channel_id=1, source_target_pairs={{0,1},{1,0},{2,3},{3,2},{4,5},{5,4},{6,7},{7,6},{8,9},{9,8},{10,11... | collective-permute-start | bytes 835592 | tf_op jit(solution)/shard_map/ppermute | solution.py:308
  3.3 29.6 %collective-permute-start.5 = (bf16[544,256]{1,0:T(8,128)(2,1)S(1)}, bf16[544,256]{1,0:T(8,128)(2,1)S(1)}, u32[]{:S(2)}, u32[]{:S(2)}) collective-permute-start(bf16[544,256]{1,0:T(8,128)(2,1)S(1)} %get-tuple-element.19), channel_id=1, source_target_pairs={{0,5},{1,4},{2,7},{3,6},{4,1},{5,0},{6,3},{7,2},{8,13},{9,12},{10,... | collective-permute-start | bytes 835592 | tf_op jit(solution)/shard_map/ppermute | solution.py:308
  7.1 25.2 %collective-permute-start.4 = (bf16[544,256]{1,0:T(8,128)(2,1)S(1)}, bf16[544,256]{1,0:T(8,128)(2,1)S(1)}, u32[]{:S(2)}, u32[]{:S(2)}) collective-permute-start(bf16[544,256]{1,0:T(8,128)(2,1)S(1)} %get-tuple-element.18.refs_3_.refs_6_), channel_id=1, source_target_pairs={{0,4},{1,5},{2,6},{3,7},{4,0},{5,1},{6,2},{7,3},{8,12},{9,13},{10,... | collective-permute-start | bytes 835592 | tf_op jit(solution)/shard_map/ppermute | solution.py:308
  7.4 18.2 %collective-permute-start.19 = (bf16[256,512]{1,0:T(8,128)(2,1)}, bf16[256,512]{1,0:T(8,128)(2,1)S(1)}, u32[]{:S(2)}, u32[]{:S(2)}) collective-permute-start(bf16[256,512]{1,0:T(8,128)(2,1)} %param.13), channel_id=1, source_target_pairs={{0,2},{1,3},{6,4},{7,5},{8,10},{9,11},{14,12},{15,13},{16,18},{17,... | collective-permute-start | bytes 786440 | tf_op jit(solution)/shard_map/ppermute | solution.py:350
  25.6 24.6 %collective-permute-start.2 = (bf16[544,256]{1,0:T(8,128)(2,1)S(1)}, bf16[544,256]{1,0:T(8,128)(2,1)S(1)}, u32[]{:S(2)}, u32[]{:S(2)}) collective-permute-start(bf16[544,256]{1,0:T(8,128)(2,1)S(1)} %get-tuple-element.18.refs_3_.refs_6_), channel_id=1, source_target_pairs={{0,2},{1,3},{2,0},{3,1},{4,6},{5,7},{6,4},{7,5},{8,10},{9,11},{10,... | collective-permute-start | bytes 835592 | tf_op jit(solution)/shard_map/ppermute | solution.py:308
  32.3 6.2 %collective-permute-start.20 = (bf16[256,512]{1,0:T(8,128)(2,1)S(1)}, bf16[256,512]{1,0:T(8,128)(2,1)S(1)}, u32[]{:S(2)}, u32[]{:S(2)}) collective-permute-start(bf16[256,512]{1,0:T(8,128)(2,1)S(1)} %collective-permute-done.19), channel_id=1, source_target_pairs={{2,4},{3,5},{4,2},{5,3},{10,12},{11,13},{12,10},{13,11},{18,20},{1... | collective-permute-start | bytes 786440 | tf_op jit(solution)/shard_map/ppermute | solution.py:351
  33.0 11.4 %collective-permute-start.18 = (bf16[256,512]{1,0:T(8,128)(2,1)}, bf16[256,512]{1,0:T(8,128)(2,1)S(1)}, u32[]{:S(2)}, u32[]{:S(2)}) collective-permute-start(bf16[256,512]{1,0:T(8,128)(2,1)} %param.13), channel_id=1, source_target_pairs={{2,4},{3,5},{4,2},{5,3},{10,12},{11,13},{12,10},{13,11},{18,20},{1... | collective-permute-start | bytes 786440 | tf_op jit(solution)/shard_map/ppermute | solution.py:351
  33.8 17.9 %collective-permute-start.3 = (bf16[544,256]{1,0:T(8,128)(2,1)S(1)}, bf16[544,256]{1,0:T(8,128)(2,1)S(1)}, u32[]{:S(2)}, u32[]{:S(2)}) collective-permute-start(bf16[544,256]{1,0:T(8,128)(2,1)S(1)} %get-tuple-element.19), channel_id=1, source_target_pairs={{0,3},{1,2},{2,1},{3,0},{4,7},{5,6},{6,5},{7,4},{8,11},{9,10},{10,... | collective-permute-start | bytes 835592 | tf_op jit(solution)/shard_map/ppermute | solution.py:308
  38.4 24.8 %collective-permute-start.6 = (bf16[544,256]{1,0:T(8,128)(2,1)S(1)}, bf16[544,256]{1,0:T(8,128)(2,1)S(1)}, u32[]{:S(2)}, u32[]{:S(2)}) collective-permute-start(bf16[544,256]{1,0:T(8,128)(2,1)S(1)} %collective-permute-done.4.refs_5_.refs_10_), channel_id=1, source_target_pairs={{0,2},{1,3},{2,0},{3,1},{4,6},{5,7},{6,4},{7,5},{8,10},{9,11},{10,... | collective-permute-start | bytes 835592 | tf_op jit(solution)/shard_map/ppermute | solution.py:308
  44.3 19.5 %collective-permute-start.7 = (bf16[544,256]{1,0:T(8,128)(2,1)S(1)}, bf16[544,256]{1,0:T(8,128)(2,1)S(1)}, u32[]{:S(2)}, u32[]{:S(2)}) collective-permute-start(bf16[544,256]{1,0:T(8,128)(2,1)S(1)} %collective-permute-done.5.refs_6_.refs_11_), channel_id=1, source_target_pairs={{0,2},{1,3},{2,0},{3,1},{4,6},{5,7},{6,4},{7,5},{8,10},{9,11},{10,... | collective-permute-start | bytes 835592 | tf_op jit(solution)/shard_map/ppermute | solution.py:308
  50.2 13.2 %collective-permute-start.21 = (bf16[256,512]{1,0:T(8,128)(2,1)S(1)}, bf16[256,512]{1,0:T(8,128)(2,1)S(1)}, u32[]{:S(2)}, u32[]{:S(2)}) collective-permute-start(bf16[256,512]{1,0:T(8,128)(2,1)S(1)} %get-tuple-element.33), channel_id=1, source_target_pairs={{0,8},{8,0},{16,24},{24,16},{1,9},{9,1},{17,25},{25,17},{2,10},{10... | collective-permute-start | bytes 786440 | tf_op jit(solution)/shard_map/ppermute | solution.py:311
  51.7 18.1 %collective-permute-start.22 = (bf16[256,512]{1,0:T(8,128)(2,1)S(1)}, bf16[256,512]{1,0:T(8,128)(2,1)S(1)}, u32[]{:S(2)}, u32[]{:S(2)}) collective-permute-start(bf16[256,512]{1,0:T(8,128)(2,1)S(1)} %get-tuple-element.32), channel_id=1, source_target_pairs={{0,16},{8,24},{16,0},{24,8},{1,17},{9,25},{17,1},{25,9},{2,18},{10... | collective-permute-start | bytes 786440 | tf_op jit(solution)/shard_map/ppermute | solution.py:311
  53.2 17.9 %collective-permute-start.23 = (bf16[256,512]{1,0:T(8,128)(2,1)S(1)}, bf16[256,512]{1,0:T(8,128)(2,1)S(1)}, u32[]{:S(2)}, u32[]{:S(2)}) collective-permute-start(bf16[256,512]{1,0:T(8,128)(2,1)S(1)} %get-tuple-element.31), channel_id=1, source_target_pairs={{0,24},{8,16},{16,8},{24,0},{1,25},{9,17},{17,9},{25,1},{2,26},{10... | collective-permute-start | bytes 786440 | tf_op jit(solution)/shard_map/ppermute | solution.py:311
  53.8 2.2 %copy-start = (bf16[512,4096]{1,0:T(8,128)(2,1)S(1)}, bf16[512,4096]{1,0:T(8,128)(2,1)}, u32[]{:S(2)}) copy-start(bf16[512,4096]{1,0:T(8,128)(2,1)} %refs_4_.1) | copy-start | bytes 12582916
  56.0 3.2 %copy-start.1 = (bf16[512,4096]{1,0:T(8,128)(2,1)S(1)}, bf16[512,4096]{1,0:T(8,128)(2,1)}, u32[]{:S(2)}) copy-start(bf16[512,4096]{1,0:T(8,128)(2,1)} %refs_4_.1) | copy-start | bytes 12582916
  63.3 38.7 %collective-permute-start.24 = (bf16[256,512]{1,0:T(8,128)(2,1)S(1)}, bf16[256,512]{1,0:T(8,128)(2,1)S(1)}, u32[]{:S(2)}, u32[]{:S(2)}) collective-permute-start(bf16[256,512]{1,0:T(8,128)(2,1)S(1)} %get-tuple-element.34.refs_4_), channel_id=1, source_target_pairs={{0,1},{1,0},{2,3},{3,2},{4,5},{5,4},{6,7},{7,6},{8,9},{9,8},{10,11... | collective-permute-start | bytes 786440 | tf_op jit(solution)/shard_map/ppermute | solution.py:308
  63.3 40.1 %collective-permute-start.25 = (bf16[256,512]{1,0:T(8,128)(2,1)S(1)}, bf16[256,512]{1,0:T(8,128)(2,1)S(1)}, u32[]{:S(2)}, u32[]{:S(2)}) collective-permute-start(bf16[256,512]{1,0:T(8,128)(2,1)S(1)} %collective-permute-done.21.refs_5_), channel_id=1, source_target_pairs={{0,1},{1,0},{2,3},{3,2},{4,5},{5,4},{6,7},{7,6},{8,9},{9,8},{10,11... | collective-permute-start | bytes 786440 | tf_op jit(solution)/shard_map/ppermute | solution.py:308
  63.8 34.7 %copy-start.5 = (bf16[256]{0:T(256)(128)(2,1)S(1)}, bf16[256]{0:T(256)(128)(2,1)}, u32[]{:S(2)}) copy-start(bf16[256]{0:T(256)(128)(2,1)} %param.12) | copy-start | bytes 1540
  68.2 3.4 %collective-permute-start.10 = (bf16[144,128]{1,0:T(8,128)(2,1)S(1)}, bf16[144,128]{1,0:T(8,128)(2,1)S(1)}, u32[]{:S(2)}, u32[]{:S(2)}) collective-permute-start(bf16[144,128]{1,0:T(8,128)(2,1)S(1)} %get-tuple-element.23), channel_id=1, source_target_pairs={{1,2},{0,3},{7,4},{6,5},{9,10},{8,11},{15,12},{14,13},{17,18},{16,... | collective-permute-start | bytes 110600 | tf_op jit(solution)/shard_map/ppermute | solution.py:362
  69.8 3.0 %collective-permute-start.11 = (bf16[144,128]{1,0:T(8,128)(2,1)S(1)}, bf16[144,128]{1,0:T(8,128)(2,1)S(1)}, u32[]{:S(2)}, u32[]{:S(2)}) collective-permute-start(bf16[144,128]{1,0:T(8,128)(2,1)S(1)} %get-tuple-element.24), channel_id=1, source_target_pairs={{6,2},{7,3},{0,4},{1,5},{14,10},{15,11},{8,12},{9,13},{22,18},{23,... | collective-permute-start | bytes 110600 | tf_op jit(solution)/shard_map/ppermute | solution.py:362
  71.2 32.8 %collective-permute-start.26 = (bf16[256,512]{1,0:T(8,128)(2,1)S(1)}, bf16[256,512]{1,0:T(8,128)(2,1)S(1)}, u32[]{:S(2)}, u32[]{:S(2)}) collective-permute-start(bf16[256,512]{1,0:T(8,128)(2,1)S(1)} %collective-permute-done.22.refs_6_), channel_id=1, source_target_pairs={{0,1},{1,0},{2,3},{3,2},{4,5},{5,4},{6,7},{7,6},{8,9},{9,8},{10,11... | collective-permute-start | bytes 786440 | tf_op jit(solution)/shard_map/ppermute | solution.py:308
  71.6 32.3 %collective-permute-start.27 = (bf16[256,512]{1,0:T(8,128)(2,1)S(1)}, bf16[256,512]{1,0:T(8,128)(2,1)S(1)}, u32[]{:S(2)}, u32[]{:S(2)}) collective-permute-start(bf16[256,512]{1,0:T(8,128)(2,1)S(1)} %collective-permute-done.23.refs_7_), channel_id=1, source_target_pairs={{0,1},{1,0},{2,3},{3,2},{4,5},{5,4},{6,7},{7,6},{8,9},{9,8},{10,11... | collective-permute-start | bytes 786440 | tf_op jit(solution)/shard_map/ppermute | solution.py:308
  72.8 6.5 %collective-permute-start.12 = (bf16[144,128]{1,0:T(8,128)(2,1)S(1)}, bf16[144,128]{1,0:T(8,128)(2,1)S(1)}, u32[]{:S(2)}, u32[]{:S(2)}) collective-permute-start(bf16[144,128]{1,0:T(8,128)(2,1)S(1)} %get-tuple-element.25), channel_id=1, source_target_pairs={{7,2},{6,3},{1,4},{0,5},{15,10},{14,11},{9,12},{8,13},{23,18},{22,... | collective-permute-start | bytes 110600 | tf_op jit(solution)/shard_map/ppermute | solution.py:362
  79.3 0.7 collective-permute-start.13
  79.9 0.7 collective-permute-start.14
  80.6 0.7 collective-permute-start.8
  81.3 18.9 %collective-permute-start.9 = (bf16[144,128]{1,0:T(8,128)(2,1)S(1)}, bf16[144,128]{1,0:T(8,128)(2,1)S(1)}, u32[]{:S(2)}, u32[]{:S(2)}) collective-permute-start(bf16[144,128]{1,0:T(8,128)(2,1)S(1)} %get-tuple-element.22), channel_id=1, source_target_pairs={{0,2},{1,3},{6,4},{7,5},{8,10},{9,11},{14,12},{15,13},{16,18},{17,... | collective-permute-start | bytes 110600 | tf_op jit(solution)/shard_map/ppermute | solution.py:362
  100.4 4.3 %collective-permute-start.15 = (bf16[128,256]{1,0:T(8,128)(2,1)S(1)}, bf16[128,256]{1,0:T(8,128)(2,1)S(1)}, u32[]{:S(2)}, u32[]{:S(2)}) collective-permute-start(bf16[128,256]{1,0:T(8,128)(2,1)S(1)} %shard_map.77.refs_0_), channel_id=1, source_target_pairs={{0,8},{8,0},{16,24},{24,16},{1,9},{9,1},{17,25},{25,17},{2,10},{10... | collective-permute-start | bytes 196616 | tf_op jit(solution)/shard_map/ppermute | solution.py:311
  101.9 5.0 %collective-permute-start.16 = (bf16[128,256]{1,0:T(8,128)(2,1)S(1)}, bf16[128,256]{1,0:T(8,128)(2,1)S(1)}, u32[]{:S(2)}, u32[]{:S(2)}) collective-permute-start(bf16[128,256]{1,0:T(8,128)(2,1)S(1)} %shard_map.77.refs_0_), channel_id=1, source_target_pairs={{0,16},{8,24},{16,0},{24,8},{1,17},{9,25},{17,1},{25,9},{2,18},{10... | collective-permute-start | bytes 196616 | tf_op jit(solution)/shard_map/ppermute | solution.py:311
  103.5 5.2 %collective-permute-start.17 = (bf16[128,256]{1,0:T(8,128)(2,1)S(1)}, bf16[128,256]{1,0:T(8,128)(2,1)S(1)}, u32[]{:S(2)}, u32[]{:S(2)}) collective-permute-start(bf16[128,256]{1,0:T(8,128)(2,1)S(1)} %shard_map.77.refs_0_), channel_id=1, source_target_pairs={{0,24},{8,16},{16,8},{24,0},{1,25},{9,17},{17,9},{25,1},{2,26},{10... | collective-permute-start | bytes 196616 | tf_op jit(solution)/shard_map/ppermute | solution.py:311
  109.1 6.9 %collective-permute-start.28 = (bf16[64,1024]{1,0:T(8,128)(2,1)S(1)}, bf16[64,1024]{1,0:T(8,128)(2,1)S(1)}, u32[]{:S(2)}, u32[]{:S(2)}) collective-permute-start(bf16[64,1024]{1,0:T(8,128)(2,1)S(1)} %get-tuple-element.30), channel_id=1, source_target_pairs={{2,0},{3,1},{4,6},{5,7},{10,8},{11,9},{12,14},{13,15},{18,16},{19,... | collective-permute-start | bytes 393224 | tf_op jit(solution)/shard_map/ppermute | solution.py:367

commit v4 on v3

v4 whole, which is shorter than its diff:
```python
import functools
import math

import jax
import jax.numpy as jnp
from jax import lax
from jax.experimental import pallas as pl
from jax.experimental.pallas import tpu as pltpu
from jax.sharding import PartitionSpec as P

DH = 128
NEGATIVE = -1e30
CORES = 2
STATS = 16
VMEM = pl.BlockSpec(memory_space=pltpu.VMEM)
SMEM = pl.BlockSpec(memory_space=pltpu.SMEM)
ANY = pl.BlockSpec(memory_space=pl.ANY)
PARAMS = pltpu.CompilerParams(vmem_limit_bytes=40 * 2**20)
WIDE = pltpu.CompilerParams(vmem_limit_bytes=60 * 2**20)


def three_parts(value):
    high = value.astype(jnp.bfloat16).astype(jnp.float32)
    rest = value - high
    middle = rest.astype(jnp.bfloat16).astype(jnp.float32)
    low = (rest - middle).astype(jnp.bfloat16).astype(jnp.float32)
    return [high, middle, low]


def start_slices(starts_ref, skip, contexts, buffer, sems, count, depth):
    copies = []
    for b in range(count):
        first = pl.multiple_of(starts_ref[skip + b], DH)
        for which in range(CORES):
            slot = b * CORES + which
            copies.append(
                pltpu.make_async_copy(
                    contexts[which].at[:, pl.ds(first, depth)], buffer.at[slot],
                    sems.at[skip * CORES + slot],
                )
            )
    for copy in copies:
        copy.start()
    return copies


def add_products(copies, buffer, blocks, acc_ref, rows, depth, fresh):
    for b, block in enumerate(blocks):
        for which in range(CORES):
            slot = b * CORES + which
            if copies is not None:
                copies[slot].wait()
            product = jnp.dot(buffer[slot], block[:depth, :], preferred_element_type=jnp.float32)
            place = slice(which * rows, (which + 1) * rows)
            if fresh and b == 0:
                acc_ref[place, :] = product
            else:
                acc_ref[place, :] += product


def project_kernel(count, extra, has_acc, depth, *refs):
    starts_ref, own_ref, sibling_ref = refs[:3]
    blocks = refs[3 : 3 + count]
    acc_in = refs[3 + count] if has_acc else None
    acc_ref, later_ref, buffer, sems = refs[-4:]
    contexts = (own_ref, sibling_ref)
    copies = start_slices(starts_ref, 0, contexts, buffer, sems, count, depth)
    later = start_slices(starts_ref, count, contexts, later_ref, sems, extra, depth)
    if has_acc:
        acc_ref[...] = acc_in[...]
    add_products(copies, buffer, blocks, acc_ref, own_ref.shape[0], depth, not has_acc)
    for copy in later:
        copy.wait()


def project(starts, own, sibling, blocks, acc, depth):
    count, extra = len(blocks), starts.shape[0] - len(blocks)
    rows = own.shape[0]
    width = blocks[0].shape[1]
    operands = [starts, own, sibling, *blocks] + ([acc] if acc is not None else [])
    return pl.pallas_call(
        functools.partial(project_kernel, count, extra, acc is not None, depth),
        out_shape=[
            jax.ShapeDtypeStruct((CORES * rows, width), jnp.float32),
            jax.ShapeDtypeStruct((max(extra, 1) * CORES, rows if extra else 16, depth), own.dtype),
        ],
        in_specs=[SMEM, ANY, ANY] + [VMEM] * (len(operands) - 3),
        out_specs=[VMEM, VMEM],
        scratch_shapes=[
            pltpu.VMEM((count * CORES, rows, depth), own.dtype),
            pltpu.SemaphoreType.DMA(((count + extra) * CORES,)),
        ],
        compiler_params=PARAMS,
        cost_estimate=pl.CostEstimate(
            flops=2 * count * CORES * rows * depth * width,
            bytes_accessed=2 * count * CORES * rows * depth,
            transcendentals=0,
        ),
    )(*operands)


def attend_kernel(count, heads, depth, groups, slots, *refs):
    firsts_ref, slots_ref, places_ref, slices_ref = refs[:4]
    blocks = refs[4 : 4 + count]
    acc_in, offsets_ref = refs[4 + count : 6 + count]
    messages = refs[6 + count : 6 + count + slots]
    acc_ref, query_ref, group_ref = refs[6 + count + slots :]
    rows = slices_ref.shape[1]
    half = heads * DH
    lines = blocks[0].shape[0] - depth
    acc_ref[...] = acc_in[...]
    for b, block in enumerate(blocks):
        query_ref[places_ref[b], :lines, :] = block[depth:, :half]
        query_ref[places_ref[b], lines:, :] = block[depth:, half:]
    add_products(None, slices_ref, blocks[-CORES:], acc_ref, rows, depth, False)
    score_scale = 1.0 / math.sqrt(DH)
    line = lax.broadcasted_iota(jnp.int32, (CORES * rows, 1), 0)
    positions = jnp.where(line < rows, firsts_ref[0] + line, firsts_ref[1] + line - rows)
    for h in range(heads):
        keys = acc_ref[:, h * DH : (h + 1) * DH].astype(jnp.bfloat16)
        values = acc_ref[:, half + h * DH : half + (h + 1) * DH].T.astype(jnp.bfloat16)
        for g, members in enumerate(groups):
            query = jnp.concatenate(
                [query_ref[c, :, h * DH : (h + 1) * DH] for c in members], axis=0
            )
            scores = lax.dot_general(
                keys, query, (((1,), (1,)), ((), ())), preferred_element_type=jnp.float32
            ) * score_scale
            live = positions <= offsets_ref[g : g + 1, :]
            masked = jnp.where(live, scores, NEGATIVE)
            peak = jnp.max(masked, axis=0, keepdims=True)
            weights = jnp.where(live, jnp.exp(masked - peak), 0.0).astype(jnp.bfloat16)
            total = jnp.sum(weights.astype(jnp.float32), axis=0, keepdims=True)
            numerator = jnp.dot(values, weights, preferred_element_type=jnp.float32)
            stats = three_parts(peak) + three_parts(total)
            stats.append(jnp.zeros((STATS - len(stats), peak.shape[1]), jnp.float32))
            base = h * (DH + STATS)
            group_ref[g, base : base + DH, :] = numerator.astype(jnp.bfloat16)
            group_ref[g, base + DH : base + DH + STATS, :] = jnp.concatenate(
                stats, axis=0
            ).astype(jnp.bfloat16)
    for m in range(slots):
        messages[m][...] = group_ref[slots_ref[m]]


def attend(firsts, slot_groups, places, slices, blocks, acc, offsets, groups, heads, depth):
    count, slots = len(blocks), slot_groups.shape[0]
    rows, width = slices.shape[1], blocks[0].shape[1]
    lat_count = 2 * (blocks[0].shape[0] - depth)
    group = lat_count * len(groups[0])
    length = heads * (DH + STATS)
    group_offsets = jnp.stack(
        [
            jnp.concatenate([offsets[c * lat_count : (c + 1) * lat_count] for c in members])
            for members in groups
        ]
    )
    return pl.pallas_call(
        functools.partial(attend_kernel, count, heads, depth, groups, slots),
        out_shape=[jax.ShapeDtypeStruct((length, group), jnp.bfloat16)] * slots,
        in_specs=[SMEM] * 3 + [VMEM] * (count + 3),
        out_specs=[VMEM] * slots,
        scratch_shapes=[
            pltpu.VMEM((CORES * rows, width), jnp.float32),
            pltpu.VMEM((count, lat_count, heads * DH), jnp.bfloat16),
            pltpu.VMEM((len(groups), length, group), jnp.bfloat16),
        ],
        compiler_params=PARAMS,
        cost_estimate=pl.CostEstimate(
            flops=8 * CORES * rows * group * len(groups) * heads * DH,
            bytes_accessed=2 * CORES * CORES * rows * depth,
            transcendentals=CORES * rows * group * len(groups) * heads,
        ),
    )(firsts, slot_groups, places, slices, *blocks, acc, group_offsets)


def normed_head(messages, base):
    peaks, totals = [], []
    for message in messages:
        stats = message[base + DH : base + DH + STATS, :].astype(jnp.float32)
        peaks.append(stats[0:1] + stats[1:2] + stats[2:3])
        totals.append(stats[3:4] + stats[4:5] + stats[5:6])
    top = functools.reduce(jnp.maximum, peaks)
    total, numerator = 0.0, 0.0
    for message, peak, part in zip(messages, peaks, totals):
        scale = jnp.exp(peak - top)
        total += part * scale
        numerator += message[base : base + DH, :].astype(jnp.float32) * scale
    attended = numerator / total
    mean_square = jnp.mean(attended * attended, axis=0, keepdims=True)
    return (attended * lax.rsqrt(mean_square + 1e-05)).T


def combine_kernel(heads, core_ref, *refs):
    messages, gain_ref, out_ref = refs[:-2], refs[-2], refs[-1]
    half = out_ref.shape[1]
    for h in range(heads):
        place = pl.ds(pl.multiple_of(core_ref[0] * half, DH) + h * DH, DH)
        normed = normed_head(messages, h * (DH + STATS))
        normed = normed * gain_ref[:, place].astype(jnp.float32)
        out_ref[:, h * DH : (h + 1) * DH] = normed.astype(jnp.bfloat16)


def combine(core, messages, gain, heads):
    return pl.pallas_call(
        functools.partial(combine_kernel, heads),
        out_shape=jax.ShapeDtypeStruct((messages[0].shape[1], heads * DH), jnp.bfloat16),
        in_specs=[SMEM] + [VMEM] * (len(messages) + 1),
        out_specs=VMEM,
        compiler_params=PARAMS,
    )(core, *messages, gain)


def pack_kernel(core_ref, key_ref, value_ref, query_ref, own_ref, other_ref, sems):
    depth, half = key_ref.shape[0], key_ref.shape[1] // CORES
    lines = query_ref.shape[0] // 2
    copies = []
    for out_ref, who in ((own_ref, core_ref[0]), (other_ref, 1 - core_ref[0])):
        place = pl.ds(pl.multiple_of(who * half, DH), half)
        for source, target in (
            (key_ref.at[:, place], out_ref.at[pl.ds(0, depth), pl.ds(0, half)]),
            (value_ref.at[:, place], out_ref.at[pl.ds(0, depth), pl.ds(half, half)]),
            (query_ref.at[pl.ds(0, lines), place], out_ref.at[pl.ds(depth, lines), pl.ds(0, half)]),
            (query_ref.at[pl.ds(lines, lines), place], out_ref.at[pl.ds(depth, lines), pl.ds(half, half)]),
        ):
            copies.append(pltpu.make_async_copy(source, target, sems.at[len(copies)]))
            copies[-1].start()
    for copy in copies:
        copy.wait()


def pack(core, w_key, w_value, queries):
    depth, panel = w_key.shape
    out = jax.ShapeDtypeStruct((depth + queries.shape[0] // 2, panel), w_key.dtype)
    return pl.pallas_call(
        pack_kernel,
        out_shape=[out, out],
        in_specs=[SMEM, ANY, ANY, ANY],
        out_specs=[VMEM, VMEM],
        scratch_shapes=[pltpu.SemaphoreType.DMA((8,))],
        compiler_params=WIDE,
    )(core, w_key, w_value, queries)


def output_kernel(place_ref, own_ref, sibling_ref, *refs):
    chips = (len(refs) - 1) // 2
    weights, terms, result = refs[:chips], refs[chips:-1], refs[-1]
    half = own_ref.shape[1]
    mine = pl.ds(pl.multiple_of(place_ref[1] * half, DH), half)
    other = pl.ds(pl.multiple_of((1 - place_ref[1]) * half, DH), half)
    own, sibling = own_ref[...], sibling_ref[...]
    for j, w_ref in enumerate(weights):
        total = jnp.dot(own, w_ref[mine, :], preferred_element_type=jnp.float32)
        total += jnp.dot(sibling, w_ref[other, :], preferred_element_type=jnp.float32)
        result[j] = total.astype(jnp.bfloat16)
    for i, term in enumerate(terms):
        term[...] = result[place_ref[0] ^ i]


def output_terms(place, own, sibling, weights):
    chips, shape = len(weights), (own.shape[0], weights[0].shape[1])
    return pl.pallas_call(
        output_kernel,
        out_shape=[jax.ShapeDtypeStruct(shape, jnp.bfloat16)] * chips,
        in_specs=[SMEM] + [VMEM] * (2 + chips),
        out_specs=[VMEM] * chips,
        scratch_shapes=[pltpu.VMEM((chips, *shape), jnp.bfloat16)],
        compiler_params=PARAMS,
    )(place, own, sibling, *weights)


def add_kernel(core_ref, *refs):
    terms, (own_ref, other_ref) = refs[:-2], refs[-2:]
    count = own_ref.shape[0]
    for out_ref, who in ((own_ref, core_ref[0]), (other_ref, 1 - core_ref[0])):
        lines = pl.ds(pl.multiple_of(who * count, count), count)
        total = terms[0][lines, :].astype(jnp.float32)
        for term in terms[1:]:
            total += term[lines, :].astype(jnp.float32)
        out_ref[...] = total.astype(jnp.bfloat16)


def add_terms(core, terms):
    rows, width = terms[0].shape
    out = jax.ShapeDtypeStruct((rows // CORES, width), jnp.bfloat16)
    return pl.pallas_call(
        add_kernel,
        out_shape=[out, out],
        in_specs=[SMEM] + [VMEM] * len(terms),
        out_specs=[VMEM, VMEM],
        compiler_params=PARAMS,
    )(core, *terms)


def on_device(n_dp, n_ctx, context, w_key, w_value, queries, offsets, head_gain, w_out):
    chips = n_ctx // CORES
    rows = context.shape[0]
    depth, panel = w_key.shape
    heads = panel // CORES // DH
    lat_count = queries.shape[0]
    me, mine_dp = lax.axis_index("ctx"), lax.axis_index("dp")
    chip, core = me // CORES, lax.rem(me, CORES)
    core_only = core.reshape(1)

    def across(array, bits):
        return lax.ppermute(array, "ctx", [(i, i ^ bits) for i in range(n_ctx)])

    def over_dp(array, bits):
        return lax.ppermute(array, "dp", [(d, d ^ bits) for d in range(n_dp)])

    def after(array, *others):
        return lax.optimization_barrier((array, others))[0]

    near_first = sorted(range(1, chips), key=lambda j: (j.bit_count(), -j))
    own_part, other_part = pack(core_only, w_key, w_value, queries)
    pairs = [None] * chips
    for j in near_first:
        low = j & -j
        if j == low:
            pairs[j] = (across(own_part, CORES * j), across(other_part, CORES * j + 1))
        else:
            pairs[j] = tuple(across(part, CORES * low) for part in pairs[j ^ low])
    context_sibling = across(context, 1)
    pairs[0] = (own_part, across(after(other_part, pairs[1], pairs[chips // 2]), 1))

    places = jnp.stack(
        [(chip ^ j) * CORES + who for j in range(chips) for who in (core, 1 - core)]
    ).astype(jnp.int32)
    starts = places * depth
    blocks = [part for pair in pairs for part in pair]
    last = CORES * (chips - 1)
    acc, _ = project(starts[:CORES], context, context_sibling, blocks[:CORES], None, depth)
    acc, slices = project(
        starts[CORES:], context, context_sibling, blocks[CORES:last], acc, depth
    )
    firsts = jnp.stack([me * rows, (me ^ 1) * rows]).astype(jnp.int32)
    groups = tuple((CORES * z, CORES * z + 1) for z in range(chips))
    slot_groups = (chip ^ jnp.arange(chips)).astype(jnp.int32)
    messages = attend(
        firsts, slot_groups, places, slices, blocks, acc, offsets, groups, heads, depth
    )
    arrived = [messages[0]] + [across(messages[j], CORES * j) for j in range(1, chips)]
    normed = combine(core_only, arrived, head_gain.reshape(1, panel), heads)

    shards = [after(w_out, *pairs[-1], acc)] + [None] * (chips - 1)
    for j in near_first:
        low = j & -j
        shard = shards[j ^ low]
        shards[j] = across(shard if j == low else after(shard, normed), CORES * low)
    terms = output_terms(
        jnp.stack([mine_dp ^ chip, core]).astype(jnp.int32), normed, across(normed, 1), shards
    )
    terms = [terms[0]] + [over_dp(terms[i], i) for i in range(1, n_dp)]
    mine, other = add_terms(core_only, terms)
    theirs = across(other, 1)
    return jnp.where(
        core == 0, jnp.concatenate([mine, theirs], axis=1), jnp.concatenate([theirs, mine], axis=1)
    )


def solution(mesh):
    n_dp, n_ctx = mesh.shape["dp"], mesh.shape["ctx"]
    placed = (
        P("ctx", None),
        P("ctx", "dp"),
        P("ctx", "dp"),
        P("ctx", "dp"),
        P(),
        P("dp"),
        P("dp", "ctx"),
    )

    def body(*args):
        return on_device(n_dp, n_ctx, *args)

    return jax.shard_map(
        body, mesh=mesh, in_specs=placed, out_specs=P("ctx", "dp"), check_vma=False
    )
```

time: 117 us -> 86.8 us (0.74)
  starting transfers between devices: 63.4 us -> 20.2 us
  waiting for transfers between devices: 32.5 us -> 47.7 us
  local copies, waits for them, and re-layouts: 6.06 us -> 4.15 us
  Pallas kernels: 12.3 us -> 13.5 us
    ppermute x12 -> x16, waiting for transfers between devices: 4.35 us -> 41.9 us  [across(): return lax.ppermute(array, 'ctx', [(i, i ^ bits) for i in range(n_ctx)])]
    ppermute x11 -> x0, starting transfers between devices: 32.9 us -> none  [the longest x7 26.8 us: on_device(): lax.ppermute(messages[m], 'ctx', [(c ^ m, c) for c in middle])]
    ppermute x11 -> x0, waiting for transfers between devices: 23.5 us -> none  [the longest x1 13.4 us: on_device(): outer = lax.ppermute(w_out, 'ctx', [(c ^ CORES, c) for c in middle])]
    ppermute x12 -> x16, starting transfers between devices: 23.4 us -> 16.6 us  [across(): return lax.ppermute(array, 'ctx', [(i, i ^ bits) for i in range(n_ctx)])]
    ppermute x6 -> x3, starting transfers between devices: 7.11 us -> 3.55 us  [over_dp(): return lax.ppermute(array, 'dp', [(d, d ^ bits) for d in range(n_dp)])]
    pallas_call x5 -> x6, Pallas kernels: 7.98 us -> 10.7 us  [the longest x2 7.48 us: project(): pl.pallas_call(functools.partial(project_kernel, count, extra, acc is not...]
    unnamed x12 -> x10, local copies, waits for them, and re-layouts: 4.85 us -> 3.15 us
    pallas_call x1, Pallas kernels: 4.36 us -> 2.82 us  [attend(): pl.pallas_call(functools.partial(attend_kernel, count, heads, depth, grou...]
  transfers between devices with their start and end apart: 29 -> 19, of which waited for: 9 -> 13; matrix products, arithmetic and copies ran while one was open for 2% -> 1% of each run, Pallas kernels for 10% -> 14%
where the time goes in v4:
time: 86.8 us; the launch traced here: 86.5 us
  waiting for transfers between devices  47.7 us (55%)
  starting transfers between devices  20.2 us (23%)
  Pallas kernels  13.5 us (16%)
  local copies, waits for them, and re-layouts  4.15 us (5%)
    ppermute x16, waiting for transfers between devices, across(): return lax.ppermute(array, 'ctx', [(i, i ^ bits) for i in range(n_ctx)])  41.9 us
    ppermute x16, starting transfers between devices, across(): return lax.ppermute(array, 'ctx', [(i, i ^ bits) for i in range(n_ctx)])  16.6 us
    pallas_call x2, Pallas kernels, project(): pl.pallas_call(functools.partial(project_kernel, count, extra, acc is not...  7.48 us
    ppermute x3, waiting for transfers between devices, over_dp(): return lax.ppermute(array, 'dp', [(d, d ^ bits) for d in range(n_dp)])  5.79 us
    ppermute x3, starting transfers between devices, over_dp(): return lax.ppermute(array, 'dp', [(d, d ^ bits) for d in range(n_dp)])  3.55 us
    unnamed x10, local copies, waits for them, and re-layouts  3.15 us
    pallas_call x1, Pallas kernels, attend(): pl.pallas_call(functools.partial(attend_kernel, count, heads, depth, grou...  2.82 us
    pallas_call x1, Pallas kernels, pack(): pl.pallas_call(pack_kernel, out_shape=[out, out], in_specs=[SMEM, ANY, AN...  2.02 us
  transfers between devices with their start and end apart: 19, of which 13 were waited for; matrix products, arithmetic and copies ran while one was open for 1% of the time, Pallas kernels for 14%

profile of v4, /device:TPU:0, one launch (start us, length us, event | category | flops | bytes accessed | tf_op | source)
XLA Modules:
  0.0 86.5 jit_solution(16684855010924889561)
XLA Ops:
  0.0 0.5 collective-permute-start
  0.5 2.0 %shard_map.73 = (bf16[544,256]{1,0:T(8,128)(2,1)}, bf16[544,256]{1,0:T(8,128)(2,1)}) custom-call(s32[1]{0:T(128)} %bitcast.core_ref, bf16[512,256]{1,0:T(8,128)(2,1)} %key_ref.1, bf16[512,256]{1,0:T(8,128)(2,1)} %value_ref.1, bf16[64,256]{1,0:T(8,128)(2,1)} %query_ref.1), custom_call_target="tpu_custom_call" | custom-call | tf_op jit(solution)/shard_map/pallas_call | solution.py:235
  2.5 3.7 %collective-permute-start.3 = (bf16[544,256]{1,0:T(8,128)(2,1)}, bf16[544,256]{1,0:T(8,128)(2,1)S(1)}, u32[]{:S(2)}, u32[]{:S(2)}) collective-permute-start(bf16[544,256]{1,0:T(8,128)(2,1)} %get-tuple-element.23.refs_3_.refs_4_), channel_id=1, source_target_pairs={{0,4},{1,5},{2,6},{3,7},{4,0},{5,1},{6,2},{7,3},{8,12},{9,13},{10,... | collective-permute-start | bytes 835592 | tf_op jit(solution)/shard_map/ppermute | solution.py:306
  6.1 1.6 %collective-permute-start.1 = (bf16[544,256]{1,0:T(8,128)(2,1)}, bf16[544,256]{1,0:T(8,128)(2,1)S(1)}, u32[]{:S(2)}, u32[]{:S(2)}) collective-permute-start(bf16[544,256]{1,0:T(8,128)(2,1)} %get-tuple-element.23.refs_3_.refs_4_), channel_id=1, source_target_pairs={{0,2},{1,3},{2,0},{3,1},{4,6},{5,7},{6,4},{7,5},{8,10},{9,11},{10,... | collective-permute-start | bytes 835592 | tf_op jit(solution)/shard_map/ppermute | solution.py:306
  7.7 0.0 collective-permute-start.4
  7.7 0.2 collective-permute-start.2
  8.0 0.1 stack.71.refs_2_
  8.0 0.8 slice_bitcast_fusion.3
  8.9 11.0 %collective-permute-done.3.refs_5_.refs_8_ = bf16[544,256]{1,0:T(8,128)(2,1)S(1)} collective-permute-done((bf16[544,256]{1,0:T(8,128)(2,1)}, bf16[544,256]{1,0:T(8,128)(2,1)S(1)}, u32[]{:S(2)}, u32[]{:S(2)}) %collective-permute-start.3) | collective-permute-done | bytes 278560 | tf_op jit(solution)/shard_map/ppermute | solution.py:306
  19.9 1.9 %collective-permute-done.1.refs_3_.refs_6_ = bf16[544,256]{1,0:T(8,128)(2,1)S(1)} collective-permute-done((bf16[544,256]{1,0:T(8,128)(2,1)}, bf16[544,256]{1,0:T(8,128)(2,1)S(1)}, u32[]{:S(2)}, u32[]{:S(2)}) %collective-permute-start.1) | collective-permute-done | bytes 278560 | tf_op jit(solution)/shard_map/ppermute | solution.py:306
  21.8 9.7 %collective-permute-done.4.refs_6_.refs_9_ = bf16[544,256]{1,0:T(8,128)(2,1)S(1)} collective-permute-done((bf16[544,256]{1,0:T(8,128)(2,1)}, bf16[544,256]{1,0:T(8,128)(2,1)S(1)}, u32[]{:S(2)}, u32[]{:S(2)}) %collective-permute-start.4) | collective-permute-done | bytes 278560 | tf_op jit(solution)/shard_map/ppermute | solution.py:306
  31.5 0.0 collective-permute-done.2.refs_4_.refs_7_
  31.5 0.2 collective-permute-start.5
  31.7 1.5 %collective-permute-start.6 = (bf16[544,256]{1,0:T(8,128)(2,1)S(1)}, bf16[544,256]{1,0:T(8,128)(2,1)S(1)}, u32[]{:S(2)}, u32[]{:S(2)}) collective-permute-start(bf16[544,256]{1,0:T(8,128)(2,1)S(1)} %collective-permute-done.3.refs_5_.refs_8_), channel_id=1, source_target_pairs={{0,2},{1,3},{2,0},{3,1},{4,6},{5,7},{6,4},{7,5},{8,10},{9,11},{10,... | collective-permute-start | bytes 835592 | tf_op jit(solution)/shard_map/ppermute | solution.py:306
  33.2 0.5 collective-permute-start.7
  33.7 0.1 slice.8.refs_0_
  33.8 0.0 collective-permute-done.5.refs_4_.refs_5_
  33.8 0.0 collective-permute-done.refs_2_
  33.8 0.0 copy-start
  33.8 2.2 %copy-done = bf16[512,4096]{1,0:T(8,128)(2,1)S(1)} copy-done((bf16[512,4096]{1,0:T(8,128)(2,1)S(1)}, bf16[512,4096]{1,0:T(8,128)(2,1)}, u32[]{:S(2)}) %copy-start) | copy-done | bytes 4194328
  36.0 0.0 copy-start.2
  36.0 1.0 %copy-done.2 = bf16[544,256]{1,0:T(8,128)(2,1)S(1)} copy-done((bf16[544,256]{1,0:T(8,128)(2,1)S(1)}, bf16[544,256]{1,0:T(8,128)(2,1)}, u32[]{:S(2)}) %copy-start.2) | copy-done | bytes 278552
  37.0 0.0 copy-start.1
  37.0 3.3 %shard_map.74 = (f32[1024,256]{1,0:T(8,128)S(1)}, bf16[2,16,512]{2,1,0:T(8,128)(2,1)}) custom-call(s32[2]{0:T(128)S(1)} %bitcast.21, bf16[512,4096]{1,0:T(8,128)(2,1)S(1)} %copy-done, bf16[512,4096]{1,0:T(8,128)(2,1)} %collective-permute-done.refs_2_, bf16[544,256]{1,0:T(8,128)(2,1)S(1)} %copy-done.2, bf16[544,256]{1,0:T(8,128)(2,1)S(1)} %collective-permute-done.5.refs_4_.refs_5_), custom_call_target="tpu_custom_call" | custom-call | flops 536870912 | bytes 2097152 | tf_op jit(solution)/shard_map/pallas_call | solution.py:81
  40.3 0.0 copy-done.1
  40.3 0.0 copy-start.3
  40.3 4.1 %shard_map.75 = (f32[1024,256]{1,0:T(8,128)S(1)}, bf16[4,512,512]{2,1,0:T(8,128)(2,1)S(1)}) custom-call(s32[6]{0:T(128)S(1)} %slice.8.refs_0_, bf16[512,4096]{1,0:T(8,128)(2,1)S(1)} %copy-done.1, bf16[512,4096]{1,0:T(8,128)(2,1)} %collective-permute-done.refs_2_, bf16[544,256]{1,0:T(8,128)(2,1)S(1)} %collective-permute-done.1.refs_3_.refs_6_, ...), custom_call_target="tpu_custom_call" | custom-call | flops 1073741824 | bytes 4194304 | tf_op jit(solution)/shard_map/pallas_call | solution.py:81
  44.5 0.0 copy-start.4
  44.5 0.0 collective-permute-done.6.refs_10_
  44.5 2.1 %collective-permute-done.7.refs_11_ = bf16[544,256]{1,0:T(8,128)(2,1)S(1)} collective-permute-done((bf16[544,256]{1,0:T(8,128)(2,1)S(1)}, bf16[544,256]{1,0:T(8,128)(2,1)S(1)}, u32[]{:S(2)}, u32[]{:S(2)}) %collective-permute-start.7) | collective-permute-done | bytes 278560 | tf_op jit(solution)/shard_map/ppermute | solution.py:306
  46.6 0.0 copy-done.3
  46.6 2.4 %collective-permute-start.13 = (bf16[256,512]{1,0:T(8,128)(2,1)S(1)}, bf16[256,512]{1,0:T(8,128)(2,1)S(1)}, u32[]{:S(2)}, u32[]{:S(2)}) collective-permute-start(bf16[256,512]{1,0:T(8,128)(2,1)S(1)} %copy-done.3), channel_id=1, source_target_pairs={{0,4},{1,5},{2,6},{3,7},{4,0},{5,1},{6,2},{7,3},{8,12},{9,13},{10,... | collective-permute-start | bytes 786440 | tf_op jit(solution)/shard_map/ppermute | solution.py:306
  49.0 0.1 pad_add_fusion.2.refs_0_
  49.1 2.8 %shard_map.76 = (bf16[144,128]{1,0:T(8,128)(2,1)S(1)}, bf16[144,128]{1,0:T(8,128)(2,1)S(1)}, bf16[144,128]{1,0:T(8,128)(2,1)S(1)}, bf16[144,128]{1,0:T(8,128)(2,1)S(1)}) custom-call(s32[2]{0:T(128)S(1)} %pad_add_fusion.2.refs_0_, s32[4]{0:T(128)S(1)} %iota_xor_fusion.refs_1_, s32[8]{0:T(128)S(1)} %stack.71.refs_2_, ...), custom_call_target="tpu_custom_call" | custom-call | flops 536870912 | bytes 2097152 | tf_op jit(solution)/shard_map/pallas_call | solution.py:158
  51.9 1.5 %collective-permute-start.10 = (bf16[144,128]{1,0:T(8,128)(2,1)S(1)}, bf16[144,128]{1,0:T(8,128)(2,1)S(1)}, u32[]{:S(2)}, u32[]{:S(2)}) collective-permute-start(bf16[144,128]{1,0:T(8,128)(2,1)S(1)} %get-tuple-element.32), channel_id=1, source_target_pairs={{0,6},{1,7},{2,4},{3,5},{4,2},{5,3},{6,0},{7,1},{8,14},{9,15},{10,... | collective-permute-start | bytes 110600 | tf_op jit(solution)/shard_map/ppermute | solution.py:306
  53.4 0.4 collective-permute-start.8
  53.8 2.6 %collective-permute-start.9 = (bf16[144,128]{1,0:T(8,128)(2,1)S(1)}, bf16[144,128]{1,0:T(8,128)(2,1)S(1)}, u32[]{:S(2)}, u32[]{:S(2)}) collective-permute-start(bf16[144,128]{1,0:T(8,128)(2,1)S(1)} %get-tuple-element.31), channel_id=1, source_target_pairs={{0,4},{1,5},{2,6},{3,7},{4,0},{5,1},{6,2},{7,3},{8,12},{9,13},{10,... | collective-permute-start | bytes 110600 | tf_op jit(solution)/shard_map/ppermute | solution.py:306
  56.4 0.0 copy-done.4
  56.4 0.8 collective-permute-start.12
  57.2 1.0 %collective-permute-done.10.refs_3_ = bf16[144,128]{1,0:T(8,128)(2,1)S(1)} collective-permute-done((bf16[144,128]{1,0:T(8,128)(2,1)S(1)}, bf16[144,128]{1,0:T(8,128)(2,1)S(1)}, u32[]{:S(2)}, u32[]{:S(2)}) %collective-permute-start.10) | collective-permute-done | bytes 36896 | tf_op jit(solution)/shard_map/ppermute | solution.py:306
  58.2 1.4 %collective-permute-done.8.refs_1_ = bf16[144,128]{1,0:T(8,128)(2,1)S(1)} collective-permute-done((bf16[144,128]{1,0:T(8,128)(2,1)S(1)}, bf16[144,128]{1,0:T(8,128)(2,1)S(1)}, u32[]{:S(2)}, u32[]{:S(2)}) %collective-permute-start.8) | collective-permute-done | bytes 36896 | tf_op jit(solution)/shard_map/ppermute | solution.py:306
  59.5 4.6 %collective-permute-done.9.refs_2_ = bf16[144,128]{1,0:T(8,128)(2,1)S(1)} collective-permute-done((bf16[144,128]{1,0:T(8,128)(2,1)S(1)}, bf16[144,128]{1,0:T(8,128)(2,1)S(1)}, u32[]{:S(2)}, u32[]{:S(2)}) %collective-permute-start.9) | collective-permute-done | bytes 36896 | tf_op jit(solution)/shard_map/ppermute | solution.py:306
  64.1 0.2 shard_map.77.own_ref
  64.3 0.0 collective-permute-done.13.refs_2_
  64.3 0.8 collective-permute-start.14
  65.0 0.0 collective-permute-start.11
  65.0 0.1 pad_add_fusion.1.place_ref
  65.1 1.1 %collective-permute-done.11.sibling_ref = bf16[128,128]{1,0:T(8,128)(2,1)S(1)} collective-permute-done((bf16[128,128]{1,0:T(8,128)(2,1)S(1)}, bf16[128,128]{1,0:T(8,128)(2,1)S(1)}, u32[]{:S(2)}, u32[]{:S(2)}) %collective-permute-start.11) | collective-permute-done | bytes 32800 | tf_op jit(solution)/shard_map/ppermute | solution.py:306
  66.2 2.5 %collective-permute-done.12.refs_1_ = bf16[256,512]{1,0:T(8,128)(2,1)S(1)} collective-permute-done((bf16[256,512]{1,0:T(8,128)(2,1)S(1)}, bf16[256,512]{1,0:T(8,128)(2,1)S(1)}, u32[]{:S(2)}, u32[]{:S(2)}) %collective-permute-start.12) | collective-permute-done | bytes 262176 | tf_op jit(solution)/shard_map/ppermute | solution.py:306
  68.7 5.4 %collective-permute-done.14.refs_3_ = bf16[256,512]{1,0:T(8,128)(2,1)S(1)} collective-permute-done((bf16[256,512]{1,0:T(8,128)(2,1)S(1)}, bf16[256,512]{1,0:T(8,128)(2,1)S(1)}, u32[]{:S(2)}, u32[]{:S(2)}) %collective-permute-start.14) | collective-permute-done | bytes 262176 | tf_op jit(solution)/shard_map/ppermute | solution.py:306
  74.1 1.0 %shard_map.78 = (bf16[128,512]{1,0:T(8,128)(2,1)S(1)}, bf16[128,512]{1,0:T(8,128)(2,1)S(1)}, bf16[128,512]{1,0:T(8,128)(2,1)S(1)}, bf16[128,512]{1,0:T(8,128)(2,1)S(1)}) custom-call(s32[2]{0:T(128)S(1)} %pad_add_fusion.1.place_ref, bf16[128,128]{1,0:T(8,128)(2,1)S(1)} %shard_map.77.own_ref, bf16[128,128]{1,0:T(8,128)(2,1)S(1)} %collective-permute-done.11.sibling_ref, ...), custom_call_target="tpu_custom_call" | custom-call | tf_op jit(solution)/shard_map/pallas_call | solution.py:262
  75.1 1.6 %collective-permute-start.15 = (bf16[128,512]{1,0:T(8,128)(2,1)S(1)}, bf16[128,512]{1,0:T(8,128)(2,1)S(1)}, u32[]{:S(2)}, u32[]{:S(2)}) collective-permute-start(bf16[128,512]{1,0:T(8,128)(2,1)S(1)} %get-tuple-element.36), channel_id=1, source_target_pairs={{0,8},{8,0},{16,24},{24,16},{1,9},{9,1},{17,25},{25,17},{2,10},{10... | collective-permute-start | bytes 393224 | tf_op jit(solution)/shard_map/ppermute | solution.py:309
  76.7 1.5 %collective-permute-start.16 = (bf16[128,512]{1,0:T(8,128)(2,1)S(1)}, bf16[128,512]{1,0:T(8,128)(2,1)S(1)}, u32[]{:S(2)}, u32[]{:S(2)}) collective-permute-start(bf16[128,512]{1,0:T(8,128)(2,1)S(1)} %get-tuple-element.37), channel_id=1, source_target_pairs={{0,16},{8,24},{16,0},{24,8},{1,17},{9,25},{17,1},{25,9},{2,18},{10... | collective-permute-start | bytes 393224 | tf_op jit(solution)/shard_map/ppermute | solution.py:309
  78.2 0.5 collective-permute-start.17
  78.7 2.1 %collective-permute-done.15.refs_1_ = bf16[128,512]{1,0:T(8,128)(2,1)S(1)} collective-permute-done((bf16[128,512]{1,0:T(8,128)(2,1)S(1)}, bf16[128,512]{1,0:T(8,128)(2,1)S(1)}, u32[]{:S(2)}, u32[]{:S(2)}) %collective-permute-start.15) | collective-permute-done | bytes 131104 | tf_op jit(solution)/shard_map/ppermute | solution.py:309
  80.8 3.6 %collective-permute-done.16.refs_2_ = bf16[128,512]{1,0:T(8,128)(2,1)S(1)} collective-permute-done((bf16[128,512]{1,0:T(8,128)(2,1)S(1)}, bf16[128,512]{1,0:T(8,128)(2,1)S(1)}, u32[]{:S(2)}, u32[]{:S(2)}) %collective-permute-start.16) | collective-permute-done | bytes 131104 | tf_op jit(solution)/shard_map/ppermute | solution.py:309
  84.5 0.0 collective-permute-done.17.refs_3_
  84.5 0.1 shard_map.79
  84.5 0.1 collective-permute-start.18
  84.6 1.2 %collective-permute-done.18 = bf16[64,512]{1,0:T(8,128)(2,1)S(1)} collective-permute-done((bf16[64,512]{1,0:T(8,128)(2,1)S(1)}, bf16[64,512]{1,0:T(8,128)(2,1)S(1)}, u32[]{:S(2)}, u32[]{:S(2)}) %collective-permute-start.18) | collective-permute-done | bytes 65568 | tf_op jit(solution)/shard_map/ppermute | solution.py:306
  85.8 0.7 maximum_select_fusion
  (4 shorter events, 0.0 us)
Async XLA Ops:
  0.0 33.8 %collective-permute-start = (bf16[512,4096]{1,0:T(8,128)(2,1)}, bf16[512,4096]{1,0:T(8,128)(2,1)}, u32[]{:S(2)}, u32[]{:S(2)}) collective-permute-start(bf16[512,4096]{1,0:T(8,128)(2,1)} %refs_1_.3), channel_id=1, source_target_pairs={{0,1},{1,0},{2,3},{3,2},{4,5},{5,4},{6,7},{7,6},{8,9},{9,8},{10,11... | collective-permute-start | bytes 12582920 | tf_op jit(solution)/shard_map/ppermute | solution.py:306
  2.5 17.4 %collective-permute-start.3 = (bf16[544,256]{1,0:T(8,128)(2,1)}, bf16[544,256]{1,0:T(8,128)(2,1)S(1)}, u32[]{:S(2)}, u32[]{:S(2)}) collective-permute-start(bf16[544,256]{1,0:T(8,128)(2,1)} %get-tuple-element.23.refs_3_.refs_4_), channel_id=1, source_target_pairs={{0,4},{1,5},{2,6},{3,7},{4,0},{5,1},{6,2},{7,3},{8,12},{9,13},{10,... | collective-permute-start | bytes 835592 | tf_op jit(solution)/shard_map/ppermute | solution.py:306
  6.1 15.7 %collective-permute-start.1 = (bf16[544,256]{1,0:T(8,128)(2,1)}, bf16[544,256]{1,0:T(8,128)(2,1)S(1)}, u32[]{:S(2)}, u32[]{:S(2)}) collective-permute-start(bf16[544,256]{1,0:T(8,128)(2,1)} %get-tuple-element.23.refs_3_.refs_4_), channel_id=1, source_target_pairs={{0,2},{1,3},{2,0},{3,1},{4,6},{5,7},{6,4},{7,5},{8,10},{9,11},{10,... | collective-permute-start | bytes 835592 | tf_op jit(solution)/shard_map/ppermute | solution.py:306
  7.7 23.8 %collective-permute-start.4 = (bf16[544,256]{1,0:T(8,128)(2,1)}, bf16[544,256]{1,0:T(8,128)(2,1)S(1)}, u32[]{:S(2)}, u32[]{:S(2)}) collective-permute-start(bf16[544,256]{1,0:T(8,128)(2,1)} %get-tuple-element.25), channel_id=1, source_target_pairs={{0,5},{1,4},{2,7},{3,6},{4,1},{5,0},{6,3},{7,2},{8,13},{9,12},{10,... | collective-permute-start | bytes 835592 | tf_op jit(solution)/shard_map/ppermute | solution.py:306
  7.7 23.8 %collective-permute-start.2 = (bf16[544,256]{1,0:T(8,128)(2,1)}, bf16[544,256]{1,0:T(8,128)(2,1)S(1)}, u32[]{:S(2)}, u32[]{:S(2)}) collective-permute-start(bf16[544,256]{1,0:T(8,128)(2,1)} %get-tuple-element.25), channel_id=1, source_target_pairs={{0,3},{1,2},{2,1},{3,0},{4,7},{5,6},{6,5},{7,4},{8,11},{9,10},{10,... | collective-permute-start | bytes 835592 | tf_op jit(solution)/shard_map/ppermute | solution.py:306
  31.5 2.3 %collective-permute-start.5 = (bf16[544,256]{1,0:T(8,128)(2,1)}, bf16[544,256]{1,0:T(8,128)(2,1)S(1)}, u32[]{:S(2)}, u32[]{:S(2)}) collective-permute-start(bf16[544,256]{1,0:T(8,128)(2,1)} %get-tuple-element.25), channel_id=1, source_target_pairs={{0,1},{1,0},{2,3},{3,2},{4,5},{5,4},{6,7},{7,6},{8,9},{9,8},{10,11... | collective-permute-start | bytes 835592 | tf_op jit(solution)/shard_map/ppermute | solution.py:306
  31.7 12.8 %collective-permute-start.6 = (bf16[544,256]{1,0:T(8,128)(2,1)S(1)}, bf16[544,256]{1,0:T(8,128)(2,1)S(1)}, u32[]{:S(2)}, u32[]{:S(2)}) collective-permute-start(bf16[544,256]{1,0:T(8,128)(2,1)S(1)} %collective-permute-done.3.refs_5_.refs_8_), channel_id=1, source_target_pairs={{0,2},{1,3},{2,0},{3,1},{4,6},{5,7},{6,4},{7,5},{8,10},{9,11},{10,... | collective-permute-start | bytes 835592 | tf_op jit(solution)/shard_map/ppermute | solution.py:306
  33.2 13.4 %collective-permute-start.7 = (bf16[544,256]{1,0:T(8,128)(2,1)S(1)}, bf16[544,256]{1,0:T(8,128)(2,1)S(1)}, u32[]{:S(2)}, u32[]{:S(2)}) collective-permute-start(bf16[544,256]{1,0:T(8,128)(2,1)S(1)} %collective-permute-done.4.refs_6_.refs_9_), channel_id=1, source_target_pairs={{0,2},{1,3},{2,0},{3,1},{4,6},{5,7},{6,4},{7,5},{8,10},{9,11},{10,... | collective-permute-start | bytes 835592 | tf_op jit(solution)/shard_map/ppermute | solution.py:306
  33.8 2.2 %copy-start = (bf16[512,4096]{1,0:T(8,128)(2,1)S(1)}, bf16[512,4096]{1,0:T(8,128)(2,1)}, u32[]{:S(2)}) copy-start(bf16[512,4096]{1,0:T(8,128)(2,1)} %refs_1_.3) | copy-start | bytes 12582916
  36.0 1.0 %copy-start.2 = (bf16[544,256]{1,0:T(8,128)(2,1)S(1)}, bf16[544,256]{1,0:T(8,128)(2,1)}, u32[]{:S(2)}) copy-start(bf16[544,256]{1,0:T(8,128)(2,1)} %get-tuple-element.23.refs_3_.refs_4_) | copy-start | bytes 835588
  37.0 3.4 %copy-start.1 = (bf16[512,4096]{1,0:T(8,128)(2,1)S(1)}, bf16[512,4096]{1,0:T(8,128)(2,1)}, u32[]{:S(2)}) copy-start(bf16[512,4096]{1,0:T(8,128)(2,1)} %refs_1_.3) | copy-start | bytes 12582916
  40.3 6.3 %copy-start.3 = (bf16[256,512]{1,0:T(8,128)(2,1)S(1)}, bf16[256,512]{1,0:T(8,128)(2,1)}, u32[]{:S(2)}) copy-start(bf16[256,512]{1,0:T(8,128)(2,1)} %refs_0_) | copy-start | bytes 786436
  44.5 11.9 %copy-start.4 = (bf16[256]{0:T(256)(128)(2,1)S(1)}, bf16[256]{0:T(256)(128)(2,1)}, u32[]{:S(2)}) copy-start(bf16[256]{0:T(256)(128)(2,1)} %param.12) | copy-start | bytes 1540
  46.6 17.7 %collective-permute-start.13 = (bf16[256,512]{1,0:T(8,128)(2,1)S(1)}, bf16[256,512]{1,0:T(8,128)(2,1)S(1)}, u32[]{:S(2)}, u32[]{:S(2)}) collective-permute-start(bf16[256,512]{1,0:T(8,128)(2,1)S(1)} %copy-done.3), channel_id=1, source_target_pairs={{0,4},{1,5},{2,6},{3,7},{4,0},{5,1},{6,2},{7,3},{8,12},{9,13},{10,... | collective-permute-start | bytes 786440 | tf_op jit(solution)/shard_map/ppermute | solution.py:306
  51.9 6.3 %collective-permute-start.10 = (bf16[144,128]{1,0:T(8,128)(2,1)S(1)}, bf16[144,128]{1,0:T(8,128)(2,1)S(1)}, u32[]{:S(2)}, u32[]{:S(2)}) collective-permute-start(bf16[144,128]{1,0:T(8,128)(2,1)S(1)} %get-tuple-element.32), channel_id=1, source_target_pairs={{0,6},{1,7},{2,4},{3,5},{4,2},{5,3},{6,0},{7,1},{8,14},{9,15},{10,... | collective-permute-start | bytes 110600 | tf_op jit(solution)/shard_map/ppermute | solution.py:306
  53.4 6.1 %collective-permute-start.8 = (bf16[144,128]{1,0:T(8,128)(2,1)S(1)}, bf16[144,128]{1,0:T(8,128)(2,1)S(1)}, u32[]{:S(2)}, u32[]{:S(2)}) collective-permute-start(bf16[144,128]{1,0:T(8,128)(2,1)S(1)} %get-tuple-element.30), channel_id=1, source_target_pairs={{0,2},{1,3},{2,0},{3,1},{4,6},{5,7},{6,4},{7,5},{8,10},{9,11},{10,... | collective-permute-start | bytes 110600 | tf_op jit(solution)/shard_map/ppermute | solution.py:306
  53.8 10.3 %collective-permute-start.9 = (bf16[144,128]{1,0:T(8,128)(2,1)S(1)}, bf16[144,128]{1,0:T(8,128)(2,1)S(1)}, u32[]{:S(2)}, u32[]{:S(2)}) collective-permute-start(bf16[144,128]{1,0:T(8,128)(2,1)S(1)} %get-tuple-element.31), channel_id=1, source_target_pairs={{0,4},{1,5},{2,6},{3,7},{4,0},{5,1},{6,2},{7,3},{8,12},{9,13},{10,... | collective-permute-start | bytes 110600 | tf_op jit(solution)/shard_map/ppermute | solution.py:306
  56.4 12.4 %collective-permute-start.12 = (bf16[256,512]{1,0:T(8,128)(2,1)S(1)}, bf16[256,512]{1,0:T(8,128)(2,1)S(1)}, u32[]{:S(2)}, u32[]{:S(2)}) collective-permute-start(bf16[256,512]{1,0:T(8,128)(2,1)S(1)} %copy-done.3), channel_id=1, source_target_pairs={{0,2},{1,3},{2,0},{3,1},{4,6},{5,7},{6,4},{7,5},{8,10},{9,11},{10,... | collective-permute-start | bytes 786440 | tf_op jit(solution)/shard_map/ppermute | solution.py:306
  64.3 9.8 %collective-permute-start.14 = (bf16[256,512]{1,0:T(8,128)(2,1)S(1)}, bf16[256,512]{1,0:T(8,128)(2,1)S(1)}, u32[]{:S(2)}, u32[]{:S(2)}) collective-permute-start(bf16[256,512]{1,0:T(8,128)(2,1)S(1)} %collective-permute-done.13.refs_2_), channel_id=1, source_target_pairs={{0,2},{1,3},{2,0},{3,1},{4,6},{5,7},{6,4},{7,5},{8,10},{9,11},{10,... | collective-permute-start | bytes 786440 | tf_op jit(solution)/shard_map/ppermute | solution.py:306
  65.0 1.2 %collective-permute-start.11 = (bf16[128,128]{1,0:T(8,128)(2,1)S(1)}, bf16[128,128]{1,0:T(8,128)(2,1)S(1)}, u32[]{:S(2)}, u32[]{:S(2)}) collective-permute-start(bf16[128,128]{1,0:T(8,128)(2,1)S(1)} %shard_map.77.own_ref), channel_id=1, source_target_pairs={{0,1},{1,0},{2,3},{3,2},{4,5},{5,4},{6,7},{7,6},{8,9},{9,8},{10,11... | collective-permute-start | bytes 98312 | tf_op jit(solution)/shard_map/ppermute | solution.py:306
  75.1 5.7 %collective-permute-start.15 = (bf16[128,512]{1,0:T(8,128)(2,1)S(1)}, bf16[128,512]{1,0:T(8,128)(2,1)S(1)}, u32[]{:S(2)}, u32[]{:S(2)}) collective-permute-start(bf16[128,512]{1,0:T(8,128)(2,1)S(1)} %get-tuple-element.36), channel_id=1, source_target_pairs={{0,8},{8,0},{16,24},{24,16},{1,9},{9,1},{17,25},{25,17},{2,10},{10... | collective-permute-start | bytes 393224 | tf_op jit(solution)/shard_map/ppermute | solution.py:309
  76.7 7.8 %collective-permute-start.16 = (bf16[128,512]{1,0:T(8,128)(2,1)S(1)}, bf16[128,512]{1,0:T(8,128)(2,1)S(1)}, u32[]{:S(2)}, u32[]{:S(2)}) collective-permute-start(bf16[128,512]{1,0:T(8,128)(2,1)S(1)} %get-tuple-element.37), channel_id=1, source_target_pairs={{0,16},{8,24},{16,0},{24,8},{1,17},{9,25},{17,1},{25,9},{2,18},{10... | collective-permute-start | bytes 393224 | tf_op jit(solution)/shard_map/ppermute | solution.py:309
  78.2 6.3 %collective-permute-start.17 = (bf16[128,512]{1,0:T(8,128)(2,1)S(1)}, bf16[128,512]{1,0:T(8,128)(2,1)S(1)}, u32[]{:S(2)}, u32[]{:S(2)}) collective-permute-start(bf16[128,512]{1,0:T(8,128)(2,1)S(1)} %get-tuple-element.38), channel_id=1, source_target_pairs={{0,24},{8,16},{16,8},{24,0},{1,25},{9,17},{17,9},{25,1},{2,26},{10... | collective-permute-start | bytes 393224 | tf_op jit(solution)/shard_map/ppermute | solution.py:309
  84.5 1.3 %collective-permute-start.18 = (bf16[64,512]{1,0:T(8,128)(2,1)S(1)}, bf16[64,512]{1,0:T(8,128)(2,1)S(1)}, u32[]{:S(2)}, u32[]{:S(2)}) collective-permute-start(bf16[64,512]{1,0:T(8,128)(2,1)S(1)} %get-tuple-element.40), channel_id=1, source_target_pairs={{0,1},{1,0},{2,3},{3,2},{4,5},{5,4},{6,7},{7,6},{8,9},{9,8},{10,11... | collective-permute-start | bytes 196616 | tf_op jit(solution)/shard_map/ppermute | solution.py:306

commit v5 on v4

--- a/solution.py
+++ b/solution.py
@@ -236,7 +236,7 @@
         pack_kernel,
         out_shape=[out, out],
         in_specs=[SMEM, ANY, ANY, ANY],
-        out_specs=[VMEM, VMEM],
+        out_specs=[ANY, ANY],
         scratch_shapes=[pltpu.SemaphoreType.DMA((8,))],
         compiler_params=WIDE,
     )(core, w_key, w_value, queries)
@@ -320,7 +320,7 @@
             pairs[j] = (across(own_part, CORES * j), across(other_part, CORES * j + 1))
         else:
             pairs[j] = tuple(across(part, CORES * low) for part in pairs[j ^ low])
-    context_sibling = across(context, 1)
+    context_sibling = across(after(context, own_part), 1)
     pairs[0] = (own_part, across(after(other_part, pairs[1], pairs[chips // 2]), 1))
 
     places = jnp.stack(
@@ -329,9 +329,9 @@
     starts = places * depth
     blocks = [part for pair in pairs for part in pair]
     last = CORES * (chips - 1)
-    acc, _ = project(starts[:CORES], context, context_sibling, blocks[:CORES], None, depth)
+    first_acc, _ = project(starts[:CORES], context, context_sibling, blocks[:CORES], None, depth)
     acc, slices = project(
-        starts[CORES:], context, context_sibling, blocks[CORES:last], acc, depth
+        starts[CORES:], context, context_sibling, blocks[CORES:last], first_acc, depth
     )
     firsts = jnp.stack([me * rows, (me ^ 1) * rows]).astype(jnp.int32)
     groups = tuple((CORES * z, CORES * z + 1) for z in range(chips))
@@ -340,13 +340,13 @@
         firsts, slot_groups, places, slices, blocks, acc, offsets, groups, heads, depth
     )
     arrived = [messages[0]] + [across(messages[j], CORES * j) for j in range(1, chips)]
-    normed = combine(core_only, arrived, head_gain.reshape(1, panel), heads)
-
-    shards = [after(w_out, *pairs[-1], acc)] + [None] * (chips - 1)
+    shards = [after(w_out, acc, *pairs[-1])] + [None] * (chips - 1)
     for j in near_first:
         low = j & -j
         shard = shards[j ^ low]
-        shards[j] = across(shard if j == low else after(shard, normed), CORES * low)
+        shards[j] = across(shard if j == low else after(shard, *arrived[1:]), CORES * low)
+    normed = combine(core_only, arrived, head_gain.reshape(1, panel), heads)
+
     terms = output_terms(
         jnp.stack([mine_dp ^ chip, core]).astype(jnp.int32), normed, across(normed, 1), shards
     )

time: 86.8 us -> 103 us (1.19)
  Pallas kernels: 13.5 us -> 29.3 us
    pallas_call x1, Pallas kernels: 2.02 us -> 18 us  [pack(): pl.pallas_call(pack_kernel, out_shape=[out, out], in_specs=[SMEM, ANY, AN...]
  transfers between devices with their start and end apart: 19 -> 19, of which waited for: 13 -> 13; matrix products, arithmetic and copies ran while one was open for 1% -> 1% of each run, Pallas kernels for 14% -> 10%
where the time goes in v5:
time: 103 us
  waiting for transfers between devices  47.7 us (46%)
  Pallas kernels  29.3 us (28%)
  starting transfers between devices  20.4 us (20%)
  local copies, waits for them, and re-layouts  4.15 us (4%)
    ppermute x16, waiting for transfers between devices, across(): return lax.ppermute(array, 'ctx', [(i, i ^ bits) for i in range(n_ctx)])  41.9 us
    pallas_call x1, Pallas kernels, pack(): pl.pallas_call(pack_kernel, out_shape=[out, out], in_specs=[SMEM, ANY, AN...  18 us
    ppermute x16, starting transfers between devices, across(): return lax.ppermute(array, 'ctx', [(i, i ^ bits) for i in range(n_ctx)])  16.9 us
    pallas_call x2, Pallas kernels, project(): pl.pallas_call(functools.partial(project_kernel, count, extra, acc is not...  7.2 us
    ppermute x3, waiting for transfers between devices, over_dp(): return lax.ppermute(array, 'dp', [(d, d ^ bits) for d in range(n_dp)])  5.78 us
    ppermute x3, starting transfers between devices, over_dp(): return lax.ppermute(array, 'dp', [(d, d ^ bits) for d in range(n_dp)])  3.55 us
    unnamed x10, local copies, waits for them, and re-layouts  3.16 us
    pallas_call x1, Pallas kernels, attend(): pl.pallas_call(functools.partial(attend_kernel, count, heads, depth, grou...  2.82 us
  transfers between devices with their start and end apart: 19, of which 13 were waited for; matrix products, arithmetic and copies ran while one was open for 1% of the time, Pallas kernels for 10%

profile of v5, /device:TPU:0, one launch (start us, length us, event | category | flops | bytes accessed | tf_op | source)
XLA Modules:
  0.0 102.6 jit_solution(8671673989684505272)
XLA Ops:
  0.0 18.0 %shard_map.73 = (bf16[544,256]{1,0:T(8,128)(2,1)}, bf16[544,256]{1,0:T(8,128)(2,1)}) custom-call(s32[1]{0:T(128)} %bitcast.core_ref, bf16[512,256]{1,0:T(8,128)(2,1)} %key_ref.1, bf16[512,256]{1,0:T(8,128)(2,1)} %value_ref.1, bf16[64,256]{1,0:T(8,128)(2,1)} %query_ref.1), custom_call_target="tpu_custom_call" | custom-call | tf_op jit(solution)/shard_map/pallas_call | solution.py:235
  18.1 0.5 collective-permute-start
  18.6 3.7 %collective-permute-start.3 = (bf16[544,256]{1,0:T(8,128)(2,1)}, bf16[544,256]{1,0:T(8,128)(2,1)S(1)}, u32[]{:S(2)}, u32[]{:S(2)}) collective-permute-start(bf16[544,256]{1,0:T(8,128)(2,1)} %get-tuple-element.24.refs_3_.refs_4_), channel_id=1, source_target_pairs={{0,4},{1,5},{2,6},{3,7},{4,0},{5,1},{6,2},{7,3},{8,12},{9,13},{10,... | collective-permute-start | bytes 835592 | tf_op jit(solution)/shard_map/ppermute | solution.py:306
  22.2 1.6 %collective-permute-start.1 = (bf16[544,256]{1,0:T(8,128)(2,1)}, bf16[544,256]{1,0:T(8,128)(2,1)S(1)}, u32[]{:S(2)}, u32[]{:S(2)}) collective-permute-start(bf16[544,256]{1,0:T(8,128)(2,1)} %get-tuple-element.24.refs_3_.refs_4_), channel_id=1, source_target_pairs={{0,2},{1,3},{2,0},{3,1},{4,6},{5,7},{6,4},{7,5},{8,10},{9,11},{10,... | collective-permute-start | bytes 835592 | tf_op jit(solution)/shard_map/ppermute | solution.py:306
  23.8 0.0 collective-permute-start.4
  23.8 0.2 collective-permute-start.2
  24.1 0.1 stack.71.refs_2_
  24.1 0.8 slice_bitcast_fusion.3
  25.0 11.0 %collective-permute-done.3.refs_5_.refs_8_ = bf16[544,256]{1,0:T(8,128)(2,1)S(1)} collective-permute-done((bf16[544,256]{1,0:T(8,128)(2,1)}, bf16[544,256]{1,0:T(8,128)(2,1)S(1)}, u32[]{:S(2)}, u32[]{:S(2)}) %collective-permute-start.3) | collective-permute-done | bytes 278560 | tf_op jit(solution)/shard_map/ppermute | solution.py:306
  36.0 1.9 %collective-permute-done.1.refs_3_.refs_6_ = bf16[544,256]{1,0:T(8,128)(2,1)S(1)} collective-permute-done((bf16[544,256]{1,0:T(8,128)(2,1)}, bf16[544,256]{1,0:T(8,128)(2,1)S(1)}, u32[]{:S(2)}, u32[]{:S(2)}) %collective-permute-start.1) | collective-permute-done | bytes 278560 | tf_op jit(solution)/shard_map/ppermute | solution.py:306
  37.9 9.6 %collective-permute-done.4.refs_6_.refs_9_ = bf16[544,256]{1,0:T(8,128)(2,1)S(1)} collective-permute-done((bf16[544,256]{1,0:T(8,128)(2,1)}, bf16[544,256]{1,0:T(8,128)(2,1)S(1)}, u32[]{:S(2)}, u32[]{:S(2)}) %collective-permute-start.4) | collective-permute-done | bytes 278560 | tf_op jit(solution)/shard_map/ppermute | solution.py:306
  47.5 0.0 collective-permute-done.2.refs_4_.refs_7_
  47.5 0.2 collective-permute-start.5
  47.7 1.5 %collective-permute-start.6 = (bf16[544,256]{1,0:T(8,128)(2,1)S(1)}, bf16[544,256]{1,0:T(8,128)(2,1)S(1)}, u32[]{:S(2)}, u32[]{:S(2)}) collective-permute-start(bf16[544,256]{1,0:T(8,128)(2,1)S(1)} %collective-permute-done.3.refs_5_.refs_8_), channel_id=1, source_target_pairs={{0,2},{1,3},{2,0},{3,1},{4,6},{5,7},{6,4},{7,5},{8,10},{9,11},{10,... | collective-permute-start | bytes 835592 | tf_op jit(solution)/shard_map/ppermute | solution.py:306
  49.3 0.5 collective-permute-start.7
  49.8 0.1 slice.8.refs_0_
  49.8 0.0 collective-permute-done.5.refs_4_.refs_5_
  49.8 0.0 collective-permute-done.refs_2_
  49.8 0.0 copy-start
  49.9 2.2 %copy-done = bf16[512,4096]{1,0:T(8,128)(2,1)S(1)} copy-done((bf16[512,4096]{1,0:T(8,128)(2,1)S(1)}, bf16[512,4096]{1,0:T(8,128)(2,1)}, u32[]{:S(2)}) %copy-start) | copy-done | bytes 4194328
  52.0 0.0 copy-start.1
  52.0 1.0 copy-done.1
  53.0 3.1 %shard_map.74 = (f32[1024,256]{1,0:T(8,128)S(1)}, bf16[2,16,512]{2,1,0:T(8,128)(2,1)}) custom-call(s32[2]{0:T(128)S(1)} %bitcast.21, bf16[512,4096]{1,0:T(8,128)(2,1)S(1)} %copy-done, bf16[512,4096]{1,0:T(8,128)(2,1)} %collective-permute-done.refs_2_, bf16[544,256]{1,0:T(8,128)(2,1)S(1)} %copy-done.1, bf16[544,256]{1,0:T(8,128)(2,1)S(1)} %collective-permute-done.5.refs_4_.refs_5_), custom_call_target="tpu_custom_call" | custom-call | flops 536870912 | bytes 2097152 | tf_op jit(solution)/shard_map/pallas_call | solution.py:81
  56.0 0.0 copy-start.3
  56.1 0.0 copy-start.2
  56.1 4.1 %shard_map.75 = (f32[1024,256]{1,0:T(8,128)S(1)}, bf16[4,512,512]{2,1,0:T(8,128)(2,1)S(1)}) custom-call(s32[6]{0:T(128)S(1)} %slice.8.refs_0_, bf16[512,4096]{1,0:T(8,128)(2,1)S(1)} %copy-done, bf16[512,4096]{1,0:T(8,128)(2,1)} %collective-permute-done.refs_2_, bf16[544,256]{1,0:T(8,128)(2,1)S(1)} %collective-permute-done.1.refs_3_.refs_6_, ...), custom_call_target="tpu_custom_call" | custom-call | flops 1073741824 | bytes 4194304 | tf_op jit(solution)/shard_map/pallas_call | solution.py:81
  60.2 0.0 copy-start.4
  60.2 0.0 collective-permute-done.6.refs_10_
  60.2 2.3 %collective-permute-done.7.refs_11_ = bf16[544,256]{1,0:T(8,128)(2,1)S(1)} collective-permute-done((bf16[544,256]{1,0:T(8,128)(2,1)S(1)}, bf16[544,256]{1,0:T(8,128)(2,1)S(1)}, u32[]{:S(2)}, u32[]{:S(2)}) %collective-permute-start.7) | collective-permute-done | bytes 278560 | tf_op jit(solution)/shard_map/ppermute | solution.py:306
  62.5 0.0 copy-done.3
  62.5 2.5 %collective-permute-start.13 = (bf16[256,512]{1,0:T(8,128)(2,1)S(1)}, bf16[256,512]{1,0:T(8,128)(2,1)S(1)}, u32[]{:S(2)}, u32[]{:S(2)}) collective-permute-start(bf16[256,512]{1,0:T(8,128)(2,1)S(1)} %copy-done.3), channel_id=1, source_target_pairs={{0,4},{1,5},{2,6},{3,7},{4,0},{5,1},{6,2},{7,3},{8,12},{9,13},{10,... | collective-permute-start | bytes 786440 | tf_op jit(solution)/shard_map/ppermute | solution.py:306
  65.0 0.1 pad_add_fusion.2.refs_0_
  65.1 0.0 copy-done.2
  65.1 2.8 %shard_map.76 = (bf16[144,128]{1,0:T(8,128)(2,1)S(1)}, bf16[144,128]{1,0:T(8,128)(2,1)S(1)}, bf16[144,128]{1,0:T(8,128)(2,1)S(1)}, bf16[144,128]{1,0:T(8,128)(2,1)S(1)}) custom-call(s32[2]{0:T(128)S(1)} %pad_add_fusion.2.refs_0_, s32[4]{0:T(128)S(1)} %iota_xor_fusion.refs_1_, s32[8]{0:T(128)S(1)} %stack.71.refs_2_, ...), custom_call_target="tpu_custom_call" | custom-call | flops 536870912 | bytes 2097152 | tf_op jit(solution)/shard_map/pallas_call | solution.py:158
  67.9 1.4 %collective-permute-start.10 = (bf16[144,128]{1,0:T(8,128)(2,1)S(1)}, bf16[144,128]{1,0:T(8,128)(2,1)S(1)}, u32[]{:S(2)}, u32[]{:S(2)}) collective-permute-start(bf16[144,128]{1,0:T(8,128)(2,1)S(1)} %get-tuple-element.34), channel_id=1, source_target_pairs={{0,6},{1,7},{2,4},{3,5},{4,2},{5,3},{6,0},{7,1},{8,14},{9,15},{10,... | collective-permute-start | bytes 110600 | tf_op jit(solution)/shard_map/ppermute | solution.py:306
  69.4 0.5 collective-permute-start.8
  69.8 2.6 %collective-permute-start.9 = (bf16[144,128]{1,0:T(8,128)(2,1)S(1)}, bf16[144,128]{1,0:T(8,128)(2,1)S(1)}, u32[]{:S(2)}, u32[]{:S(2)}) collective-permute-start(bf16[144,128]{1,0:T(8,128)(2,1)S(1)} %get-tuple-element.33), channel_id=1, source_target_pairs={{0,4},{1,5},{2,6},{3,7},{4,0},{5,1},{6,2},{7,3},{8,12},{9,13},{10,... | collective-permute-start | bytes 110600 | tf_op jit(solution)/shard_map/ppermute | solution.py:306
  72.4 0.8 collective-permute-start.12
  73.2 1.0 collective-permute-done.10.refs_3_
  74.2 0.1 collective-permute-done.8.refs_1_
  74.3 5.9 %collective-permute-done.9.refs_2_ = bf16[144,128]{1,0:T(8,128)(2,1)S(1)} collective-permute-done((bf16[144,128]{1,0:T(8,128)(2,1)S(1)}, bf16[144,128]{1,0:T(8,128)(2,1)S(1)}, u32[]{:S(2)}, u32[]{:S(2)}) %collective-permute-start.9) | collective-permute-done | bytes 36896 | tf_op jit(solution)/shard_map/ppermute | solution.py:306
  80.1 0.0 collective-permute-done.13.refs_2_
  80.1 0.7 collective-permute-start.14
  80.8 0.0 copy-done.4
  80.8 0.2 shard_map.77.own_ref
  81.0 0.1 collective-permute-start.11
  81.1 0.1 pad_add_fusion.1.place_ref
  81.2 1.1 %collective-permute-done.11.sibling_ref = bf16[128,128]{1,0:T(8,128)(2,1)S(1)} collective-permute-done((bf16[128,128]{1,0:T(8,128)(2,1)S(1)}, bf16[128,128]{1,0:T(8,128)(2,1)S(1)}, u32[]{:S(2)}, u32[]{:S(2)}) %collective-permute-start.11) | collective-permute-done | bytes 32800 | tf_op jit(solution)/shard_map/ppermute | solution.py:306
  82.3 2.5 %collective-permute-done.12.refs_1_ = bf16[256,512]{1,0:T(8,128)(2,1)S(1)} collective-permute-done((bf16[256,512]{1,0:T(8,128)(2,1)S(1)}, bf16[256,512]{1,0:T(8,128)(2,1)S(1)}, u32[]{:S(2)}, u32[]{:S(2)}) %collective-permute-start.12) | collective-permute-done | bytes 262176 | tf_op jit(solution)/shard_map/ppermute | solution.py:306
  84.8 5.3 %collective-permute-done.14.refs_3_ = bf16[256,512]{1,0:T(8,128)(2,1)S(1)} collective-permute-done((bf16[256,512]{1,0:T(8,128)(2,1)S(1)}, bf16[256,512]{1,0:T(8,128)(2,1)S(1)}, u32[]{:S(2)}, u32[]{:S(2)}) %collective-permute-start.14) | collective-permute-done | bytes 262176 | tf_op jit(solution)/shard_map/ppermute | solution.py:306
  90.1 1.0 shard_map.78
  91.1 1.6 %collective-permute-start.15 = (bf16[128,512]{1,0:T(8,128)(2,1)S(1)}, bf16[128,512]{1,0:T(8,128)(2,1)S(1)}, u32[]{:S(2)}, u32[]{:S(2)}) collective-permute-start(bf16[128,512]{1,0:T(8,128)(2,1)S(1)} %get-tuple-element.38), channel_id=1, source_target_pairs={{0,8},{8,0},{16,24},{24,16},{1,9},{9,1},{17,25},{25,17},{2,10},{10... | collective-permute-start | bytes 393224 | tf_op jit(solution)/shard_map/ppermute | solution.py:309
  92.7 1.5 %collective-permute-start.16 = (bf16[128,512]{1,0:T(8,128)(2,1)S(1)}, bf16[128,512]{1,0:T(8,128)(2,1)S(1)}, u32[]{:S(2)}, u32[]{:S(2)}) collective-permute-start(bf16[128,512]{1,0:T(8,128)(2,1)S(1)} %get-tuple-element.39), channel_id=1, source_target_pairs={{0,16},{8,24},{16,0},{24,8},{1,17},{9,25},{17,1},{25,9},{2,18},{10... | collective-permute-start | bytes 393224 | tf_op jit(solution)/shard_map/ppermute | solution.py:309
  94.2 0.5 collective-permute-start.17
  94.7 2.1 %collective-permute-done.15.refs_1_ = bf16[128,512]{1,0:T(8,128)(2,1)S(1)} collective-permute-done((bf16[128,512]{1,0:T(8,128)(2,1)S(1)}, bf16[128,512]{1,0:T(8,128)(2,1)S(1)}, u32[]{:S(2)}, u32[]{:S(2)}) %collective-permute-start.15) | collective-permute-done | bytes 131104 | tf_op jit(solution)/shard_map/ppermute | solution.py:309
  96.8 3.7 %collective-permute-done.16.refs_2_ = bf16[128,512]{1,0:T(8,128)(2,1)S(1)} collective-permute-done((bf16[128,512]{1,0:T(8,128)(2,1)S(1)}, bf16[128,512]{1,0:T(8,128)(2,1)S(1)}, u32[]{:S(2)}, u32[]{:S(2)}) %collective-permute-start.16) | collective-permute-done | bytes 131104 | tf_op jit(solution)/shard_map/ppermute | solution.py:309
  100.5 0.0 collective-permute-done.17.refs_3_
  100.5 0.1 shard_map.79
  100.6 0.1 collective-permute-start.18
  100.6 1.2 %collective-permute-done.18 = bf16[64,512]{1,0:T(8,128)(2,1)S(1)} collective-permute-done((bf16[64,512]{1,0:T(8,128)(2,1)S(1)}, bf16[64,512]{1,0:T(8,128)(2,1)S(1)}, u32[]{:S(2)}, u32[]{:S(2)}) %collective-permute-start.18) | collective-permute-done | bytes 65568 | tf_op jit(solution)/shard_map/ppermute | solution.py:306
  101.9 0.7 maximum_select_fusion
  (4 shorter events, 0.0 us)
Async XLA Ops:
  18.1 31.8 %collective-permute-start = (bf16[512,4096]{1,0:T(8,128)(2,1)}, bf16[512,4096]{1,0:T(8,128)(2,1)}, u32[]{:S(2)}, u32[]{:S(2)}) collective-permute-start(bf16[512,4096]{1,0:T(8,128)(2,1)} %refs_1_.3), channel_id=1, source_target_pairs={{0,1},{1,0},{2,3},{3,2},{4,5},{5,4},{6,7},{7,6},{8,9},{9,8},{10,11... | collective-permute-start | bytes 12582920 | tf_op jit(solution)/shard_map/ppermute | solution.py:306
  18.6 17.5 %collective-permute-start.3 = (bf16[544,256]{1,0:T(8,128)(2,1)}, bf16[544,256]{1,0:T(8,128)(2,1)S(1)}, u32[]{:S(2)}, u32[]{:S(2)}) collective-permute-start(bf16[544,256]{1,0:T(8,128)(2,1)} %get-tuple-element.24.refs_3_.refs_4_), channel_id=1, source_target_pairs={{0,4},{1,5},{2,6},{3,7},{4,0},{5,1},{6,2},{7,3},{8,12},{9,13},{10,... | collective-permute-start | bytes 835592 | tf_op jit(solution)/shard_map/ppermute | solution.py:306
  22.2 15.7 %collective-permute-start.1 = (bf16[544,256]{1,0:T(8,128)(2,1)}, bf16[544,256]{1,0:T(8,128)(2,1)S(1)}, u32[]{:S(2)}, u32[]{:S(2)}) collective-permute-start(bf16[544,256]{1,0:T(8,128)(2,1)} %get-tuple-element.24.refs_3_.refs_4_), channel_id=1, source_target_pairs={{0,2},{1,3},{2,0},{3,1},{4,6},{5,7},{6,4},{7,5},{8,10},{9,11},{10,... | collective-permute-start | bytes 835592 | tf_op jit(solution)/shard_map/ppermute | solution.py:306
  23.8 23.7 %collective-permute-start.4 = (bf16[544,256]{1,0:T(8,128)(2,1)}, bf16[544,256]{1,0:T(8,128)(2,1)S(1)}, u32[]{:S(2)}, u32[]{:S(2)}) collective-permute-start(bf16[544,256]{1,0:T(8,128)(2,1)} %get-tuple-element.27), channel_id=1, source_target_pairs={{0,5},{1,4},{2,7},{3,6},{4,1},{5,0},{6,3},{7,2},{8,13},{9,12},{10,... | collective-permute-start | bytes 835592 | tf_op jit(solution)/shard_map/ppermute | solution.py:306
  23.8 23.7 %collective-permute-start.2 = (bf16[544,256]{1,0:T(8,128)(2,1)}, bf16[544,256]{1,0:T(8,128)(2,1)S(1)}, u32[]{:S(2)}, u32[]{:S(2)}) collective-permute-start(bf16[544,256]{1,0:T(8,128)(2,1)} %get-tuple-element.27), channel_id=1, source_target_pairs={{0,3},{1,2},{2,1},{3,0},{4,7},{5,6},{6,5},{7,4},{8,11},{9,10},{10,... | collective-permute-start | bytes 835592 | tf_op jit(solution)/shard_map/ppermute | solution.py:306
  47.5 2.4 %collective-permute-start.5 = (bf16[544,256]{1,0:T(8,128)(2,1)}, bf16[544,256]{1,0:T(8,128)(2,1)S(1)}, u32[]{:S(2)}, u32[]{:S(2)}) collective-permute-start(bf16[544,256]{1,0:T(8,128)(2,1)} %get-tuple-element.27), channel_id=1, source_target_pairs={{0,1},{1,0},{2,3},{3,2},{4,5},{5,4},{6,7},{7,6},{8,9},{9,8},{10,11... | collective-permute-start | bytes 835592 | tf_op jit(solution)/shard_map/ppermute | solution.py:306
  47.7 12.5 %collective-permute-start.6 = (bf16[544,256]{1,0:T(8,128)(2,1)S(1)}, bf16[544,256]{1,0:T(8,128)(2,1)S(1)}, u32[]{:S(2)}, u32[]{:S(2)}) collective-permute-start(bf16[544,256]{1,0:T(8,128)(2,1)S(1)} %collective-permute-done.3.refs_5_.refs_8_), channel_id=1, source_target_pairs={{0,2},{1,3},{2,0},{3,1},{4,6},{5,7},{6,4},{7,5},{8,10},{9,11},{10,... | collective-permute-start | bytes 835592 | tf_op jit(solution)/shard_map/ppermute | solution.py:306
  49.3 13.3 %collective-permute-start.7 = (bf16[544,256]{1,0:T(8,128)(2,1)S(1)}, bf16[544,256]{1,0:T(8,128)(2,1)S(1)}, u32[]{:S(2)}, u32[]{:S(2)}) collective-permute-start(bf16[544,256]{1,0:T(8,128)(2,1)S(1)} %collective-permute-done.4.refs_6_.refs_9_), channel_id=1, source_target_pairs={{0,2},{1,3},{2,0},{3,1},{4,6},{5,7},{6,4},{7,5},{8,10},{9,11},{10,... | collective-permute-start | bytes 835592 | tf_op jit(solution)/shard_map/ppermute | solution.py:306
  49.8 2.2 %copy-start = (bf16[512,4096]{1,0:T(8,128)(2,1)S(1)}, bf16[512,4096]{1,0:T(8,128)(2,1)}, u32[]{:S(2)}) copy-start(bf16[512,4096]{1,0:T(8,128)(2,1)} %refs_1_.3) | copy-start | bytes 12582916
  52.0 1.0 copy-start.1
  56.0 6.5 %copy-start.3 = (bf16[256,512]{1,0:T(8,128)(2,1)S(1)}, bf16[256,512]{1,0:T(8,128)(2,1)}, u32[]{:S(2)}) copy-start(bf16[256,512]{1,0:T(8,128)(2,1)} %refs_0_) | copy-start | bytes 786436
  56.1 9.1 %copy-start.2 = (bf16[544,256]{1,0:T(8,128)(2,1)S(1)}, bf16[544,256]{1,0:T(8,128)(2,1)}, u32[]{:S(2)}) copy-start(bf16[544,256]{1,0:T(8,128)(2,1)} %get-tuple-element.24.refs_3_.refs_4_) | copy-start | bytes 835588
  60.2 20.6 %copy-start.4 = (bf16[256]{0:T(256)(128)(2,1)S(1)}, bf16[256]{0:T(256)(128)(2,1)}, u32[]{:S(2)}) copy-start(bf16[256]{0:T(256)(128)(2,1)} %param.12) | copy-start | bytes 1540
  62.5 17.6 %collective-permute-start.13 = (bf16[256,512]{1,0:T(8,128)(2,1)S(1)}, bf16[256,512]{1,0:T(8,128)(2,1)S(1)}, u32[]{:S(2)}, u32[]{:S(2)}) collective-permute-start(bf16[256,512]{1,0:T(8,128)(2,1)S(1)} %copy-done.3), channel_id=1, source_target_pairs={{0,4},{1,5},{2,6},{3,7},{4,0},{5,1},{6,2},{7,3},{8,12},{9,13},{10,... | collective-permute-start | bytes 786440 | tf_op jit(solution)/shard_map/ppermute | solution.py:306
  67.9 6.3 %collective-permute-start.10 = (bf16[144,128]{1,0:T(8,128)(2,1)S(1)}, bf16[144,128]{1,0:T(8,128)(2,1)S(1)}, u32[]{:S(2)}, u32[]{:S(2)}) collective-permute-start(bf16[144,128]{1,0:T(8,128)(2,1)S(1)} %get-tuple-element.34), channel_id=1, source_target_pairs={{0,6},{1,7},{2,4},{3,5},{4,2},{5,3},{6,0},{7,1},{8,14},{9,15},{10,... | collective-permute-start | bytes 110600 | tf_op jit(solution)/shard_map/ppermute | solution.py:306
  69.4 4.9 %collective-permute-start.8 = (bf16[144,128]{1,0:T(8,128)(2,1)S(1)}, bf16[144,128]{1,0:T(8,128)(2,1)S(1)}, u32[]{:S(2)}, u32[]{:S(2)}) collective-permute-start(bf16[144,128]{1,0:T(8,128)(2,1)S(1)} %get-tuple-element.32), channel_id=1, source_target_pairs={{0,2},{1,3},{2,0},{3,1},{4,6},{5,7},{6,4},{7,5},{8,10},{9,11},{10,... | collective-permute-start | bytes 110600 | tf_op jit(solution)/shard_map/ppermute | solution.py:306
  69.8 10.3 %collective-permute-start.9 = (bf16[144,128]{1,0:T(8,128)(2,1)S(1)}, bf16[144,128]{1,0:T(8,128)(2,1)S(1)}, u32[]{:S(2)}, u32[]{:S(2)}) collective-permute-start(bf16[144,128]{1,0:T(8,128)(2,1)S(1)} %get-tuple-element.33), channel_id=1, source_target_pairs={{0,4},{1,5},{2,6},{3,7},{4,0},{5,1},{6,2},{7,3},{8,12},{9,13},{10,... | collective-permute-start | bytes 110600 | tf_op jit(solution)/shard_map/ppermute | solution.py:306
  72.4 12.4 %collective-permute-start.12 = (bf16[256,512]{1,0:T(8,128)(2,1)S(1)}, bf16[256,512]{1,0:T(8,128)(2,1)S(1)}, u32[]{:S(2)}, u32[]{:S(2)}) collective-permute-start(bf16[256,512]{1,0:T(8,128)(2,1)S(1)} %copy-done.3), channel_id=1, source_target_pairs={{0,2},{1,3},{2,0},{3,1},{4,6},{5,7},{6,4},{7,5},{8,10},{9,11},{10,... | collective-permute-start | bytes 786440 | tf_op jit(solution)/shard_map/ppermute | solution.py:306
  80.1 10.0 %collective-permute-start.14 = (bf16[256,512]{1,0:T(8,128)(2,1)S(1)}, bf16[256,512]{1,0:T(8,128)(2,1)S(1)}, u32[]{:S(2)}, u32[]{:S(2)}) collective-permute-start(bf16[256,512]{1,0:T(8,128)(2,1)S(1)} %collective-permute-done.13.refs_2_), channel_id=1, source_target_pairs={{0,2},{1,3},{2,0},{3,1},{4,6},{5,7},{6,4},{7,5},{8,10},{9,11},{10,... | collective-permute-start | bytes 786440 | tf_op jit(solution)/shard_map/ppermute | solution.py:306
  81.0 1.3 %collective-permute-start.11 = (bf16[128,128]{1,0:T(8,128)(2,1)S(1)}, bf16[128,128]{1,0:T(8,128)(2,1)S(1)}, u32[]{:S(2)}, u32[]{:S(2)}) collective-permute-start(bf16[128,128]{1,0:T(8,128)(2,1)S(1)} %shard_map.77.own_ref), channel_id=1, source_target_pairs={{0,1},{1,0},{2,3},{3,2},{4,5},{5,4},{6,7},{7,6},{8,9},{9,8},{10,11... | collective-permute-start | bytes 98312 | tf_op jit(solution)/shard_map/ppermute | solution.py:306
  91.1 5.7 %collective-permute-start.15 = (bf16[128,512]{1,0:T(8,128)(2,1)S(1)}, bf16[128,512]{1,0:T(8,128)(2,1)S(1)}, u32[]{:S(2)}, u32[]{:S(2)}) collective-permute-start(bf16[128,512]{1,0:T(8,128)(2,1)S(1)} %get-tuple-element.38), channel_id=1, source_target_pairs={{0,8},{8,0},{16,24},{24,16},{1,9},{9,1},{17,25},{25,17},{2,10},{10... | collective-permute-start | bytes 393224 | tf_op jit(solution)/shard_map/ppermute | solution.py:309
  92.7 7.8 %collective-permute-start.16 = (bf16[128,512]{1,0:T(8,128)(2,1)S(1)}, bf16[128,512]{1,0:T(8,128)(2,1)S(1)}, u32[]{:S(2)}, u32[]{:S(2)}) collective-permute-start(bf16[128,512]{1,0:T(8,128)(2,1)S(1)} %get-tuple-element.39), channel_id=1, source_target_pairs={{0,16},{8,24},{16,0},{24,8},{1,17},{9,25},{17,1},{25,9},{2,18},{10... | collective-permute-start | bytes 393224 | tf_op jit(solution)/shard_map/ppermute | solution.py:309
  94.2 6.3 %collective-permute-start.17 = (bf16[128,512]{1,0:T(8,128)(2,1)S(1)}, bf16[128,512]{1,0:T(8,128)(2,1)S(1)}, u32[]{:S(2)}, u32[]{:S(2)}) collective-permute-start(bf16[128,512]{1,0:T(8,128)(2,1)S(1)} %get-tuple-element.40), channel_id=1, source_target_pairs={{0,24},{8,16},{16,8},{24,0},{1,25},{9,17},{17,9},{25,1},{2,26},{10... | collective-permute-start | bytes 393224 | tf_op jit(solution)/shard_map/ppermute | solution.py:309
  100.6 1.3 %collective-permute-start.18 = (bf16[64,512]{1,0:T(8,128)(2,1)S(1)}, bf16[64,512]{1,0:T(8,128)(2,1)S(1)}, u32[]{:S(2)}, u32[]{:S(2)}) collective-permute-start(bf16[64,512]{1,0:T(8,128)(2,1)S(1)} %get-tuple-element.42), channel_id=1, source_target_pairs={{0,1},{1,0},{2,3},{3,2},{4,5},{5,4},{6,7},{7,6},{8,9},{9,8},{10,11... | collective-permute-start | bytes 196616 | tf_op jit(solution)/shard_map/ppermute | solution.py:306

commit v6 on v5

--- a/solution.py
+++ b/solution.py
@@ -236,7 +236,7 @@
         pack_kernel,
         out_shape=[out, out],
         in_specs=[SMEM, ANY, ANY, ANY],
-        out_specs=[ANY, ANY],
+        out_specs=[VMEM, VMEM],
         scratch_shapes=[pltpu.SemaphoreType.DMA((8,))],
         compiler_params=WIDE,
     )(core, w_key, w_value, queries)
@@ -269,6 +269,42 @@
     )(place, own, sibling, *weights)
 
 
+def finish_kernel(core_ref, own_ref, sibling_ref, *refs):
+    outs = refs[-2 * CORES - 1 : -1]
+    weights, total_ref = refs[: -2 * CORES - 1], refs[-1]
+    core = core_ref[0]
+    half = own_ref.shape[1] // len(weights)
+    count = outs[0].shape[0]
+    for i, w_ref in enumerate(weights):
+        for rows_ref, who in ((own_ref, core), (sibling_ref, 1 - core)):
+            product = jnp.dot(
+                rows_ref[:, i * half : (i + 1) * half],
+                w_ref[pl.ds(pl.multiple_of(who * half, DH), half), :],
+                preferred_element_type=jnp.float32,
+            )
+            if i == 0 and rows_ref is own_ref:
+                total_ref[...] = product
+            else:
+                total_ref[...] += product
+    for o, out_ref in enumerate(outs):
+        block = (o // CORES) * CORES + (core if o % CORES == 0 else 1 - core)
+        lines = pl.ds(pl.multiple_of(block * count, count), count)
+        out_ref[...] = total_ref[lines, :].astype(jnp.bfloat16)
+
+
+def finish(core, own, sibling, weights):
+    rows, width = own.shape[0], weights[0].shape[1]
+    out = jax.ShapeDtypeStruct((rows // (2 * CORES), width), jnp.bfloat16)
+    return pl.pallas_call(
+        finish_kernel,
+        out_shape=[out] * (2 * CORES),
+        in_specs=[SMEM] + [VMEM] * (2 + len(weights)),
+        out_specs=[VMEM] * (2 * CORES),
+        scratch_shapes=[pltpu.VMEM((rows, width), jnp.float32)],
+        compiler_params=PARAMS,
+    )(core, own, sibling, *weights)
+
+
 def add_kernel(core_ref, *refs):
     terms, (own_ref, other_ref) = refs[:-2], refs[-2:]
     count = own_ref.shape[0]
@@ -319,9 +355,18 @@
         if j == low:
             pairs[j] = (across(own_part, CORES * j), across(other_part, CORES * j + 1))
         else:
-            pairs[j] = tuple(across(part, CORES * low) for part in pairs[j ^ low])
-    context_sibling = across(after(context, own_part), 1)
-    pairs[0] = (own_part, across(after(other_part, pairs[1], pairs[chips // 2]), 1))
+            pairs[j] = tuple(
+                across(after(part, near), CORES * low) for part, near in zip(pairs[j ^ low], pairs[1])
+            )
+    in_middle = chips == 4 and n_dp == chips
+    middle = [CORES + c for c in range(2 * CORES)]
+
+    def to_middle(array, bits):
+        return lax.ppermute(array, "ctx", [(c ^ bits, c) for c in middle])
+
+    outer = to_middle(after(w_out, own_part), CORES) if in_middle else w_out
+    context_sibling = across(after(context, outer, *pairs[1], *pairs[chips // 2]), 1)
+    pairs[0] = (own_part, across(after(other_part, outer, *pairs[1], *pairs[chips // 2]), 1))
 
     places = jnp.stack(
         [(chip ^ j) * CORES + who for j in range(chips) for who in (core, 1 - core)]
@@ -334,18 +379,55 @@
         starts[CORES:], context, context_sibling, blocks[CORES:last], first_acc, depth
     )
     firsts = jnp.stack([me * rows, (me ^ 1) * rows]).astype(jnp.int32)
+    gain = head_gain.reshape(1, panel)
+
+    def messages_to(groups, slot_groups):
+        return attend(
+            firsts, slot_groups.astype(jnp.int32), places, slices, blocks, acc, offsets, groups,
+            heads, depth,
+        )
+
+    if in_middle:
+        both = after(jnp.concatenate([outer, w_out], axis=0), *pairs[1], *pairs[2])
+        shards = [w_out, outer, *jnp.split(after(to_middle(both, 3 * CORES), acc), 2)]
+        line = tuple(range(n_ctx))
+        groups = (line[2:4] + line[0:2], line[4:6] + line[6:8])
+        messages = messages_to(groups, jnp.clip((chip ^ jnp.arange(chips)) - 1, 0, 1))
+        arrived = [messages[0]] + [to_middle(messages[j], CORES * j) for j in range(1, chips)]
+        picked = []
+        for i in range(n_dp):
+            wanted = chip ^ mine_dp ^ i
+            shard = shards[0]
+            for j in range(1, chips):
+                shard = jnp.where(wanted == j, shards[j], shard)
+            picked.append(shard)
+        weights = [picked[0]] + [over_dp(picked[i], i) for i in range(1, n_dp)]
+
+        normed = combine(core_only, arrived, after(gain, *weights[1:3]), heads)
+        normed = [normed] + [over_dp(normed, i) for i in range(1, n_dp)]
+        normed = jnp.concatenate(normed, axis=1)
+        mine, sibling, outer_mine, outer_sibling = finish(
+            core_only, normed, across(normed, 1), weights
+        )
+        is_middle = (chip == 1) | (chip == 2)
+        theirs = to_middle(sibling, 1)
+        outer_mine = lax.ppermute(outer_mine, "ctx", [(c, c ^ CORES) for c in middle])
+        outer_theirs = lax.ppermute(outer_sibling, "ctx", [(c, c ^ CORES ^ 1) for c in middle])
+        mine = jnp.where(is_middle, mine, outer_mine)
+        theirs = jnp.where(is_middle, theirs, outer_theirs)
+        return jnp.where(
+            core == 0, jnp.concatenate([mine, theirs], axis=1), jnp.concatenate([theirs, mine], axis=1)
+        )
+
     groups = tuple((CORES * z, CORES * z + 1) for z in range(chips))
-    slot_groups = (chip ^ jnp.arange(chips)).astype(jnp.int32)
-    messages = attend(
-        firsts, slot_groups, places, slices, blocks, acc, offsets, groups, heads, depth
-    )
+    messages = messages_to(groups, chip ^ jnp.arange(chips))
     arrived = [messages[0]] + [across(messages[j], CORES * j) for j in range(1, chips)]
     shards = [after(w_out, acc, *pairs[-1])] + [None] * (chips - 1)
     for j in near_first:
         low = j & -j
         shard = shards[j ^ low]
         shards[j] = across(shard if j == low else after(shard, *arrived[1:]), CORES * low)
-    normed = combine(core_only, arrived, head_gain.reshape(1, panel), heads)
+    normed = combine(core_only, arrived, gain, heads)
 
     terms = output_terms(
         jnp.stack([mine_dp ^ chip, core]).astype(jnp.int32), normed, across(normed, 1), shards

time: 103 us -> 95.4 us (0.926)
  Pallas kernels: 29.3 us -> 13.2 us
  starting transfers between devices: 20.4 us -> 35 us
  waiting for transfers between devices: 47.7 us -> 40.3 us
  other arithmetic: 0.85 us -> 1.98 us
    ppermute x16 -> x9, waiting for transfers between devices: 41.9 us -> 1.53 us  [across(): return lax.ppermute(array, 'ctx', [(i, i ^ bits) for i in range(n_ctx)])]
    ppermute x0 -> x8, waiting for transfers between devices: none -> 31.6 us  [the longest x6 25.2 us: to_middle(): return lax.ppermute(array, 'ctx', [(c ^ bits, c) for c in middle])]
    ppermute x0 -> x8, starting transfers between devices: none -> 16 us  [the longest x6 13.4 us: to_middle(): return lax.ppermute(array, 'ctx', [(c ^ bits, c) for c in middle])]
    pallas_call x1, Pallas kernels: 18 us -> 2.02 us  [pack(): pl.pallas_call(pack_kernel, out_shape=[out, out], in_specs=[SMEM, ANY, AN...]
    ppermute x16 -> x9, starting transfers between devices: 16.9 us -> 11.8 us  [across(): return lax.ppermute(array, 'ctx', [(i, i ^ bits) for i in range(n_ctx)])]
    ppermute x3 -> x6, starting transfers between devices: 3.55 us -> 7.17 us  [over_dp(): return lax.ppermute(array, 'dp', [(d, d ^ bits) for d in range(n_dp)])]
    ppermute x3 -> x6, waiting for transfers between devices: 5.78 us -> 7.16 us  [over_dp(): return lax.ppermute(array, 'dp', [(d, d ^ bits) for d in range(n_dp)])]
    unnamed x10 -> x12, local copies, waits for them, and re-layouts: 3.16 us -> 3.17 us
  transfers between devices with their start and end apart: 19 -> 23, of which waited for: 13 -> 7; matrix products, arithmetic and copies ran while one was open for 1% -> 2% of each run, Pallas kernels for 10% -> 11%
where the time goes in v6:
time: 95.4 us; the launch traced here: 95 us
  waiting for transfers between devices  40.3 us (42%)
  starting transfers between devices  35 us (37%)
  Pallas kernels  13.2 us (14%)
  local copies, waits for them, and re-layouts  4.09 us (4%)
  other arithmetic  1.98 us (2%)
    ppermute x6, waiting for transfers between devices, to_middle(): return lax.ppermute(array, 'ctx', [(c ^ bits, c) for c in middle])  25.2 us
    ppermute x6, starting transfers between devices, to_middle(): return lax.ppermute(array, 'ctx', [(c ^ bits, c) for c in middle])  13.4 us
    ppermute x9, starting transfers between devices, across(): return lax.ppermute(array, 'ctx', [(i, i ^ bits) for i in range(n_ctx)])  11.8 us
    pallas_call x2, Pallas kernels, project(): pl.pallas_call(functools.partial(project_kernel, count, extra, acc is not...  7.2 us
    ppermute x6, starting transfers between devices, over_dp(): return lax.ppermute(array, 'dp', [(d, d ^ bits) for d in range(n_dp)])  7.17 us
    ppermute x6, waiting for transfers between devices, over_dp(): return lax.ppermute(array, 'dp', [(d, d ^ bits) for d in range(n_dp)])  7.16 us
    ppermute x1, waiting for transfers between devices, on_device(): lax.ppermute(outer_sibling, 'ctx', [(c, c ^ CORES ^ 1) for c in middle])  3.53 us
    unnamed x12, local copies, waits for them, and re-layouts  3.17 us
  transfers between devices with their start and end apart: 23, of which 7 were waited for; matrix products, arithmetic and copies ran while one was open for 2% of the time, Pallas kernels for 11%

profile of v6, /device:TPU:0, one launch (start us, length us, event | category | flops | bytes accessed | tf_op | source)
XLA Modules:
  0.0 95.0 jit_solution(10027246014386239183)
XLA Ops:
  0.0 2.0 %shard_map.73 = (bf16[544,256]{1,0:T(8,128)(2,1)}, bf16[544,256]{1,0:T(8,128)(2,1)}) custom-call(s32[1]{0:T(128)} %bitcast.core_ref, bf16[512,256]{1,0:T(8,128)(2,1)} %key_ref.1, bf16[512,256]{1,0:T(8,128)(2,1)} %value_ref.1, bf16[64,256]{1,0:T(8,128)(2,1)} %query_ref.1), custom_call_target="tpu_custom_call" | custom-call | tf_op jit(solution)/shard_map/pallas_call | solution.py:235
  2.0 3.1 %collective-permute-start.1 = (bf16[544,256]{1,0:T(8,128)(2,1)}, bf16[544,256]{1,0:T(8,128)(2,1)S(1)}, u32[]{:S(2)}, u32[]{:S(2)}) collective-permute-start(bf16[544,256]{1,0:T(8,128)(2,1)} %get-tuple-element.26.refs_3_.refs_4_), channel_id=1, source_target_pairs={{0,2},{1,3},{2,0},{3,1},{4,6},{5,7},{6,4},{7,5},{8,10},{9,11},{10,... | collective-permute-start | bytes 835592 | tf_op jit(solution)/shard_map/ppermute | solution.py:342
  5.1 2.6 %collective-permute-start.3 = (bf16[544,256]{1,0:T(8,128)(2,1)}, bf16[544,256]{1,0:T(8,128)(2,1)S(1)}, u32[]{:S(2)}, u32[]{:S(2)}) collective-permute-start(bf16[544,256]{1,0:T(8,128)(2,1)} %get-tuple-element.26.refs_3_.refs_4_), channel_id=1, source_target_pairs={{0,4},{1,5},{2,6},{3,7},{4,0},{5,1},{6,2},{7,3},{8,12},{9,13},{10,... | collective-permute-start | bytes 835592 | tf_op jit(solution)/shard_map/ppermute | solution.py:342
  7.7 0.0 collective-permute-start.2
  7.7 0.2 collective-permute-start.4
  7.9 3.8 %collective-permute-start = (bf16[256,512]{1,0:T(8,128)(2,1)}, bf16[256,512]{1,0:T(8,128)(2,1)S(1)}, u32[]{:S(2)}, u32[]{:S(2)}) collective-permute-start(bf16[256,512]{1,0:T(8,128)(2,1)} %param.13), channel_id=1, source_target_pairs={{0,2},{1,3},{6,4},{7,5},{8,10},{9,11},{14,12},{15,13},{16,18},{17,... | collective-permute-start | bytes 786440 | tf_op jit(solution)/shard_map/ppermute | solution.py:365
  11.7 23.3 %collective-permute-done = bf16[256,512]{1,0:T(8,128)(2,1)S(1)} collective-permute-done((bf16[256,512]{1,0:T(8,128)(2,1)}, bf16[256,512]{1,0:T(8,128)(2,1)S(1)}, u32[]{:S(2)}, u32[]{:S(2)}) %collective-permute-start) | collective-permute-done | bytes 262176 | tf_op jit(solution)/shard_map/ppermute | solution.py:365
  35.0 0.0 collective-permute-done.1.refs_3_.refs_6_
  35.0 0.0 collective-permute-done.3.refs_5_.refs_8_
  35.0 0.0 collective-permute-done.2.refs_4_.refs_7_
  35.0 0.0 collective-permute-done.4.refs_6_.refs_9_
  35.0 0.1 collective-permute-start.5
  35.1 0.1 stack.56.refs_2_
  35.2 0.8 fusion
  35.9 1.0 %pad_maximum_fusion = bf16[512,512]{1,0:T(8,128)(2,1)S(1)} fusion(bf16[256,512]{1,0:T(8,128)(2,1)} %param.13, bf16[256,512]{1,0:T(8,128)(2,1)S(1)} %collective-permute-done), kind=kLoop, calls=%fused_computation | loop fusion | flops 1048576 | bytes 1048576 | tf_op jit(solution)/shard_map/concatenate | solution.py:391
  36.9 0.5 collective-permute-start.6
  37.5 0.7 collective-permute-start.12
  38.2 0.1 slice.23.refs_0_
  38.3 5.2 %collective-permute-start.7 = (bf16[544,256]{1,0:T(8,128)(2,1)S(1)}, bf16[544,256]{1,0:T(8,128)(2,1)S(1)}, u32[]{:S(2)}, u32[]{:S(2)}) collective-permute-start(bf16[544,256]{1,0:T(8,128)(2,1)S(1)} %collective-permute-done.3.refs_5_.refs_8_), channel_id=1, source_target_pairs={{0,2},{1,3},{2,0},{3,1},{4,6},{5,7},{6,4},{7,5},{8,10},{9,11},{10,... | collective-permute-start | bytes 835592 | tf_op jit(solution)/shard_map/ppermute | solution.py:342
  43.5 0.1 collective-permute-start.8
  43.6 0.0 collective-permute-done.6.refs_4_.refs_5_
  43.6 0.0 collective-permute-done.5.refs_2_
  43.6 2.2 %copy-done = bf16[512,4096]{1,0:T(8,128)(2,1)S(1)} copy-done((bf16[512,4096]{1,0:T(8,128)(2,1)S(1)}, bf16[512,4096]{1,0:T(8,128)(2,1)}, u32[]{:S(2)}) %copy-start) | copy-done | bytes 4194328
  45.8 1.0 %copy-done.1 = bf16[544,256]{1,0:T(8,128)(2,1)S(1)} copy-done((bf16[544,256]{1,0:T(8,128)(2,1)S(1)}, bf16[544,256]{1,0:T(8,128)(2,1)}, u32[]{:S(2)}) %copy-start.1) | copy-done | bytes 278552
  46.7 3.1 %shard_map.74 = (f32[1024,256]{1,0:T(8,128)S(1)}, bf16[2,16,512]{2,1,0:T(8,128)(2,1)}) custom-call(s32[2]{0:T(128)S(1)} %bitcast.14, bf16[512,4096]{1,0:T(8,128)(2,1)S(1)} %copy-done, bf16[512,4096]{1,0:T(8,128)(2,1)} %collective-permute-done.5.refs_2_, bf16[544,256]{1,0:T(8,128)(2,1)S(1)} %copy-done.1, ...), custom_call_target="tpu_custom_call" | custom-call | flops 536870912 | bytes 2097152 | tf_op jit(solution)/shard_map/pallas_call | solution.py:81
  49.8 0.0 copy-start.3
  49.8 0.0 copy-start.4
  49.8 4.1 %shard_map.75 = (f32[1024,256]{1,0:T(8,128)S(1)}, bf16[4,512,512]{2,1,0:T(8,128)(2,1)S(1)}) custom-call(s32[6]{0:T(128)S(1)} %slice.23.refs_0_, bf16[512,4096]{1,0:T(8,128)(2,1)S(1)} %copy-done, bf16[512,4096]{1,0:T(8,128)(2,1)} %collective-permute-done.5.refs_2_, bf16[544,256]{1,0:T(8,128)(2,1)S(1)} %collective-permute-done.1.refs_3_.refs_6_, ...), custom_call_target="tpu_custom_call" | custom-call | flops 1073741824 | bytes 4194304 | tf_op jit(solution)/shard_map/pallas_call | solution.py:81
  54.0 0.0 collective-permute-done.12
  54.0 0.0 copy-start.5
  54.0 0.1 select_select_fusion
  54.1 1.6 %collective-permute-start.14 = (bf16[256,512]{1,0:T(8,128)(2,1)S(1)}, bf16[256,512]{1,0:T(8,128)(2,1)S(1)}, u32[]{:S(2)}, u32[]{:S(2)}) collective-permute-start(bf16[256,512]{1,0:T(8,128)(2,1)S(1)} %get-tuple-element.49), channel_id=1, source_target_pairs={{0,16},{8,24},{16,0},{24,8},{1,17},{9,25},{17,1},{25,9},{2,18},{10... | collective-permute-start | bytes 786440 | tf_op jit(solution)/shard_map/ppermute | solution.py:345
  55.7 0.1 select_select_fusion.3
  55.8 1.6 %collective-permute-start.13 = (bf16[256,512]{1,0:T(8,128)(2,1)S(1)}, bf16[256,512]{1,0:T(8,128)(2,1)S(1)}, u32[]{:S(2)}, u32[]{:S(2)}) collective-permute-start(bf16[256,512]{1,0:T(8,128)(2,1)S(1)} %select_select_fusion.3), channel_id=1, source_target_pairs={{0,8},{8,0},{16,24},{24,16},{1,9},{9,1},{17,25},{25,17},{2,10},{10... | collective-permute-start | bytes 786440 | tf_op jit(solution)/shard_map/ppermute | solution.py:345
  57.3 0.1 pad_add_fusion.2.refs_0_
  57.4 0.0 collective-permute-done.7.refs_10_
  57.4 0.0 collective-permute-done.8.refs_11_
  57.5 3.1 %shard_map.76 = (bf16[144,256]{1,0:T(8,128)(2,1)S(1)}, bf16[144,256]{1,0:T(8,128)(2,1)S(1)}, bf16[144,256]{1,0:T(8,128)(2,1)S(1)}, bf16[144,256]{1,0:T(8,128)(2,1)S(1)}) custom-call(s32[2]{0:T(128)S(1)} %pad_add_fusion.2.refs_0_, s32[4]{0:T(128)S(1)} %add_clamp_fusion.refs_1_, s32[8]{0:T(128)S(1)} %stack.56.refs_2_, ...), custom_call_target="tpu_custom_call" | custom-call | flops 536870912 | bytes 2097152 | tf_op jit(solution)/shard_map/pallas_call | solution.py:158
  60.5 4.5 %collective-permute-start.10 = (bf16[144,256]{1,0:T(8,128)(2,1)S(1)}, bf16[144,256]{1,0:T(8,128)(2,1)S(1)}, u32[]{:S(2)}, u32[]{:S(2)}) collective-permute-start(bf16[144,256]{1,0:T(8,128)(2,1)S(1)} %get-tuple-element.38), channel_id=1, source_target_pairs={{6,2},{7,3},{0,4},{1,5},{14,10},{15,11},{8,12},{9,13},{22,18},{23,... | collective-permute-start | bytes 221192 | tf_op jit(solution)/shard_map/ppermute | solution.py:365
  65.1 0.7 collective-permute-start.11
  65.7 3.1 %collective-permute-start.9 = (bf16[144,256]{1,0:T(8,128)(2,1)S(1)}, bf16[144,256]{1,0:T(8,128)(2,1)S(1)}, u32[]{:S(2)}, u32[]{:S(2)}) collective-permute-start(bf16[144,256]{1,0:T(8,128)(2,1)S(1)} %get-tuple-element.37), channel_id=1, source_target_pairs={{0,2},{1,3},{6,4},{7,5},{8,10},{9,11},{14,12},{15,13},{16,18},{17,... | collective-permute-start | bytes 221192 | tf_op jit(solution)/shard_map/ppermute | solution.py:365
  68.9 0.0 collective-permute-done.14.refs_2_
  68.9 0.0 collective-permute-done.13.refs_1_
  68.9 0.0 collective-permute-done.10.refs_2_
  68.9 0.0 collective-permute-done.11.refs_3_
  68.9 1.9 %collective-permute-done.9.refs_1_ = bf16[144,256]{1,0:T(8,128)(2,1)S(1)} collective-permute-done((bf16[144,256]{1,0:T(8,128)(2,1)S(1)}, bf16[144,256]{1,0:T(8,128)(2,1)S(1)}, u32[]{:S(2)}, u32[]{:S(2)}) %collective-permute-start.9) | collective-permute-done | bytes 73760 | tf_op jit(solution)/shard_map/ppermute | solution.py:365
  70.8 0.2 shard_map.77
  71.0 0.6 collective-permute-start.15
  71.6 0.5 collective-permute-start.16
  72.1 2.4 %collective-permute-start.17 = (bf16[256,128]{1,0:T(8,128)(2,1)S(1)}, bf16[256,128]{1,0:T(8,128)(2,1)S(1)}, u32[]{:S(2)}, u32[]{:S(2)}) collective-permute-start(bf16[256,128]{1,0:T(8,128)(2,1)S(1)} %shard_map.77), channel_id=1, source_target_pairs={{0,24},{8,16},{16,8},{24,0},{1,25},{9,17},{17,9},{25,1},{2,26},{10... | collective-permute-start | bytes 196616 | tf_op jit(solution)/shard_map/ppermute | solution.py:345
  74.6 0.5 collective-permute-start.19
  75.1 0.9 collective-permute-done.15
  76.0 6.2 %collective-permute-done.16 = bf16[256,128]{1,0:T(8,128)(2,1)S(1)} collective-permute-done((bf16[256,128]{1,0:T(8,128)(2,1)S(1)}, bf16[256,128]{1,0:T(8,128)(2,1)S(1)}, u32[]{:S(2)}, u32[]{:S(2)}) %collective-permute-start.16) | collective-permute-done | bytes 65568 | tf_op jit(solution)/shard_map/ppermute | solution.py:345
  82.2 0.0 collective-permute-done.17
  82.3 0.1 collective-permute-start.18
  82.3 0.0 collective-permute-done.19.refs_3_
  82.3 1.5 %collective-permute-done.18.sibling_ref = bf16[256,512]{1,0:T(8,128)(2,1)S(1)} collective-permute-done((bf16[256,512]{1,0:T(8,128)(2,1)S(1)}, bf16[256,512]{1,0:T(8,128)(2,1)S(1)}, u32[]{:S(2)}, u32[]{:S(2)}) %collective-permute-start.18) | collective-permute-done | bytes 262176 | tf_op jit(solution)/shard_map/ppermute | solution.py:342
  83.9 0.7 shard_map.78
  84.6 1.3 %collective-permute-start.20 = (bf16[64,512]{1,0:T(8,128)(2,1)S(1)}, bf16[64,512]{1,0:T(8,128)(2,1)S(1)}, u32[]{:S(2)}, u32[]{:S(2)}) collective-permute-start(bf16[64,512]{1,0:T(8,128)(2,1)S(1)} %get-tuple-element.44), channel_id=1, source_target_pairs={{2,0},{3,1},{4,6},{5,7},{10,8},{11,9},{12,14},{13,15},{18,16},{19,... | collective-permute-start | bytes 196616 | tf_op jit(solution)/shard_map/ppermute | solution.py:414
  85.9 0.7 collective-permute-start.21
  86.6 1.3 %collective-permute-start.22 = (bf16[64,512]{1,0:T(8,128)(2,1)S(1)}, bf16[64,512]{1,0:T(8,128)(2,1)S(1)}, u32[]{:S(2)}, u32[]{:S(2)}) collective-permute-start(bf16[64,512]{1,0:T(8,128)(2,1)S(1)} %get-tuple-element.46), channel_id=1, source_target_pairs={{2,1},{3,0},{4,7},{5,6},{10,9},{11,8},{12,15},{13,14},{18,17},{19,... | collective-permute-start | bytes 196616 | tf_op jit(solution)/shard_map/ppermute | solution.py:415
  87.9 2.9 %collective-permute-done.20 = bf16[64,512]{1,0:T(8,128)(2,1)S(1)} collective-permute-done((bf16[64,512]{1,0:T(8,128)(2,1)S(1)}, bf16[64,512]{1,0:T(8,128)(2,1)S(1)}, u32[]{:S(2)}, u32[]{:S(2)}) %collective-permute-start.20) | collective-permute-done | bytes 65568 | tf_op jit(solution)/shard_map/ppermute | solution.py:414
  90.8 3.5 %collective-permute-done.22 = bf16[64,512]{1,0:T(8,128)(2,1)S(1)} collective-permute-done((bf16[64,512]{1,0:T(8,128)(2,1)S(1)}, bf16[64,512]{1,0:T(8,128)(2,1)S(1)}, u32[]{:S(2)}, u32[]{:S(2)}) %collective-permute-start.22) | collective-permute-done | bytes 65568 | tf_op jit(solution)/shard_map/ppermute | solution.py:415
  94.3 0.7 maximum_select_fusion
  (17 shorter events, 0.1 us)
Async XLA Ops:
  2.0 32.9 %collective-permute-start.1 = (bf16[544,256]{1,0:T(8,128)(2,1)}, bf16[544,256]{1,0:T(8,128)(2,1)S(1)}, u32[]{:S(2)}, u32[]{:S(2)}) collective-permute-start(bf16[544,256]{1,0:T(8,128)(2,1)} %get-tuple-element.26.refs_3_.refs_4_), channel_id=1, source_target_pairs={{0,2},{1,3},{2,0},{3,1},{4,6},{5,7},{6,4},{7,5},{8,10},{9,11},{10,... | collective-permute-start | bytes 835592 | tf_op jit(solution)/shard_map/ppermute | solution.py:342
  5.1 29.9 %collective-permute-start.3 = (bf16[544,256]{1,0:T(8,128)(2,1)}, bf16[544,256]{1,0:T(8,128)(2,1)S(1)}, u32[]{:S(2)}, u32[]{:S(2)}) collective-permute-start(bf16[544,256]{1,0:T(8,128)(2,1)} %get-tuple-element.26.refs_3_.refs_4_), channel_id=1, source_target_pairs={{0,4},{1,5},{2,6},{3,7},{4,0},{5,1},{6,2},{7,3},{8,12},{9,13},{10,... | collective-permute-start | bytes 835592 | tf_op jit(solution)/shard_map/ppermute | solution.py:342
  7.7 27.3 %collective-permute-start.2 = (bf16[544,256]{1,0:T(8,128)(2,1)}, bf16[544,256]{1,0:T(8,128)(2,1)S(1)}, u32[]{:S(2)}, u32[]{:S(2)}) collective-permute-start(bf16[544,256]{1,0:T(8,128)(2,1)} %get-tuple-element.30), channel_id=1, source_target_pairs={{0,3},{1,2},{2,1},{3,0},{4,7},{5,6},{6,5},{7,4},{8,11},{9,10},{10,... | collective-permute-start | bytes 835592 | tf_op jit(solution)/shard_map/ppermute | solution.py:342
  7.7 27.3 %collective-permute-start.4 = (bf16[544,256]{1,0:T(8,128)(2,1)}, bf16[544,256]{1,0:T(8,128)(2,1)S(1)}, u32[]{:S(2)}, u32[]{:S(2)}) collective-permute-start(bf16[544,256]{1,0:T(8,128)(2,1)} %get-tuple-element.30), channel_id=1, source_target_pairs={{0,5},{1,4},{2,7},{3,6},{4,1},{5,0},{6,3},{7,2},{8,13},{9,12},{10,... | collective-permute-start | bytes 835592 | tf_op jit(solution)/shard_map/ppermute | solution.py:342
  7.9 27.1 %collective-permute-start = (bf16[256,512]{1,0:T(8,128)(2,1)}, bf16[256,512]{1,0:T(8,128)(2,1)S(1)}, u32[]{:S(2)}, u32[]{:S(2)}) collective-permute-start(bf16[256,512]{1,0:T(8,128)(2,1)} %param.13), channel_id=1, source_target_pairs={{0,2},{1,3},{6,4},{7,5},{8,10},{9,11},{14,12},{15,13},{16,18},{17,... | collective-permute-start | bytes 786440 | tf_op jit(solution)/shard_map/ppermute | solution.py:365
  35.0 8.6 %collective-permute-start.5 = (bf16[512,4096]{1,0:T(8,128)(2,1)}, bf16[512,4096]{1,0:T(8,128)(2,1)}, u32[]{:S(2)}, u32[]{:S(2)}) collective-permute-start(bf16[512,4096]{1,0:T(8,128)(2,1)} %refs_1_.3), channel_id=1, source_target_pairs={{0,1},{1,0},{2,3},{3,2},{4,5},{5,4},{6,7},{7,6},{8,9},{9,8},{10,11... | collective-permute-start | bytes 12582920 | tf_op jit(solution)/shard_map/ppermute | solution.py:342
  36.9 6.7 %collective-permute-start.6 = (bf16[544,256]{1,0:T(8,128)(2,1)}, bf16[544,256]{1,0:T(8,128)(2,1)S(1)}, u32[]{:S(2)}, u32[]{:S(2)}) collective-permute-start(bf16[544,256]{1,0:T(8,128)(2,1)} %get-tuple-element.30), channel_id=1, source_target_pairs={{0,1},{1,0},{2,3},{3,2},{4,5},{5,4},{6,7},{7,6},{8,9},{9,8},{10,11... | collective-permute-start | bytes 835592 | tf_op jit(solution)/shard_map/ppermute | solution.py:342
  37.5 16.5 %collective-permute-start.12 = (bf16[512,512]{1,0:T(8,128)(2,1)S(1)}, bf16[512,512]{1,0:T(8,128)(2,1)S(1)}, u32[]{:S(2)}, u32[]{:S(2)}) collective-permute-start(bf16[512,512]{1,0:T(8,128)(2,1)S(1)} %pad_maximum_fusion), channel_id=1, source_target_pairs={{4,2},{5,3},{2,4},{3,5},{12,10},{13,11},{10,12},{11,13},{20,18},{2... | collective-permute-start | bytes 1572872 | tf_op jit(solution)/shard_map/ppermute | solution.py:365
  38.3 19.2 %collective-permute-start.7 = (bf16[544,256]{1,0:T(8,128)(2,1)S(1)}, bf16[544,256]{1,0:T(8,128)(2,1)S(1)}, u32[]{:S(2)}, u32[]{:S(2)}) collective-permute-start(bf16[544,256]{1,0:T(8,128)(2,1)S(1)} %collective-permute-done.3.refs_5_.refs_8_), channel_id=1, source_target_pairs={{0,2},{1,3},{2,0},{3,1},{4,6},{5,7},{6,4},{7,5},{8,10},{9,11},{10,... | collective-permute-start | bytes 835592 | tf_op jit(solution)/shard_map/ppermute | solution.py:342
  43.5 13.9 %collective-permute-start.8 = (bf16[544,256]{1,0:T(8,128)(2,1)S(1)}, bf16[544,256]{1,0:T(8,128)(2,1)S(1)}, u32[]{:S(2)}, u32[]{:S(2)}) collective-permute-start(bf16[544,256]{1,0:T(8,128)(2,1)S(1)} %collective-permute-done.4.refs_6_.refs_9_), channel_id=1, source_target_pairs={{0,2},{1,3},{2,0},{3,1},{4,6},{5,7},{6,4},{7,5},{8,10},{9,11},{10,... | collective-permute-start | bytes 835592 | tf_op jit(solution)/shard_map/ppermute | solution.py:342
  43.6 2.2 %copy-start = (bf16[512,4096]{1,0:T(8,128)(2,1)S(1)}, bf16[512,4096]{1,0:T(8,128)(2,1)}, u32[]{:S(2)}) copy-start(bf16[512,4096]{1,0:T(8,128)(2,1)} %refs_1_.3) | copy-start | bytes 12582916
  45.8 1.0 %copy-start.1 = (bf16[544,256]{1,0:T(8,128)(2,1)S(1)}, bf16[544,256]{1,0:T(8,128)(2,1)}, u32[]{:S(2)}) copy-start(bf16[544,256]{1,0:T(8,128)(2,1)} %get-tuple-element.26.refs_3_.refs_4_) | copy-start | bytes 835588
  49.8 4.2 %copy-start.3 = (bf16[256,512]{1,0:T(8,128)(2,1)S(1)}, bf16[256,512]{1,0:T(8,128)(2,1)}, u32[]{:S(2)}) copy-start(bf16[256,512]{1,0:T(8,128)(2,1)} %param.13) | copy-start | bytes 786436
  49.8 7.6 %copy-start.4 = (s32[512]{0:T(512)S(1)}, s32[512]{0:T(512)}, u32[]{:S(2)}) copy-start(s32[512]{0:T(512)} %param.11) | copy-start | bytes 6148
  49.8 7.6 %copy-start.2 = (bf16[544,256]{1,0:T(8,128)(2,1)S(1)}, bf16[544,256]{1,0:T(8,128)(2,1)}, u32[]{:S(2)}) copy-start(bf16[544,256]{1,0:T(8,128)(2,1)} %get-tuple-element.26.refs_3_.refs_4_) | copy-start | bytes 835588
  54.0 14.8 %copy-start.5 = (bf16[256]{0:T(256)(128)(2,1)S(1)}, bf16[256]{0:T(256)(128)(2,1)}, u32[]{:S(2)}) copy-start(bf16[256]{0:T(256)(128)(2,1)} %param.12) | copy-start | bytes 1540
  54.1 14.7 %collective-permute-start.14 = (bf16[256,512]{1,0:T(8,128)(2,1)S(1)}, bf16[256,512]{1,0:T(8,128)(2,1)S(1)}, u32[]{:S(2)}, u32[]{:S(2)}) collective-permute-start(bf16[256,512]{1,0:T(8,128)(2,1)S(1)} %get-tuple-element.49), channel_id=1, source_target_pairs={{0,16},{8,24},{16,0},{24,8},{1,17},{9,25},{17,1},{25,9},{2,18},{10... | collective-permute-start | bytes 786440 | tf_op jit(solution)/shard_map/ppermute | solution.py:345
  55.8 13.1 %collective-permute-start.13 = (bf16[256,512]{1,0:T(8,128)(2,1)S(1)}, bf16[256,512]{1,0:T(8,128)(2,1)S(1)}, u32[]{:S(2)}, u32[]{:S(2)}) collective-permute-start(bf16[256,512]{1,0:T(8,128)(2,1)S(1)} %select_select_fusion.3), channel_id=1, source_target_pairs={{0,8},{8,0},{16,24},{24,16},{1,9},{9,1},{17,25},{25,17},{2,10},{10... | collective-permute-start | bytes 786440 | tf_op jit(solution)/shard_map/ppermute | solution.py:345
  60.5 8.4 %collective-permute-start.10 = (bf16[144,256]{1,0:T(8,128)(2,1)S(1)}, bf16[144,256]{1,0:T(8,128)(2,1)S(1)}, u32[]{:S(2)}, u32[]{:S(2)}) collective-permute-start(bf16[144,256]{1,0:T(8,128)(2,1)S(1)} %get-tuple-element.38), channel_id=1, source_target_pairs={{6,2},{7,3},{0,4},{1,5},{14,10},{15,11},{8,12},{9,13},{22,18},{23,... | collective-permute-start | bytes 221192 | tf_op jit(solution)/shard_map/ppermute | solution.py:365
  65.1 3.8 %collective-permute-start.11 = (bf16[144,256]{1,0:T(8,128)(2,1)S(1)}, bf16[144,256]{1,0:T(8,128)(2,1)S(1)}, u32[]{:S(2)}, u32[]{:S(2)}) collective-permute-start(bf16[144,256]{1,0:T(8,128)(2,1)S(1)} %get-tuple-element.39), channel_id=1, source_target_pairs={{4,2},{5,3},{2,4},{3,5},{12,10},{13,11},{10,12},{11,13},{20,18},{2... | collective-permute-start | bytes 221192 | tf_op jit(solution)/shard_map/ppermute | solution.py:365
  65.7 5.1 %collective-permute-start.9 = (bf16[144,256]{1,0:T(8,128)(2,1)S(1)}, bf16[144,256]{1,0:T(8,128)(2,1)S(1)}, u32[]{:S(2)}, u32[]{:S(2)}) collective-permute-start(bf16[144,256]{1,0:T(8,128)(2,1)S(1)} %get-tuple-element.37), channel_id=1, source_target_pairs={{0,2},{1,3},{6,4},{7,5},{8,10},{9,11},{14,12},{15,13},{16,18},{17,... | collective-permute-start | bytes 221192 | tf_op jit(solution)/shard_map/ppermute | solution.py:365
  71.0 5.0 %collective-permute-start.15 = (bf16[256,128]{1,0:T(8,128)(2,1)S(1)}, bf16[256,128]{1,0:T(8,128)(2,1)S(1)}, u32[]{:S(2)}, u32[]{:S(2)}) collective-permute-start(bf16[256,128]{1,0:T(8,128)(2,1)S(1)} %shard_map.77), channel_id=1, source_target_pairs={{0,8},{8,0},{16,24},{24,16},{1,9},{9,1},{17,25},{25,17},{2,10},{10... | collective-permute-start | bytes 196616 | tf_op jit(solution)/shard_map/ppermute | solution.py:345
  71.6 10.6 %collective-permute-start.16 = (bf16[256,128]{1,0:T(8,128)(2,1)S(1)}, bf16[256,128]{1,0:T(8,128)(2,1)S(1)}, u32[]{:S(2)}, u32[]{:S(2)}) collective-permute-start(bf16[256,128]{1,0:T(8,128)(2,1)S(1)} %shard_map.77), channel_id=1, source_target_pairs={{0,16},{8,24},{16,0},{24,8},{1,17},{9,25},{17,1},{25,9},{2,18},{10... | collective-permute-start | bytes 196616 | tf_op jit(solution)/shard_map/ppermute | solution.py:345
  72.1 10.1 %collective-permute-start.17 = (bf16[256,128]{1,0:T(8,128)(2,1)S(1)}, bf16[256,128]{1,0:T(8,128)(2,1)S(1)}, u32[]{:S(2)}, u32[]{:S(2)}) collective-permute-start(bf16[256,128]{1,0:T(8,128)(2,1)S(1)} %shard_map.77), channel_id=1, source_target_pairs={{0,24},{8,16},{16,8},{24,0},{1,25},{9,17},{17,9},{25,1},{2,26},{10... | collective-permute-start | bytes 196616 | tf_op jit(solution)/shard_map/ppermute | solution.py:345
  74.6 7.8 %collective-permute-start.19 = (bf16[256,512]{1,0:T(8,128)(2,1)S(1)}, bf16[256,512]{1,0:T(8,128)(2,1)S(1)}, u32[]{:S(2)}, u32[]{:S(2)}) collective-permute-start(bf16[256,512]{1,0:T(8,128)(2,1)S(1)} %get-tuple-element.47), channel_id=1, source_target_pairs={{0,24},{8,16},{16,8},{24,0},{1,25},{9,17},{17,9},{25,1},{2,26},{10... | collective-permute-start | bytes 786440 | tf_op jit(solution)/shard_map/ppermute | solution.py:345
  82.3 1.6 %collective-permute-start.18 = (bf16[256,512]{1,0:T(8,128)(2,1)S(1)}, bf16[256,512]{1,0:T(8,128)(2,1)S(1)}, u32[]{:S(2)}, u32[]{:S(2)}) collective-permute-start(bf16[256,512]{1,0:T(8,128)(2,1)S(1)} %pad_maximum_fusion.1.own_ref), channel_id=1, source_target_pairs={{0,1},{1,0},{2,3},{3,2},{4,5},{5,4},{6,7},{7,6},{8,9},{9,8},{10,11... | collective-permute-start | bytes 786440 | tf_op jit(solution)/shard_map/ppermute | solution.py:342
  84.6 6.2 %collective-permute-start.20 = (bf16[64,512]{1,0:T(8,128)(2,1)S(1)}, bf16[64,512]{1,0:T(8,128)(2,1)S(1)}, u32[]{:S(2)}, u32[]{:S(2)}) collective-permute-start(bf16[64,512]{1,0:T(8,128)(2,1)S(1)} %get-tuple-element.44), channel_id=1, source_target_pairs={{2,0},{3,1},{4,6},{5,7},{10,8},{11,9},{12,14},{13,15},{18,16},{19,... | collective-permute-start | bytes 196616 | tf_op jit(solution)/shard_map/ppermute | solution.py:414
  85.9 4.9 %collective-permute-start.21 = (bf16[64,512]{1,0:T(8,128)(2,1)S(1)}, bf16[64,512]{1,0:T(8,128)(2,1)S(1)}, u32[]{:S(2)}, u32[]{:S(2)}) collective-permute-start(bf16[64,512]{1,0:T(8,128)(2,1)S(1)} %get-tuple-element.45), channel_id=1, source_target_pairs={{3,2},{2,3},{5,4},{4,5},{11,10},{10,11},{13,12},{12,13},{19,18},{1... | collective-permute-start | bytes 196616 | tf_op jit(solution)/shard_map/ppermute | solution.py:365
  86.6 7.7 %collective-permute-start.22 = (bf16[64,512]{1,0:T(8,128)(2,1)S(1)}, bf16[64,512]{1,0:T(8,128)(2,1)S(1)}, u32[]{:S(2)}, u32[]{:S(2)}) collective-permute-start(bf16[64,512]{1,0:T(8,128)(2,1)S(1)} %get-tuple-element.46), channel_id=1, source_target_pairs={{2,1},{3,0},{4,7},{5,6},{10,9},{11,8},{12,15},{13,14},{18,17},{19,... | collective-permute-start | bytes 196616 | tf_op jit(solution)/shard_map/ppermute | solution.py:415

commit v7 on v6

--- a/solution.py
+++ b/solution.py
@@ -364,9 +364,9 @@
     def to_middle(array, bits):
         return lax.ppermute(array, "ctx", [(c ^ bits, c) for c in middle])
 
-    outer = to_middle(after(w_out, own_part), CORES) if in_middle else w_out
-    context_sibling = across(after(context, outer, *pairs[1], *pairs[chips // 2]), 1)
-    pairs[0] = (own_part, across(after(other_part, outer, *pairs[1], *pairs[chips // 2]), 1))
+    context_sibling = across(after(context, own_part), 1)
+    pairs[0] = (own_part, across(after(other_part, context_sibling), 1))
+    outer = to_middle(after(w_out, context_sibling, pairs[1][0], pairs[2][0]), CORES) if in_middle else w_out
 
     places = jnp.stack(
         [(chip ^ j) * CORES + who for j in range(chips) for who in (core, 1 - core)]
@@ -403,7 +403,7 @@
             picked.append(shard)
         weights = [picked[0]] + [over_dp(picked[i], i) for i in range(1, n_dp)]
 
-        normed = combine(core_only, arrived, after(gain, *weights[1:3]), heads)
+        normed = combine(core_only, arrived, after(gain, *weights[1:]), heads)
         normed = [normed] + [over_dp(normed, i) for i in range(1, n_dp)]
         normed = jnp.concatenate(normed, axis=1)
         mine, sibling, outer_mine, outer_sibling = finish(

time: 95.4 us -> 96.6 us (1.013)
  starting transfers between devices: 35 us -> 30.7 us
  local copies, waits for them, and re-layouts: 4.09 us -> 8.26 us
  waiting for transfers between devices: 40.3 us -> 42 us
    ppermute x9, waiting for transfers between devices: 1.53 us -> 24.4 us  [across(): return lax.ppermute(array, 'ctx', [(i, i ^ bits) for i in range(n_ctx)])]
    ppermute x6, waiting for transfers between devices: 25.2 us -> 4.43 us  [to_middle(): return lax.ppermute(array, 'ctx', [(c ^ bits, c) for c in middle])]
    unnamed x12 -> x16, local copies, waits for them, and re-layouts: 3.17 us -> 7.33 us
    ppermute x6, starting transfers between devices: 13.4 us -> 9.5 us  [to_middle(): return lax.ppermute(array, 'ctx', [(c ^ bits, c) for c in middle])]
    ppermute x1, waiting for transfers between devices: 3.53 us -> 5.05 us  [on_device(): lax.ppermute(outer_sibling, 'ctx', [(c, c ^ CORES ^ 1) for c in middle])]
    ppermute x1, waiting for transfers between devices: 2.87 us -> 1.71 us  [on_device(): lax.ppermute(outer_mine, 'ctx', [(c, c ^ CORES) for c in middle])]
  transfers between devices with their start and end apart: 23 -> 23, of which waited for: 7 -> 12; matrix products, arithmetic and copies ran while one was open for 2% -> 2% of each run, Pallas kernels for 11% -> 10%
where the time goes in v7:
time: 96.6 us; the launch traced here: 96.1 us
  waiting for transfers between devices  42 us (43%)
  starting transfers between devices  30.7 us (32%)
  Pallas kernels  12.9 us (13%)
  local copies, waits for them, and re-layouts  8.26 us (9%)
  other arithmetic  1.97 us (2%)
    ppermute x9, waiting for transfers between devices, across(): return lax.ppermute(array, 'ctx', [(i, i ^ bits) for i in range(n_ctx)])  24.4 us
    ppermute x9, starting transfers between devices, across(): return lax.ppermute(array, 'ctx', [(i, i ^ bits) for i in range(n_ctx)])  11.4 us
    ppermute x6, starting transfers between devices, to_middle(): return lax.ppermute(array, 'ctx', [(c ^ bits, c) for c in middle])  9.5 us
    unnamed x16, local copies, waits for them, and re-layouts  7.33 us
    ppermute x6, starting transfers between devices, over_dp(): return lax.ppermute(array, 'dp', [(d, d ^ bits) for d in range(n_dp)])  7.2 us
    pallas_call x2, Pallas kernels, project(): pl.pallas_call(functools.partial(project_kernel, count, extra, acc is not...  6.92 us
    ppermute x6, waiting for transfers between devices, over_dp(): return lax.ppermute(array, 'dp', [(d, d ^ bits) for d in range(n_dp)])  6.43 us
    ppermute x1, waiting for transfers between devices, on_device(): lax.ppermute(outer_sibling, 'ctx', [(c, c ^ CORES ^ 1) for c in middle])  5.05 us
  transfers between devices with their start and end apart: 23, of which 12 were waited for; matrix products, arithmetic and copies ran while one was open for 2% of the time, Pallas kernels for 10%

profile of v7, /device:TPU:0, one launch (start us, length us, event | category | flops | bytes accessed | tf_op | source)
XLA Modules:
  0.0 96.1 jit_solution(4952050117776132524)
XLA Ops:
  0.0 2.0 %shard_map.73 = (bf16[544,256]{1,0:T(8,128)(2,1)}, bf16[544,256]{1,0:T(8,128)(2,1)}) custom-call(s32[1]{0:T(128)} %bitcast.core_ref, bf16[512,256]{1,0:T(8,128)(2,1)} %key_ref.1, bf16[512,256]{1,0:T(8,128)(2,1)} %value_ref.1, bf16[64,256]{1,0:T(8,128)(2,1)} %query_ref.1), custom_call_target="tpu_custom_call" | custom-call | tf_op jit(solution)/shard_map/pallas_call | solution.py:235
  2.0 0.5 collective-permute-start
  2.5 2.7 %collective-permute-start.1 = (bf16[544,256]{1,0:T(8,128)(2,1)}, bf16[544,256]{1,0:T(8,128)(2,1)S(1)}, u32[]{:S(2)}, u32[]{:S(2)}) collective-permute-start(bf16[544,256]{1,0:T(8,128)(2,1)} %get-tuple-element.26.refs_3_.refs_4_), channel_id=1, source_target_pairs={{0,2},{1,3},{2,0},{3,1},{4,6},{5,7},{6,4},{7,5},{8,10},{9,11},{10,... | collective-permute-start | bytes 835592 | tf_op jit(solution)/shard_map/ppermute | solution.py:342
  5.2 2.6 %collective-permute-start.3 = (bf16[544,256]{1,0:T(8,128)(2,1)}, bf16[544,256]{1,0:T(8,128)(2,1)S(1)}, u32[]{:S(2)}, u32[]{:S(2)}) collective-permute-start(bf16[544,256]{1,0:T(8,128)(2,1)} %get-tuple-element.26.refs_3_.refs_4_), channel_id=1, source_target_pairs={{0,4},{1,5},{2,6},{3,7},{4,0},{5,1},{6,2},{7,3},{8,12},{9,13},{10,... | collective-permute-start | bytes 835592 | tf_op jit(solution)/shard_map/ppermute | solution.py:342
  7.8 10.7 %collective-permute-done.1.refs_3_.refs_6_ = bf16[544,256]{1,0:T(8,128)(2,1)S(1)} collective-permute-done((bf16[544,256]{1,0:T(8,128)(2,1)}, bf16[544,256]{1,0:T(8,128)(2,1)S(1)}, u32[]{:S(2)}, u32[]{:S(2)}) %collective-permute-start.1) | collective-permute-done | bytes 278560 | tf_op jit(solution)/shard_map/ppermute | solution.py:342
  18.5 2.6 %collective-permute-done.3.refs_5_.refs_8_ = bf16[544,256]{1,0:T(8,128)(2,1)S(1)} collective-permute-done((bf16[544,256]{1,0:T(8,128)(2,1)}, bf16[544,256]{1,0:T(8,128)(2,1)S(1)}, u32[]{:S(2)}, u32[]{:S(2)}) %collective-permute-start.3) | collective-permute-done | bytes 278560 | tf_op jit(solution)/shard_map/ppermute | solution.py:342
  21.1 0.0 collective-permute-done.refs_2_
  21.1 2.0 %copy-done.1 = bf16[512,4096]{1,0:T(8,128)(2,1)} copy-done((bf16[512,4096]{1,0:T(8,128)(2,1)}, bf16[512,4096]{1,0:T(8,128)(2,1)S(1)}, u32[]{:S(2)}) %copy-start.1) | copy-done | bytes 4194328
  23.0 2.3 %collective-permute-start.11 = (bf16[256,512]{1,0:T(8,128)(2,1)}, bf16[256,512]{1,0:T(8,128)(2,1)S(1)}, u32[]{:S(2)}, u32[]{:S(2)}) collective-permute-start(bf16[256,512]{1,0:T(8,128)(2,1)} %param.13), channel_id=1, source_target_pairs={{0,2},{1,3},{6,4},{7,5},{8,10},{9,11},{14,12},{15,13},{16,18},{17,... | collective-permute-start | bytes 786440 | tf_op jit(solution)/shard_map/ppermute | solution.py:365
  25.4 0.1 collective-permute-start.2
  25.5 1.7 %collective-permute-start.4 = (bf16[544,256]{1,0:T(8,128)(2,1)}, bf16[544,256]{1,0:T(8,128)(2,1)S(1)}, u32[]{:S(2)}, u32[]{:S(2)}) collective-permute-start(bf16[544,256]{1,0:T(8,128)(2,1)} %get-tuple-element.29), channel_id=1, source_target_pairs={{0,5},{1,4},{2,7},{3,6},{4,1},{5,0},{6,3},{7,2},{8,13},{9,12},{10,... | collective-permute-start | bytes 835592 | tf_op jit(solution)/shard_map/ppermute | solution.py:342
  27.1 0.1 stack.56.refs_2_
  27.2 0.8 fusion
  28.0 0.0 collective-permute-start.5
  28.0 4.4 %collective-permute-done.11 = bf16[256,512]{1,0:T(8,128)(2,1)S(1)} collective-permute-done((bf16[256,512]{1,0:T(8,128)(2,1)}, bf16[256,512]{1,0:T(8,128)(2,1)S(1)}, u32[]{:S(2)}, u32[]{:S(2)}) %collective-permute-start.11) | collective-permute-done | bytes 262176 | tf_op jit(solution)/shard_map/ppermute | solution.py:365
  32.4 1.0 %pad_maximum_fusion = bf16[512,512]{1,0:T(8,128)(2,1)S(1)} fusion(bf16[256,512]{1,0:T(8,128)(2,1)} %param.13, bf16[256,512]{1,0:T(8,128)(2,1)S(1)} %collective-permute-done.11), kind=kLoop, calls=%fused_computation | loop fusion | flops 1048576 | bytes 1048576 | tf_op jit(solution)/shard_map/concatenate | solution.py:391
  33.4 6.7 %collective-permute-done.2.refs_4_.refs_7_ = bf16[544,256]{1,0:T(8,128)(2,1)S(1)} collective-permute-done((bf16[544,256]{1,0:T(8,128)(2,1)}, bf16[544,256]{1,0:T(8,128)(2,1)S(1)}, u32[]{:S(2)}, u32[]{:S(2)}) %collective-permute-start.2) | collective-permute-done | bytes 278560 | tf_op jit(solution)/shard_map/ppermute | solution.py:342
  40.1 2.8 %collective-permute-done.4.refs_6_.refs_9_ = bf16[544,256]{1,0:T(8,128)(2,1)S(1)} collective-permute-done((bf16[544,256]{1,0:T(8,128)(2,1)}, bf16[544,256]{1,0:T(8,128)(2,1)S(1)}, u32[]{:S(2)}, u32[]{:S(2)}) %collective-permute-start.4) | collective-permute-done | bytes 278560 | tf_op jit(solution)/shard_map/ppermute | solution.py:342
  42.9 0.7 collective-permute-start.12
  43.7 0.1 slice.23.refs_0_
  43.8 3.7 %collective-permute-start.6 = (bf16[544,256]{1,0:T(8,128)(2,1)S(1)}, bf16[544,256]{1,0:T(8,128)(2,1)S(1)}, u32[]{:S(2)}, u32[]{:S(2)}) collective-permute-start(bf16[544,256]{1,0:T(8,128)(2,1)S(1)} %collective-permute-done.3.refs_5_.refs_8_), channel_id=1, source_target_pairs={{0,2},{1,3},{2,0},{3,1},{4,6},{5,7},{6,4},{7,5},{8,10},{9,11},{10,... | collective-permute-start | bytes 835592 | tf_op jit(solution)/shard_map/ppermute | solution.py:342
  47.5 0.1 collective-permute-start.7
  47.5 0.0 collective-permute-done.5.refs_4_.refs_5_
  47.6 2.2 %copy-done = bf16[512,4096]{1,0:T(8,128)(2,1)S(1)} copy-done((bf16[512,4096]{1,0:T(8,128)(2,1)S(1)}, bf16[512,4096]{1,0:T(8,128)(2,1)}, u32[]{:S(2)}) %copy-start) | copy-done | bytes 4194328
  49.7 2.2 %copy-done.2 = bf16[512,4096]{1,0:T(8,128)(2,1)S(1)} copy-done((bf16[512,4096]{1,0:T(8,128)(2,1)S(1)}, bf16[512,4096]{1,0:T(8,128)(2,1)}, u32[]{:S(2)}) %copy-start.2) | copy-done | bytes 4194328
  51.9 1.0 copy-done.3
  52.9 2.6 %shard_map.74 = (f32[1024,256]{1,0:T(8,128)S(1)}, bf16[2,16,512]{2,1,0:T(8,128)(2,1)}) custom-call(s32[2]{0:T(128)S(1)} %bitcast.14, bf16[512,4096]{1,0:T(8,128)(2,1)S(1)} %copy-done, bf16[512,4096]{1,0:T(8,128)(2,1)S(1)} %copy-done.2, bf16[544,256]{1,0:T(8,128)(2,1)S(1)} %copy-done.3, bf16[544,256]{1,0:T(8,128)(2,1)S(1)} %collective-permute-done.5.refs_4_.refs_5_), custom_call_target="tpu_custom_call" | custom-call | flops 536870912 | bytes 2097152 | tf_op jit(solution)/shard_map/pallas_call | solution.py:81
  55.5 0.0 copy-start.5
  55.5 0.0 copy-start.6
  55.5 4.4 %shard_map.75 = (f32[1024,256]{1,0:T(8,128)S(1)}, bf16[4,512,512]{2,1,0:T(8,128)(2,1)S(1)}) custom-call(s32[6]{0:T(128)S(1)} %slice.23.refs_0_, bf16[512,4096]{1,0:T(8,128)(2,1)S(1)} %copy-done, bf16[512,4096]{1,0:T(8,128)(2,1)S(1)} %copy-done.2, bf16[544,256]{1,0:T(8,128)(2,1)S(1)} %collective-permute-done.1.refs_3_.refs_6_, ...), custom_call_target="tpu_custom_call" | custom-call | flops 1073741824 | bytes 4194304 | tf_op jit(solution)/shard_map/pallas_call | solution.py:81
  59.9 0.0 collective-permute-done.12
  59.9 0.0 copy-start.7
  59.9 0.1 select_select_fusion.3
  60.0 1.6 %collective-permute-start.13 = (bf16[256,512]{1,0:T(8,128)(2,1)S(1)}, bf16[256,512]{1,0:T(8,128)(2,1)S(1)}, u32[]{:S(2)}, u32[]{:S(2)}) collective-permute-start(bf16[256,512]{1,0:T(8,128)(2,1)S(1)} %select_select_fusion.3), channel_id=1, source_target_pairs={{0,8},{8,0},{16,24},{24,16},{1,9},{9,1},{17,25},{25,17},{2,10},{10... | collective-permute-start | bytes 786440 | tf_op jit(solution)/shard_map/ppermute | solution.py:345
  61.5 0.1 select_select_fusion
  61.6 1.6 %collective-permute-start.14 = (bf16[256,512]{1,0:T(8,128)(2,1)S(1)}, bf16[256,512]{1,0:T(8,128)(2,1)S(1)}, u32[]{:S(2)}, u32[]{:S(2)}) collective-permute-start(bf16[256,512]{1,0:T(8,128)(2,1)S(1)} %get-tuple-element.49), channel_id=1, source_target_pairs={{0,16},{8,24},{16,0},{24,8},{1,17},{9,25},{17,1},{25,9},{2,18},{10... | collective-permute-start | bytes 786440 | tf_op jit(solution)/shard_map/ppermute | solution.py:345
  63.2 0.5 collective-permute-start.15
  63.7 0.1 pad_add_fusion.2.refs_0_
  63.8 0.0 collective-permute-done.6.refs_10_
  63.8 0.0 collective-permute-done.7.refs_11_
  63.8 3.1 %shard_map.76 = (bf16[144,256]{1,0:T(8,128)(2,1)S(1)}, bf16[144,256]{1,0:T(8,128)(2,1)S(1)}, bf16[144,256]{1,0:T(8,128)(2,1)S(1)}, bf16[144,256]{1,0:T(8,128)(2,1)S(1)}) custom-call(s32[2]{0:T(128)S(1)} %pad_add_fusion.2.refs_0_, s32[4]{0:T(128)S(1)} %add_clamp_fusion.refs_1_, s32[8]{0:T(128)S(1)} %stack.56.refs_2_, ...), custom_call_target="tpu_custom_call" | custom-call | flops 536870912 | bytes 2097152 | tf_op jit(solution)/shard_map/pallas_call | solution.py:158
  66.9 3.9 %collective-permute-start.8 = (bf16[144,256]{1,0:T(8,128)(2,1)S(1)}, bf16[144,256]{1,0:T(8,128)(2,1)S(1)}, u32[]{:S(2)}, u32[]{:S(2)}) collective-permute-start(bf16[144,256]{1,0:T(8,128)(2,1)S(1)} %get-tuple-element.36), channel_id=1, source_target_pairs={{0,2},{1,3},{6,4},{7,5},{8,10},{9,11},{14,12},{15,13},{16,18},{17,... | collective-permute-start | bytes 221192 | tf_op jit(solution)/shard_map/ppermute | solution.py:365
  70.8 1.3 %collective-permute-start.9 = (bf16[144,256]{1,0:T(8,128)(2,1)S(1)}, bf16[144,256]{1,0:T(8,128)(2,1)S(1)}, u32[]{:S(2)}, u32[]{:S(2)}) collective-permute-start(bf16[144,256]{1,0:T(8,128)(2,1)S(1)} %get-tuple-element.37), channel_id=1, source_target_pairs={{6,2},{7,3},{0,4},{1,5},{14,10},{15,11},{8,12},{9,13},{22,18},{23,... | collective-permute-start | bytes 221192 | tf_op jit(solution)/shard_map/ppermute | solution.py:365
  72.1 0.0 collective-permute-done.13.refs_1_
  72.1 0.7 collective-permute-start.10
  72.8 3.2 %collective-permute-done.14.refs_2_ = bf16[256,512]{1,0:T(8,128)(2,1)S(1)} collective-permute-done((bf16[256,512]{1,0:T(8,128)(2,1)S(1)}, bf16[256,512]{1,0:T(8,128)(2,1)S(1)}, u32[]{:S(2)}, u32[]{:S(2)}) %collective-permute-start.14) | collective-permute-done | bytes 262176 | tf_op jit(solution)/shard_map/ppermute | solution.py:345
  75.9 0.0 collective-permute-done.15.refs_3_
  75.9 0.0 collective-permute-done.8.refs_1_
  76.0 0.2 shard_map.77
  76.2 1.6 %collective-permute-start.18 = (bf16[256,128]{1,0:T(8,128)(2,1)S(1)}, bf16[256,128]{1,0:T(8,128)(2,1)S(1)}, u32[]{:S(2)}, u32[]{:S(2)}) collective-permute-start(bf16[256,128]{1,0:T(8,128)(2,1)S(1)} %shard_map.77), channel_id=1, source_target_pairs={{0,24},{8,16},{16,8},{24,0},{1,25},{9,17},{17,9},{25,1},{2,26},{10... | collective-permute-start | bytes 196616 | tf_op jit(solution)/shard_map/ppermute | solution.py:345
  77.7 1.0 %collective-permute-start.17 = (bf16[256,128]{1,0:T(8,128)(2,1)S(1)}, bf16[256,128]{1,0:T(8,128)(2,1)S(1)}, u32[]{:S(2)}, u32[]{:S(2)}) collective-permute-start(bf16[256,128]{1,0:T(8,128)(2,1)S(1)} %shard_map.77), channel_id=1, source_target_pairs={{0,16},{8,24},{16,0},{24,8},{1,17},{9,25},{17,1},{25,9},{2,18},{10... | collective-permute-start | bytes 196616 | tf_op jit(solution)/shard_map/ppermute | solution.py:345
  78.7 1.0 %collective-permute-start.16 = (bf16[256,128]{1,0:T(8,128)(2,1)S(1)}, bf16[256,128]{1,0:T(8,128)(2,1)S(1)}, u32[]{:S(2)}, u32[]{:S(2)}) collective-permute-start(bf16[256,128]{1,0:T(8,128)(2,1)S(1)} %shard_map.77), channel_id=1, source_target_pairs={{0,8},{8,0},{16,24},{24,16},{1,9},{9,1},{17,25},{25,17},{2,10},{10... | collective-permute-start | bytes 196616 | tf_op jit(solution)/shard_map/ppermute | solution.py:345
  79.7 2.4 %collective-permute-done.18 = bf16[256,128]{1,0:T(8,128)(2,1)S(1)} collective-permute-done((bf16[256,128]{1,0:T(8,128)(2,1)S(1)}, bf16[256,128]{1,0:T(8,128)(2,1)S(1)}, u32[]{:S(2)}, u32[]{:S(2)}) %collective-permute-start.18) | collective-permute-done | bytes 65568 | tf_op jit(solution)/shard_map/ppermute | solution.py:345
  82.1 0.3 collective-permute-done.17
  82.4 0.6 collective-permute-done.16
  83.0 0.1 collective-permute-start.19
  83.1 1.5 %collective-permute-done.19.sibling_ref = bf16[256,512]{1,0:T(8,128)(2,1)S(1)} collective-permute-done((bf16[256,512]{1,0:T(8,128)(2,1)S(1)}, bf16[256,512]{1,0:T(8,128)(2,1)S(1)}, u32[]{:S(2)}, u32[]{:S(2)}) %collective-permute-start.19) | collective-permute-done | bytes 262176 | tf_op jit(solution)/shard_map/ppermute | solution.py:342
  84.6 0.7 shard_map.78
  85.4 0.7 collective-permute-start.21
  86.0 1.3 %collective-permute-start.22 = (bf16[64,512]{1,0:T(8,128)(2,1)S(1)}, bf16[64,512]{1,0:T(8,128)(2,1)S(1)}, u32[]{:S(2)}, u32[]{:S(2)}) collective-permute-start(bf16[64,512]{1,0:T(8,128)(2,1)S(1)} %get-tuple-element.46), channel_id=1, source_target_pairs={{2,1},{3,0},{4,7},{5,6},{10,9},{11,8},{12,15},{13,14},{18,17},{19,... | collective-permute-start | bytes 196616 | tf_op jit(solution)/shard_map/ppermute | solution.py:415
  87.4 1.3 %collective-permute-start.20 = (bf16[64,512]{1,0:T(8,128)(2,1)S(1)}, bf16[64,512]{1,0:T(8,128)(2,1)S(1)}, u32[]{:S(2)}, u32[]{:S(2)}) collective-permute-start(bf16[64,512]{1,0:T(8,128)(2,1)S(1)} %get-tuple-element.44), channel_id=1, source_target_pairs={{2,0},{3,1},{4,6},{5,7},{10,8},{11,9},{12,14},{13,15},{18,16},{19,... | collective-permute-start | bytes 196616 | tf_op jit(solution)/shard_map/ppermute | solution.py:414
  88.7 5.1 %collective-permute-done.22 = bf16[64,512]{1,0:T(8,128)(2,1)S(1)} collective-permute-done((bf16[64,512]{1,0:T(8,128)(2,1)S(1)}, bf16[64,512]{1,0:T(8,128)(2,1)S(1)}, u32[]{:S(2)}, u32[]{:S(2)}) %collective-permute-start.22) | collective-permute-done | bytes 65568 | tf_op jit(solution)/shard_map/ppermute | solution.py:415
  93.7 1.7 %collective-permute-done.20 = bf16[64,512]{1,0:T(8,128)(2,1)S(1)} collective-permute-done((bf16[64,512]{1,0:T(8,128)(2,1)S(1)}, bf16[64,512]{1,0:T(8,128)(2,1)S(1)}, u32[]{:S(2)}, u32[]{:S(2)}) %collective-permute-start.20) | collective-permute-done | bytes 65568 | tf_op jit(solution)/shard_map/ppermute | solution.py:414
  95.5 0.7 maximum_select_fusion
  (21 shorter events, 0.1 us)
Async XLA Ops:
  2.0 19.0 %collective-permute-start = (bf16[512,4096]{1,0:T(8,128)(2,1)}, bf16[512,4096]{1,0:T(8,128)(2,1)S(1)}, u32[]{:S(2)}, u32[]{:S(2)}) collective-permute-start(bf16[512,4096]{1,0:T(8,128)(2,1)} %refs_1_.3), channel_id=1, source_target_pairs={{0,1},{1,0},{2,3},{3,2},{4,5},{5,4},{6,7},{7,6},{8,9},{9,8},{10,11... | collective-permute-start | bytes 12582920 | tf_op jit(solution)/shard_map/ppermute | solution.py:342
  2.5 15.9 %collective-permute-start.1 = (bf16[544,256]{1,0:T(8,128)(2,1)}, bf16[544,256]{1,0:T(8,128)(2,1)S(1)}, u32[]{:S(2)}, u32[]{:S(2)}) collective-permute-start(bf16[544,256]{1,0:T(8,128)(2,1)} %get-tuple-element.26.refs_3_.refs_4_), channel_id=1, source_target_pairs={{0,2},{1,3},{2,0},{3,1},{4,6},{5,7},{6,4},{7,5},{8,10},{9,11},{10,... | collective-permute-start | bytes 835592 | tf_op jit(solution)/shard_map/ppermute | solution.py:342
  5.2 15.9 %collective-permute-start.3 = (bf16[544,256]{1,0:T(8,128)(2,1)}, bf16[544,256]{1,0:T(8,128)(2,1)S(1)}, u32[]{:S(2)}, u32[]{:S(2)}) collective-permute-start(bf16[544,256]{1,0:T(8,128)(2,1)} %get-tuple-element.26.refs_3_.refs_4_), channel_id=1, source_target_pairs={{0,4},{1,5},{2,6},{3,7},{4,0},{5,1},{6,2},{7,3},{8,12},{9,13},{10,... | collective-permute-start | bytes 835592 | tf_op jit(solution)/shard_map/ppermute | solution.py:342
  21.1 2.0 %copy-start.1 = (bf16[512,4096]{1,0:T(8,128)(2,1)}, bf16[512,4096]{1,0:T(8,128)(2,1)S(1)}, u32[]{:S(2)}) copy-start(bf16[512,4096]{1,0:T(8,128)(2,1)S(1)} %collective-permute-done.refs_2_) | copy-start | bytes 12582916
  23.0 9.4 %collective-permute-start.11 = (bf16[256,512]{1,0:T(8,128)(2,1)}, bf16[256,512]{1,0:T(8,128)(2,1)S(1)}, u32[]{:S(2)}, u32[]{:S(2)}) collective-permute-start(bf16[256,512]{1,0:T(8,128)(2,1)} %param.13), channel_id=1, source_target_pairs={{0,2},{1,3},{6,4},{7,5},{8,10},{9,11},{14,12},{15,13},{16,18},{17,... | collective-permute-start | bytes 786440 | tf_op jit(solution)/shard_map/ppermute | solution.py:365
  25.4 14.7 %collective-permute-start.2 = (bf16[544,256]{1,0:T(8,128)(2,1)}, bf16[544,256]{1,0:T(8,128)(2,1)S(1)}, u32[]{:S(2)}, u32[]{:S(2)}) collective-permute-start(bf16[544,256]{1,0:T(8,128)(2,1)} %get-tuple-element.29), channel_id=1, source_target_pairs={{0,3},{1,2},{2,1},{3,0},{4,7},{5,6},{6,5},{7,4},{8,11},{9,10},{10,... | collective-permute-start | bytes 835592 | tf_op jit(solution)/shard_map/ppermute | solution.py:342
  25.5 17.5 %collective-permute-start.4 = (bf16[544,256]{1,0:T(8,128)(2,1)}, bf16[544,256]{1,0:T(8,128)(2,1)S(1)}, u32[]{:S(2)}, u32[]{:S(2)}) collective-permute-start(bf16[544,256]{1,0:T(8,128)(2,1)} %get-tuple-element.29), channel_id=1, source_target_pairs={{0,5},{1,4},{2,7},{3,6},{4,1},{5,0},{6,3},{7,2},{8,13},{9,12},{10,... | collective-permute-start | bytes 835592 | tf_op jit(solution)/shard_map/ppermute | solution.py:342
  28.0 19.6 %collective-permute-start.5 = (bf16[544,256]{1,0:T(8,128)(2,1)}, bf16[544,256]{1,0:T(8,128)(2,1)S(1)}, u32[]{:S(2)}, u32[]{:S(2)}) collective-permute-start(bf16[544,256]{1,0:T(8,128)(2,1)} %get-tuple-element.29), channel_id=1, source_target_pairs={{0,1},{1,0},{2,3},{3,2},{4,5},{5,4},{6,7},{7,6},{8,9},{9,8},{10,11... | collective-permute-start | bytes 835592 | tf_op jit(solution)/shard_map/ppermute | solution.py:342
  42.9 16.9 %collective-permute-start.12 = (bf16[512,512]{1,0:T(8,128)(2,1)S(1)}, bf16[512,512]{1,0:T(8,128)(2,1)S(1)}, u32[]{:S(2)}, u32[]{:S(2)}) collective-permute-start(bf16[512,512]{1,0:T(8,128)(2,1)S(1)} %pad_maximum_fusion), channel_id=1, source_target_pairs={{4,2},{5,3},{2,4},{3,5},{12,10},{13,11},{10,12},{11,13},{20,18},{2... | collective-permute-start | bytes 1572872 | tf_op jit(solution)/shard_map/ppermute | solution.py:365
  43.8 20.0 %collective-permute-start.6 = (bf16[544,256]{1,0:T(8,128)(2,1)S(1)}, bf16[544,256]{1,0:T(8,128)(2,1)S(1)}, u32[]{:S(2)}, u32[]{:S(2)}) collective-permute-start(bf16[544,256]{1,0:T(8,128)(2,1)S(1)} %collective-permute-done.3.refs_5_.refs_8_), channel_id=1, source_target_pairs={{0,2},{1,3},{2,0},{3,1},{4,6},{5,7},{6,4},{7,5},{8,10},{9,11},{10,... | collective-permute-start | bytes 835592 | tf_op jit(solution)/shard_map/ppermute | solution.py:342
  47.5 16.3 %collective-permute-start.7 = (bf16[544,256]{1,0:T(8,128)(2,1)S(1)}, bf16[544,256]{1,0:T(8,128)(2,1)S(1)}, u32[]{:S(2)}, u32[]{:S(2)}) collective-permute-start(bf16[544,256]{1,0:T(8,128)(2,1)S(1)} %collective-permute-done.4.refs_6_.refs_9_), channel_id=1, source_target_pairs={{0,2},{1,3},{2,0},{3,1},{4,6},{5,7},{6,4},{7,5},{8,10},{9,11},{10,... | collective-permute-start | bytes 835592 | tf_op jit(solution)/shard_map/ppermute | solution.py:342
  47.5 2.2 %copy-start = (bf16[512,4096]{1,0:T(8,128)(2,1)S(1)}, bf16[512,4096]{1,0:T(8,128)(2,1)}, u32[]{:S(2)}) copy-start(bf16[512,4096]{1,0:T(8,128)(2,1)} %refs_1_.3) | copy-start | bytes 12582916
  49.7 2.2 %copy-start.2 = (bf16[512,4096]{1,0:T(8,128)(2,1)S(1)}, bf16[512,4096]{1,0:T(8,128)(2,1)}, u32[]{:S(2)}) copy-start(bf16[512,4096]{1,0:T(8,128)(2,1)} %copy-done.1) | copy-start | bytes 12582916
  51.9 1.0 copy-start.3
  55.5 4.4 %copy-start.5 = (bf16[256,512]{1,0:T(8,128)(2,1)S(1)}, bf16[256,512]{1,0:T(8,128)(2,1)}, u32[]{:S(2)}) copy-start(bf16[256,512]{1,0:T(8,128)(2,1)} %param.13) | copy-start | bytes 786436
  55.5 8.3 %copy-start.6 = (s32[512]{0:T(512)S(1)}, s32[512]{0:T(512)}, u32[]{:S(2)}) copy-start(s32[512]{0:T(512)} %param.11) | copy-start | bytes 6148
  55.5 8.3 %copy-start.4 = (bf16[544,256]{1,0:T(8,128)(2,1)S(1)}, bf16[544,256]{1,0:T(8,128)(2,1)}, u32[]{:S(2)}) copy-start(bf16[544,256]{1,0:T(8,128)(2,1)} %get-tuple-element.26.refs_3_.refs_4_) | copy-start | bytes 835588
  59.9 12.9 %copy-start.7 = (bf16[256]{0:T(256)(128)(2,1)S(1)}, bf16[256]{0:T(256)(128)(2,1)}, u32[]{:S(2)}) copy-start(bf16[256]{0:T(256)(128)(2,1)} %param.12) | copy-start | bytes 1540
  60.0 12.1 %collective-permute-start.13 = (bf16[256,512]{1,0:T(8,128)(2,1)S(1)}, bf16[256,512]{1,0:T(8,128)(2,1)S(1)}, u32[]{:S(2)}, u32[]{:S(2)}) collective-permute-start(bf16[256,512]{1,0:T(8,128)(2,1)S(1)} %select_select_fusion.3), channel_id=1, source_target_pairs={{0,8},{8,0},{16,24},{24,16},{1,9},{9,1},{17,25},{25,17},{2,10},{10... | collective-permute-start | bytes 786440 | tf_op jit(solution)/shard_map/ppermute | solution.py:345
  61.6 14.3 %collective-permute-start.14 = (bf16[256,512]{1,0:T(8,128)(2,1)S(1)}, bf16[256,512]{1,0:T(8,128)(2,1)S(1)}, u32[]{:S(2)}, u32[]{:S(2)}) collective-permute-start(bf16[256,512]{1,0:T(8,128)(2,1)S(1)} %get-tuple-element.49), channel_id=1, source_target_pairs={{0,16},{8,24},{16,0},{24,8},{1,17},{9,25},{17,1},{25,9},{2,18},{10... | collective-permute-start | bytes 786440 | tf_op jit(solution)/shard_map/ppermute | solution.py:345
  63.2 12.7 %collective-permute-start.15 = (bf16[256,512]{1,0:T(8,128)(2,1)S(1)}, bf16[256,512]{1,0:T(8,128)(2,1)S(1)}, u32[]{:S(2)}, u32[]{:S(2)}) collective-permute-start(bf16[256,512]{1,0:T(8,128)(2,1)S(1)} %get-tuple-element.48), channel_id=1, source_target_pairs={{0,24},{8,16},{16,8},{24,0},{1,25},{9,17},{17,9},{25,1},{2,26},{10... | collective-permute-start | bytes 786440 | tf_op jit(solution)/shard_map/ppermute | solution.py:345
  66.9 9.0 %collective-permute-start.8 = (bf16[144,256]{1,0:T(8,128)(2,1)S(1)}, bf16[144,256]{1,0:T(8,128)(2,1)S(1)}, u32[]{:S(2)}, u32[]{:S(2)}) collective-permute-start(bf16[144,256]{1,0:T(8,128)(2,1)S(1)} %get-tuple-element.36), channel_id=1, source_target_pairs={{0,2},{1,3},{6,4},{7,5},{8,10},{9,11},{14,12},{15,13},{16,18},{17,... | collective-permute-start | bytes 221192 | tf_op jit(solution)/shard_map/ppermute | solution.py:365
  70.8 5.2 %collective-permute-start.9 = (bf16[144,256]{1,0:T(8,128)(2,1)S(1)}, bf16[144,256]{1,0:T(8,128)(2,1)S(1)}, u32[]{:S(2)}, u32[]{:S(2)}) collective-permute-start(bf16[144,256]{1,0:T(8,128)(2,1)S(1)} %get-tuple-element.37), channel_id=1, source_target_pairs={{6,2},{7,3},{0,4},{1,5},{14,10},{15,11},{8,12},{9,13},{22,18},{23,... | collective-permute-start | bytes 221192 | tf_op jit(solution)/shard_map/ppermute | solution.py:365
  72.1 3.9 %collective-permute-start.10 = (bf16[144,256]{1,0:T(8,128)(2,1)S(1)}, bf16[144,256]{1,0:T(8,128)(2,1)S(1)}, u32[]{:S(2)}, u32[]{:S(2)}) collective-permute-start(bf16[144,256]{1,0:T(8,128)(2,1)S(1)} %get-tuple-element.38), channel_id=1, source_target_pairs={{4,2},{5,3},{2,4},{3,5},{12,10},{13,11},{10,12},{11,13},{20,18},{2... | collective-permute-start | bytes 221192 | tf_op jit(solution)/shard_map/ppermute | solution.py:365
  76.2 5.9 %collective-permute-start.18 = (bf16[256,128]{1,0:T(8,128)(2,1)S(1)}, bf16[256,128]{1,0:T(8,128)(2,1)S(1)}, u32[]{:S(2)}, u32[]{:S(2)}) collective-permute-start(bf16[256,128]{1,0:T(8,128)(2,1)S(1)} %shard_map.77), channel_id=1, source_target_pairs={{0,24},{8,16},{16,8},{24,0},{1,25},{9,17},{17,9},{25,1},{2,26},{10... | collective-permute-start | bytes 196616 | tf_op jit(solution)/shard_map/ppermute | solution.py:345
  77.7 4.7 %collective-permute-start.17 = (bf16[256,128]{1,0:T(8,128)(2,1)S(1)}, bf16[256,128]{1,0:T(8,128)(2,1)S(1)}, u32[]{:S(2)}, u32[]{:S(2)}) collective-permute-start(bf16[256,128]{1,0:T(8,128)(2,1)S(1)} %shard_map.77), channel_id=1, source_target_pairs={{0,16},{8,24},{16,0},{24,8},{1,17},{9,25},{17,1},{25,9},{2,18},{10... | collective-permute-start | bytes 196616 | tf_op jit(solution)/shard_map/ppermute | solution.py:345
  78.7 4.3 %collective-permute-start.16 = (bf16[256,128]{1,0:T(8,128)(2,1)S(1)}, bf16[256,128]{1,0:T(8,128)(2,1)S(1)}, u32[]{:S(2)}, u32[]{:S(2)}) collective-permute-start(bf16[256,128]{1,0:T(8,128)(2,1)S(1)} %shard_map.77), channel_id=1, source_target_pairs={{0,8},{8,0},{16,24},{24,16},{1,9},{9,1},{17,25},{25,17},{2,10},{10... | collective-permute-start | bytes 196616 | tf_op jit(solution)/shard_map/ppermute | solution.py:345
  83.0 1.6 %collective-permute-start.19 = (bf16[256,512]{1,0:T(8,128)(2,1)S(1)}, bf16[256,512]{1,0:T(8,128)(2,1)S(1)}, u32[]{:S(2)}, u32[]{:S(2)}) collective-permute-start(bf16[256,512]{1,0:T(8,128)(2,1)S(1)} %pad_maximum_fusion.1.own_ref), channel_id=1, source_target_pairs={{0,1},{1,0},{2,3},{3,2},{4,5},{5,4},{6,7},{7,6},{8,9},{9,8},{10,11... | collective-permute-start | bytes 786440 | tf_op jit(solution)/shard_map/ppermute | solution.py:342
  85.4 3.3 %collective-permute-start.21 = (bf16[64,512]{1,0:T(8,128)(2,1)S(1)}, bf16[64,512]{1,0:T(8,128)(2,1)S(1)}, u32[]{:S(2)}, u32[]{:S(2)}) collective-permute-start(bf16[64,512]{1,0:T(8,128)(2,1)S(1)} %get-tuple-element.45), channel_id=1, source_target_pairs={{3,2},{2,3},{5,4},{4,5},{11,10},{10,11},{13,12},{12,13},{19,18},{1... | collective-permute-start | bytes 196616 | tf_op jit(solution)/shard_map/ppermute | solution.py:365
  86.0 7.7 %collective-permute-start.22 = (bf16[64,512]{1,0:T(8,128)(2,1)S(1)}, bf16[64,512]{1,0:T(8,128)(2,1)S(1)}, u32[]{:S(2)}, u32[]{:S(2)}) collective-permute-start(bf16[64,512]{1,0:T(8,128)(2,1)S(1)} %get-tuple-element.46), channel_id=1, source_target_pairs={{2,1},{3,0},{4,7},{5,6},{10,9},{11,8},{12,15},{13,14},{18,17},{19,... | collective-permute-start | bytes 196616 | tf_op jit(solution)/shard_map/ppermute | solution.py:415
  87.4 8.1 %collective-permute-start.20 = (bf16[64,512]{1,0:T(8,128)(2,1)S(1)}, bf16[64,512]{1,0:T(8,128)(2,1)S(1)}, u32[]{:S(2)}, u32[]{:S(2)}) collective-permute-start(bf16[64,512]{1,0:T(8,128)(2,1)S(1)} %get-tuple-element.44), channel_id=1, source_target_pairs={{2,0},{3,1},{4,6},{5,7},{10,8},{11,9},{12,14},{13,15},{18,16},{19,... | collective-permute-start | bytes 196616 | tf_op jit(solution)/shard_map/ppermute | solution.py:414

commit v8 on v5

--- a/solution.py
+++ b/solution.py
@@ -236,7 +236,7 @@
         pack_kernel,
         out_shape=[out, out],
         in_specs=[SMEM, ANY, ANY, ANY],
-        out_specs=[ANY, ANY],
+        out_specs=[VMEM, VMEM],
         scratch_shapes=[pltpu.SemaphoreType.DMA((8,))],
         compiler_params=WIDE,
     )(core, w_key, w_value, queries)
@@ -344,7 +344,7 @@
     for j in near_first:
         low = j & -j
         shard = shards[j ^ low]
-        shards[j] = across(shard if j == low else after(shard, *arrived[1:]), CORES * low)
+        shards[j] = across(shard if j == low else after(shard, shards[1], *arrived[1:]), CORES * low)
     normed = combine(core_only, arrived, head_gain.reshape(1, panel), heads)
 
     terms = output_terms(

time: 103 us -> 84.6 us (0.82)
  Pallas kernels: 29.3 us -> 13.3 us
  waiting for transfers between devices: 47.7 us -> 45 us
    pallas_call x1, Pallas kernels: 18 us -> 2.02 us  [pack(): pl.pallas_call(pack_kernel, out_shape=[out, out], in_specs=[SMEM, ANY, AN...]
    ppermute x16, waiting for transfers between devices: 41.9 us -> 39.7 us  [across(): return lax.ppermute(array, 'ctx', [(i, i ^ bits) for i in range(n_ctx)])]
  transfers between devices with their start and end apart: 19 -> 19, of which waited for: 13 -> 12; matrix products, arithmetic and copies ran while one was open for 1% -> 1% of each run, Pallas kernels for 10% -> 12%
where the time goes in v8:
time: 84.6 us; the launch traced here: 84.4 us
  waiting for transfers between devices  45 us (53%)
  starting transfers between devices  20.9 us (25%)
  Pallas kernels  13.3 us (16%)
  local copies, waits for them, and re-layouts  4.15 us (5%)
  other arithmetic  0.85 us (1%)
    ppermute x16, waiting for transfers between devices, across(): return lax.ppermute(array, 'ctx', [(i, i ^ bits) for i in range(n_ctx)])  39.7 us
    ppermute x16, starting transfers between devices, across(): return lax.ppermute(array, 'ctx', [(i, i ^ bits) for i in range(n_ctx)])  17.4 us
    pallas_call x2, Pallas kernels, project(): pl.pallas_call(functools.partial(project_kernel, count, extra, acc is not...  7.2 us
    ppermute x3, waiting for transfers between devices, over_dp(): return lax.ppermute(array, 'dp', [(d, d ^ bits) for d in range(n_dp)])  5.39 us
    ppermute x3, starting transfers between devices, over_dp(): return lax.ppermute(array, 'dp', [(d, d ^ bits) for d in range(n_dp)])  3.55 us
    unnamed x10, local copies, waits for them, and re-layouts  3.16 us
    pallas_call x1, Pallas kernels, attend(): pl.pallas_call(functools.partial(attend_kernel, count, heads, depth, grou...  2.82 us
    pallas_call x1, Pallas kernels, pack(): pl.pallas_call(pack_kernel, out_shape=[out, out], in_specs=[SMEM, ANY, AN...  2.02 us
  transfers between devices with their start and end apart: 19, of which 12 were waited for; matrix products, arithmetic and copies ran while one was open for 1% of the time, Pallas kernels for 12%

profile of v8, /device:TPU:0, one launch (start us, length us, event | category | flops | bytes accessed | tf_op | source)
XLA Modules:
  0.0 84.4 jit_solution(9374092826139320670)
XLA Ops:
  0.0 2.0 %shard_map.73 = (bf16[544,256]{1,0:T(8,128)(2,1)}, bf16[544,256]{1,0:T(8,128)(2,1)}) custom-call(s32[1]{0:T(128)} %bitcast.core_ref, bf16[512,256]{1,0:T(8,128)(2,1)} %key_ref.1, bf16[512,256]{1,0:T(8,128)(2,1)} %value_ref.1, bf16[64,256]{1,0:T(8,128)(2,1)} %query_ref.1), custom_call_target="tpu_custom_call" | custom-call | tf_op jit(solution)/shard_map/pallas_call | solution.py:235
  2.0 0.5 collective-permute-start
  2.5 3.7 %collective-permute-start.3 = (bf16[544,256]{1,0:T(8,128)(2,1)}, bf16[544,256]{1,0:T(8,128)(2,1)S(1)}, u32[]{:S(2)}, u32[]{:S(2)}) collective-permute-start(bf16[544,256]{1,0:T(8,128)(2,1)} %get-tuple-element.24.refs_3_.refs_4_), channel_id=1, source_target_pairs={{0,4},{1,5},{2,6},{3,7},{4,0},{5,1},{6,2},{7,3},{8,12},{9,13},{10,... | collective-permute-start | bytes 835592 | tf_op jit(solution)/shard_map/ppermute | solution.py:306
  6.2 1.6 %collective-permute-start.1 = (bf16[544,256]{1,0:T(8,128)(2,1)}, bf16[544,256]{1,0:T(8,128)(2,1)S(1)}, u32[]{:S(2)}, u32[]{:S(2)}) collective-permute-start(bf16[544,256]{1,0:T(8,128)(2,1)} %get-tuple-element.24.refs_3_.refs_4_), channel_id=1, source_target_pairs={{0,2},{1,3},{2,0},{3,1},{4,6},{5,7},{6,4},{7,5},{8,10},{9,11},{10,... | collective-permute-start | bytes 835592 | tf_op jit(solution)/shard_map/ppermute | solution.py:306
  7.8 0.0 collective-permute-start.4
  7.8 0.2 collective-permute-start.2
  8.0 0.1 stack.71.refs_2_
  8.1 0.8 slice_bitcast_fusion.3
  9.0 11.0 %collective-permute-done.3.refs_5_.refs_8_ = bf16[544,256]{1,0:T(8,128)(2,1)S(1)} collective-permute-done((bf16[544,256]{1,0:T(8,128)(2,1)}, bf16[544,256]{1,0:T(8,128)(2,1)S(1)}, u32[]{:S(2)}, u32[]{:S(2)}) %collective-permute-start.3) | collective-permute-done | bytes 278560 | tf_op jit(solution)/shard_map/ppermute | solution.py:306
  20.0 1.9 %collective-permute-done.1.refs_3_.refs_6_ = bf16[544,256]{1,0:T(8,128)(2,1)S(1)} collective-permute-done((bf16[544,256]{1,0:T(8,128)(2,1)}, bf16[544,256]{1,0:T(8,128)(2,1)S(1)}, u32[]{:S(2)}, u32[]{:S(2)}) %collective-permute-start.1) | collective-permute-done | bytes 278560 | tf_op jit(solution)/shard_map/ppermute | solution.py:306
  21.9 9.6 %collective-permute-done.4.refs_6_.refs_9_ = bf16[544,256]{1,0:T(8,128)(2,1)S(1)} collective-permute-done((bf16[544,256]{1,0:T(8,128)(2,1)}, bf16[544,256]{1,0:T(8,128)(2,1)S(1)}, u32[]{:S(2)}, u32[]{:S(2)}) %collective-permute-start.4) | collective-permute-done | bytes 278560 | tf_op jit(solution)/shard_map/ppermute | solution.py:306
  31.5 0.0 collective-permute-done.2.refs_4_.refs_7_
  31.5 0.2 collective-permute-start.5
  31.7 1.5 %collective-permute-start.6 = (bf16[544,256]{1,0:T(8,128)(2,1)S(1)}, bf16[544,256]{1,0:T(8,128)(2,1)S(1)}, u32[]{:S(2)}, u32[]{:S(2)}) collective-permute-start(bf16[544,256]{1,0:T(8,128)(2,1)S(1)} %collective-permute-done.3.refs_5_.refs_8_), channel_id=1, source_target_pairs={{0,2},{1,3},{2,0},{3,1},{4,6},{5,7},{6,4},{7,5},{8,10},{9,11},{10,... | collective-permute-start | bytes 835592 | tf_op jit(solution)/shard_map/ppermute | solution.py:306
  33.2 0.5 collective-permute-start.7
  33.7 0.1 slice.8.refs_0_
  33.8 0.0 collective-permute-done.5.refs_4_.refs_5_
  33.8 0.0 collective-permute-done.refs_2_
  33.8 0.0 copy-start
  33.8 2.2 %copy-done = bf16[512,4096]{1,0:T(8,128)(2,1)S(1)} copy-done((bf16[512,4096]{1,0:T(8,128)(2,1)S(1)}, bf16[512,4096]{1,0:T(8,128)(2,1)}, u32[]{:S(2)}) %copy-start) | copy-done | bytes 4194328
  36.0 0.0 copy-start.1
  36.0 1.0 %copy-done.1 = bf16[544,256]{1,0:T(8,128)(2,1)S(1)} copy-done((bf16[544,256]{1,0:T(8,128)(2,1)S(1)}, bf16[544,256]{1,0:T(8,128)(2,1)}, u32[]{:S(2)}) %copy-start.1) | copy-done | bytes 278552
  37.0 3.1 %shard_map.74 = (f32[1024,256]{1,0:T(8,128)S(1)}, bf16[2,16,512]{2,1,0:T(8,128)(2,1)}) custom-call(s32[2]{0:T(128)S(1)} %bitcast.21, bf16[512,4096]{1,0:T(8,128)(2,1)S(1)} %copy-done, bf16[512,4096]{1,0:T(8,128)(2,1)} %collective-permute-done.refs_2_, bf16[544,256]{1,0:T(8,128)(2,1)S(1)} %copy-done.1, bf16[544,256]{1,0:T(8,128)(2,1)S(1)} %collective-permute-done.5.refs_4_.refs_5_), custom_call_target="tpu_custom_call" | custom-call | flops 536870912 | bytes 2097152 | tf_op jit(solution)/shard_map/pallas_call | solution.py:81
  40.0 0.0 copy-start.3
  40.0 0.0 copy-start.2
  40.0 4.1 %shard_map.75 = (f32[1024,256]{1,0:T(8,128)S(1)}, bf16[4,512,512]{2,1,0:T(8,128)(2,1)S(1)}) custom-call(s32[6]{0:T(128)S(1)} %slice.8.refs_0_, bf16[512,4096]{1,0:T(8,128)(2,1)S(1)} %copy-done, bf16[512,4096]{1,0:T(8,128)(2,1)} %collective-permute-done.refs_2_, bf16[544,256]{1,0:T(8,128)(2,1)S(1)} %collective-permute-done.1.refs_3_.refs_6_, ...), custom_call_target="tpu_custom_call" | custom-call | flops 1073741824 | bytes 4194304 | tf_op jit(solution)/shard_map/pallas_call | solution.py:81
  44.2 0.0 copy-start.4
  44.2 0.0 collective-permute-done.6.refs_10_
  44.2 2.3 %collective-permute-done.7.refs_11_ = bf16[544,256]{1,0:T(8,128)(2,1)S(1)} collective-permute-done((bf16[544,256]{1,0:T(8,128)(2,1)S(1)}, bf16[544,256]{1,0:T(8,128)(2,1)S(1)}, u32[]{:S(2)}, u32[]{:S(2)}) %collective-permute-start.7) | collective-permute-done | bytes 278560 | tf_op jit(solution)/shard_map/ppermute | solution.py:306
  46.5 0.0 copy-done.3
  46.5 1.5 %collective-permute-start.12 = (bf16[256,512]{1,0:T(8,128)(2,1)S(1)}, bf16[256,512]{1,0:T(8,128)(2,1)S(1)}, u32[]{:S(2)}, u32[]{:S(2)}) collective-permute-start(bf16[256,512]{1,0:T(8,128)(2,1)S(1)} %copy-done.3), channel_id=1, source_target_pairs={{0,2},{1,3},{2,0},{3,1},{4,6},{5,7},{6,4},{7,5},{8,10},{9,11},{10,... | collective-permute-start | bytes 786440 | tf_op jit(solution)/shard_map/ppermute | solution.py:306
  48.0 2.7 %collective-permute-start.13 = (bf16[256,512]{1,0:T(8,128)(2,1)S(1)}, bf16[256,512]{1,0:T(8,128)(2,1)S(1)}, u32[]{:S(2)}, u32[]{:S(2)}) collective-permute-start(bf16[256,512]{1,0:T(8,128)(2,1)S(1)} %copy-done.3), channel_id=1, source_target_pairs={{0,4},{1,5},{2,6},{3,7},{4,0},{5,1},{6,2},{7,3},{8,12},{9,13},{10,... | collective-permute-start | bytes 786440 | tf_op jit(solution)/shard_map/ppermute | solution.py:306
  50.7 0.1 pad_add_fusion.2.refs_0_
  50.8 0.0 copy-done.2
  50.8 2.8 %shard_map.76 = (bf16[144,128]{1,0:T(8,128)(2,1)S(1)}, bf16[144,128]{1,0:T(8,128)(2,1)S(1)}, bf16[144,128]{1,0:T(8,128)(2,1)S(1)}, bf16[144,128]{1,0:T(8,128)(2,1)S(1)}) custom-call(s32[2]{0:T(128)S(1)} %pad_add_fusion.2.refs_0_, s32[4]{0:T(128)S(1)} %iota_xor_fusion.refs_1_, s32[8]{0:T(128)S(1)} %stack.71.refs_2_, ...), custom_call_target="tpu_custom_call" | custom-call | flops 536870912 | bytes 2097152 | tf_op jit(solution)/shard_map/pallas_call | solution.py:158
  53.7 0.2 collective-permute-start.10
  53.9 0.6 collective-permute-start.8
  54.5 3.6 %collective-permute-start.9 = (bf16[144,128]{1,0:T(8,128)(2,1)S(1)}, bf16[144,128]{1,0:T(8,128)(2,1)S(1)}, u32[]{:S(2)}, u32[]{:S(2)}) collective-permute-start(bf16[144,128]{1,0:T(8,128)(2,1)S(1)} %get-tuple-element.33), channel_id=1, source_target_pairs={{0,4},{1,5},{2,6},{3,7},{4,0},{5,1},{6,2},{7,3},{8,12},{9,13},{10,... | collective-permute-start | bytes 110600 | tf_op jit(solution)/shard_map/ppermute | solution.py:306
  58.1 5.6 %collective-permute-done.10.refs_3_ = bf16[144,128]{1,0:T(8,128)(2,1)S(1)} collective-permute-done((bf16[144,128]{1,0:T(8,128)(2,1)S(1)}, bf16[144,128]{1,0:T(8,128)(2,1)S(1)}, u32[]{:S(2)}, u32[]{:S(2)}) %collective-permute-start.10) | collective-permute-done | bytes 36896 | tf_op jit(solution)/shard_map/ppermute | solution.py:306
  63.7 0.0 collective-permute-done.8.refs_1_
  63.7 1.6 %collective-permute-done.9.refs_2_ = bf16[144,128]{1,0:T(8,128)(2,1)S(1)} collective-permute-done((bf16[144,128]{1,0:T(8,128)(2,1)S(1)}, bf16[144,128]{1,0:T(8,128)(2,1)S(1)}, u32[]{:S(2)}, u32[]{:S(2)}) %collective-permute-start.9) | collective-permute-done | bytes 36896 | tf_op jit(solution)/shard_map/ppermute | solution.py:306
  65.3 0.0 collective-permute-done.12.refs_1_
  65.3 0.0 collective-permute-done.13.refs_2_
  65.3 0.3 collective-permute-start.14
  65.6 0.0 copy-done.4
  65.6 0.2 shard_map.77.own_ref
  65.7 0.1 collective-permute-start.11
  65.8 0.1 pad_add_fusion.1.place_ref
  65.9 1.1 %collective-permute-done.11.sibling_ref = bf16[128,128]{1,0:T(8,128)(2,1)S(1)} collective-permute-done((bf16[128,128]{1,0:T(8,128)(2,1)S(1)}, bf16[128,128]{1,0:T(8,128)(2,1)S(1)}, u32[]{:S(2)}, u32[]{:S(2)}) %collective-permute-start.11) | collective-permute-done | bytes 32800 | tf_op jit(solution)/shard_map/ppermute | solution.py:306
  67.0 5.3 %collective-permute-done.14.refs_3_ = bf16[256,512]{1,0:T(8,128)(2,1)S(1)} collective-permute-done((bf16[256,512]{1,0:T(8,128)(2,1)S(1)}, bf16[256,512]{1,0:T(8,128)(2,1)S(1)}, u32[]{:S(2)}, u32[]{:S(2)}) %collective-permute-start.14) | collective-permute-done | bytes 262176 | tf_op jit(solution)/shard_map/ppermute | solution.py:306
  72.3 1.0 %shard_map.78 = (bf16[128,512]{1,0:T(8,128)(2,1)S(1)}, bf16[128,512]{1,0:T(8,128)(2,1)S(1)}, bf16[128,512]{1,0:T(8,128)(2,1)S(1)}, bf16[128,512]{1,0:T(8,128)(2,1)S(1)}) custom-call(s32[2]{0:T(128)S(1)} %pad_add_fusion.1.place_ref, bf16[128,128]{1,0:T(8,128)(2,1)S(1)} %shard_map.77.own_ref, bf16[128,128]{1,0:T(8,128)(2,1)S(1)} %collective-permute-done.11.sibling_ref, ...), custom_call_target="tpu_custom_call" | custom-call | tf_op jit(solution)/shard_map/pallas_call | solution.py:262
  73.3 1.6 %collective-permute-start.15 = (bf16[128,512]{1,0:T(8,128)(2,1)S(1)}, bf16[128,512]{1,0:T(8,128)(2,1)S(1)}, u32[]{:S(2)}, u32[]{:S(2)}) collective-permute-start(bf16[128,512]{1,0:T(8,128)(2,1)S(1)} %get-tuple-element.38), channel_id=1, source_target_pairs={{0,8},{8,0},{16,24},{24,16},{1,9},{9,1},{17,25},{25,17},{2,10},{10... | collective-permute-start | bytes 393224 | tf_op jit(solution)/shard_map/ppermute | solution.py:309
  74.9 1.5 %collective-permute-start.16 = (bf16[128,512]{1,0:T(8,128)(2,1)S(1)}, bf16[128,512]{1,0:T(8,128)(2,1)S(1)}, u32[]{:S(2)}, u32[]{:S(2)}) collective-permute-start(bf16[128,512]{1,0:T(8,128)(2,1)S(1)} %get-tuple-element.39), channel_id=1, source_target_pairs={{0,16},{8,24},{16,0},{24,8},{1,17},{9,25},{17,1},{25,9},{2,18},{10... | collective-permute-start | bytes 393224 | tf_op jit(solution)/shard_map/ppermute | solution.py:309
  76.4 0.5 collective-permute-start.17
  76.9 2.2 %collective-permute-done.15.refs_1_ = bf16[128,512]{1,0:T(8,128)(2,1)S(1)} collective-permute-done((bf16[128,512]{1,0:T(8,128)(2,1)S(1)}, bf16[128,512]{1,0:T(8,128)(2,1)S(1)}, u32[]{:S(2)}, u32[]{:S(2)}) %collective-permute-start.15) | collective-permute-done | bytes 131104 | tf_op jit(solution)/shard_map/ppermute | solution.py:309
  79.1 1.3 %collective-permute-done.16.refs_2_ = bf16[128,512]{1,0:T(8,128)(2,1)S(1)} collective-permute-done((bf16[128,512]{1,0:T(8,128)(2,1)S(1)}, bf16[128,512]{1,0:T(8,128)(2,1)S(1)}, u32[]{:S(2)}, u32[]{:S(2)}) %collective-permute-start.16) | collective-permute-done | bytes 131104 | tf_op jit(solution)/shard_map/ppermute | solution.py:309
  80.4 1.9 %collective-permute-done.17.refs_3_ = bf16[128,512]{1,0:T(8,128)(2,1)S(1)} collective-permute-done((bf16[128,512]{1,0:T(8,128)(2,1)S(1)}, bf16[128,512]{1,0:T(8,128)(2,1)S(1)}, u32[]{:S(2)}, u32[]{:S(2)}) %collective-permute-start.17) | collective-permute-done | bytes 131104 | tf_op jit(solution)/shard_map/ppermute | solution.py:309
  82.3 0.1 shard_map.79
  82.4 0.1 collective-permute-start.18
  82.4 1.2 %collective-permute-done.18 = bf16[64,512]{1,0:T(8,128)(2,1)S(1)} collective-permute-done((bf16[64,512]{1,0:T(8,128)(2,1)S(1)}, bf16[64,512]{1,0:T(8,128)(2,1)S(1)}, u32[]{:S(2)}, u32[]{:S(2)}) %collective-permute-start.18) | collective-permute-done | bytes 65568 | tf_op jit(solution)/shard_map/ppermute | solution.py:306
  83.7 0.7 maximum_select_fusion
  (4 shorter events, 0.0 us)
Async XLA Ops:
  2.0 31.8 %collective-permute-start = (bf16[512,4096]{1,0:T(8,128)(2,1)}, bf16[512,4096]{1,0:T(8,128)(2,1)}, u32[]{:S(2)}, u32[]{:S(2)}) collective-permute-start(bf16[512,4096]{1,0:T(8,128)(2,1)} %refs_1_.3), channel_id=1, source_target_pairs={{0,1},{1,0},{2,3},{3,2},{4,5},{5,4},{6,7},{7,6},{8,9},{9,8},{10,11... | collective-permute-start | bytes 12582920 | tf_op jit(solution)/shard_map/ppermute | solution.py:306
  2.5 17.5 %collective-permute-start.3 = (bf16[544,256]{1,0:T(8,128)(2,1)}, bf16[544,256]{1,0:T(8,128)(2,1)S(1)}, u32[]{:S(2)}, u32[]{:S(2)}) collective-permute-start(bf16[544,256]{1,0:T(8,128)(2,1)} %get-tuple-element.24.refs_3_.refs_4_), channel_id=1, source_target_pairs={{0,4},{1,5},{2,6},{3,7},{4,0},{5,1},{6,2},{7,3},{8,12},{9,13},{10,... | collective-permute-start | bytes 835592 | tf_op jit(solution)/shard_map/ppermute | solution.py:306
  6.2 15.7 %collective-permute-start.1 = (bf16[544,256]{1,0:T(8,128)(2,1)}, bf16[544,256]{1,0:T(8,128)(2,1)S(1)}, u32[]{:S(2)}, u32[]{:S(2)}) collective-permute-start(bf16[544,256]{1,0:T(8,128)(2,1)} %get-tuple-element.24.refs_3_.refs_4_), channel_id=1, source_target_pairs={{0,2},{1,3},{2,0},{3,1},{4,6},{5,7},{6,4},{7,5},{8,10},{9,11},{10,... | collective-permute-start | bytes 835592 | tf_op jit(solution)/shard_map/ppermute | solution.py:306
  7.8 23.7 %collective-permute-start.4 = (bf16[544,256]{1,0:T(8,128)(2,1)}, bf16[544,256]{1,0:T(8,128)(2,1)S(1)}, u32[]{:S(2)}, u32[]{:S(2)}) collective-permute-start(bf16[544,256]{1,0:T(8,128)(2,1)} %get-tuple-element.27), channel_id=1, source_target_pairs={{0,5},{1,4},{2,7},{3,6},{4,1},{5,0},{6,3},{7,2},{8,13},{9,12},{10,... | collective-permute-start | bytes 835592 | tf_op jit(solution)/shard_map/ppermute | solution.py:306
  7.8 23.7 %collective-permute-start.2 = (bf16[544,256]{1,0:T(8,128)(2,1)}, bf16[544,256]{1,0:T(8,128)(2,1)S(1)}, u32[]{:S(2)}, u32[]{:S(2)}) collective-permute-start(bf16[544,256]{1,0:T(8,128)(2,1)} %get-tuple-element.27), channel_id=1, source_target_pairs={{0,3},{1,2},{2,1},{3,0},{4,7},{5,6},{6,5},{7,4},{8,11},{9,10},{10,... | collective-permute-start | bytes 835592 | tf_op jit(solution)/shard_map/ppermute | solution.py:306
  31.5 2.4 %collective-permute-start.5 = (bf16[544,256]{1,0:T(8,128)(2,1)}, bf16[544,256]{1,0:T(8,128)(2,1)S(1)}, u32[]{:S(2)}, u32[]{:S(2)}) collective-permute-start(bf16[544,256]{1,0:T(8,128)(2,1)} %get-tuple-element.27), channel_id=1, source_target_pairs={{0,1},{1,0},{2,3},{3,2},{4,5},{5,4},{6,7},{7,6},{8,9},{9,8},{10,11... | collective-permute-start | bytes 835592 | tf_op jit(solution)/shard_map/ppermute | solution.py:306
  31.7 12.5 %collective-permute-start.6 = (bf16[544,256]{1,0:T(8,128)(2,1)S(1)}, bf16[544,256]{1,0:T(8,128)(2,1)S(1)}, u32[]{:S(2)}, u32[]{:S(2)}) collective-permute-start(bf16[544,256]{1,0:T(8,128)(2,1)S(1)} %collective-permute-done.3.refs_5_.refs_8_), channel_id=1, source_target_pairs={{0,2},{1,3},{2,0},{3,1},{4,6},{5,7},{6,4},{7,5},{8,10},{9,11},{10,... | collective-permute-start | bytes 835592 | tf_op jit(solution)/shard_map/ppermute | solution.py:306
  33.2 13.3 %collective-permute-start.7 = (bf16[544,256]{1,0:T(8,128)(2,1)S(1)}, bf16[544,256]{1,0:T(8,128)(2,1)S(1)}, u32[]{:S(2)}, u32[]{:S(2)}) collective-permute-start(bf16[544,256]{1,0:T(8,128)(2,1)S(1)} %collective-permute-done.4.refs_6_.refs_9_), channel_id=1, source_target_pairs={{0,2},{1,3},{2,0},{3,1},{4,6},{5,7},{6,4},{7,5},{8,10},{9,11},{10,... | collective-permute-start | bytes 835592 | tf_op jit(solution)/shard_map/ppermute | solution.py:306
  33.8 2.2 %copy-start = (bf16[512,4096]{1,0:T(8,128)(2,1)S(1)}, bf16[512,4096]{1,0:T(8,128)(2,1)}, u32[]{:S(2)}) copy-start(bf16[512,4096]{1,0:T(8,128)(2,1)} %refs_1_.3) | copy-start | bytes 12582916
  36.0 1.0 %copy-start.1 = (bf16[544,256]{1,0:T(8,128)(2,1)S(1)}, bf16[544,256]{1,0:T(8,128)(2,1)}, u32[]{:S(2)}) copy-start(bf16[544,256]{1,0:T(8,128)(2,1)} %get-tuple-element.24.refs_3_.refs_4_) | copy-start | bytes 835588
  40.0 6.5 %copy-start.3 = (bf16[256,512]{1,0:T(8,128)(2,1)S(1)}, bf16[256,512]{1,0:T(8,128)(2,1)}, u32[]{:S(2)}) copy-start(bf16[256,512]{1,0:T(8,128)(2,1)} %refs_0_) | copy-start | bytes 786436
  40.0 10.8 %copy-start.2 = (bf16[544,256]{1,0:T(8,128)(2,1)S(1)}, bf16[544,256]{1,0:T(8,128)(2,1)}, u32[]{:S(2)}) copy-start(bf16[544,256]{1,0:T(8,128)(2,1)} %get-tuple-element.24.refs_3_.refs_4_) | copy-start | bytes 835588
  44.2 21.4 %copy-start.4 = (bf16[256]{0:T(256)(128)(2,1)S(1)}, bf16[256]{0:T(256)(128)(2,1)}, u32[]{:S(2)}) copy-start(bf16[256]{0:T(256)(128)(2,1)} %param.12) | copy-start | bytes 1540
  46.5 18.8 %collective-permute-start.12 = (bf16[256,512]{1,0:T(8,128)(2,1)S(1)}, bf16[256,512]{1,0:T(8,128)(2,1)S(1)}, u32[]{:S(2)}, u32[]{:S(2)}) collective-permute-start(bf16[256,512]{1,0:T(8,128)(2,1)S(1)} %copy-done.3), channel_id=1, source_target_pairs={{0,2},{1,3},{2,0},{3,1},{4,6},{5,7},{6,4},{7,5},{8,10},{9,11},{10,... | collective-permute-start | bytes 786440 | tf_op jit(solution)/shard_map/ppermute | solution.py:306
  48.0 17.3 %collective-permute-start.13 = (bf16[256,512]{1,0:T(8,128)(2,1)S(1)}, bf16[256,512]{1,0:T(8,128)(2,1)S(1)}, u32[]{:S(2)}, u32[]{:S(2)}) collective-permute-start(bf16[256,512]{1,0:T(8,128)(2,1)S(1)} %copy-done.3), channel_id=1, source_target_pairs={{0,4},{1,5},{2,6},{3,7},{4,0},{5,1},{6,2},{7,3},{8,12},{9,13},{10,... | collective-permute-start | bytes 786440 | tf_op jit(solution)/shard_map/ppermute | solution.py:306
  53.7 10.1 %collective-permute-start.10 = (bf16[144,128]{1,0:T(8,128)(2,1)S(1)}, bf16[144,128]{1,0:T(8,128)(2,1)S(1)}, u32[]{:S(2)}, u32[]{:S(2)}) collective-permute-start(bf16[144,128]{1,0:T(8,128)(2,1)S(1)} %get-tuple-element.34), channel_id=1, source_target_pairs={{0,6},{1,7},{2,4},{3,5},{4,2},{5,3},{6,0},{7,1},{8,14},{9,15},{10,... | collective-permute-start | bytes 110600 | tf_op jit(solution)/shard_map/ppermute | solution.py:306
  53.9 9.8 %collective-permute-start.8 = (bf16[144,128]{1,0:T(8,128)(2,1)S(1)}, bf16[144,128]{1,0:T(8,128)(2,1)S(1)}, u32[]{:S(2)}, u32[]{:S(2)}) collective-permute-start(bf16[144,128]{1,0:T(8,128)(2,1)S(1)} %get-tuple-element.32), channel_id=1, source_target_pairs={{0,2},{1,3},{2,0},{3,1},{4,6},{5,7},{6,4},{7,5},{8,10},{9,11},{10,... | collective-permute-start | bytes 110600 | tf_op jit(solution)/shard_map/ppermute | solution.py:306
  54.5 10.8 %collective-permute-start.9 = (bf16[144,128]{1,0:T(8,128)(2,1)S(1)}, bf16[144,128]{1,0:T(8,128)(2,1)S(1)}, u32[]{:S(2)}, u32[]{:S(2)}) collective-permute-start(bf16[144,128]{1,0:T(8,128)(2,1)S(1)} %get-tuple-element.33), channel_id=1, source_target_pairs={{0,4},{1,5},{2,6},{3,7},{4,0},{5,1},{6,2},{7,3},{8,12},{9,13},{10,... | collective-permute-start | bytes 110600 | tf_op jit(solution)/shard_map/ppermute | solution.py:306
  65.3 7.0 %collective-permute-start.14 = (bf16[256,512]{1,0:T(8,128)(2,1)S(1)}, bf16[256,512]{1,0:T(8,128)(2,1)S(1)}, u32[]{:S(2)}, u32[]{:S(2)}) collective-permute-start(bf16[256,512]{1,0:T(8,128)(2,1)S(1)} %collective-permute-done.13.refs_2_), channel_id=1, source_target_pairs={{0,2},{1,3},{2,0},{3,1},{4,6},{5,7},{6,4},{7,5},{8,10},{9,11},{10,... | collective-permute-start | bytes 786440 | tf_op jit(solution)/shard_map/ppermute | solution.py:306
  65.7 1.3 %collective-permute-start.11 = (bf16[128,128]{1,0:T(8,128)(2,1)S(1)}, bf16[128,128]{1,0:T(8,128)(2,1)S(1)}, u32[]{:S(2)}, u32[]{:S(2)}) collective-permute-start(bf16[128,128]{1,0:T(8,128)(2,1)S(1)} %shard_map.77.own_ref), channel_id=1, source_target_pairs={{0,1},{1,0},{2,3},{3,2},{4,5},{5,4},{6,7},{7,6},{8,9},{9,8},{10,11... | collective-permute-start | bytes 98312 | tf_op jit(solution)/shard_map/ppermute | solution.py:306
  73.3 5.8 %collective-permute-start.15 = (bf16[128,512]{1,0:T(8,128)(2,1)S(1)}, bf16[128,512]{1,0:T(8,128)(2,1)S(1)}, u32[]{:S(2)}, u32[]{:S(2)}) collective-permute-start(bf16[128,512]{1,0:T(8,128)(2,1)S(1)} %get-tuple-element.38), channel_id=1, source_target_pairs={{0,8},{8,0},{16,24},{24,16},{1,9},{9,1},{17,25},{25,17},{2,10},{10... | collective-permute-start | bytes 393224 | tf_op jit(solution)/shard_map/ppermute | solution.py:309
  74.9 5.4 %collective-permute-start.16 = (bf16[128,512]{1,0:T(8,128)(2,1)S(1)}, bf16[128,512]{1,0:T(8,128)(2,1)S(1)}, u32[]{:S(2)}, u32[]{:S(2)}) collective-permute-start(bf16[128,512]{1,0:T(8,128)(2,1)S(1)} %get-tuple-element.39), channel_id=1, source_target_pairs={{0,16},{8,24},{16,0},{24,8},{1,17},{9,25},{17,1},{25,9},{2,18},{10... | collective-permute-start | bytes 393224 | tf_op jit(solution)/shard_map/ppermute | solution.py:309
  76.4 5.9 %collective-permute-start.17 = (bf16[128,512]{1,0:T(8,128)(2,1)S(1)}, bf16[128,512]{1,0:T(8,128)(2,1)S(1)}, u32[]{:S(2)}, u32[]{:S(2)}) collective-permute-start(bf16[128,512]{1,0:T(8,128)(2,1)S(1)} %get-tuple-element.40), channel_id=1, source_target_pairs={{0,24},{8,16},{16,8},{24,0},{1,25},{9,17},{17,9},{25,1},{2,26},{10... | collective-permute-start | bytes 393224 | tf_op jit(solution)/shard_map/ppermute | solution.py:309
  82.4 1.3 %collective-permute-start.18 = (bf16[64,512]{1,0:T(8,128)(2,1)S(1)}, bf16[64,512]{1,0:T(8,128)(2,1)S(1)}, u32[]{:S(2)}, u32[]{:S(2)}) collective-permute-start(bf16[64,512]{1,0:T(8,128)(2,1)S(1)} %get-tuple-element.42), channel_id=1, source_target_pairs={{0,1},{1,0},{2,3},{3,2},{4,5},{5,4},{6,7},{7,6},{8,9},{9,8},{10,11... | collective-permute-start | bytes 196616 | tf_op jit(solution)/shard_map/ppermute | solution.py:306

commit v9 on v8

--- a/solution.py
+++ b/solution.py
@@ -319,9 +319,11 @@
         if j == low:
             pairs[j] = (across(own_part, CORES * j), across(other_part, CORES * j + 1))
         else:
-            pairs[j] = tuple(across(part, CORES * low) for part in pairs[j ^ low])
+            pairs[j] = tuple(
+                across(after(part, near), CORES * low) for part, near in zip(pairs[j ^ low], pairs[1])
+            )
     context_sibling = across(after(context, own_part), 1)
-    pairs[0] = (own_part, across(after(other_part, pairs[1], pairs[chips // 2]), 1))
+    pairs[0] = (own_part, across(after(other_part, context_sibling), 1))
 
     places = jnp.stack(
         [(chip ^ j) * CORES + who for j in range(chips) for who in (core, 1 - core)]

time: 84.6 us -> 83.5 us (0.987)
  starting transfers between devices: 20.9 us -> 19.9 us
    ppermute x16, starting transfers between devices: 17.4 us -> 16.4 us  [across(): return lax.ppermute(array, 'ctx', [(i, i ^ bits) for i in range(n_ctx)])]
  transfers between devices with their start and end apart: 19 -> 19, of which waited for: 12 -> 13; matrix products, arithmetic and copies ran while one was open for 1% -> 1% of each run, Pallas kernels for 12% -> 12%
where the time goes in v9:
time: 83.5 us; the launch traced here: 83.2 us
  waiting for transfers between devices  44.9 us (54%)
  starting transfers between devices  19.9 us (24%)
  Pallas kernels  13.3 us (16%)
  local copies, waits for them, and re-layouts  4.16 us (5%)
  other arithmetic  0.85 us (1%)
    ppermute x16, waiting for transfers between devices, across(): return lax.ppermute(array, 'ctx', [(i, i ^ bits) for i in range(n_ctx)])  39.5 us
    ppermute x16, starting transfers between devices, across(): return lax.ppermute(array, 'ctx', [(i, i ^ bits) for i in range(n_ctx)])  16.4 us
    pallas_call x2, Pallas kernels, project(): pl.pallas_call(functools.partial(project_kernel, count, extra, acc is not...  7.2 us
    ppermute x3, waiting for transfers between devices, over_dp(): return lax.ppermute(array, 'dp', [(d, d ^ bits) for d in range(n_dp)])  5.39 us
    ppermute x3, starting transfers between devices, over_dp(): return lax.ppermute(array, 'dp', [(d, d ^ bits) for d in range(n_dp)])  3.55 us
    unnamed x10, local copies, waits for them, and re-layouts  3.16 us
    pallas_call x1, Pallas kernels, attend(): pl.pallas_call(functools.partial(attend_kernel, count, heads, depth, grou...  2.82 us
    pallas_call x1, Pallas kernels, pack(): pl.pallas_call(pack_kernel, out_shape=[out, out], in_specs=[SMEM, ANY, AN...  2.02 us
  transfers between devices with their start and end apart: 19, of which 13 were waited for; matrix products, arithmetic and copies ran while one was open for 1% of the time, Pallas kernels for 12%

profile of v9, /device:TPU:0, one launch (start us, length us, event | category | flops | bytes accessed | tf_op | source)
XLA Modules:
  0.0 83.2 jit_solution(14918796045956565006)
XLA Ops:
  0.0 2.0 %shard_map.73 = (bf16[544,256]{1,0:T(8,128)(2,1)}, bf16[544,256]{1,0:T(8,128)(2,1)}) custom-call(s32[1]{0:T(128)} %bitcast.core_ref, bf16[512,256]{1,0:T(8,128)(2,1)} %key_ref.1, bf16[512,256]{1,0:T(8,128)(2,1)} %value_ref.1, bf16[64,256]{1,0:T(8,128)(2,1)} %query_ref.1), custom_call_target="tpu_custom_call" | custom-call | tf_op jit(solution)/shard_map/pallas_call | solution.py:235
  2.0 0.5 collective-permute-start
  2.5 2.7 %collective-permute-start.1 = (bf16[544,256]{1,0:T(8,128)(2,1)}, bf16[544,256]{1,0:T(8,128)(2,1)S(1)}, u32[]{:S(2)}, u32[]{:S(2)}) collective-permute-start(bf16[544,256]{1,0:T(8,128)(2,1)} %get-tuple-element.26.refs_3_.refs_4_), channel_id=1, source_target_pairs={{0,2},{1,3},{2,0},{3,1},{4,6},{5,7},{6,4},{7,5},{8,10},{9,11},{10,... | collective-permute-start | bytes 835592 | tf_op jit(solution)/shard_map/ppermute | solution.py:306
  5.2 2.6 %collective-permute-start.3 = (bf16[544,256]{1,0:T(8,128)(2,1)}, bf16[544,256]{1,0:T(8,128)(2,1)S(1)}, u32[]{:S(2)}, u32[]{:S(2)}) collective-permute-start(bf16[544,256]{1,0:T(8,128)(2,1)} %get-tuple-element.26.refs_3_.refs_4_), channel_id=1, source_target_pairs={{0,4},{1,5},{2,6},{3,7},{4,0},{5,1},{6,2},{7,3},{8,12},{9,13},{10,... | collective-permute-start | bytes 835592 | tf_op jit(solution)/shard_map/ppermute | solution.py:306
  7.8 0.0 collective-permute-start.2
  7.8 0.2 collective-permute-start.4
  8.0 0.1 stack.71.refs_2_
  8.0 0.8 %slice_bitcast_fusion.3 = (s32[1,128]{1,0:T(1,128)S(1)}, s32[1,128]{1,0:T(1,128)S(1)}, s32[1,128]{1,0:T(1,128)S(1)}, s32[1,128]{1,0:T(1,128)S(1)}) fusion(s32[512]{0:T(512)} %param.11), kind=kLoop, calls=%fused_computation.7 | loop fusion | bytes 4096 | tf_op jit(solution)/shard_map/stack | solution.py:152
  8.9 9.9 %collective-permute-done.1.refs_3_.refs_6_ = bf16[544,256]{1,0:T(8,128)(2,1)S(1)} collective-permute-done((bf16[544,256]{1,0:T(8,128)(2,1)}, bf16[544,256]{1,0:T(8,128)(2,1)S(1)}, u32[]{:S(2)}, u32[]{:S(2)}) %collective-permute-start.1) | collective-permute-done | bytes 278560 | tf_op jit(solution)/shard_map/ppermute | solution.py:306
  18.8 3.2 %collective-permute-done.3.refs_5_.refs_8_ = bf16[544,256]{1,0:T(8,128)(2,1)S(1)} collective-permute-done((bf16[544,256]{1,0:T(8,128)(2,1)}, bf16[544,256]{1,0:T(8,128)(2,1)S(1)}, u32[]{:S(2)}, u32[]{:S(2)}) %collective-permute-start.3) | collective-permute-done | bytes 278560 | tf_op jit(solution)/shard_map/ppermute | solution.py:306
  21.9 0.0 collective-permute-start.6
  21.9 8.2 %collective-permute-done.2.refs_4_.refs_7_ = bf16[544,256]{1,0:T(8,128)(2,1)S(1)} collective-permute-done((bf16[544,256]{1,0:T(8,128)(2,1)}, bf16[544,256]{1,0:T(8,128)(2,1)S(1)}, u32[]{:S(2)}, u32[]{:S(2)}) %collective-permute-start.2) | collective-permute-done | bytes 278560 | tf_op jit(solution)/shard_map/ppermute | solution.py:306
  30.2 0.3 collective-permute-done.4.refs_6_.refs_9_
  30.5 2.5 %collective-permute-start.7 = (bf16[544,256]{1,0:T(8,128)(2,1)S(1)}, bf16[544,256]{1,0:T(8,128)(2,1)S(1)}, u32[]{:S(2)}, u32[]{:S(2)}) collective-permute-start(bf16[544,256]{1,0:T(8,128)(2,1)S(1)} %collective-permute-done.4.refs_6_.refs_9_), channel_id=1, source_target_pairs={{0,2},{1,3},{2,0},{3,1},{4,6},{5,7},{6,4},{7,5},{8,10},{9,11},{10,... | collective-permute-start | bytes 835592 | tf_op jit(solution)/shard_map/ppermute | solution.py:306
  33.0 0.0 collective-permute-done.refs_2_
  33.0 0.4 collective-permute-start.5
  33.4 0.1 slice.8.refs_0_
  33.5 1.3 %collective-permute-done.5.refs_4_.refs_5_ = bf16[544,256]{1,0:T(8,128)(2,1)S(1)} collective-permute-done((bf16[544,256]{1,0:T(8,128)(2,1)}, bf16[544,256]{1,0:T(8,128)(2,1)S(1)}, u32[]{:S(2)}, u32[]{:S(2)}) %collective-permute-start.5) | collective-permute-done | bytes 278560 | tf_op jit(solution)/shard_map/ppermute | solution.py:306
  34.8 0.0 copy-start
  34.8 2.2 %copy-done = bf16[512,4096]{1,0:T(8,128)(2,1)S(1)} copy-done((bf16[512,4096]{1,0:T(8,128)(2,1)S(1)}, bf16[512,4096]{1,0:T(8,128)(2,1)}, u32[]{:S(2)}) %copy-start) | copy-done | bytes 4194328
  37.0 0.0 copy-start.1
  37.0 1.0 %copy-done.1 = bf16[544,256]{1,0:T(8,128)(2,1)S(1)} copy-done((bf16[544,256]{1,0:T(8,128)(2,1)S(1)}, bf16[544,256]{1,0:T(8,128)(2,1)}, u32[]{:S(2)}) %copy-start.1) | copy-done | bytes 278552
  38.0 3.1 %shard_map.74 = (f32[1024,256]{1,0:T(8,128)S(1)}, bf16[2,16,512]{2,1,0:T(8,128)(2,1)}) custom-call(s32[2]{0:T(128)S(1)} %bitcast.21, bf16[512,4096]{1,0:T(8,128)(2,1)S(1)} %copy-done, bf16[512,4096]{1,0:T(8,128)(2,1)} %collective-permute-done.refs_2_, bf16[544,256]{1,0:T(8,128)(2,1)S(1)} %copy-done.1, bf16[544,256]{1,0:T(8,128)(2,1)S(1)} %collective-permute-done.5.refs_4_.refs_5_), custom_call_target="tpu_custom_call" | custom-call | flops 536870912 | bytes 2097152 | tf_op jit(solution)/shard_map/pallas_call | solution.py:81
  41.0 0.0 copy-start.3
  41.0 0.0 copy-start.2
  41.1 4.1 %shard_map.75 = (f32[1024,256]{1,0:T(8,128)S(1)}, bf16[4,512,512]{2,1,0:T(8,128)(2,1)S(1)}) custom-call(s32[6]{0:T(128)S(1)} %slice.8.refs_0_, bf16[512,4096]{1,0:T(8,128)(2,1)S(1)} %copy-done, bf16[512,4096]{1,0:T(8,128)(2,1)} %collective-permute-done.refs_2_, bf16[544,256]{1,0:T(8,128)(2,1)S(1)} %collective-permute-done.1.refs_3_.refs_6_, ...), custom_call_target="tpu_custom_call" | custom-call | flops 1073741824 | bytes 4194304 | tf_op jit(solution)/shard_map/pallas_call | solution.py:81
  45.2 0.0 copy-start.4
  45.2 0.0 collective-permute-done.6.refs_10_
  45.2 0.0 collective-permute-done.7.refs_11_
  45.2 0.0 copy-done.3
  45.2 1.0 %collective-permute-start.12 = (bf16[256,512]{1,0:T(8,128)(2,1)S(1)}, bf16[256,512]{1,0:T(8,128)(2,1)S(1)}, u32[]{:S(2)}, u32[]{:S(2)}) collective-permute-start(bf16[256,512]{1,0:T(8,128)(2,1)S(1)} %copy-done.3), channel_id=1, source_target_pairs={{0,2},{1,3},{2,0},{3,1},{4,6},{5,7},{6,4},{7,5},{8,10},{9,11},{10,... | collective-permute-start | bytes 786440 | tf_op jit(solution)/shard_map/ppermute | solution.py:306
  46.2 1.7 %collective-permute-start.13 = (bf16[256,512]{1,0:T(8,128)(2,1)S(1)}, bf16[256,512]{1,0:T(8,128)(2,1)S(1)}, u32[]{:S(2)}, u32[]{:S(2)}) collective-permute-start(bf16[256,512]{1,0:T(8,128)(2,1)S(1)} %copy-done.3), channel_id=1, source_target_pairs={{0,4},{1,5},{2,6},{3,7},{4,0},{5,1},{6,2},{7,3},{8,12},{9,13},{10,... | collective-permute-start | bytes 786440 | tf_op jit(solution)/shard_map/ppermute | solution.py:306
  47.9 0.1 pad_add_fusion.2.refs_0_
  48.0 0.0 copy-done.2
  48.0 2.8 %shard_map.76 = (bf16[144,128]{1,0:T(8,128)(2,1)S(1)}, bf16[144,128]{1,0:T(8,128)(2,1)S(1)}, bf16[144,128]{1,0:T(8,128)(2,1)S(1)}, bf16[144,128]{1,0:T(8,128)(2,1)S(1)}) custom-call(s32[2]{0:T(128)S(1)} %pad_add_fusion.2.refs_0_, s32[4]{0:T(128)S(1)} %iota_xor_fusion.refs_1_, s32[8]{0:T(128)S(1)} %stack.71.refs_2_, ...), custom_call_target="tpu_custom_call" | custom-call | flops 536870912 | bytes 2097152 | tf_op jit(solution)/shard_map/pallas_call | solution.py:158
  50.8 1.9 %collective-permute-start.10 = (bf16[144,128]{1,0:T(8,128)(2,1)S(1)}, bf16[144,128]{1,0:T(8,128)(2,1)S(1)}, u32[]{:S(2)}, u32[]{:S(2)}) collective-permute-start(bf16[144,128]{1,0:T(8,128)(2,1)S(1)} %get-tuple-element.38), channel_id=1, source_target_pairs={{0,6},{1,7},{2,4},{3,5},{4,2},{5,3},{6,0},{7,1},{8,14},{9,15},{10,... | collective-permute-start | bytes 110600 | tf_op jit(solution)/shard_map/ppermute | solution.py:306
  52.7 0.0 collective-permute-start.8
  52.7 2.5 %collective-permute-start.9 = (bf16[144,128]{1,0:T(8,128)(2,1)S(1)}, bf16[144,128]{1,0:T(8,128)(2,1)S(1)}, u32[]{:S(2)}, u32[]{:S(2)}) collective-permute-start(bf16[144,128]{1,0:T(8,128)(2,1)S(1)} %get-tuple-element.37), channel_id=1, source_target_pairs={{0,4},{1,5},{2,6},{3,7},{4,0},{5,1},{6,2},{7,3},{8,12},{9,13},{10,... | collective-permute-start | bytes 110600 | tf_op jit(solution)/shard_map/ppermute | solution.py:306
  55.3 7.4 %collective-permute-done.10.refs_3_ = bf16[144,128]{1,0:T(8,128)(2,1)S(1)} collective-permute-done((bf16[144,128]{1,0:T(8,128)(2,1)S(1)}, bf16[144,128]{1,0:T(8,128)(2,1)S(1)}, u32[]{:S(2)}, u32[]{:S(2)}) %collective-permute-start.10) | collective-permute-done | bytes 36896 | tf_op jit(solution)/shard_map/ppermute | solution.py:306
  62.7 0.0 collective-permute-done.8.refs_1_
  62.7 1.6 %collective-permute-done.9.refs_2_ = bf16[144,128]{1,0:T(8,128)(2,1)S(1)} collective-permute-done((bf16[144,128]{1,0:T(8,128)(2,1)S(1)}, bf16[144,128]{1,0:T(8,128)(2,1)S(1)}, u32[]{:S(2)}, u32[]{:S(2)}) %collective-permute-start.9) | collective-permute-done | bytes 36896 | tf_op jit(solution)/shard_map/ppermute | solution.py:306
  64.3 0.0 collective-permute-done.12.refs_1_
  64.3 0.0 collective-permute-done.13.refs_2_
  64.3 0.3 collective-permute-start.14
  64.5 0.0 copy-done.4
  64.5 0.2 shard_map.77.own_ref
  64.7 0.1 collective-permute-start.11
  64.8 0.1 pad_add_fusion.1.place_ref
  64.8 1.1 %collective-permute-done.11.sibling_ref = bf16[128,128]{1,0:T(8,128)(2,1)S(1)} collective-permute-done((bf16[128,128]{1,0:T(8,128)(2,1)S(1)}, bf16[128,128]{1,0:T(8,128)(2,1)S(1)}, u32[]{:S(2)}, u32[]{:S(2)}) %collective-permute-start.11) | collective-permute-done | bytes 32800 | tf_op jit(solution)/shard_map/ppermute | solution.py:306
  66.0 5.3 %collective-permute-done.14.refs_3_ = bf16[256,512]{1,0:T(8,128)(2,1)S(1)} collective-permute-done((bf16[256,512]{1,0:T(8,128)(2,1)S(1)}, bf16[256,512]{1,0:T(8,128)(2,1)S(1)}, u32[]{:S(2)}, u32[]{:S(2)}) %collective-permute-start.14) | collective-permute-done | bytes 262176 | tf_op jit(solution)/shard_map/ppermute | solution.py:306
  71.2 1.0 %shard_map.78 = (bf16[128,512]{1,0:T(8,128)(2,1)S(1)}, bf16[128,512]{1,0:T(8,128)(2,1)S(1)}, bf16[128,512]{1,0:T(8,128)(2,1)S(1)}, bf16[128,512]{1,0:T(8,128)(2,1)S(1)}) custom-call(s32[2]{0:T(128)S(1)} %pad_add_fusion.1.place_ref, bf16[128,128]{1,0:T(8,128)(2,1)S(1)} %shard_map.77.own_ref, bf16[128,128]{1,0:T(8,128)(2,1)S(1)} %collective-permute-done.11.sibling_ref, ...), custom_call_target="tpu_custom_call" | custom-call | tf_op jit(solution)/shard_map/pallas_call | solution.py:262
  72.2 1.6 %collective-permute-start.15 = (bf16[128,512]{1,0:T(8,128)(2,1)S(1)}, bf16[128,512]{1,0:T(8,128)(2,1)S(1)}, u32[]{:S(2)}, u32[]{:S(2)}) collective-permute-start(bf16[128,512]{1,0:T(8,128)(2,1)S(1)} %get-tuple-element.42), channel_id=1, source_target_pairs={{0,8},{8,0},{16,24},{24,16},{1,9},{9,1},{17,25},{25,17},{2,10},{10... | collective-permute-start | bytes 393224 | tf_op jit(solution)/shard_map/ppermute | solution.py:309
  73.8 1.5 %collective-permute-start.16 = (bf16[128,512]{1,0:T(8,128)(2,1)S(1)}, bf16[128,512]{1,0:T(8,128)(2,1)S(1)}, u32[]{:S(2)}, u32[]{:S(2)}) collective-permute-start(bf16[128,512]{1,0:T(8,128)(2,1)S(1)} %get-tuple-element.43), channel_id=1, source_target_pairs={{0,16},{8,24},{16,0},{24,8},{1,17},{9,25},{17,1},{25,9},{2,18},{10... | collective-permute-start | bytes 393224 | tf_op jit(solution)/shard_map/ppermute | solution.py:309
  75.3 0.5 collective-permute-start.17
  75.8 2.1 %collective-permute-done.15.refs_1_ = bf16[128,512]{1,0:T(8,128)(2,1)S(1)} collective-permute-done((bf16[128,512]{1,0:T(8,128)(2,1)S(1)}, bf16[128,512]{1,0:T(8,128)(2,1)S(1)}, u32[]{:S(2)}, u32[]{:S(2)}) %collective-permute-start.15) | collective-permute-done | bytes 131104 | tf_op jit(solution)/shard_map/ppermute | solution.py:309
  77.9 1.2 %collective-permute-done.16.refs_2_ = bf16[128,512]{1,0:T(8,128)(2,1)S(1)} collective-permute-done((bf16[128,512]{1,0:T(8,128)(2,1)S(1)}, bf16[128,512]{1,0:T(8,128)(2,1)S(1)}, u32[]{:S(2)}, u32[]{:S(2)}) %collective-permute-start.16) | collective-permute-done | bytes 131104 | tf_op jit(solution)/shard_map/ppermute | solution.py:309
  79.1 2.0 %collective-permute-done.17.refs_3_ = bf16[128,512]{1,0:T(8,128)(2,1)S(1)} collective-permute-done((bf16[128,512]{1,0:T(8,128)(2,1)S(1)}, bf16[128,512]{1,0:T(8,128)(2,1)S(1)}, u32[]{:S(2)}, u32[]{:S(2)}) %collective-permute-start.17) | collective-permute-done | bytes 131104 | tf_op jit(solution)/shard_map/ppermute | solution.py:309
  81.2 0.1 shard_map.79
  81.2 0.1 collective-permute-start.18
  81.3 1.2 %collective-permute-done.18 = bf16[64,512]{1,0:T(8,128)(2,1)S(1)} collective-permute-done((bf16[64,512]{1,0:T(8,128)(2,1)S(1)}, bf16[64,512]{1,0:T(8,128)(2,1)S(1)}, u32[]{:S(2)}, u32[]{:S(2)}) %collective-permute-start.18) | collective-permute-done | bytes 65568 | tf_op jit(solution)/shard_map/ppermute | solution.py:306
  82.6 0.7 maximum_select_fusion
  (4 shorter events, 0.0 us)
Async XLA Ops:
  2.0 31.0 %collective-permute-start = (bf16[512,4096]{1,0:T(8,128)(2,1)}, bf16[512,4096]{1,0:T(8,128)(2,1)}, u32[]{:S(2)}, u32[]{:S(2)}) collective-permute-start(bf16[512,4096]{1,0:T(8,128)(2,1)} %refs_1_.3), channel_id=1, source_target_pairs={{0,1},{1,0},{2,3},{3,2},{4,5},{5,4},{6,7},{7,6},{8,9},{9,8},{10,11... | collective-permute-start | bytes 12582920 | tf_op jit(solution)/shard_map/ppermute | solution.py:306
  2.5 16.2 %collective-permute-start.1 = (bf16[544,256]{1,0:T(8,128)(2,1)}, bf16[544,256]{1,0:T(8,128)(2,1)S(1)}, u32[]{:S(2)}, u32[]{:S(2)}) collective-permute-start(bf16[544,256]{1,0:T(8,128)(2,1)} %get-tuple-element.26.refs_3_.refs_4_), channel_id=1, source_target_pairs={{0,2},{1,3},{2,0},{3,1},{4,6},{5,7},{6,4},{7,5},{8,10},{9,11},{10,... | collective-permute-start | bytes 835592 | tf_op jit(solution)/shard_map/ppermute | solution.py:306
  5.2 16.7 %collective-permute-start.3 = (bf16[544,256]{1,0:T(8,128)(2,1)}, bf16[544,256]{1,0:T(8,128)(2,1)S(1)}, u32[]{:S(2)}, u32[]{:S(2)}) collective-permute-start(bf16[544,256]{1,0:T(8,128)(2,1)} %get-tuple-element.26.refs_3_.refs_4_), channel_id=1, source_target_pairs={{0,4},{1,5},{2,6},{3,7},{4,0},{5,1},{6,2},{7,3},{8,12},{9,13},{10,... | collective-permute-start | bytes 835592 | tf_op jit(solution)/shard_map/ppermute | solution.py:306
  7.8 22.4 %collective-permute-start.2 = (bf16[544,256]{1,0:T(8,128)(2,1)}, bf16[544,256]{1,0:T(8,128)(2,1)S(1)}, u32[]{:S(2)}, u32[]{:S(2)}) collective-permute-start(bf16[544,256]{1,0:T(8,128)(2,1)} %get-tuple-element.29), channel_id=1, source_target_pairs={{0,3},{1,2},{2,1},{3,0},{4,7},{5,6},{6,5},{7,4},{8,11},{9,10},{10,... | collective-permute-start | bytes 835592 | tf_op jit(solution)/shard_map/ppermute | solution.py:306
  7.8 22.7 %collective-permute-start.4 = (bf16[544,256]{1,0:T(8,128)(2,1)}, bf16[544,256]{1,0:T(8,128)(2,1)S(1)}, u32[]{:S(2)}, u32[]{:S(2)}) collective-permute-start(bf16[544,256]{1,0:T(8,128)(2,1)} %get-tuple-element.29), channel_id=1, source_target_pairs={{0,5},{1,4},{2,7},{3,6},{4,1},{5,0},{6,3},{7,2},{8,13},{9,12},{10,... | collective-permute-start | bytes 835592 | tf_op jit(solution)/shard_map/ppermute | solution.py:306
  21.9 23.3 %collective-permute-start.6 = (bf16[544,256]{1,0:T(8,128)(2,1)S(1)}, bf16[544,256]{1,0:T(8,128)(2,1)S(1)}, u32[]{:S(2)}, u32[]{:S(2)}) collective-permute-start(bf16[544,256]{1,0:T(8,128)(2,1)S(1)} %collective-permute-done.3.refs_5_.refs_8_), channel_id=1, source_target_pairs={{0,2},{1,3},{2,0},{3,1},{4,6},{5,7},{6,4},{7,5},{8,10},{9,11},{10,... | collective-permute-start | bytes 835592 | tf_op jit(solution)/shard_map/ppermute | solution.py:306
  30.5 14.7 %collective-permute-start.7 = (bf16[544,256]{1,0:T(8,128)(2,1)S(1)}, bf16[544,256]{1,0:T(8,128)(2,1)S(1)}, u32[]{:S(2)}, u32[]{:S(2)}) collective-permute-start(bf16[544,256]{1,0:T(8,128)(2,1)S(1)} %collective-permute-done.4.refs_6_.refs_9_), channel_id=1, source_target_pairs={{0,2},{1,3},{2,0},{3,1},{4,6},{5,7},{6,4},{7,5},{8,10},{9,11},{10,... | collective-permute-start | bytes 835592 | tf_op jit(solution)/shard_map/ppermute | solution.py:306
  33.0 1.8 %collective-permute-start.5 = (bf16[544,256]{1,0:T(8,128)(2,1)}, bf16[544,256]{1,0:T(8,128)(2,1)S(1)}, u32[]{:S(2)}, u32[]{:S(2)}) collective-permute-start(bf16[544,256]{1,0:T(8,128)(2,1)} %get-tuple-element.29), channel_id=1, source_target_pairs={{0,1},{1,0},{2,3},{3,2},{4,5},{5,4},{6,7},{7,6},{8,9},{9,8},{10,11... | collective-permute-start | bytes 835592 | tf_op jit(solution)/shard_map/ppermute | solution.py:306
  34.8 2.2 %copy-start = (bf16[512,4096]{1,0:T(8,128)(2,1)S(1)}, bf16[512,4096]{1,0:T(8,128)(2,1)}, u32[]{:S(2)}) copy-start(bf16[512,4096]{1,0:T(8,128)(2,1)} %refs_1_.3) | copy-start | bytes 12582916
  37.0 1.0 %copy-start.1 = (bf16[544,256]{1,0:T(8,128)(2,1)S(1)}, bf16[544,256]{1,0:T(8,128)(2,1)}, u32[]{:S(2)}) copy-start(bf16[544,256]{1,0:T(8,128)(2,1)} %get-tuple-element.26.refs_3_.refs_4_) | copy-start | bytes 835588
  41.0 4.2 %copy-start.3 = (bf16[256,512]{1,0:T(8,128)(2,1)S(1)}, bf16[256,512]{1,0:T(8,128)(2,1)}, u32[]{:S(2)}) copy-start(bf16[256,512]{1,0:T(8,128)(2,1)} %refs_0_) | copy-start | bytes 786436
  41.0 6.9 %copy-start.2 = (bf16[544,256]{1,0:T(8,128)(2,1)S(1)}, bf16[544,256]{1,0:T(8,128)(2,1)}, u32[]{:S(2)}) copy-start(bf16[544,256]{1,0:T(8,128)(2,1)} %get-tuple-element.26.refs_3_.refs_4_) | copy-start | bytes 835588
  45.2 19.3 %copy-start.4 = (bf16[256]{0:T(256)(128)(2,1)S(1)}, bf16[256]{0:T(256)(128)(2,1)}, u32[]{:S(2)}) copy-start(bf16[256]{0:T(256)(128)(2,1)} %param.12) | copy-start | bytes 1540
  45.2 19.0 %collective-permute-start.12 = (bf16[256,512]{1,0:T(8,128)(2,1)S(1)}, bf16[256,512]{1,0:T(8,128)(2,1)S(1)}, u32[]{:S(2)}, u32[]{:S(2)}) collective-permute-start(bf16[256,512]{1,0:T(8,128)(2,1)S(1)} %copy-done.3), channel_id=1, source_target_pairs={{0,2},{1,3},{2,0},{3,1},{4,6},{5,7},{6,4},{7,5},{8,10},{9,11},{10,... | collective-permute-start | bytes 786440 | tf_op jit(solution)/shard_map/ppermute | solution.py:306
  46.2 18.0 %collective-permute-start.13 = (bf16[256,512]{1,0:T(8,128)(2,1)S(1)}, bf16[256,512]{1,0:T(8,128)(2,1)S(1)}, u32[]{:S(2)}, u32[]{:S(2)}) collective-permute-start(bf16[256,512]{1,0:T(8,128)(2,1)S(1)} %copy-done.3), channel_id=1, source_target_pairs={{0,4},{1,5},{2,6},{3,7},{4,0},{5,1},{6,2},{7,3},{8,12},{9,13},{10,... | collective-permute-start | bytes 786440 | tf_op jit(solution)/shard_map/ppermute | solution.py:306
  50.8 11.8 %collective-permute-start.10 = (bf16[144,128]{1,0:T(8,128)(2,1)S(1)}, bf16[144,128]{1,0:T(8,128)(2,1)S(1)}, u32[]{:S(2)}, u32[]{:S(2)}) collective-permute-start(bf16[144,128]{1,0:T(8,128)(2,1)S(1)} %get-tuple-element.38), channel_id=1, source_target_pairs={{0,6},{1,7},{2,4},{3,5},{4,2},{5,3},{6,0},{7,1},{8,14},{9,15},{10,... | collective-permute-start | bytes 110600 | tf_op jit(solution)/shard_map/ppermute | solution.py:306
  52.7 10.0 %collective-permute-start.8 = (bf16[144,128]{1,0:T(8,128)(2,1)S(1)}, bf16[144,128]{1,0:T(8,128)(2,1)S(1)}, u32[]{:S(2)}, u32[]{:S(2)}) collective-permute-start(bf16[144,128]{1,0:T(8,128)(2,1)S(1)} %get-tuple-element.36), channel_id=1, source_target_pairs={{0,2},{1,3},{2,0},{3,1},{4,6},{5,7},{6,4},{7,5},{8,10},{9,11},{10,... | collective-permute-start | bytes 110600 | tf_op jit(solution)/shard_map/ppermute | solution.py:306
  52.7 11.5 %collective-permute-start.9 = (bf16[144,128]{1,0:T(8,128)(2,1)S(1)}, bf16[144,128]{1,0:T(8,128)(2,1)S(1)}, u32[]{:S(2)}, u32[]{:S(2)}) collective-permute-start(bf16[144,128]{1,0:T(8,128)(2,1)S(1)} %get-tuple-element.37), channel_id=1, source_target_pairs={{0,4},{1,5},{2,6},{3,7},{4,0},{5,1},{6,2},{7,3},{8,12},{9,13},{10,... | collective-permute-start | bytes 110600 | tf_op jit(solution)/shard_map/ppermute | solution.py:306
  64.3 7.0 %collective-permute-start.14 = (bf16[256,512]{1,0:T(8,128)(2,1)S(1)}, bf16[256,512]{1,0:T(8,128)(2,1)S(1)}, u32[]{:S(2)}, u32[]{:S(2)}) collective-permute-start(bf16[256,512]{1,0:T(8,128)(2,1)S(1)} %collective-permute-done.13.refs_2_), channel_id=1, source_target_pairs={{0,2},{1,3},{2,0},{3,1},{4,6},{5,7},{6,4},{7,5},{8,10},{9,11},{10,... | collective-permute-start | bytes 786440 | tf_op jit(solution)/shard_map/ppermute | solution.py:306
  64.7 1.3 %collective-permute-start.11 = (bf16[128,128]{1,0:T(8,128)(2,1)S(1)}, bf16[128,128]{1,0:T(8,128)(2,1)S(1)}, u32[]{:S(2)}, u32[]{:S(2)}) collective-permute-start(bf16[128,128]{1,0:T(8,128)(2,1)S(1)} %shard_map.77.own_ref), channel_id=1, source_target_pairs={{0,1},{1,0},{2,3},{3,2},{4,5},{5,4},{6,7},{7,6},{8,9},{9,8},{10,11... | collective-permute-start | bytes 98312 | tf_op jit(solution)/shard_map/ppermute | solution.py:306
  72.2 5.7 %collective-permute-start.15 = (bf16[128,512]{1,0:T(8,128)(2,1)S(1)}, bf16[128,512]{1,0:T(8,128)(2,1)S(1)}, u32[]{:S(2)}, u32[]{:S(2)}) collective-permute-start(bf16[128,512]{1,0:T(8,128)(2,1)S(1)} %get-tuple-element.42), channel_id=1, source_target_pairs={{0,8},{8,0},{16,24},{24,16},{1,9},{9,1},{17,25},{25,17},{2,10},{10... | collective-permute-start | bytes 393224 | tf_op jit(solution)/shard_map/ppermute | solution.py:309
  73.8 5.4 %collective-permute-start.16 = (bf16[128,512]{1,0:T(8,128)(2,1)S(1)}, bf16[128,512]{1,0:T(8,128)(2,1)S(1)}, u32[]{:S(2)}, u32[]{:S(2)}) collective-permute-start(bf16[128,512]{1,0:T(8,128)(2,1)S(1)} %get-tuple-element.43), channel_id=1, source_target_pairs={{0,16},{8,24},{16,0},{24,8},{1,17},{9,25},{17,1},{25,9},{2,18},{10... | collective-permute-start | bytes 393224 | tf_op jit(solution)/shard_map/ppermute | solution.py:309
  75.3 5.9 %collective-permute-start.17 = (bf16[128,512]{1,0:T(8,128)(2,1)S(1)}, bf16[128,512]{1,0:T(8,128)(2,1)S(1)}, u32[]{:S(2)}, u32[]{:S(2)}) collective-permute-start(bf16[128,512]{1,0:T(8,128)(2,1)S(1)} %get-tuple-element.44), channel_id=1, source_target_pairs={{0,24},{8,16},{16,8},{24,0},{1,25},{9,17},{17,9},{25,1},{2,26},{10... | collective-permute-start | bytes 393224 | tf_op jit(solution)/shard_map/ppermute | solution.py:309
  81.2 1.3 %collective-permute-start.18 = (bf16[64,512]{1,0:T(8,128)(2,1)S(1)}, bf16[64,512]{1,0:T(8,128)(2,1)S(1)}, u32[]{:S(2)}, u32[]{:S(2)}) collective-permute-start(bf16[64,512]{1,0:T(8,128)(2,1)S(1)} %get-tuple-element.46), channel_id=1, source_target_pairs={{0,1},{1,0},{2,3},{3,2},{4,5},{5,4},{6,7},{7,6},{8,9},{9,8},{10,11... | collective-permute-start | bytes 196616 | tf_op jit(solution)/shard_map/ppermute | solution.py:306

commit v10 on v9

--- a/solution.py
+++ b/solution.py
@@ -315,13 +315,8 @@
     own_part, other_part = pack(core_only, w_key, w_value, queries)
     pairs = [None] * chips
     for j in near_first:
-        low = j & -j
-        if j == low:
+        if j & (j - 1) == 0:
             pairs[j] = (across(own_part, CORES * j), across(other_part, CORES * j + 1))
-        else:
-            pairs[j] = tuple(
-                across(after(part, near), CORES * low) for part, near in zip(pairs[j ^ low], pairs[1])
-            )
     context_sibling = across(after(context, own_part), 1)
     pairs[0] = (own_part, across(after(other_part, context_sibling), 1))
 
@@ -329,9 +324,17 @@
         [(chip ^ j) * CORES + who for j in range(chips) for who in (core, 1 - core)]
     ).astype(jnp.int32)
     starts = places * depth
+    first_acc, _ = project(starts[:CORES], context, context_sibling, pairs[0], None, depth)
+    for j in near_first:
+        low = j & -j
+        if j != low:
+            held, near = pairs[j ^ low], pairs[1]
+            pairs[j] = (
+                across(after(held[0], near[0]), CORES * low),
+                across(after(held[1], near[1], first_acc), CORES * low),
+            )
     blocks = [part for pair in pairs for part in pair]
     last = CORES * (chips - 1)
-    first_acc, _ = project(starts[:CORES], context, context_sibling, blocks[:CORES], None, depth)
     acc, slices = project(
         starts[CORES:], context, context_sibling, blocks[CORES:last], first_acc, depth
     )
@@ -342,7 +345,7 @@
         firsts, slot_groups, places, slices, blocks, acc, offsets, groups, heads, depth
     )
     arrived = [messages[0]] + [across(messages[j], CORES * j) for j in range(1, chips)]
-    shards = [after(w_out, acc, *pairs[-1])] + [None] * (chips - 1)
+    shards = [after(w_out, acc)] + [None] * (chips - 1)
     for j in near_first:
         low = j & -j
         shard = shards[j ^ low]

time: 83.5 us -> 79.2 us (0.949)
  waiting for transfers between devices: 44.9 us -> 38.4 us
  starting transfers between devices: 19.9 us -> 22.1 us
    ppermute x16, waiting for transfers between devices: 39.5 us -> 33 us  [across(): return lax.ppermute(array, 'ctx', [(i, i ^ bits) for i in range(n_ctx)])]
    ppermute x16, starting transfers between devices: 16.4 us -> 18.6 us  [across(): return lax.ppermute(array, 'ctx', [(i, i ^ bits) for i in range(n_ctx)])]
  transfers between devices with their start and end apart: 19 -> 19, of which waited for: 13 -> 15; matrix products, arithmetic and copies ran while one was open for 1% -> 1% of each run, Pallas kernels for 12% -> 13%
where the time goes in v10:
time: 79.2 us; the launch traced here: 78.9 us
  waiting for transfers between devices  38.4 us (48%)
  starting transfers between devices  22.1 us (28%)
  Pallas kernels  13.3 us (17%)
  local copies, waits for them, and re-layouts  4.15 us (5%)
  other arithmetic  0.86 us (1%)
    ppermute x16, waiting for transfers between devices, across(): return lax.ppermute(array, 'ctx', [(i, i ^ bits) for i in range(n_ctx)])  33 us
    ppermute x16, starting transfers between devices, across(): return lax.ppermute(array, 'ctx', [(i, i ^ bits) for i in range(n_ctx)])  18.6 us
    pallas_call x2, Pallas kernels, project(): pl.pallas_call(functools.partial(project_kernel, count, extra, acc is not...  7.19 us
    ppermute x3, waiting for transfers between devices, over_dp(): return lax.ppermute(array, 'dp', [(d, d ^ bits) for d in range(n_dp)])  5.38 us
    ppermute x3, starting transfers between devices, over_dp(): return lax.ppermute(array, 'dp', [(d, d ^ bits) for d in range(n_dp)])  3.55 us
    unnamed x10, local copies, waits for them, and re-layouts  3.16 us
    pallas_call x1, Pallas kernels, attend(): pl.pallas_call(functools.partial(attend_kernel, count, heads, depth, grou...  2.81 us
    pallas_call x1, Pallas kernels, pack(): pl.pallas_call(pack_kernel, out_shape=[out, out], in_specs=[SMEM, ANY, AN...  2.02 us
  transfers between devices with their start and end apart: 19, of which 15 were waited for; matrix products, arithmetic and copies ran while one was open for 1% of the time, Pallas kernels for 13%

profile of v10, /device:TPU:0, one launch (start us, length us, event | category | flops | bytes accessed | tf_op | source)
XLA Modules:
  0.0 78.9 jit_solution(18348807941157048571)
XLA Ops:
  0.0 2.0 %shard_map.73 = (bf16[544,256]{1,0:T(8,128)(2,1)}, bf16[544,256]{1,0:T(8,128)(2,1)}) custom-call(s32[1]{0:T(128)} %bitcast.core_ref, bf16[512,256]{1,0:T(8,128)(2,1)} %key_ref.1, bf16[512,256]{1,0:T(8,128)(2,1)} %value_ref.1, bf16[64,256]{1,0:T(8,128)(2,1)} %query_ref.1), custom_call_target="tpu_custom_call" | custom-call | tf_op jit(solution)/shard_map/pallas_call | solution.py:235
  2.0 0.5 collective-permute-start
  2.5 2.7 %collective-permute-start.1 = (bf16[544,256]{1,0:T(8,128)(2,1)}, bf16[544,256]{1,0:T(8,128)(2,1)S(1)}, u32[]{:S(2)}, u32[]{:S(2)}) collective-permute-start(bf16[544,256]{1,0:T(8,128)(2,1)} %get-tuple-element.26.refs_3_.refs_4_), channel_id=1, source_target_pairs={{0,2},{1,3},{2,0},{3,1},{4,6},{5,7},{6,4},{7,5},{8,10},{9,11},{10,... | collective-permute-start | bytes 835592 | tf_op jit(solution)/shard_map/ppermute | solution.py:306
  5.2 2.6 %collective-permute-start.3 = (bf16[544,256]{1,0:T(8,128)(2,1)}, bf16[544,256]{1,0:T(8,128)(2,1)S(1)}, u32[]{:S(2)}, u32[]{:S(2)}) collective-permute-start(bf16[544,256]{1,0:T(8,128)(2,1)} %get-tuple-element.26.refs_3_.refs_4_), channel_id=1, source_target_pairs={{0,4},{1,5},{2,6},{3,7},{4,0},{5,1},{6,2},{7,3},{8,12},{9,13},{10,... | collective-permute-start | bytes 835592 | tf_op jit(solution)/shard_map/ppermute | solution.py:306
  7.8 0.0 collective-permute-start.2
  7.8 0.2 collective-permute-start.4
  8.0 0.1 stack.71.refs_2_
  8.1 1.6 %collective-permute-done.refs_2_ = bf16[512,4096]{1,0:T(8,128)(2,1)} collective-permute-done((bf16[512,4096]{1,0:T(8,128)(2,1)}, bf16[512,4096]{1,0:T(8,128)(2,1)}, u32[]{:S(2)}, u32[]{:S(2)}) %collective-permute-start) | collective-permute-done | bytes 4194336 | tf_op jit(solution)/shard_map/ppermute | solution.py:306
  9.7 0.4 collective-permute-start.5
  10.1 0.1 slice.8.refs_0_
  10.1 0.8 %slice_bitcast_fusion.3 = (s32[1,128]{1,0:T(1,128)S(1)}, s32[1,128]{1,0:T(1,128)S(1)}, s32[1,128]{1,0:T(1,128)S(1)}, s32[1,128]{1,0:T(1,128)S(1)}) fusion(s32[512]{0:T(512)} %param.11), kind=kLoop, calls=%fused_computation.7 | loop fusion | bytes 4096 | tf_op jit(solution)/shard_map/stack | solution.py:152
  11.0 7.8 %collective-permute-done.1.refs_3_.refs_6_ = bf16[544,256]{1,0:T(8,128)(2,1)S(1)} collective-permute-done((bf16[544,256]{1,0:T(8,128)(2,1)}, bf16[544,256]{1,0:T(8,128)(2,1)S(1)}, u32[]{:S(2)}, u32[]{:S(2)}) %collective-permute-start.1) | collective-permute-done | bytes 278560 | tf_op jit(solution)/shard_map/ppermute | solution.py:306
  18.8 3.2 %collective-permute-done.3.refs_5_.refs_8_ = bf16[544,256]{1,0:T(8,128)(2,1)S(1)} collective-permute-done((bf16[544,256]{1,0:T(8,128)(2,1)}, bf16[544,256]{1,0:T(8,128)(2,1)S(1)}, u32[]{:S(2)}, u32[]{:S(2)}) %collective-permute-start.3) | collective-permute-done | bytes 278560 | tf_op jit(solution)/shard_map/ppermute | solution.py:306
  21.9 0.0 collective-permute-start.6
  21.9 0.0 collective-permute-done.5.refs_4_.refs_5_
  21.9 0.0 copy-start
  21.9 2.2 %copy-done = bf16[512,4096]{1,0:T(8,128)(2,1)S(1)} copy-done((bf16[512,4096]{1,0:T(8,128)(2,1)S(1)}, bf16[512,4096]{1,0:T(8,128)(2,1)}, u32[]{:S(2)}) %copy-start) | copy-done | bytes 4194328
  24.1 0.0 copy-start.1
  24.1 1.0 %copy-done.1 = bf16[544,256]{1,0:T(8,128)(2,1)S(1)} copy-done((bf16[544,256]{1,0:T(8,128)(2,1)S(1)}, bf16[544,256]{1,0:T(8,128)(2,1)}, u32[]{:S(2)}) %copy-start.1) | copy-done | bytes 278552
  25.1 3.1 %shard_map.74 = (f32[1024,256]{1,0:T(8,128)S(1)}, bf16[2,16,512]{2,1,0:T(8,128)(2,1)}) custom-call(s32[2]{0:T(128)S(1)} %bitcast.21, bf16[512,4096]{1,0:T(8,128)(2,1)S(1)} %copy-done, bf16[512,4096]{1,0:T(8,128)(2,1)} %collective-permute-done.refs_2_, bf16[544,256]{1,0:T(8,128)(2,1)S(1)} %copy-done.1, bf16[544,256]{1,0:T(8,128)(2,1)S(1)} %collective-permute-done.5.refs_4_.refs_5_), custom_call_target="tpu_custom_call" | custom-call | flops 536870912 | bytes 2097152 | tf_op jit(solution)/shard_map/pallas_call | solution.py:81
  28.1 2.0 %collective-permute-done.2.refs_4_.refs_7_ = bf16[544,256]{1,0:T(8,128)(2,1)S(1)} collective-permute-done((bf16[544,256]{1,0:T(8,128)(2,1)}, bf16[544,256]{1,0:T(8,128)(2,1)S(1)}, u32[]{:S(2)}, u32[]{:S(2)}) %collective-permute-start.2) | collective-permute-done | bytes 278560 | tf_op jit(solution)/shard_map/ppermute | solution.py:306
  30.2 0.3 collective-permute-done.4.refs_6_.refs_9_
  30.5 0.0 copy-start.3
  30.5 0.0 copy-start.2
  30.5 2.5 %collective-permute-start.7 = (bf16[544,256]{1,0:T(8,128)(2,1)S(1)}, bf16[544,256]{1,0:T(8,128)(2,1)S(1)}, u32[]{:S(2)}, u32[]{:S(2)}) collective-permute-start(bf16[544,256]{1,0:T(8,128)(2,1)S(1)} %collective-permute-done.4.refs_6_.refs_9_), channel_id=1, source_target_pairs={{0,2},{1,3},{2,0},{3,1},{4,6},{5,7},{6,4},{7,5},{8,10},{9,11},{10,... | collective-permute-start | bytes 835592 | tf_op jit(solution)/shard_map/ppermute | solution.py:306
  33.0 4.1 %shard_map.75 = (f32[1024,256]{1,0:T(8,128)S(1)}, bf16[4,512,512]{2,1,0:T(8,128)(2,1)S(1)}) custom-call(s32[6]{0:T(128)S(1)} %slice.8.refs_0_, bf16[512,4096]{1,0:T(8,128)(2,1)S(1)} %copy-done, bf16[512,4096]{1,0:T(8,128)(2,1)} %collective-permute-done.refs_2_, bf16[544,256]{1,0:T(8,128)(2,1)S(1)} %collective-permute-done.1.refs_3_.refs_6_, ...), custom_call_target="tpu_custom_call" | custom-call | flops 1073741824 | bytes 4194304 | tf_op jit(solution)/shard_map/pallas_call | solution.py:81
  37.2 0.0 copy-start.4
  37.2 0.0 copy-done.3
  37.2 0.1 collective-permute-start.12
  37.3 2.4 %collective-permute-start.13 = (bf16[256,512]{1,0:T(8,128)(2,1)S(1)}, bf16[256,512]{1,0:T(8,128)(2,1)S(1)}, u32[]{:S(2)}, u32[]{:S(2)}) collective-permute-start(bf16[256,512]{1,0:T(8,128)(2,1)S(1)} %copy-done.3), channel_id=1, source_target_pairs={{0,4},{1,5},{2,6},{3,7},{4,0},{5,1},{6,2},{7,3},{8,12},{9,13},{10,... | collective-permute-start | bytes 786440 | tf_op jit(solution)/shard_map/ppermute | solution.py:306
  39.7 0.1 pad_add_fusion.2.refs_0_
  39.8 0.0 collective-permute-done.6.refs_10_
  39.8 8.6 %collective-permute-done.7.refs_11_ = bf16[544,256]{1,0:T(8,128)(2,1)S(1)} collective-permute-done((bf16[544,256]{1,0:T(8,128)(2,1)S(1)}, bf16[544,256]{1,0:T(8,128)(2,1)S(1)}, u32[]{:S(2)}, u32[]{:S(2)}) %collective-permute-start.7) | collective-permute-done | bytes 278560 | tf_op jit(solution)/shard_map/ppermute | solution.py:306
  48.4 0.0 copy-done.2
  48.4 2.8 %shard_map.76 = (bf16[144,128]{1,0:T(8,128)(2,1)S(1)}, bf16[144,128]{1,0:T(8,128)(2,1)S(1)}, bf16[144,128]{1,0:T(8,128)(2,1)S(1)}, bf16[144,128]{1,0:T(8,128)(2,1)S(1)}) custom-call(s32[2]{0:T(128)S(1)} %pad_add_fusion.2.refs_0_, s32[4]{0:T(128)S(1)} %iota_xor_fusion.refs_1_, s32[8]{0:T(128)S(1)} %stack.71.refs_2_, ...), custom_call_target="tpu_custom_call" | custom-call | flops 536870912 | bytes 2097152 | tf_op jit(solution)/shard_map/pallas_call | solution.py:158
  51.2 4.1 %collective-permute-start.10 = (bf16[144,128]{1,0:T(8,128)(2,1)S(1)}, bf16[144,128]{1,0:T(8,128)(2,1)S(1)}, u32[]{:S(2)}, u32[]{:S(2)}) collective-permute-start(bf16[144,128]{1,0:T(8,128)(2,1)S(1)} %get-tuple-element.38), channel_id=1, source_target_pairs={{0,6},{1,7},{2,4},{3,5},{4,2},{5,3},{6,0},{7,1},{8,14},{9,15},{10,... | collective-permute-start | bytes 110600 | tf_op jit(solution)/shard_map/ppermute | solution.py:306
  55.3 0.0 collective-permute-start.8
  55.3 0.6 collective-permute-start.9
  55.9 0.0 collective-permute-done.12.refs_1_
  55.9 0.0 collective-permute-done.13.refs_2_
  55.9 1.5 %collective-permute-done.10.refs_3_ = bf16[144,128]{1,0:T(8,128)(2,1)S(1)} collective-permute-done((bf16[144,128]{1,0:T(8,128)(2,1)S(1)}, bf16[144,128]{1,0:T(8,128)(2,1)S(1)}, u32[]{:S(2)}, u32[]{:S(2)}) %collective-permute-start.10) | collective-permute-done | bytes 36896 | tf_op jit(solution)/shard_map/ppermute | solution.py:306
  57.4 1.8 %collective-permute-done.8.refs_1_ = bf16[144,128]{1,0:T(8,128)(2,1)S(1)} collective-permute-done((bf16[144,128]{1,0:T(8,128)(2,1)S(1)}, bf16[144,128]{1,0:T(8,128)(2,1)S(1)}, u32[]{:S(2)}, u32[]{:S(2)}) %collective-permute-start.8) | collective-permute-done | bytes 36896 | tf_op jit(solution)/shard_map/ppermute | solution.py:306
  59.2 0.9 %collective-permute-done.9.refs_2_ = bf16[144,128]{1,0:T(8,128)(2,1)S(1)} collective-permute-done((bf16[144,128]{1,0:T(8,128)(2,1)S(1)}, bf16[144,128]{1,0:T(8,128)(2,1)S(1)}, u32[]{:S(2)}, u32[]{:S(2)}) %collective-permute-start.9) | collective-permute-done | bytes 36896 | tf_op jit(solution)/shard_map/ppermute | solution.py:306
  60.1 2.4 %collective-permute-start.14 = (bf16[256,512]{1,0:T(8,128)(2,1)S(1)}, bf16[256,512]{1,0:T(8,128)(2,1)S(1)}, u32[]{:S(2)}, u32[]{:S(2)}) collective-permute-start(bf16[256,512]{1,0:T(8,128)(2,1)S(1)} %collective-permute-done.13.refs_2_), channel_id=1, source_target_pairs={{0,2},{1,3},{2,0},{3,1},{4,6},{5,7},{6,4},{7,5},{8,10},{9,11},{10,... | collective-permute-start | bytes 786440 | tf_op jit(solution)/shard_map/ppermute | solution.py:306
  62.5 0.0 copy-done.4
  62.5 0.2 shard_map.77.own_ref
  62.7 0.1 collective-permute-start.11
  62.8 0.1 pad_add_fusion.1.place_ref
  62.9 1.1 %collective-permute-done.11.sibling_ref = bf16[128,128]{1,0:T(8,128)(2,1)S(1)} collective-permute-done((bf16[128,128]{1,0:T(8,128)(2,1)S(1)}, bf16[128,128]{1,0:T(8,128)(2,1)S(1)}, u32[]{:S(2)}, u32[]{:S(2)}) %collective-permute-start.11) | collective-permute-done | bytes 32800 | tf_op jit(solution)/shard_map/ppermute | solution.py:306
  64.0 2.9 %collective-permute-done.14.refs_3_ = bf16[256,512]{1,0:T(8,128)(2,1)S(1)} collective-permute-done((bf16[256,512]{1,0:T(8,128)(2,1)S(1)}, bf16[256,512]{1,0:T(8,128)(2,1)S(1)}, u32[]{:S(2)}, u32[]{:S(2)}) %collective-permute-start.14) | collective-permute-done | bytes 262176 | tf_op jit(solution)/shard_map/ppermute | solution.py:306
  66.9 1.0 %shard_map.78 = (bf16[128,512]{1,0:T(8,128)(2,1)S(1)}, bf16[128,512]{1,0:T(8,128)(2,1)S(1)}, bf16[128,512]{1,0:T(8,128)(2,1)S(1)}, bf16[128,512]{1,0:T(8,128)(2,1)S(1)}) custom-call(s32[2]{0:T(128)S(1)} %pad_add_fusion.1.place_ref, bf16[128,128]{1,0:T(8,128)(2,1)S(1)} %shard_map.77.own_ref, bf16[128,128]{1,0:T(8,128)(2,1)S(1)} %collective-permute-done.11.sibling_ref, ...), custom_call_target="tpu_custom_call" | custom-call | tf_op jit(solution)/shard_map/pallas_call | solution.py:262
  67.9 1.6 %collective-permute-start.15 = (bf16[128,512]{1,0:T(8,128)(2,1)S(1)}, bf16[128,512]{1,0:T(8,128)(2,1)S(1)}, u32[]{:S(2)}, u32[]{:S(2)}) collective-permute-start(bf16[128,512]{1,0:T(8,128)(2,1)S(1)} %get-tuple-element.42), channel_id=1, source_target_pairs={{0,8},{8,0},{16,24},{24,16},{1,9},{9,1},{17,25},{25,17},{2,10},{10... | collective-permute-start | bytes 393224 | tf_op jit(solution)/shard_map/ppermute | solution.py:309
  69.5 1.5 %collective-permute-start.16 = (bf16[128,512]{1,0:T(8,128)(2,1)S(1)}, bf16[128,512]{1,0:T(8,128)(2,1)S(1)}, u32[]{:S(2)}, u32[]{:S(2)}) collective-permute-start(bf16[128,512]{1,0:T(8,128)(2,1)S(1)} %get-tuple-element.43), channel_id=1, source_target_pairs={{0,16},{8,24},{16,0},{24,8},{1,17},{9,25},{17,1},{25,9},{2,18},{10... | collective-permute-start | bytes 393224 | tf_op jit(solution)/shard_map/ppermute | solution.py:309
  71.0 0.5 collective-permute-start.17
  71.5 1.6 %collective-permute-done.15.refs_1_ = bf16[128,512]{1,0:T(8,128)(2,1)S(1)} collective-permute-done((bf16[128,512]{1,0:T(8,128)(2,1)S(1)}, bf16[128,512]{1,0:T(8,128)(2,1)S(1)}, u32[]{:S(2)}, u32[]{:S(2)}) %collective-permute-start.15) | collective-permute-done | bytes 131104 | tf_op jit(solution)/shard_map/ppermute | solution.py:309
  73.1 1.3 %collective-permute-done.16.refs_2_ = bf16[128,512]{1,0:T(8,128)(2,1)S(1)} collective-permute-done((bf16[128,512]{1,0:T(8,128)(2,1)S(1)}, bf16[128,512]{1,0:T(8,128)(2,1)S(1)}, u32[]{:S(2)}, u32[]{:S(2)}) %collective-permute-start.16) | collective-permute-done | bytes 131104 | tf_op jit(solution)/shard_map/ppermute | solution.py:309
  74.4 2.4 %collective-permute-done.17.refs_3_ = bf16[128,512]{1,0:T(8,128)(2,1)S(1)} collective-permute-done((bf16[128,512]{1,0:T(8,128)(2,1)S(1)}, bf16[128,512]{1,0:T(8,128)(2,1)S(1)}, u32[]{:S(2)}, u32[]{:S(2)}) %collective-permute-start.17) | collective-permute-done | bytes 131104 | tf_op jit(solution)/shard_map/ppermute | solution.py:309
  76.8 0.1 shard_map.79
  76.9 0.1 collective-permute-start.18
  77.0 1.2 %collective-permute-done.18 = bf16[64,512]{1,0:T(8,128)(2,1)S(1)} collective-permute-done((bf16[64,512]{1,0:T(8,128)(2,1)S(1)}, bf16[64,512]{1,0:T(8,128)(2,1)S(1)}, u32[]{:S(2)}, u32[]{:S(2)}) %collective-permute-start.18) | collective-permute-done | bytes 65568 | tf_op jit(solution)/shard_map/ppermute | solution.py:306
  78.2 0.7 maximum_select_fusion
  (4 shorter events, 0.0 us)
Async XLA Ops:
  2.0 7.6 %collective-permute-start = (bf16[512,4096]{1,0:T(8,128)(2,1)}, bf16[512,4096]{1,0:T(8,128)(2,1)}, u32[]{:S(2)}, u32[]{:S(2)}) collective-permute-start(bf16[512,4096]{1,0:T(8,128)(2,1)} %refs_1_.3), channel_id=1, source_target_pairs={{0,1},{1,0},{2,3},{3,2},{4,5},{5,4},{6,7},{7,6},{8,9},{9,8},{10,11... | collective-permute-start | bytes 12582920 | tf_op jit(solution)/shard_map/ppermute | solution.py:306
  2.5 16.2 %collective-permute-start.1 = (bf16[544,256]{1,0:T(8,128)(2,1)}, bf16[544,256]{1,0:T(8,128)(2,1)S(1)}, u32[]{:S(2)}, u32[]{:S(2)}) collective-permute-start(bf16[544,256]{1,0:T(8,128)(2,1)} %get-tuple-element.26.refs_3_.refs_4_), channel_id=1, source_target_pairs={{0,2},{1,3},{2,0},{3,1},{4,6},{5,7},{6,4},{7,5},{8,10},{9,11},{10,... | collective-permute-start | bytes 835592 | tf_op jit(solution)/shard_map/ppermute | solution.py:306
  5.2 16.7 %collective-permute-start.3 = (bf16[544,256]{1,0:T(8,128)(2,1)}, bf16[544,256]{1,0:T(8,128)(2,1)S(1)}, u32[]{:S(2)}, u32[]{:S(2)}) collective-permute-start(bf16[544,256]{1,0:T(8,128)(2,1)} %get-tuple-element.26.refs_3_.refs_4_), channel_id=1, source_target_pairs={{0,4},{1,5},{2,6},{3,7},{4,0},{5,1},{6,2},{7,3},{8,12},{9,13},{10,... | collective-permute-start | bytes 835592 | tf_op jit(solution)/shard_map/ppermute | solution.py:306
  7.8 22.4 %collective-permute-start.2 = (bf16[544,256]{1,0:T(8,128)(2,1)}, bf16[544,256]{1,0:T(8,128)(2,1)S(1)}, u32[]{:S(2)}, u32[]{:S(2)}) collective-permute-start(bf16[544,256]{1,0:T(8,128)(2,1)} %get-tuple-element.29), channel_id=1, source_target_pairs={{0,3},{1,2},{2,1},{3,0},{4,7},{5,6},{6,5},{7,4},{8,11},{9,10},{10,... | collective-permute-start | bytes 835592 | tf_op jit(solution)/shard_map/ppermute | solution.py:306
  7.8 22.7 %collective-permute-start.4 = (bf16[544,256]{1,0:T(8,128)(2,1)}, bf16[544,256]{1,0:T(8,128)(2,1)S(1)}, u32[]{:S(2)}, u32[]{:S(2)}) collective-permute-start(bf16[544,256]{1,0:T(8,128)(2,1)} %get-tuple-element.29), channel_id=1, source_target_pairs={{0,5},{1,4},{2,7},{3,6},{4,1},{5,0},{6,3},{7,2},{8,13},{9,12},{10,... | collective-permute-start | bytes 835592 | tf_op jit(solution)/shard_map/ppermute | solution.py:306
  9.7 12.2 %collective-permute-start.5 = (bf16[544,256]{1,0:T(8,128)(2,1)}, bf16[544,256]{1,0:T(8,128)(2,1)S(1)}, u32[]{:S(2)}, u32[]{:S(2)}) collective-permute-start(bf16[544,256]{1,0:T(8,128)(2,1)} %get-tuple-element.29), channel_id=1, source_target_pairs={{0,1},{1,0},{2,3},{3,2},{4,5},{5,4},{6,7},{7,6},{8,9},{9,8},{10,11... | collective-permute-start | bytes 835592 | tf_op jit(solution)/shard_map/ppermute | solution.py:306
  21.9 17.9 %collective-permute-start.6 = (bf16[544,256]{1,0:T(8,128)(2,1)S(1)}, bf16[544,256]{1,0:T(8,128)(2,1)S(1)}, u32[]{:S(2)}, u32[]{:S(2)}) collective-permute-start(bf16[544,256]{1,0:T(8,128)(2,1)S(1)} %collective-permute-done.3.refs_5_.refs_8_), channel_id=1, source_target_pairs={{0,2},{1,3},{2,0},{3,1},{4,6},{5,7},{6,4},{7,5},{8,10},{9,11},{10,... | collective-permute-start | bytes 835592 | tf_op jit(solution)/shard_map/ppermute | solution.py:306
  21.9 2.2 %copy-start = (bf16[512,4096]{1,0:T(8,128)(2,1)S(1)}, bf16[512,4096]{1,0:T(8,128)(2,1)}, u32[]{:S(2)}) copy-start(bf16[512,4096]{1,0:T(8,128)(2,1)} %refs_1_.3) | copy-start | bytes 12582916
  24.1 1.0 %copy-start.1 = (bf16[544,256]{1,0:T(8,128)(2,1)S(1)}, bf16[544,256]{1,0:T(8,128)(2,1)}, u32[]{:S(2)}) copy-start(bf16[544,256]{1,0:T(8,128)(2,1)} %get-tuple-element.26.refs_3_.refs_4_) | copy-start | bytes 835588
  30.5 6.7 %copy-start.3 = (bf16[256,512]{1,0:T(8,128)(2,1)S(1)}, bf16[256,512]{1,0:T(8,128)(2,1)}, u32[]{:S(2)}) copy-start(bf16[256,512]{1,0:T(8,128)(2,1)} %refs_0_) | copy-start | bytes 786436
  30.5 17.9 %copy-start.2 = (bf16[544,256]{1,0:T(8,128)(2,1)S(1)}, bf16[544,256]{1,0:T(8,128)(2,1)}, u32[]{:S(2)}) copy-start(bf16[544,256]{1,0:T(8,128)(2,1)} %get-tuple-element.26.refs_3_.refs_4_) | copy-start | bytes 835588
  30.5 17.9 %collective-permute-start.7 = (bf16[544,256]{1,0:T(8,128)(2,1)S(1)}, bf16[544,256]{1,0:T(8,128)(2,1)S(1)}, u32[]{:S(2)}, u32[]{:S(2)}) collective-permute-start(bf16[544,256]{1,0:T(8,128)(2,1)S(1)} %collective-permute-done.4.refs_6_.refs_9_), channel_id=1, source_target_pairs={{0,2},{1,3},{2,0},{3,1},{4,6},{5,7},{6,4},{7,5},{8,10},{9,11},{10,... | collective-permute-start | bytes 835592 | tf_op jit(solution)/shard_map/ppermute | solution.py:306
  37.2 25.4 %copy-start.4 = (bf16[256]{0:T(256)(128)(2,1)S(1)}, bf16[256]{0:T(256)(128)(2,1)}, u32[]{:S(2)}) copy-start(bf16[256]{0:T(256)(128)(2,1)} %param.12) | copy-start | bytes 1540
  37.2 18.7 %collective-permute-start.12 = (bf16[256,512]{1,0:T(8,128)(2,1)S(1)}, bf16[256,512]{1,0:T(8,128)(2,1)S(1)}, u32[]{:S(2)}, u32[]{:S(2)}) collective-permute-start(bf16[256,512]{1,0:T(8,128)(2,1)S(1)} %copy-done.3), channel_id=1, source_target_pairs={{0,2},{1,3},{2,0},{3,1},{4,6},{5,7},{6,4},{7,5},{8,10},{9,11},{10,... | collective-permute-start | bytes 786440 | tf_op jit(solution)/shard_map/ppermute | solution.py:306
  37.3 18.6 %collective-permute-start.13 = (bf16[256,512]{1,0:T(8,128)(2,1)S(1)}, bf16[256,512]{1,0:T(8,128)(2,1)S(1)}, u32[]{:S(2)}, u32[]{:S(2)}) collective-permute-start(bf16[256,512]{1,0:T(8,128)(2,1)S(1)} %copy-done.3), channel_id=1, source_target_pairs={{0,4},{1,5},{2,6},{3,7},{4,0},{5,1},{6,2},{7,3},{8,12},{9,13},{10,... | collective-permute-start | bytes 786440 | tf_op jit(solution)/shard_map/ppermute | solution.py:306
  51.2 6.2 %collective-permute-start.10 = (bf16[144,128]{1,0:T(8,128)(2,1)S(1)}, bf16[144,128]{1,0:T(8,128)(2,1)S(1)}, u32[]{:S(2)}, u32[]{:S(2)}) collective-permute-start(bf16[144,128]{1,0:T(8,128)(2,1)S(1)} %get-tuple-element.38), channel_id=1, source_target_pairs={{0,6},{1,7},{2,4},{3,5},{4,2},{5,3},{6,0},{7,1},{8,14},{9,15},{10,... | collective-permute-start | bytes 110600 | tf_op jit(solution)/shard_map/ppermute | solution.py:306
  55.3 4.0 %collective-permute-start.8 = (bf16[144,128]{1,0:T(8,128)(2,1)S(1)}, bf16[144,128]{1,0:T(8,128)(2,1)S(1)}, u32[]{:S(2)}, u32[]{:S(2)}) collective-permute-start(bf16[144,128]{1,0:T(8,128)(2,1)S(1)} %get-tuple-element.36), channel_id=1, source_target_pairs={{0,2},{1,3},{2,0},{3,1},{4,6},{5,7},{6,4},{7,5},{8,10},{9,11},{10,... | collective-permute-start | bytes 110600 | tf_op jit(solution)/shard_map/ppermute | solution.py:306
  55.3 4.9 %collective-permute-start.9 = (bf16[144,128]{1,0:T(8,128)(2,1)S(1)}, bf16[144,128]{1,0:T(8,128)(2,1)S(1)}, u32[]{:S(2)}, u32[]{:S(2)}) collective-permute-start(bf16[144,128]{1,0:T(8,128)(2,1)S(1)} %get-tuple-element.37), channel_id=1, source_target_pairs={{0,4},{1,5},{2,6},{3,7},{4,0},{5,1},{6,2},{7,3},{8,12},{9,13},{10,... | collective-permute-start | bytes 110600 | tf_op jit(solution)/shard_map/ppermute | solution.py:306
  60.1 6.8 %collective-permute-start.14 = (bf16[256,512]{1,0:T(8,128)(2,1)S(1)}, bf16[256,512]{1,0:T(8,128)(2,1)S(1)}, u32[]{:S(2)}, u32[]{:S(2)}) collective-permute-start(bf16[256,512]{1,0:T(8,128)(2,1)S(1)} %collective-permute-done.13.refs_2_), channel_id=1, source_target_pairs={{0,2},{1,3},{2,0},{3,1},{4,6},{5,7},{6,4},{7,5},{8,10},{9,11},{10,... | collective-permute-start | bytes 786440 | tf_op jit(solution)/shard_map/ppermute | solution.py:306
  62.7 1.3 %collective-permute-start.11 = (bf16[128,128]{1,0:T(8,128)(2,1)S(1)}, bf16[128,128]{1,0:T(8,128)(2,1)S(1)}, u32[]{:S(2)}, u32[]{:S(2)}) collective-permute-start(bf16[128,128]{1,0:T(8,128)(2,1)S(1)} %shard_map.77.own_ref), channel_id=1, source_target_pairs={{0,1},{1,0},{2,3},{3,2},{4,5},{5,4},{6,7},{7,6},{8,9},{9,8},{10,11... | collective-permute-start | bytes 98312 | tf_op jit(solution)/shard_map/ppermute | solution.py:306
  67.9 5.2 %collective-permute-start.15 = (bf16[128,512]{1,0:T(8,128)(2,1)S(1)}, bf16[128,512]{1,0:T(8,128)(2,1)S(1)}, u32[]{:S(2)}, u32[]{:S(2)}) collective-permute-start(bf16[128,512]{1,0:T(8,128)(2,1)S(1)} %get-tuple-element.42), channel_id=1, source_target_pairs={{0,8},{8,0},{16,24},{24,16},{1,9},{9,1},{17,25},{25,17},{2,10},{10... | collective-permute-start | bytes 393224 | tf_op jit(solution)/shard_map/ppermute | solution.py:309
  69.5 5.0 %collective-permute-start.16 = (bf16[128,512]{1,0:T(8,128)(2,1)S(1)}, bf16[128,512]{1,0:T(8,128)(2,1)S(1)}, u32[]{:S(2)}, u32[]{:S(2)}) collective-permute-start(bf16[128,512]{1,0:T(8,128)(2,1)S(1)} %get-tuple-element.43), channel_id=1, source_target_pairs={{0,16},{8,24},{16,0},{24,8},{1,17},{9,25},{17,1},{25,9},{2,18},{10... | collective-permute-start | bytes 393224 | tf_op jit(solution)/shard_map/ppermute | solution.py:309
  71.0 5.9 %collective-permute-start.17 = (bf16[128,512]{1,0:T(8,128)(2,1)S(1)}, bf16[128,512]{1,0:T(8,128)(2,1)S(1)}, u32[]{:S(2)}, u32[]{:S(2)}) collective-permute-start(bf16[128,512]{1,0:T(8,128)(2,1)S(1)} %get-tuple-element.44), channel_id=1, source_target_pairs={{0,24},{8,16},{16,8},{24,0},{1,25},{9,17},{17,9},{25,1},{2,26},{10... | collective-permute-start | bytes 393224 | tf_op jit(solution)/shard_map/ppermute | solution.py:309
  76.9 1.3 %collective-permute-start.18 = (bf16[64,512]{1,0:T(8,128)(2,1)S(1)}, bf16[64,512]{1,0:T(8,128)(2,1)S(1)}, u32[]{:S(2)}, u32[]{:S(2)}) collective-permute-start(bf16[64,512]{1,0:T(8,128)(2,1)S(1)} %get-tuple-element.46), channel_id=1, source_target_pairs={{0,1},{1,0},{2,3},{3,2},{4,5},{5,4},{6,7},{7,6},{8,9},{9,8},{10,11... | collective-permute-start | bytes 196616 | tf_op jit(solution)/shard_map/ppermute | solution.py:306

commit v11 on v10

--- a/solution.py
+++ b/solution.py
@@ -349,7 +349,7 @@
     for j in near_first:
         low = j & -j
         shard = shards[j ^ low]
-        shards[j] = across(shard if j == low else after(shard, shards[1], *arrived[1:]), CORES * low)
+        shards[j] = across(shard if j == low else after(shard, messages[0]), CORES * low)
     normed = combine(core_only, arrived, head_gain.reshape(1, panel), heads)
 
     terms = output_terms(

time: 79.2 us -> 77.4 us (0.977)
  starting transfers between devices: 22.1 us -> 19.4 us
  waiting for transfers between devices: 38.4 us -> 39.3 us
    ppermute x16, starting transfers between devices: 18.6 us -> 15.9 us  [across(): return lax.ppermute(array, 'ctx', [(i, i ^ bits) for i in range(n_ctx)])]
  transfers between devices with their start and end apart: 19 -> 19, of which waited for: 15 -> 12; matrix products, arithmetic and copies ran while one was open for 1% -> 2% of each run, Pallas kernels for 13% -> 13%
where the time goes in v11:
time: 77.4 us; the launch traced here: 77.1 us
  waiting for transfers between devices  39.3 us (51%)
  starting transfers between devices  19.4 us (25%)
  Pallas kernels  13.3 us (17%)
  local copies, waits for them, and re-layouts  4.15 us (5%)
  other arithmetic  0.86 us (1%)
    ppermute x16, waiting for transfers between devices, across(): return lax.ppermute(array, 'ctx', [(i, i ^ bits) for i in range(n_ctx)])  33.2 us
    ppermute x16, starting transfers between devices, across(): return lax.ppermute(array, 'ctx', [(i, i ^ bits) for i in range(n_ctx)])  15.9 us
    pallas_call x2, Pallas kernels, project(): pl.pallas_call(functools.partial(project_kernel, count, extra, acc is not...  7.19 us
    ppermute x3, waiting for transfers between devices, over_dp(): return lax.ppermute(array, 'dp', [(d, d ^ bits) for d in range(n_dp)])  6.09 us
    ppermute x3, starting transfers between devices, over_dp(): return lax.ppermute(array, 'dp', [(d, d ^ bits) for d in range(n_dp)])  3.55 us
    unnamed x10, local copies, waits for them, and re-layouts  3.16 us
    pallas_call x1, Pallas kernels, attend(): pl.pallas_call(functools.partial(attend_kernel, count, heads, depth, grou...  2.82 us
    pallas_call x1, Pallas kernels, pack(): pl.pallas_call(pack_kernel, out_shape=[out, out], in_specs=[SMEM, ANY, AN...  2.02 us
  transfers between devices with their start and end apart: 19, of which 12 were waited for; matrix products, arithmetic and copies ran while one was open for 2% of the time, Pallas kernels for 13%

profile of v11, /device:TPU:0, one launch (start us, length us, event | category | flops | bytes accessed | tf_op | source)
XLA Modules:
  0.0 77.1 jit_solution(331919679868812589)
XLA Ops:
  0.0 2.0 %shard_map.73 = (bf16[544,256]{1,0:T(8,128)(2,1)}, bf16[544,256]{1,0:T(8,128)(2,1)}) custom-call(s32[1]{0:T(128)} %bitcast.core_ref, bf16[512,256]{1,0:T(8,128)(2,1)} %key_ref.1, bf16[512,256]{1,0:T(8,128)(2,1)} %value_ref.1, bf16[64,256]{1,0:T(8,128)(2,1)} %query_ref.1), custom_call_target="tpu_custom_call" | custom-call | tf_op jit(solution)/shard_map/pallas_call | solution.py:235
  2.0 0.5 collective-permute-start
  2.5 2.7 %collective-permute-start.1 = (bf16[544,256]{1,0:T(8,128)(2,1)}, bf16[544,256]{1,0:T(8,128)(2,1)S(1)}, u32[]{:S(2)}, u32[]{:S(2)}) collective-permute-start(bf16[544,256]{1,0:T(8,128)(2,1)} %get-tuple-element.26.refs_3_.refs_4_), channel_id=1, source_target_pairs={{0,2},{1,3},{2,0},{3,1},{4,6},{5,7},{6,4},{7,5},{8,10},{9,11},{10,... | collective-permute-start | bytes 835592 | tf_op jit(solution)/shard_map/ppermute | solution.py:306
  5.2 2.6 %collective-permute-start.3 = (bf16[544,256]{1,0:T(8,128)(2,1)}, bf16[544,256]{1,0:T(8,128)(2,1)S(1)}, u32[]{:S(2)}, u32[]{:S(2)}) collective-permute-start(bf16[544,256]{1,0:T(8,128)(2,1)} %get-tuple-element.26.refs_3_.refs_4_), channel_id=1, source_target_pairs={{0,4},{1,5},{2,6},{3,7},{4,0},{5,1},{6,2},{7,3},{8,12},{9,13},{10,... | collective-permute-start | bytes 835592 | tf_op jit(solution)/shard_map/ppermute | solution.py:306
  7.8 0.0 collective-permute-start.2
  7.8 0.2 collective-permute-start.4
  8.0 0.1 stack.71.refs_2_
  8.1 1.6 %collective-permute-done.refs_2_ = bf16[512,4096]{1,0:T(8,128)(2,1)} collective-permute-done((bf16[512,4096]{1,0:T(8,128)(2,1)}, bf16[512,4096]{1,0:T(8,128)(2,1)}, u32[]{:S(2)}, u32[]{:S(2)}) %collective-permute-start) | collective-permute-done | bytes 4194336 | tf_op jit(solution)/shard_map/ppermute | solution.py:306
  9.7 0.4 collective-permute-start.5
  10.1 0.1 slice.8.refs_0_
  10.1 0.8 %slice_bitcast_fusion.3 = (s32[1,128]{1,0:T(1,128)S(1)}, s32[1,128]{1,0:T(1,128)S(1)}, s32[1,128]{1,0:T(1,128)S(1)}, s32[1,128]{1,0:T(1,128)S(1)}) fusion(s32[512]{0:T(512)} %param.11), kind=kLoop, calls=%fused_computation.7 | loop fusion | bytes 4096 | tf_op jit(solution)/shard_map/stack | solution.py:152
  11.0 7.8 %collective-permute-done.1.refs_3_.refs_6_ = bf16[544,256]{1,0:T(8,128)(2,1)S(1)} collective-permute-done((bf16[544,256]{1,0:T(8,128)(2,1)}, bf16[544,256]{1,0:T(8,128)(2,1)S(1)}, u32[]{:S(2)}, u32[]{:S(2)}) %collective-permute-start.1) | collective-permute-done | bytes 278560 | tf_op jit(solution)/shard_map/ppermute | solution.py:306
  18.8 3.2 %collective-permute-done.3.refs_5_.refs_8_ = bf16[544,256]{1,0:T(8,128)(2,1)S(1)} collective-permute-done((bf16[544,256]{1,0:T(8,128)(2,1)}, bf16[544,256]{1,0:T(8,128)(2,1)S(1)}, u32[]{:S(2)}, u32[]{:S(2)}) %collective-permute-start.3) | collective-permute-done | bytes 278560 | tf_op jit(solution)/shard_map/ppermute | solution.py:306
  21.9 0.0 collective-permute-start.6
  21.9 0.0 collective-permute-done.5.refs_4_.refs_5_
  21.9 0.0 copy-start
  21.9 2.2 %copy-done = bf16[512,4096]{1,0:T(8,128)(2,1)S(1)} copy-done((bf16[512,4096]{1,0:T(8,128)(2,1)S(1)}, bf16[512,4096]{1,0:T(8,128)(2,1)}, u32[]{:S(2)}) %copy-start) | copy-done | bytes 4194328
  24.1 0.0 copy-start.1
  24.1 1.0 %copy-done.1 = bf16[544,256]{1,0:T(8,128)(2,1)S(1)} copy-done((bf16[544,256]{1,0:T(8,128)(2,1)S(1)}, bf16[544,256]{1,0:T(8,128)(2,1)}, u32[]{:S(2)}) %copy-start.1) | copy-done | bytes 278552
  25.1 3.1 %shard_map.74 = (f32[1024,256]{1,0:T(8,128)S(1)}, bf16[2,16,512]{2,1,0:T(8,128)(2,1)}) custom-call(s32[2]{0:T(128)S(1)} %bitcast.21, bf16[512,4096]{1,0:T(8,128)(2,1)S(1)} %copy-done, bf16[512,4096]{1,0:T(8,128)(2,1)} %collective-permute-done.refs_2_, bf16[544,256]{1,0:T(8,128)(2,1)S(1)} %copy-done.1, bf16[544,256]{1,0:T(8,128)(2,1)S(1)} %collective-permute-done.5.refs_4_.refs_5_), custom_call_target="tpu_custom_call" | custom-call | flops 536870912 | bytes 2097152 | tf_op jit(solution)/shard_map/pallas_call | solution.py:81
  28.1 2.0 %collective-permute-done.2.refs_4_.refs_7_ = bf16[544,256]{1,0:T(8,128)(2,1)S(1)} collective-permute-done((bf16[544,256]{1,0:T(8,128)(2,1)}, bf16[544,256]{1,0:T(8,128)(2,1)S(1)}, u32[]{:S(2)}, u32[]{:S(2)}) %collective-permute-start.2) | collective-permute-done | bytes 278560 | tf_op jit(solution)/shard_map/ppermute | solution.py:306
  30.2 0.3 collective-permute-done.4.refs_6_.refs_9_
  30.5 0.0 copy-start.3
  30.5 0.0 copy-start.2
  30.5 2.5 %collective-permute-start.7 = (bf16[544,256]{1,0:T(8,128)(2,1)S(1)}, bf16[544,256]{1,0:T(8,128)(2,1)S(1)}, u32[]{:S(2)}, u32[]{:S(2)}) collective-permute-start(bf16[544,256]{1,0:T(8,128)(2,1)S(1)} %collective-permute-done.4.refs_6_.refs_9_), channel_id=1, source_target_pairs={{0,2},{1,3},{2,0},{3,1},{4,6},{5,7},{6,4},{7,5},{8,10},{9,11},{10,... | collective-permute-start | bytes 835592 | tf_op jit(solution)/shard_map/ppermute | solution.py:306
  33.0 4.1 %shard_map.75 = (f32[1024,256]{1,0:T(8,128)S(1)}, bf16[4,512,512]{2,1,0:T(8,128)(2,1)S(1)}) custom-call(s32[6]{0:T(128)S(1)} %slice.8.refs_0_, bf16[512,4096]{1,0:T(8,128)(2,1)S(1)} %copy-done, bf16[512,4096]{1,0:T(8,128)(2,1)} %collective-permute-done.refs_2_, bf16[544,256]{1,0:T(8,128)(2,1)S(1)} %collective-permute-done.1.refs_3_.refs_6_, ...), custom_call_target="tpu_custom_call" | custom-call | flops 1073741824 | bytes 4194304 | tf_op jit(solution)/shard_map/pallas_call | solution.py:81
  37.2 0.0 copy-start.4
  37.2 0.0 copy-done.3
  37.2 2.4 %collective-permute-start.13 = (bf16[256,512]{1,0:T(8,128)(2,1)S(1)}, bf16[256,512]{1,0:T(8,128)(2,1)S(1)}, u32[]{:S(2)}, u32[]{:S(2)}) collective-permute-start(bf16[256,512]{1,0:T(8,128)(2,1)S(1)} %copy-done.3), channel_id=1, source_target_pairs={{0,4},{1,5},{2,6},{3,7},{4,0},{5,1},{6,2},{7,3},{8,12},{9,13},{10,... | collective-permute-start | bytes 786440 | tf_op jit(solution)/shard_map/ppermute | solution.py:306
  39.6 0.1 pad_add_fusion.2.refs_0_
  39.7 0.1 collective-permute-start.12
  39.8 0.0 collective-permute-done.6.refs_10_
  39.8 6.7 %collective-permute-done.7.refs_11_ = bf16[544,256]{1,0:T(8,128)(2,1)S(1)} collective-permute-done((bf16[544,256]{1,0:T(8,128)(2,1)S(1)}, bf16[544,256]{1,0:T(8,128)(2,1)S(1)}, u32[]{:S(2)}, u32[]{:S(2)}) %collective-permute-start.7) | collective-permute-done | bytes 278560 | tf_op jit(solution)/shard_map/ppermute | solution.py:306
  46.4 0.0 copy-done.2
  46.4 2.8 %shard_map.76 = (bf16[144,128]{1,0:T(8,128)(2,1)S(1)}, bf16[144,128]{1,0:T(8,128)(2,1)S(1)}, bf16[144,128]{1,0:T(8,128)(2,1)S(1)}, bf16[144,128]{1,0:T(8,128)(2,1)S(1)}) custom-call(s32[2]{0:T(128)S(1)} %pad_add_fusion.2.refs_0_, s32[4]{0:T(128)S(1)} %iota_xor_fusion.refs_1_, s32[8]{0:T(128)S(1)} %stack.71.refs_2_, ...), custom_call_target="tpu_custom_call" | custom-call | flops 536870912 | bytes 2097152 | tf_op jit(solution)/shard_map/pallas_call | solution.py:158
  49.3 3.3 %collective-permute-done.13.refs_2_ = bf16[256,512]{1,0:T(8,128)(2,1)S(1)} collective-permute-done((bf16[256,512]{1,0:T(8,128)(2,1)S(1)}, bf16[256,512]{1,0:T(8,128)(2,1)S(1)}, u32[]{:S(2)}, u32[]{:S(2)}) %collective-permute-start.13) | collective-permute-done | bytes 262176 | tf_op jit(solution)/shard_map/ppermute | solution.py:306
  52.6 0.0 collective-permute-start.14
  52.6 2.0 %collective-permute-start.10 = (bf16[144,128]{1,0:T(8,128)(2,1)S(1)}, bf16[144,128]{1,0:T(8,128)(2,1)S(1)}, u32[]{:S(2)}, u32[]{:S(2)}) collective-permute-start(bf16[144,128]{1,0:T(8,128)(2,1)S(1)} %get-tuple-element.38), channel_id=1, source_target_pairs={{0,6},{1,7},{2,4},{3,5},{4,2},{5,3},{6,0},{7,1},{8,14},{9,15},{10,... | collective-permute-start | bytes 110600 | tf_op jit(solution)/shard_map/ppermute | solution.py:306
  54.6 1.1 %collective-permute-start.8 = (bf16[144,128]{1,0:T(8,128)(2,1)S(1)}, bf16[144,128]{1,0:T(8,128)(2,1)S(1)}, u32[]{:S(2)}, u32[]{:S(2)}) collective-permute-start(bf16[144,128]{1,0:T(8,128)(2,1)S(1)} %get-tuple-element.36), channel_id=1, source_target_pairs={{0,2},{1,3},{2,0},{3,1},{4,6},{5,7},{6,4},{7,5},{8,10},{9,11},{10,... | collective-permute-start | bytes 110600 | tf_op jit(solution)/shard_map/ppermute | solution.py:306
  55.7 1.3 %collective-permute-start.9 = (bf16[144,128]{1,0:T(8,128)(2,1)S(1)}, bf16[144,128]{1,0:T(8,128)(2,1)S(1)}, u32[]{:S(2)}, u32[]{:S(2)}) collective-permute-start(bf16[144,128]{1,0:T(8,128)(2,1)S(1)} %get-tuple-element.37), channel_id=1, source_target_pairs={{0,4},{1,5},{2,6},{3,7},{4,0},{5,1},{6,2},{7,3},{8,12},{9,13},{10,... | collective-permute-start | bytes 110600 | tf_op jit(solution)/shard_map/ppermute | solution.py:306
  57.0 0.0 copy-done.4
  57.0 6.0 %collective-permute-done.10.refs_3_ = bf16[144,128]{1,0:T(8,128)(2,1)S(1)} collective-permute-done((bf16[144,128]{1,0:T(8,128)(2,1)S(1)}, bf16[144,128]{1,0:T(8,128)(2,1)S(1)}, u32[]{:S(2)}, u32[]{:S(2)}) %collective-permute-start.10) | collective-permute-done | bytes 36896 | tf_op jit(solution)/shard_map/ppermute | solution.py:306
  62.9 0.0 collective-permute-done.8.refs_1_
  63.0 0.0 collective-permute-done.9.refs_2_
  63.0 0.2 shard_map.77.own_ref
  63.1 0.1 collective-permute-start.11
  63.2 0.1 pad_add_fusion.1.place_ref
  63.3 0.0 collective-permute-done.12.refs_1_
  63.3 1.1 %collective-permute-done.11.sibling_ref = bf16[128,128]{1,0:T(8,128)(2,1)S(1)} collective-permute-done((bf16[128,128]{1,0:T(8,128)(2,1)S(1)}, bf16[128,128]{1,0:T(8,128)(2,1)S(1)}, u32[]{:S(2)}, u32[]{:S(2)}) %collective-permute-start.11) | collective-permute-done | bytes 32800 | tf_op jit(solution)/shard_map/ppermute | solution.py:306
  64.4 0.0 collective-permute-done.14.refs_3_
  64.4 1.0 %shard_map.78 = (bf16[128,512]{1,0:T(8,128)(2,1)S(1)}, bf16[128,512]{1,0:T(8,128)(2,1)S(1)}, bf16[128,512]{1,0:T(8,128)(2,1)S(1)}, bf16[128,512]{1,0:T(8,128)(2,1)S(1)}) custom-call(s32[2]{0:T(128)S(1)} %pad_add_fusion.1.place_ref, bf16[128,128]{1,0:T(8,128)(2,1)S(1)} %shard_map.77.own_ref, bf16[128,128]{1,0:T(8,128)(2,1)S(1)} %collective-permute-done.11.sibling_ref, ...), custom_call_target="tpu_custom_call" | custom-call | tf_op jit(solution)/shard_map/pallas_call | solution.py:262
  65.4 1.6 %collective-permute-start.15 = (bf16[128,512]{1,0:T(8,128)(2,1)S(1)}, bf16[128,512]{1,0:T(8,128)(2,1)S(1)}, u32[]{:S(2)}, u32[]{:S(2)}) collective-permute-start(bf16[128,512]{1,0:T(8,128)(2,1)S(1)} %get-tuple-element.42), channel_id=1, source_target_pairs={{0,8},{8,0},{16,24},{24,16},{1,9},{9,1},{17,25},{25,17},{2,10},{10... | collective-permute-start | bytes 393224 | tf_op jit(solution)/shard_map/ppermute | solution.py:309
  67.0 1.5 %collective-permute-start.16 = (bf16[128,512]{1,0:T(8,128)(2,1)S(1)}, bf16[128,512]{1,0:T(8,128)(2,1)S(1)}, u32[]{:S(2)}, u32[]{:S(2)}) collective-permute-start(bf16[128,512]{1,0:T(8,128)(2,1)S(1)} %get-tuple-element.43), channel_id=1, source_target_pairs={{0,16},{8,24},{16,0},{24,8},{1,17},{9,25},{17,1},{25,9},{2,18},{10... | collective-permute-start | bytes 393224 | tf_op jit(solution)/shard_map/ppermute | solution.py:309
  68.5 0.5 collective-permute-start.17
  69.0 2.4 %collective-permute-done.15.refs_1_ = bf16[128,512]{1,0:T(8,128)(2,1)S(1)} collective-permute-done((bf16[128,512]{1,0:T(8,128)(2,1)S(1)}, bf16[128,512]{1,0:T(8,128)(2,1)S(1)}, u32[]{:S(2)}, u32[]{:S(2)}) %collective-permute-start.15) | collective-permute-done | bytes 131104 | tf_op jit(solution)/shard_map/ppermute | solution.py:309
  71.4 3.7 %collective-permute-done.16.refs_2_ = bf16[128,512]{1,0:T(8,128)(2,1)S(1)} collective-permute-done((bf16[128,512]{1,0:T(8,128)(2,1)S(1)}, bf16[128,512]{1,0:T(8,128)(2,1)S(1)}, u32[]{:S(2)}, u32[]{:S(2)}) %collective-permute-start.16) | collective-permute-done | bytes 131104 | tf_op jit(solution)/shard_map/ppermute | solution.py:309
  75.1 0.0 collective-permute-done.17.refs_3_
  75.1 0.1 shard_map.79
  75.1 0.1 collective-permute-start.18
  75.2 1.2 %collective-permute-done.18 = bf16[64,512]{1,0:T(8,128)(2,1)S(1)} collective-permute-done((bf16[64,512]{1,0:T(8,128)(2,1)S(1)}, bf16[64,512]{1,0:T(8,128)(2,1)S(1)}, u32[]{:S(2)}, u32[]{:S(2)}) %collective-permute-start.18) | collective-permute-done | bytes 65568 | tf_op jit(solution)/shard_map/ppermute | solution.py:306
  76.5 0.7 maximum_select_fusion
  (4 shorter events, 0.0 us)
Async XLA Ops:
  2.0 7.6 %collective-permute-start = (bf16[512,4096]{1,0:T(8,128)(2,1)}, bf16[512,4096]{1,0:T(8,128)(2,1)}, u32[]{:S(2)}, u32[]{:S(2)}) collective-permute-start(bf16[512,4096]{1,0:T(8,128)(2,1)} %refs_1_.3), channel_id=1, source_target_pairs={{0,1},{1,0},{2,3},{3,2},{4,5},{5,4},{6,7},{7,6},{8,9},{9,8},{10,11... | collective-permute-start | bytes 12582920 | tf_op jit(solution)/shard_map/ppermute | solution.py:306
  2.5 16.2 %collective-permute-start.1 = (bf16[544,256]{1,0:T(8,128)(2,1)}, bf16[544,256]{1,0:T(8,128)(2,1)S(1)}, u32[]{:S(2)}, u32[]{:S(2)}) collective-permute-start(bf16[544,256]{1,0:T(8,128)(2,1)} %get-tuple-element.26.refs_3_.refs_4_), channel_id=1, source_target_pairs={{0,2},{1,3},{2,0},{3,1},{4,6},{5,7},{6,4},{7,5},{8,10},{9,11},{10,... | collective-permute-start | bytes 835592 | tf_op jit(solution)/shard_map/ppermute | solution.py:306
  5.2 16.7 %collective-permute-start.3 = (bf16[544,256]{1,0:T(8,128)(2,1)}, bf16[544,256]{1,0:T(8,128)(2,1)S(1)}, u32[]{:S(2)}, u32[]{:S(2)}) collective-permute-start(bf16[544,256]{1,0:T(8,128)(2,1)} %get-tuple-element.26.refs_3_.refs_4_), channel_id=1, source_target_pairs={{0,4},{1,5},{2,6},{3,7},{4,0},{5,1},{6,2},{7,3},{8,12},{9,13},{10,... | collective-permute-start | bytes 835592 | tf_op jit(solution)/shard_map/ppermute | solution.py:306
  7.8 22.4 %collective-permute-start.2 = (bf16[544,256]{1,0:T(8,128)(2,1)}, bf16[544,256]{1,0:T(8,128)(2,1)S(1)}, u32[]{:S(2)}, u32[]{:S(2)}) collective-permute-start(bf16[544,256]{1,0:T(8,128)(2,1)} %get-tuple-element.29), channel_id=1, source_target_pairs={{0,3},{1,2},{2,1},{3,0},{4,7},{5,6},{6,5},{7,4},{8,11},{9,10},{10,... | collective-permute-start | bytes 835592 | tf_op jit(solution)/shard_map/ppermute | solution.py:306
  7.8 22.7 %collective-permute-start.4 = (bf16[544,256]{1,0:T(8,128)(2,1)}, bf16[544,256]{1,0:T(8,128)(2,1)S(1)}, u32[]{:S(2)}, u32[]{:S(2)}) collective-permute-start(bf16[544,256]{1,0:T(8,128)(2,1)} %get-tuple-element.29), channel_id=1, source_target_pairs={{0,5},{1,4},{2,7},{3,6},{4,1},{5,0},{6,3},{7,2},{8,13},{9,12},{10,... | collective-permute-start | bytes 835592 | tf_op jit(solution)/shard_map/ppermute | solution.py:306
  9.7 12.2 %collective-permute-start.5 = (bf16[544,256]{1,0:T(8,128)(2,1)}, bf16[544,256]{1,0:T(8,128)(2,1)S(1)}, u32[]{:S(2)}, u32[]{:S(2)}) collective-permute-start(bf16[544,256]{1,0:T(8,128)(2,1)} %get-tuple-element.29), channel_id=1, source_target_pairs={{0,1},{1,0},{2,3},{3,2},{4,5},{5,4},{6,7},{7,6},{8,9},{9,8},{10,11... | collective-permute-start | bytes 835592 | tf_op jit(solution)/shard_map/ppermute | solution.py:306
  21.9 17.9 %collective-permute-start.6 = (bf16[544,256]{1,0:T(8,128)(2,1)S(1)}, bf16[544,256]{1,0:T(8,128)(2,1)S(1)}, u32[]{:S(2)}, u32[]{:S(2)}) collective-permute-start(bf16[544,256]{1,0:T(8,128)(2,1)S(1)} %collective-permute-done.3.refs_5_.refs_8_), channel_id=1, source_target_pairs={{0,2},{1,3},{2,0},{3,1},{4,6},{5,7},{6,4},{7,5},{8,10},{9,11},{10,... | collective-permute-start | bytes 835592 | tf_op jit(solution)/shard_map/ppermute | solution.py:306
  21.9 2.2 %copy-start = (bf16[512,4096]{1,0:T(8,128)(2,1)S(1)}, bf16[512,4096]{1,0:T(8,128)(2,1)}, u32[]{:S(2)}) copy-start(bf16[512,4096]{1,0:T(8,128)(2,1)} %refs_1_.3) | copy-start | bytes 12582916
  24.1 1.0 %copy-start.1 = (bf16[544,256]{1,0:T(8,128)(2,1)S(1)}, bf16[544,256]{1,0:T(8,128)(2,1)}, u32[]{:S(2)}) copy-start(bf16[544,256]{1,0:T(8,128)(2,1)} %get-tuple-element.26.refs_3_.refs_4_) | copy-start | bytes 835588
  30.5 6.7 %copy-start.3 = (bf16[256,512]{1,0:T(8,128)(2,1)S(1)}, bf16[256,512]{1,0:T(8,128)(2,1)}, u32[]{:S(2)}) copy-start(bf16[256,512]{1,0:T(8,128)(2,1)} %refs_0_) | copy-start | bytes 786436
  30.5 15.9 %copy-start.2 = (bf16[544,256]{1,0:T(8,128)(2,1)S(1)}, bf16[544,256]{1,0:T(8,128)(2,1)}, u32[]{:S(2)}) copy-start(bf16[544,256]{1,0:T(8,128)(2,1)} %get-tuple-element.26.refs_3_.refs_4_) | copy-start | bytes 835588
  30.5 15.9 %collective-permute-start.7 = (bf16[544,256]{1,0:T(8,128)(2,1)S(1)}, bf16[544,256]{1,0:T(8,128)(2,1)S(1)}, u32[]{:S(2)}, u32[]{:S(2)}) collective-permute-start(bf16[544,256]{1,0:T(8,128)(2,1)S(1)} %collective-permute-done.4.refs_6_.refs_9_), channel_id=1, source_target_pairs={{0,2},{1,3},{2,0},{3,1},{4,6},{5,7},{6,4},{7,5},{8,10},{9,11},{10,... | collective-permute-start | bytes 835592 | tf_op jit(solution)/shard_map/ppermute | solution.py:306
  37.2 19.8 %copy-start.4 = (bf16[256]{0:T(256)(128)(2,1)S(1)}, bf16[256]{0:T(256)(128)(2,1)}, u32[]{:S(2)}) copy-start(bf16[256]{0:T(256)(128)(2,1)} %param.12) | copy-start | bytes 1540
  37.2 15.4 %collective-permute-start.13 = (bf16[256,512]{1,0:T(8,128)(2,1)S(1)}, bf16[256,512]{1,0:T(8,128)(2,1)S(1)}, u32[]{:S(2)}, u32[]{:S(2)}) collective-permute-start(bf16[256,512]{1,0:T(8,128)(2,1)S(1)} %copy-done.3), channel_id=1, source_target_pairs={{0,4},{1,5},{2,6},{3,7},{4,0},{5,1},{6,2},{7,3},{8,12},{9,13},{10,... | collective-permute-start | bytes 786440 | tf_op jit(solution)/shard_map/ppermute | solution.py:306
  39.7 23.6 %collective-permute-start.12 = (bf16[256,512]{1,0:T(8,128)(2,1)S(1)}, bf16[256,512]{1,0:T(8,128)(2,1)S(1)}, u32[]{:S(2)}, u32[]{:S(2)}) collective-permute-start(bf16[256,512]{1,0:T(8,128)(2,1)S(1)} %copy-done.3), channel_id=1, source_target_pairs={{0,2},{1,3},{2,0},{3,1},{4,6},{5,7},{6,4},{7,5},{8,10},{9,11},{10,... | collective-permute-start | bytes 786440 | tf_op jit(solution)/shard_map/ppermute | solution.py:306
  52.6 11.8 %collective-permute-start.14 = (bf16[256,512]{1,0:T(8,128)(2,1)S(1)}, bf16[256,512]{1,0:T(8,128)(2,1)S(1)}, u32[]{:S(2)}, u32[]{:S(2)}) collective-permute-start(bf16[256,512]{1,0:T(8,128)(2,1)S(1)} %collective-permute-done.13.refs_2_), channel_id=1, source_target_pairs={{0,2},{1,3},{2,0},{3,1},{4,6},{5,7},{6,4},{7,5},{8,10},{9,11},{10,... | collective-permute-start | bytes 786440 | tf_op jit(solution)/shard_map/ppermute | solution.py:306
  52.6 10.4 %collective-permute-start.10 = (bf16[144,128]{1,0:T(8,128)(2,1)S(1)}, bf16[144,128]{1,0:T(8,128)(2,1)S(1)}, u32[]{:S(2)}, u32[]{:S(2)}) collective-permute-start(bf16[144,128]{1,0:T(8,128)(2,1)S(1)} %get-tuple-element.38), channel_id=1, source_target_pairs={{0,6},{1,7},{2,4},{3,5},{4,2},{5,3},{6,0},{7,1},{8,14},{9,15},{10,... | collective-permute-start | bytes 110600 | tf_op jit(solution)/shard_map/ppermute | solution.py:306
  54.6 8.4 %collective-permute-start.8 = (bf16[144,128]{1,0:T(8,128)(2,1)S(1)}, bf16[144,128]{1,0:T(8,128)(2,1)S(1)}, u32[]{:S(2)}, u32[]{:S(2)}) collective-permute-start(bf16[144,128]{1,0:T(8,128)(2,1)S(1)} %get-tuple-element.36), channel_id=1, source_target_pairs={{0,2},{1,3},{2,0},{3,1},{4,6},{5,7},{6,4},{7,5},{8,10},{9,11},{10,... | collective-permute-start | bytes 110600 | tf_op jit(solution)/shard_map/ppermute | solution.py:306
  55.7 7.3 %collective-permute-start.9 = (bf16[144,128]{1,0:T(8,128)(2,1)S(1)}, bf16[144,128]{1,0:T(8,128)(2,1)S(1)}, u32[]{:S(2)}, u32[]{:S(2)}) collective-permute-start(bf16[144,128]{1,0:T(8,128)(2,1)S(1)} %get-tuple-element.37), channel_id=1, source_target_pairs={{0,4},{1,5},{2,6},{3,7},{4,0},{5,1},{6,2},{7,3},{8,12},{9,13},{10,... | collective-permute-start | bytes 110600 | tf_op jit(solution)/shard_map/ppermute | solution.py:306
  63.1 1.3 %collective-permute-start.11 = (bf16[128,128]{1,0:T(8,128)(2,1)S(1)}, bf16[128,128]{1,0:T(8,128)(2,1)S(1)}, u32[]{:S(2)}, u32[]{:S(2)}) collective-permute-start(bf16[128,128]{1,0:T(8,128)(2,1)S(1)} %shard_map.77.own_ref), channel_id=1, source_target_pairs={{0,1},{1,0},{2,3},{3,2},{4,5},{5,4},{6,7},{7,6},{8,9},{9,8},{10,11... | collective-permute-start | bytes 98312 | tf_op jit(solution)/shard_map/ppermute | solution.py:306
  65.4 6.0 %collective-permute-start.15 = (bf16[128,512]{1,0:T(8,128)(2,1)S(1)}, bf16[128,512]{1,0:T(8,128)(2,1)S(1)}, u32[]{:S(2)}, u32[]{:S(2)}) collective-permute-start(bf16[128,512]{1,0:T(8,128)(2,1)S(1)} %get-tuple-element.42), channel_id=1, source_target_pairs={{0,8},{8,0},{16,24},{24,16},{1,9},{9,1},{17,25},{25,17},{2,10},{10... | collective-permute-start | bytes 393224 | tf_op jit(solution)/shard_map/ppermute | solution.py:309
  67.0 8.1 %collective-permute-start.16 = (bf16[128,512]{1,0:T(8,128)(2,1)S(1)}, bf16[128,512]{1,0:T(8,128)(2,1)S(1)}, u32[]{:S(2)}, u32[]{:S(2)}) collective-permute-start(bf16[128,512]{1,0:T(8,128)(2,1)S(1)} %get-tuple-element.43), channel_id=1, source_target_pairs={{0,16},{8,24},{16,0},{24,8},{1,17},{9,25},{17,1},{25,9},{2,18},{10... | collective-permute-start | bytes 393224 | tf_op jit(solution)/shard_map/ppermute | solution.py:309
  68.5 6.6 %collective-permute-start.17 = (bf16[128,512]{1,0:T(8,128)(2,1)S(1)}, bf16[128,512]{1,0:T(8,128)(2,1)S(1)}, u32[]{:S(2)}, u32[]{:S(2)}) collective-permute-start(bf16[128,512]{1,0:T(8,128)(2,1)S(1)} %get-tuple-element.44), channel_id=1, source_target_pairs={{0,24},{8,16},{16,8},{24,0},{1,25},{9,17},{17,9},{25,1},{2,26},{10... | collective-permute-start | bytes 393224 | tf_op jit(solution)/shard_map/ppermute | solution.py:309
  75.1 1.3 %collective-permute-start.18 = (bf16[64,512]{1,0:T(8,128)(2,1)S(1)}, bf16[64,512]{1,0:T(8,128)(2,1)S(1)}, u32[]{:S(2)}, u32[]{:S(2)}) collective-permute-start(bf16[64,512]{1,0:T(8,128)(2,1)S(1)} %get-tuple-element.46), channel_id=1, source_target_pairs={{0,1},{1,0},{2,3},{3,2},{4,5},{5,4},{6,7},{7,6},{8,9},{9,8},{10,11... | collective-permute-start | bytes 196616 | tf_op jit(solution)/shard_map/ppermute | solution.py:306

commit v12 on v11

--- a/solution.py
+++ b/solution.py
@@ -345,7 +345,7 @@
         firsts, slot_groups, places, slices, blocks, acc, offsets, groups, heads, depth
     )
     arrived = [messages[0]] + [across(messages[j], CORES * j) for j in range(1, chips)]
-    shards = [after(w_out, acc)] + [None] * (chips - 1)
+    shards = [after(w_out, *pairs[1], *pairs[2])] + [None] * (chips - 1)
     for j in near_first:
         low = j & -j
         shard = shards[j ^ low]

time: 77.4 us -> 77.7 us (level)
  transfers between devices with their start and end apart: 19 -> 19, of which waited for: 12 -> 11; matrix products, arithmetic and copies ran while one was open for 2% -> 2% of each run, Pallas kernels for 13% -> 13%
where the time goes in v12:
time: 77.7 us; the launch traced here: 77.4 us
  waiting for transfers between devices  38.9 us (50%)
  starting transfers between devices  20.1 us (26%)
  Pallas kernels  13.3 us (17%)
  local copies, waits for them, and re-layouts  4.15 us (5%)
  other arithmetic  0.86 us (1%)
    ppermute x16, waiting for transfers between devices, across(): return lax.ppermute(array, 'ctx', [(i, i ^ bits) for i in range(n_ctx)])  32.8 us
    ppermute x16, starting transfers between devices, across(): return lax.ppermute(array, 'ctx', [(i, i ^ bits) for i in range(n_ctx)])  16.6 us
    pallas_call x2, Pallas kernels, project(): pl.pallas_call(functools.partial(project_kernel, count, extra, acc is not...  7.19 us
    ppermute x3, waiting for transfers between devices, over_dp(): return lax.ppermute(array, 'dp', [(d, d ^ bits) for d in range(n_dp)])  6.1 us
    ppermute x3, starting transfers between devices, over_dp(): return lax.ppermute(array, 'dp', [(d, d ^ bits) for d in range(n_dp)])  3.55 us
    unnamed x10, local copies, waits for them, and re-layouts  3.16 us
    pallas_call x1, Pallas kernels, attend(): pl.pallas_call(functools.partial(attend_kernel, count, heads, depth, grou...  2.81 us
    pallas_call x1, Pallas kernels, pack(): pl.pallas_call(pack_kernel, out_shape=[out, out], in_specs=[SMEM, ANY, AN...  2.02 us
  transfers between devices with their start and end apart: 19, of which 11 were waited for; matrix products, arithmetic and copies ran while one was open for 2% of the time, Pallas kernels for 13%

profile of v12, /device:TPU:0, one launch (start us, length us, event | category | flops | bytes accessed | tf_op | source)
XLA Modules:
  0.0 77.4 jit_solution(6250843490976813237)
XLA Ops:
  0.0 2.0 %shard_map.73 = (bf16[544,256]{1,0:T(8,128)(2,1)}, bf16[544,256]{1,0:T(8,128)(2,1)}) custom-call(s32[1]{0:T(128)} %bitcast.core_ref, bf16[512,256]{1,0:T(8,128)(2,1)} %key_ref.1, bf16[512,256]{1,0:T(8,128)(2,1)} %value_ref.1, bf16[64,256]{1,0:T(8,128)(2,1)} %query_ref.1), custom_call_target="tpu_custom_call" | custom-call | tf_op jit(solution)/shard_map/pallas_call | solution.py:235
  2.0 0.5 collective-permute-start
  2.5 2.7 %collective-permute-start.1 = (bf16[544,256]{1,0:T(8,128)(2,1)}, bf16[544,256]{1,0:T(8,128)(2,1)S(1)}, u32[]{:S(2)}, u32[]{:S(2)}) collective-permute-start(bf16[544,256]{1,0:T(8,128)(2,1)} %get-tuple-element.26.refs_3_.refs_4_), channel_id=1, source_target_pairs={{0,2},{1,3},{2,0},{3,1},{4,6},{5,7},{6,4},{7,5},{8,10},{9,11},{10,... | collective-permute-start | bytes 835592 | tf_op jit(solution)/shard_map/ppermute | solution.py:306
  5.2 2.6 %collective-permute-start.3 = (bf16[544,256]{1,0:T(8,128)(2,1)}, bf16[544,256]{1,0:T(8,128)(2,1)S(1)}, u32[]{:S(2)}, u32[]{:S(2)}) collective-permute-start(bf16[544,256]{1,0:T(8,128)(2,1)} %get-tuple-element.26.refs_3_.refs_4_), channel_id=1, source_target_pairs={{0,4},{1,5},{2,6},{3,7},{4,0},{5,1},{6,2},{7,3},{8,12},{9,13},{10,... | collective-permute-start | bytes 835592 | tf_op jit(solution)/shard_map/ppermute | solution.py:306
  7.8 0.0 collective-permute-start.2
  7.8 0.2 collective-permute-start.4
  8.0 0.1 stack.71.refs_2_
  8.1 0.1 slice.8.refs_0_
  8.1 1.5 %collective-permute-done.refs_2_ = bf16[512,4096]{1,0:T(8,128)(2,1)} collective-permute-done((bf16[512,4096]{1,0:T(8,128)(2,1)}, bf16[512,4096]{1,0:T(8,128)(2,1)}, u32[]{:S(2)}, u32[]{:S(2)}) %collective-permute-start) | collective-permute-done | bytes 4194336 | tf_op jit(solution)/shard_map/ppermute | solution.py:306
  9.7 0.4 collective-permute-start.5
  10.1 0.8 %slice_bitcast_fusion.3 = (s32[1,128]{1,0:T(1,128)S(1)}, s32[1,128]{1,0:T(1,128)S(1)}, s32[1,128]{1,0:T(1,128)S(1)}, s32[1,128]{1,0:T(1,128)S(1)}) fusion(s32[512]{0:T(512)} %param.11), kind=kLoop, calls=%fused_computation.7 | loop fusion | bytes 4096 | tf_op jit(solution)/shard_map/stack | solution.py:152
  10.9 7.9 %collective-permute-done.1.refs_3_.refs_6_ = bf16[544,256]{1,0:T(8,128)(2,1)S(1)} collective-permute-done((bf16[544,256]{1,0:T(8,128)(2,1)}, bf16[544,256]{1,0:T(8,128)(2,1)S(1)}, u32[]{:S(2)}, u32[]{:S(2)}) %collective-permute-start.1) | collective-permute-done | bytes 278560 | tf_op jit(solution)/shard_map/ppermute | solution.py:306
  18.8 3.2 %collective-permute-done.3.refs_5_.refs_8_ = bf16[544,256]{1,0:T(8,128)(2,1)S(1)} collective-permute-done((bf16[544,256]{1,0:T(8,128)(2,1)}, bf16[544,256]{1,0:T(8,128)(2,1)S(1)}, u32[]{:S(2)}, u32[]{:S(2)}) %collective-permute-start.3) | collective-permute-done | bytes 278560 | tf_op jit(solution)/shard_map/ppermute | solution.py:306
  21.9 0.0 collective-permute-start.6
  21.9 0.0 collective-permute-done.5.refs_4_.refs_5_
  21.9 0.0 copy-start
  21.9 2.2 %copy-done = bf16[512,4096]{1,0:T(8,128)(2,1)S(1)} copy-done((bf16[512,4096]{1,0:T(8,128)(2,1)S(1)}, bf16[512,4096]{1,0:T(8,128)(2,1)}, u32[]{:S(2)}) %copy-start) | copy-done | bytes 4194328
  24.1 0.0 copy-start.1
  24.1 1.0 %copy-done.1 = bf16[544,256]{1,0:T(8,128)(2,1)S(1)} copy-done((bf16[544,256]{1,0:T(8,128)(2,1)S(1)}, bf16[544,256]{1,0:T(8,128)(2,1)}, u32[]{:S(2)}) %copy-start.1) | copy-done | bytes 278552
  25.1 0.0 copy-start.3
  25.1 3.1 %shard_map.74 = (f32[1024,256]{1,0:T(8,128)S(1)}, bf16[2,16,512]{2,1,0:T(8,128)(2,1)}) custom-call(s32[2]{0:T(128)S(1)} %bitcast.21, bf16[512,4096]{1,0:T(8,128)(2,1)S(1)} %copy-done, bf16[512,4096]{1,0:T(8,128)(2,1)} %collective-permute-done.refs_2_, bf16[544,256]{1,0:T(8,128)(2,1)S(1)} %copy-done.1, bf16[544,256]{1,0:T(8,128)(2,1)S(1)} %collective-permute-done.5.refs_4_.refs_5_), custom_call_target="tpu_custom_call" | custom-call | flops 536870912 | bytes 2097152 | tf_op jit(solution)/shard_map/pallas_call | solution.py:81
  28.1 2.0 %collective-permute-done.2.refs_4_.refs_7_ = bf16[544,256]{1,0:T(8,128)(2,1)S(1)} collective-permute-done((bf16[544,256]{1,0:T(8,128)(2,1)}, bf16[544,256]{1,0:T(8,128)(2,1)S(1)}, u32[]{:S(2)}, u32[]{:S(2)}) %collective-permute-start.2) | collective-permute-done | bytes 278560 | tf_op jit(solution)/shard_map/ppermute | solution.py:306
  30.2 0.3 collective-permute-done.4.refs_6_.refs_9_
  30.5 2.5 %collective-permute-start.7 = (bf16[544,256]{1,0:T(8,128)(2,1)S(1)}, bf16[544,256]{1,0:T(8,128)(2,1)S(1)}, u32[]{:S(2)}, u32[]{:S(2)}) collective-permute-start(bf16[544,256]{1,0:T(8,128)(2,1)S(1)} %collective-permute-done.4.refs_6_.refs_9_), channel_id=1, source_target_pairs={{0,2},{1,3},{2,0},{3,1},{4,6},{5,7},{6,4},{7,5},{8,10},{9,11},{10,... | collective-permute-start | bytes 835592 | tf_op jit(solution)/shard_map/ppermute | solution.py:306
  33.0 0.0 copy-done.3
  33.0 2.4 %collective-permute-start.13 = (bf16[256,512]{1,0:T(8,128)(2,1)S(1)}, bf16[256,512]{1,0:T(8,128)(2,1)S(1)}, u32[]{:S(2)}, u32[]{:S(2)}) collective-permute-start(bf16[256,512]{1,0:T(8,128)(2,1)S(1)} %copy-done.3), channel_id=1, source_target_pairs={{0,4},{1,5},{2,6},{3,7},{4,0},{5,1},{6,2},{7,3},{8,12},{9,13},{10,... | collective-permute-start | bytes 786440 | tf_op jit(solution)/shard_map/ppermute | solution.py:306
  35.4 0.1 pad_add_fusion.2.refs_0_
  35.5 0.0 copy-start.2
  35.5 0.1 collective-permute-start.12
  35.5 4.1 %shard_map.75 = (f32[1024,256]{1,0:T(8,128)S(1)}, bf16[4,512,512]{2,1,0:T(8,128)(2,1)S(1)}) custom-call(s32[6]{0:T(128)S(1)} %slice.8.refs_0_, bf16[512,4096]{1,0:T(8,128)(2,1)S(1)} %copy-done, bf16[512,4096]{1,0:T(8,128)(2,1)} %collective-permute-done.refs_2_, bf16[544,256]{1,0:T(8,128)(2,1)S(1)} %collective-permute-done.1.refs_3_.refs_6_, ...), custom_call_target="tpu_custom_call" | custom-call | flops 1073741824 | bytes 4194304 | tf_op jit(solution)/shard_map/pallas_call | solution.py:81
  39.7 0.0 copy-start.4
  39.7 0.0 collective-permute-done.6.refs_10_
  39.7 8.7 %collective-permute-done.7.refs_11_ = bf16[544,256]{1,0:T(8,128)(2,1)S(1)} collective-permute-done((bf16[544,256]{1,0:T(8,128)(2,1)S(1)}, bf16[544,256]{1,0:T(8,128)(2,1)S(1)}, u32[]{:S(2)}, u32[]{:S(2)}) %collective-permute-start.7) | collective-permute-done | bytes 278560 | tf_op jit(solution)/shard_map/ppermute | solution.py:306
  48.4 0.0 copy-done.2
  48.4 2.8 %shard_map.76 = (bf16[144,128]{1,0:T(8,128)(2,1)S(1)}, bf16[144,128]{1,0:T(8,128)(2,1)S(1)}, bf16[144,128]{1,0:T(8,128)(2,1)S(1)}, bf16[144,128]{1,0:T(8,128)(2,1)S(1)}) custom-call(s32[2]{0:T(128)S(1)} %pad_add_fusion.2.refs_0_, s32[4]{0:T(128)S(1)} %iota_xor_fusion.refs_1_, s32[8]{0:T(128)S(1)} %stack.71.refs_2_, ...), custom_call_target="tpu_custom_call" | custom-call | flops 536870912 | bytes 2097152 | tf_op jit(solution)/shard_map/pallas_call | solution.py:158
  51.2 0.0 collective-permute-done.13.refs_2_
  51.2 0.2 collective-permute-start.14
  51.4 3.9 %collective-permute-start.10 = (bf16[144,128]{1,0:T(8,128)(2,1)S(1)}, bf16[144,128]{1,0:T(8,128)(2,1)S(1)}, u32[]{:S(2)}, u32[]{:S(2)}) collective-permute-start(bf16[144,128]{1,0:T(8,128)(2,1)S(1)} %get-tuple-element.38), channel_id=1, source_target_pairs={{0,6},{1,7},{2,4},{3,5},{4,2},{5,3},{6,0},{7,1},{8,14},{9,15},{10,... | collective-permute-start | bytes 110600 | tf_op jit(solution)/shard_map/ppermute | solution.py:306
  55.4 1.0 %collective-permute-start.8 = (bf16[144,128]{1,0:T(8,128)(2,1)S(1)}, bf16[144,128]{1,0:T(8,128)(2,1)S(1)}, u32[]{:S(2)}, u32[]{:S(2)}) collective-permute-start(bf16[144,128]{1,0:T(8,128)(2,1)S(1)} %get-tuple-element.36), channel_id=1, source_target_pairs={{0,2},{1,3},{2,0},{3,1},{4,6},{5,7},{6,4},{7,5},{8,10},{9,11},{10,... | collective-permute-start | bytes 110600 | tf_op jit(solution)/shard_map/ppermute | solution.py:306
  56.4 0.0 collective-permute-start.9
  56.4 0.0 copy-done.4
  56.4 6.8 %collective-permute-done.10.refs_3_ = bf16[144,128]{1,0:T(8,128)(2,1)S(1)} collective-permute-done((bf16[144,128]{1,0:T(8,128)(2,1)S(1)}, bf16[144,128]{1,0:T(8,128)(2,1)S(1)}, u32[]{:S(2)}, u32[]{:S(2)}) %collective-permute-start.10) | collective-permute-done | bytes 36896 | tf_op jit(solution)/shard_map/ppermute | solution.py:306
  63.2 0.0 collective-permute-done.8.refs_1_
  63.2 0.0 collective-permute-done.9.refs_2_
  63.2 0.2 shard_map.77.own_ref
  63.4 0.1 collective-permute-start.11
  63.5 0.1 pad_add_fusion.1.place_ref
  63.6 0.0 collective-permute-done.12.refs_1_
  63.6 1.1 %collective-permute-done.11.sibling_ref = bf16[128,128]{1,0:T(8,128)(2,1)S(1)} collective-permute-done((bf16[128,128]{1,0:T(8,128)(2,1)S(1)}, bf16[128,128]{1,0:T(8,128)(2,1)S(1)}, u32[]{:S(2)}, u32[]{:S(2)}) %collective-permute-start.11) | collective-permute-done | bytes 32800 | tf_op jit(solution)/shard_map/ppermute | solution.py:306
  64.7 0.0 collective-permute-done.14.refs_3_
  64.7 1.0 %shard_map.78 = (bf16[128,512]{1,0:T(8,128)(2,1)S(1)}, bf16[128,512]{1,0:T(8,128)(2,1)S(1)}, bf16[128,512]{1,0:T(8,128)(2,1)S(1)}, bf16[128,512]{1,0:T(8,128)(2,1)S(1)}) custom-call(s32[2]{0:T(128)S(1)} %pad_add_fusion.1.place_ref, bf16[128,128]{1,0:T(8,128)(2,1)S(1)} %shard_map.77.own_ref, bf16[128,128]{1,0:T(8,128)(2,1)S(1)} %collective-permute-done.11.sibling_ref, ...), custom_call_target="tpu_custom_call" | custom-call | tf_op jit(solution)/shard_map/pallas_call | solution.py:262
  65.7 1.6 %collective-permute-start.15 = (bf16[128,512]{1,0:T(8,128)(2,1)S(1)}, bf16[128,512]{1,0:T(8,128)(2,1)S(1)}, u32[]{:S(2)}, u32[]{:S(2)}) collective-permute-start(bf16[128,512]{1,0:T(8,128)(2,1)S(1)} %get-tuple-element.42), channel_id=1, source_target_pairs={{0,8},{8,0},{16,24},{24,16},{1,9},{9,1},{17,25},{25,17},{2,10},{10... | collective-permute-start | bytes 393224 | tf_op jit(solution)/shard_map/ppermute | solution.py:309
  67.3 1.5 %collective-permute-start.16 = (bf16[128,512]{1,0:T(8,128)(2,1)S(1)}, bf16[128,512]{1,0:T(8,128)(2,1)S(1)}, u32[]{:S(2)}, u32[]{:S(2)}) collective-permute-start(bf16[128,512]{1,0:T(8,128)(2,1)S(1)} %get-tuple-element.43), channel_id=1, source_target_pairs={{0,16},{8,24},{16,0},{24,8},{1,17},{9,25},{17,1},{25,9},{2,18},{10... | collective-permute-start | bytes 393224 | tf_op jit(solution)/shard_map/ppermute | solution.py:309
  68.8 0.5 collective-permute-start.17
  69.3 2.4 %collective-permute-done.15.refs_1_ = bf16[128,512]{1,0:T(8,128)(2,1)S(1)} collective-permute-done((bf16[128,512]{1,0:T(8,128)(2,1)S(1)}, bf16[128,512]{1,0:T(8,128)(2,1)S(1)}, u32[]{:S(2)}, u32[]{:S(2)}) %collective-permute-start.15) | collective-permute-done | bytes 131104 | tf_op jit(solution)/shard_map/ppermute | solution.py:309
  71.7 3.7 %collective-permute-done.16.refs_2_ = bf16[128,512]{1,0:T(8,128)(2,1)S(1)} collective-permute-done((bf16[128,512]{1,0:T(8,128)(2,1)S(1)}, bf16[128,512]{1,0:T(8,128)(2,1)S(1)}, u32[]{:S(2)}, u32[]{:S(2)}) %collective-permute-start.16) | collective-permute-done | bytes 131104 | tf_op jit(solution)/shard_map/ppermute | solution.py:309
  75.3 0.0 collective-permute-done.17.refs_3_
  75.3 0.1 shard_map.79
  75.4 0.1 collective-permute-start.18
  75.5 1.2 %collective-permute-done.18 = bf16[64,512]{1,0:T(8,128)(2,1)S(1)} collective-permute-done((bf16[64,512]{1,0:T(8,128)(2,1)S(1)}, bf16[64,512]{1,0:T(8,128)(2,1)S(1)}, u32[]{:S(2)}, u32[]{:S(2)}) %collective-permute-start.18) | collective-permute-done | bytes 65568 | tf_op jit(solution)/shard_map/ppermute | solution.py:306
  76.7 0.7 maximum_select_fusion
  (4 shorter events, 0.0 us)
Async XLA Ops:
  2.0 7.6 %collective-permute-start = (bf16[512,4096]{1,0:T(8,128)(2,1)}, bf16[512,4096]{1,0:T(8,128)(2,1)}, u32[]{:S(2)}, u32[]{:S(2)}) collective-permute-start(bf16[512,4096]{1,0:T(8,128)(2,1)} %refs_1_.3), channel_id=1, source_target_pairs={{0,1},{1,0},{2,3},{3,2},{4,5},{5,4},{6,7},{7,6},{8,9},{9,8},{10,11... | collective-permute-start | bytes 12582920 | tf_op jit(solution)/shard_map/ppermute | solution.py:306
  2.5 16.2 %collective-permute-start.1 = (bf16[544,256]{1,0:T(8,128)(2,1)}, bf16[544,256]{1,0:T(8,128)(2,1)S(1)}, u32[]{:S(2)}, u32[]{:S(2)}) collective-permute-start(bf16[544,256]{1,0:T(8,128)(2,1)} %get-tuple-element.26.refs_3_.refs_4_), channel_id=1, source_target_pairs={{0,2},{1,3},{2,0},{3,1},{4,6},{5,7},{6,4},{7,5},{8,10},{9,11},{10,... | collective-permute-start | bytes 835592 | tf_op jit(solution)/shard_map/ppermute | solution.py:306
  5.2 16.7 %collective-permute-start.3 = (bf16[544,256]{1,0:T(8,128)(2,1)}, bf16[544,256]{1,0:T(8,128)(2,1)S(1)}, u32[]{:S(2)}, u32[]{:S(2)}) collective-permute-start(bf16[544,256]{1,0:T(8,128)(2,1)} %get-tuple-element.26.refs_3_.refs_4_), channel_id=1, source_target_pairs={{0,4},{1,5},{2,6},{3,7},{4,0},{5,1},{6,2},{7,3},{8,12},{9,13},{10,... | collective-permute-start | bytes 835592 | tf_op jit(solution)/shard_map/ppermute | solution.py:306
  7.8 22.4 %collective-permute-start.2 = (bf16[544,256]{1,0:T(8,128)(2,1)}, bf16[544,256]{1,0:T(8,128)(2,1)S(1)}, u32[]{:S(2)}, u32[]{:S(2)}) collective-permute-start(bf16[544,256]{1,0:T(8,128)(2,1)} %get-tuple-element.29), channel_id=1, source_target_pairs={{0,3},{1,2},{2,1},{3,0},{4,7},{5,6},{6,5},{7,4},{8,11},{9,10},{10,... | collective-permute-start | bytes 835592 | tf_op jit(solution)/shard_map/ppermute | solution.py:306
  7.8 22.7 %collective-permute-start.4 = (bf16[544,256]{1,0:T(8,128)(2,1)}, bf16[544,256]{1,0:T(8,128)(2,1)S(1)}, u32[]{:S(2)}, u32[]{:S(2)}) collective-permute-start(bf16[544,256]{1,0:T(8,128)(2,1)} %get-tuple-element.29), channel_id=1, source_target_pairs={{0,5},{1,4},{2,7},{3,6},{4,1},{5,0},{6,3},{7,2},{8,13},{9,12},{10,... | collective-permute-start | bytes 835592 | tf_op jit(solution)/shard_map/ppermute | solution.py:306
  9.7 12.2 %collective-permute-start.5 = (bf16[544,256]{1,0:T(8,128)(2,1)}, bf16[544,256]{1,0:T(8,128)(2,1)S(1)}, u32[]{:S(2)}, u32[]{:S(2)}) collective-permute-start(bf16[544,256]{1,0:T(8,128)(2,1)} %get-tuple-element.29), channel_id=1, source_target_pairs={{0,1},{1,0},{2,3},{3,2},{4,5},{5,4},{6,7},{7,6},{8,9},{9,8},{10,11... | collective-permute-start | bytes 835592 | tf_op jit(solution)/shard_map/ppermute | solution.py:306
  21.9 17.8 %collective-permute-start.6 = (bf16[544,256]{1,0:T(8,128)(2,1)S(1)}, bf16[544,256]{1,0:T(8,128)(2,1)S(1)}, u32[]{:S(2)}, u32[]{:S(2)}) collective-permute-start(bf16[544,256]{1,0:T(8,128)(2,1)S(1)} %collective-permute-done.3.refs_5_.refs_8_), channel_id=1, source_target_pairs={{0,2},{1,3},{2,0},{3,1},{4,6},{5,7},{6,4},{7,5},{8,10},{9,11},{10,... | collective-permute-start | bytes 835592 | tf_op jit(solution)/shard_map/ppermute | solution.py:306
  21.9 2.2 %copy-start = (bf16[512,4096]{1,0:T(8,128)(2,1)S(1)}, bf16[512,4096]{1,0:T(8,128)(2,1)}, u32[]{:S(2)}) copy-start(bf16[512,4096]{1,0:T(8,128)(2,1)} %refs_1_.3) | copy-start | bytes 12582916
  24.1 1.0 %copy-start.1 = (bf16[544,256]{1,0:T(8,128)(2,1)S(1)}, bf16[544,256]{1,0:T(8,128)(2,1)}, u32[]{:S(2)}) copy-start(bf16[544,256]{1,0:T(8,128)(2,1)} %get-tuple-element.26.refs_3_.refs_4_) | copy-start | bytes 835588
  25.1 7.9 %copy-start.3 = (bf16[256,512]{1,0:T(8,128)(2,1)S(1)}, bf16[256,512]{1,0:T(8,128)(2,1)}, u32[]{:S(2)}) copy-start(bf16[256,512]{1,0:T(8,128)(2,1)} %refs_0_) | copy-start | bytes 786436
  30.5 17.9 %collective-permute-start.7 = (bf16[544,256]{1,0:T(8,128)(2,1)S(1)}, bf16[544,256]{1,0:T(8,128)(2,1)S(1)}, u32[]{:S(2)}, u32[]{:S(2)}) collective-permute-start(bf16[544,256]{1,0:T(8,128)(2,1)S(1)} %collective-permute-done.4.refs_6_.refs_9_), channel_id=1, source_target_pairs={{0,2},{1,3},{2,0},{3,1},{4,6},{5,7},{6,4},{7,5},{8,10},{9,11},{10,... | collective-permute-start | bytes 835592 | tf_op jit(solution)/shard_map/ppermute | solution.py:306
  33.0 18.2 %collective-permute-start.13 = (bf16[256,512]{1,0:T(8,128)(2,1)S(1)}, bf16[256,512]{1,0:T(8,128)(2,1)S(1)}, u32[]{:S(2)}, u32[]{:S(2)}) collective-permute-start(bf16[256,512]{1,0:T(8,128)(2,1)S(1)} %copy-done.3), channel_id=1, source_target_pairs={{0,4},{1,5},{2,6},{3,7},{4,0},{5,1},{6,2},{7,3},{8,12},{9,13},{10,... | collective-permute-start | bytes 786440 | tf_op jit(solution)/shard_map/ppermute | solution.py:306
  35.5 12.9 %copy-start.2 = (bf16[544,256]{1,0:T(8,128)(2,1)S(1)}, bf16[544,256]{1,0:T(8,128)(2,1)}, u32[]{:S(2)}) copy-start(bf16[544,256]{1,0:T(8,128)(2,1)} %get-tuple-element.26.refs_3_.refs_4_) | copy-start | bytes 835588
  35.5 28.1 %collective-permute-start.12 = (bf16[256,512]{1,0:T(8,128)(2,1)S(1)}, bf16[256,512]{1,0:T(8,128)(2,1)S(1)}, u32[]{:S(2)}, u32[]{:S(2)}) collective-permute-start(bf16[256,512]{1,0:T(8,128)(2,1)S(1)} %copy-done.3), channel_id=1, source_target_pairs={{0,2},{1,3},{2,0},{3,1},{4,6},{5,7},{6,4},{7,5},{8,10},{9,11},{10,... | collective-permute-start | bytes 786440 | tf_op jit(solution)/shard_map/ppermute | solution.py:306
  39.7 16.7 %copy-start.4 = (bf16[256]{0:T(256)(128)(2,1)S(1)}, bf16[256]{0:T(256)(128)(2,1)}, u32[]{:S(2)}) copy-start(bf16[256]{0:T(256)(128)(2,1)} %param.12) | copy-start | bytes 1540
  51.2 13.5 %collective-permute-start.14 = (bf16[256,512]{1,0:T(8,128)(2,1)S(1)}, bf16[256,512]{1,0:T(8,128)(2,1)S(1)}, u32[]{:S(2)}, u32[]{:S(2)}) collective-permute-start(bf16[256,512]{1,0:T(8,128)(2,1)S(1)} %collective-permute-done.13.refs_2_), channel_id=1, source_target_pairs={{0,2},{1,3},{2,0},{3,1},{4,6},{5,7},{6,4},{7,5},{8,10},{9,11},{10,... | collective-permute-start | bytes 786440 | tf_op jit(solution)/shard_map/ppermute | solution.py:306
  51.4 11.8 %collective-permute-start.10 = (bf16[144,128]{1,0:T(8,128)(2,1)S(1)}, bf16[144,128]{1,0:T(8,128)(2,1)S(1)}, u32[]{:S(2)}, u32[]{:S(2)}) collective-permute-start(bf16[144,128]{1,0:T(8,128)(2,1)S(1)} %get-tuple-element.38), channel_id=1, source_target_pairs={{0,6},{1,7},{2,4},{3,5},{4,2},{5,3},{6,0},{7,1},{8,14},{9,15},{10,... | collective-permute-start | bytes 110600 | tf_op jit(solution)/shard_map/ppermute | solution.py:306
  55.4 7.9 %collective-permute-start.8 = (bf16[144,128]{1,0:T(8,128)(2,1)S(1)}, bf16[144,128]{1,0:T(8,128)(2,1)S(1)}, u32[]{:S(2)}, u32[]{:S(2)}) collective-permute-start(bf16[144,128]{1,0:T(8,128)(2,1)S(1)} %get-tuple-element.36), channel_id=1, source_target_pairs={{0,2},{1,3},{2,0},{3,1},{4,6},{5,7},{6,4},{7,5},{8,10},{9,11},{10,... | collective-permute-start | bytes 110600 | tf_op jit(solution)/shard_map/ppermute | solution.py:306
  56.4 6.8 %collective-permute-start.9 = (bf16[144,128]{1,0:T(8,128)(2,1)S(1)}, bf16[144,128]{1,0:T(8,128)(2,1)S(1)}, u32[]{:S(2)}, u32[]{:S(2)}) collective-permute-start(bf16[144,128]{1,0:T(8,128)(2,1)S(1)} %get-tuple-element.37), channel_id=1, source_target_pairs={{0,4},{1,5},{2,6},{3,7},{4,0},{5,1},{6,2},{7,3},{8,12},{9,13},{10,... | collective-permute-start | bytes 110600 | tf_op jit(solution)/shard_map/ppermute | solution.py:306
  63.4 1.3 %collective-permute-start.11 = (bf16[128,128]{1,0:T(8,128)(2,1)S(1)}, bf16[128,128]{1,0:T(8,128)(2,1)S(1)}, u32[]{:S(2)}, u32[]{:S(2)}) collective-permute-start(bf16[128,128]{1,0:T(8,128)(2,1)S(1)} %shard_map.77.own_ref), channel_id=1, source_target_pairs={{0,1},{1,0},{2,3},{3,2},{4,5},{5,4},{6,7},{7,6},{8,9},{9,8},{10,11... | collective-permute-start | bytes 98312 | tf_op jit(solution)/shard_map/ppermute | solution.py:306
  65.7 6.0 %collective-permute-start.15 = (bf16[128,512]{1,0:T(8,128)(2,1)S(1)}, bf16[128,512]{1,0:T(8,128)(2,1)S(1)}, u32[]{:S(2)}, u32[]{:S(2)}) collective-permute-start(bf16[128,512]{1,0:T(8,128)(2,1)S(1)} %get-tuple-element.42), channel_id=1, source_target_pairs={{0,8},{8,0},{16,24},{24,16},{1,9},{9,1},{17,25},{25,17},{2,10},{10... | collective-permute-start | bytes 393224 | tf_op jit(solution)/shard_map/ppermute | solution.py:309
  67.3 8.1 %collective-permute-start.16 = (bf16[128,512]{1,0:T(8,128)(2,1)S(1)}, bf16[128,512]{1,0:T(8,128)(2,1)S(1)}, u32[]{:S(2)}, u32[]{:S(2)}) collective-permute-start(bf16[128,512]{1,0:T(8,128)(2,1)S(1)} %get-tuple-element.43), channel_id=1, source_target_pairs={{0,16},{8,24},{16,0},{24,8},{1,17},{9,25},{17,1},{25,9},{2,18},{10... | collective-permute-start | bytes 393224 | tf_op jit(solution)/shard_map/ppermute | solution.py:309
  68.8 6.6 %collective-permute-start.17 = (bf16[128,512]{1,0:T(8,128)(2,1)S(1)}, bf16[128,512]{1,0:T(8,128)(2,1)S(1)}, u32[]{:S(2)}, u32[]{:S(2)}) collective-permute-start(bf16[128,512]{1,0:T(8,128)(2,1)S(1)} %get-tuple-element.44), channel_id=1, source_target_pairs={{0,24},{8,16},{16,8},{24,0},{1,25},{9,17},{17,9},{25,1},{2,26},{10... | collective-permute-start | bytes 393224 | tf_op jit(solution)/shard_map/ppermute | solution.py:309
  75.4 1.3 %collective-permute-start.18 = (bf16[64,512]{1,0:T(8,128)(2,1)S(1)}, bf16[64,512]{1,0:T(8,128)(2,1)S(1)}, u32[]{:S(2)}, u32[]{:S(2)}) collective-permute-start(bf16[64,512]{1,0:T(8,128)(2,1)S(1)} %get-tuple-element.46), channel_id=1, source_target_pairs={{0,1},{1,0},{2,3},{3,2},{4,5},{5,4},{6,7},{7,6},{8,9},{9,8},{10,11... | collective-permute-start | bytes 196616 | tf_op jit(solution)/shard_map/ppermute | solution.py:306

commit v13 on v12

--- a/solution.py
+++ b/solution.py
@@ -345,11 +345,11 @@
         firsts, slot_groups, places, slices, blocks, acc, offsets, groups, heads, depth
     )
     arrived = [messages[0]] + [across(messages[j], CORES * j) for j in range(1, chips)]
-    shards = [after(w_out, *pairs[1], *pairs[2])] + [None] * (chips - 1)
+    shards = [after(w_out, first_acc, *pairs[1], *pairs[2])] + [None] * (chips - 1)
     for j in near_first:
         low = j & -j
         shard = shards[j ^ low]
-        shards[j] = across(shard if j == low else after(shard, messages[0]), CORES * low)
+        shards[j] = across(shard if j == low else after(shard, acc, *pairs[-1]), CORES * low)
     normed = combine(core_only, arrived, head_gain.reshape(1, panel), heads)
 
     terms = output_terms(

time: 77.7 us -> 78.9 us (1.015)
  waiting for transfers between devices: 38.9 us -> 35.2 us
  starting transfers between devices: 20.1 us -> 22.4 us
  local copies, waits for them, and re-layouts: 4.15 us -> 6.33 us
    ppermute x16, waiting for transfers between devices: 32.8 us -> 29.1 us  [across(): return lax.ppermute(array, 'ctx', [(i, i ^ bits) for i in range(n_ctx)])]
    ppermute x16, starting transfers between devices: 16.6 us -> 18.9 us  [across(): return lax.ppermute(array, 'ctx', [(i, i ^ bits) for i in range(n_ctx)])]
    unnamed x10 -> x12, local copies, waits for them, and re-layouts: 3.16 us -> 5.34 us
  transfers between devices with their start and end apart: 19 -> 19, of which waited for: 11 -> 13; matrix products, arithmetic and copies ran while one was open for 2% -> 1% of each run, Pallas kernels for 13% -> 13%
where the time goes in v13:
time: 78.9 us; the launch traced here: 78.6 us
  waiting for transfers between devices  35.2 us (45%)
  starting transfers between devices  22.4 us (28%)
  Pallas kernels  13.7 us (17%)
  local copies, waits for them, and re-layouts  6.33 us (8%)
  other arithmetic  0.85 us (1%)
    ppermute x16, waiting for transfers between devices, across(): return lax.ppermute(array, 'ctx', [(i, i ^ bits) for i in range(n_ctx)])  29.1 us
    ppermute x16, starting transfers between devices, across(): return lax.ppermute(array, 'ctx', [(i, i ^ bits) for i in range(n_ctx)])  18.9 us
    pallas_call x2, Pallas kernels, project(): pl.pallas_call(functools.partial(project_kernel, count, extra, acc is not...  7.19 us
    ppermute x3, waiting for transfers between devices, over_dp(): return lax.ppermute(array, 'dp', [(d, d ^ bits) for d in range(n_dp)])  6.1 us
    unnamed x12, local copies, waits for them, and re-layouts  5.34 us
    ppermute x3, starting transfers between devices, over_dp(): return lax.ppermute(array, 'dp', [(d, d ^ bits) for d in range(n_dp)])  3.55 us
    pallas_call x1, Pallas kernels, attend(): pl.pallas_call(functools.partial(attend_kernel, count, heads, depth, grou...  2.81 us
    pallas_call x1, Pallas kernels, pack(): pl.pallas_call(pack_kernel, out_shape=[out, out], in_specs=[SMEM, ANY, AN...  2.02 us
  transfers between devices with their start and end apart: 19, of which 13 were waited for; matrix products, arithmetic and copies ran while one was open for 1% of the time, Pallas kernels for 13%

profile of v13, /device:TPU:0, one launch (start us, length us, event | category | flops | bytes accessed | tf_op | source)
XLA Modules:
  0.0 78.6 jit_solution(13799685626040320818)
XLA Ops:
  0.0 2.0 %shard_map.73 = (bf16[544,256]{1,0:T(8,128)(2,1)}, bf16[544,256]{1,0:T(8,128)(2,1)}) custom-call(s32[1]{0:T(128)} %bitcast.core_ref, bf16[512,256]{1,0:T(8,128)(2,1)} %key_ref.1, bf16[512,256]{1,0:T(8,128)(2,1)} %value_ref.1, bf16[64,256]{1,0:T(8,128)(2,1)} %query_ref.1), custom_call_target="tpu_custom_call" | custom-call | tf_op jit(solution)/shard_map/pallas_call | solution.py:235
  2.0 0.5 collective-permute-start
  2.5 2.7 %collective-permute-start.1 = (bf16[544,256]{1,0:T(8,128)(2,1)}, bf16[544,256]{1,0:T(8,128)(2,1)S(1)}, u32[]{:S(2)}, u32[]{:S(2)}) collective-permute-start(bf16[544,256]{1,0:T(8,128)(2,1)} %get-tuple-element.26.refs_3_.refs_4_), channel_id=1, source_target_pairs={{0,2},{1,3},{2,0},{3,1},{4,6},{5,7},{6,4},{7,5},{8,10},{9,11},{10,... | collective-permute-start | bytes 835592 | tf_op jit(solution)/shard_map/ppermute | solution.py:306
  5.2 2.6 %collective-permute-start.3 = (bf16[544,256]{1,0:T(8,128)(2,1)}, bf16[544,256]{1,0:T(8,128)(2,1)S(1)}, u32[]{:S(2)}, u32[]{:S(2)}) collective-permute-start(bf16[544,256]{1,0:T(8,128)(2,1)} %get-tuple-element.26.refs_3_.refs_4_), channel_id=1, source_target_pairs={{0,4},{1,5},{2,6},{3,7},{4,0},{5,1},{6,2},{7,3},{8,12},{9,13},{10,... | collective-permute-start | bytes 835592 | tf_op jit(solution)/shard_map/ppermute | solution.py:306
  7.8 0.0 collective-permute-start.2
  7.8 0.2 collective-permute-start.4
  8.0 0.1 stack.71.refs_2_
  8.0 1.6 %collective-permute-done.refs_2_ = bf16[512,4096]{1,0:T(8,128)(2,1)} collective-permute-done((bf16[512,4096]{1,0:T(8,128)(2,1)}, bf16[512,4096]{1,0:T(8,128)(2,1)}, u32[]{:S(2)}, u32[]{:S(2)}) %collective-permute-start) | collective-permute-done | bytes 4194336 | tf_op jit(solution)/shard_map/ppermute | solution.py:306
  9.7 0.4 collective-permute-start.5
  10.0 0.8 %slice_bitcast_fusion.3 = (s32[1,128]{1,0:T(1,128)S(1)}, s32[1,128]{1,0:T(1,128)S(1)}, s32[1,128]{1,0:T(1,128)S(1)}, s32[1,128]{1,0:T(1,128)S(1)}) fusion(s32[512]{0:T(512)} %param.11), kind=kLoop, calls=%fused_computation.7 | loop fusion | bytes 4096 | tf_op jit(solution)/shard_map/stack | solution.py:152
  10.9 7.9 %collective-permute-done.1.refs_3_.refs_6_ = bf16[544,256]{1,0:T(8,128)(2,1)S(1)} collective-permute-done((bf16[544,256]{1,0:T(8,128)(2,1)}, bf16[544,256]{1,0:T(8,128)(2,1)S(1)}, u32[]{:S(2)}, u32[]{:S(2)}) %collective-permute-start.1) | collective-permute-done | bytes 278560 | tf_op jit(solution)/shard_map/ppermute | solution.py:306
  18.8 3.2 %collective-permute-done.3.refs_5_.refs_8_ = bf16[544,256]{1,0:T(8,128)(2,1)S(1)} collective-permute-done((bf16[544,256]{1,0:T(8,128)(2,1)}, bf16[544,256]{1,0:T(8,128)(2,1)S(1)}, u32[]{:S(2)}, u32[]{:S(2)}) %collective-permute-start.3) | collective-permute-done | bytes 278560 | tf_op jit(solution)/shard_map/ppermute | solution.py:306
  21.9 0.0 collective-permute-start.6
  21.9 0.0 collective-permute-done.5.refs_4_.refs_5_
  21.9 0.0 copy-start
  21.9 2.2 %copy-done = bf16[512,4096]{1,0:T(8,128)(2,1)S(1)} copy-done((bf16[512,4096]{1,0:T(8,128)(2,1)S(1)}, bf16[512,4096]{1,0:T(8,128)(2,1)}, u32[]{:S(2)}) %copy-start) | copy-done | bytes 4194328
  24.1 0.0 copy-start.2
  24.1 1.0 %copy-done.2 = bf16[544,256]{1,0:T(8,128)(2,1)S(1)} copy-done((bf16[544,256]{1,0:T(8,128)(2,1)S(1)}, bf16[544,256]{1,0:T(8,128)(2,1)}, u32[]{:S(2)}) %copy-start.2) | copy-done | bytes 278552
  25.1 0.0 copy-start.4
  25.1 3.1 %shard_map.74 = (f32[1024,256]{1,0:T(8,128)S(1)}, bf16[2,16,512]{2,1,0:T(8,128)(2,1)}) custom-call(s32[2]{0:T(128)S(1)} %bitcast.21, bf16[512,4096]{1,0:T(8,128)(2,1)S(1)} %copy-done, bf16[512,4096]{1,0:T(8,128)(2,1)} %collective-permute-done.refs_2_, bf16[544,256]{1,0:T(8,128)(2,1)S(1)} %copy-done.2, bf16[544,256]{1,0:T(8,128)(2,1)S(1)} %collective-permute-done.5.refs_4_.refs_5_), custom_call_target="tpu_custom_call" | custom-call | flops 536870912 | bytes 2097152 | tf_op jit(solution)/shard_map/pallas_call | solution.py:81
  28.1 2.0 %collective-permute-done.2.refs_4_.refs_7_ = bf16[544,256]{1,0:T(8,128)(2,1)S(1)} collective-permute-done((bf16[544,256]{1,0:T(8,128)(2,1)}, bf16[544,256]{1,0:T(8,128)(2,1)S(1)}, u32[]{:S(2)}, u32[]{:S(2)}) %collective-permute-start.2) | collective-permute-done | bytes 278560 | tf_op jit(solution)/shard_map/ppermute | solution.py:306
  30.2 0.3 collective-permute-done.4.refs_6_.refs_9_
  30.5 2.5 %collective-permute-start.7 = (bf16[544,256]{1,0:T(8,128)(2,1)S(1)}, bf16[544,256]{1,0:T(8,128)(2,1)S(1)}, u32[]{:S(2)}, u32[]{:S(2)}) collective-permute-start(bf16[544,256]{1,0:T(8,128)(2,1)S(1)} %collective-permute-done.4.refs_6_.refs_9_), channel_id=1, source_target_pairs={{0,2},{1,3},{2,0},{3,1},{4,6},{5,7},{6,4},{7,5},{8,10},{9,11},{10,... | collective-permute-start | bytes 835592 | tf_op jit(solution)/shard_map/ppermute | solution.py:306
  33.0 0.0 copy-done.4
  33.0 2.4 %collective-permute-start.13 = (bf16[256,512]{1,0:T(8,128)(2,1)S(1)}, bf16[256,512]{1,0:T(8,128)(2,1)S(1)}, u32[]{:S(2)}, u32[]{:S(2)}) collective-permute-start(bf16[256,512]{1,0:T(8,128)(2,1)S(1)} %copy-done.4), channel_id=1, source_target_pairs={{0,4},{1,5},{2,6},{3,7},{4,0},{5,1},{6,2},{7,3},{8,12},{9,13},{10,... | collective-permute-start | bytes 786440 | tf_op jit(solution)/shard_map/ppermute | solution.py:306
  35.4 0.1 slice.8.refs_0_
  35.5 0.1 collective-permute-start.12
  35.5 0.0 copy-start.1
  35.5 2.2 %copy-done.1 = bf16[512,4096]{1,0:T(8,128)(2,1)S(1)} copy-done((bf16[512,4096]{1,0:T(8,128)(2,1)S(1)}, bf16[512,4096]{1,0:T(8,128)(2,1)}, u32[]{:S(2)}) %copy-start.1) | copy-done | bytes 4194328
  37.7 0.0 copy-start.3
  37.7 4.1 %shard_map.75 = (f32[1024,256]{1,0:T(8,128)S(1)}, bf16[4,512,512]{2,1,0:T(8,128)(2,1)S(1)}) custom-call(s32[6]{0:T(128)S(1)} %slice.8.refs_0_, bf16[512,4096]{1,0:T(8,128)(2,1)S(1)} %copy-done.1, bf16[512,4096]{1,0:T(8,128)(2,1)} %collective-permute-done.refs_2_, bf16[544,256]{1,0:T(8,128)(2,1)S(1)} %collective-permute-done.1.refs_3_.refs_6_, ...), custom_call_target="tpu_custom_call" | custom-call | flops 1073741824 | bytes 4194304 | tf_op jit(solution)/shard_map/pallas_call | solution.py:81
  41.9 0.0 copy-start.5
  41.9 0.0 collective-permute-done.6.refs_10_
  41.9 6.0 %collective-permute-done.13.refs_2_ = bf16[256,512]{1,0:T(8,128)(2,1)S(1)} collective-permute-done((bf16[256,512]{1,0:T(8,128)(2,1)S(1)}, bf16[256,512]{1,0:T(8,128)(2,1)S(1)}, u32[]{:S(2)}, u32[]{:S(2)}) %collective-permute-start.13) | collective-permute-done | bytes 262176 | tf_op jit(solution)/shard_map/ppermute | solution.py:306
  47.9 0.4 collective-permute-done.7.refs_11_
  48.4 3.1 %collective-permute-start.14 = (bf16[256,512]{1,0:T(8,128)(2,1)S(1)}, bf16[256,512]{1,0:T(8,128)(2,1)S(1)}, u32[]{:S(2)}, u32[]{:S(2)}) collective-permute-start(bf16[256,512]{1,0:T(8,128)(2,1)S(1)} %collective-permute-done.13.refs_2_), channel_id=1, source_target_pairs={{0,2},{1,3},{2,0},{3,1},{4,6},{5,7},{6,4},{7,5},{8,10},{9,11},{10,... | collective-permute-start | bytes 786440 | tf_op jit(solution)/shard_map/ppermute | solution.py:306
  51.4 0.1 pad_add_fusion.2.refs_0_
  51.5 0.0 copy-done.3
  51.5 2.8 %shard_map.76 = (bf16[144,128]{1,0:T(8,128)(2,1)S(1)}, bf16[144,128]{1,0:T(8,128)(2,1)S(1)}, bf16[144,128]{1,0:T(8,128)(2,1)S(1)}, bf16[144,128]{1,0:T(8,128)(2,1)S(1)}) custom-call(s32[2]{0:T(128)S(1)} %pad_add_fusion.2.refs_0_, s32[4]{0:T(128)S(1)} %iota_xor_fusion.refs_1_, s32[8]{0:T(128)S(1)} %stack.71.refs_2_, ...), custom_call_target="tpu_custom_call" | custom-call | flops 536870912 | bytes 2097152 | tf_op jit(solution)/shard_map/pallas_call | solution.py:158
  54.3 0.1 collective-permute-start.8
  54.4 1.9 %collective-permute-start.9 = (bf16[144,128]{1,0:T(8,128)(2,1)S(1)}, bf16[144,128]{1,0:T(8,128)(2,1)S(1)}, u32[]{:S(2)}, u32[]{:S(2)}) collective-permute-start(bf16[144,128]{1,0:T(8,128)(2,1)S(1)} %get-tuple-element.37), channel_id=1, source_target_pairs={{0,4},{1,5},{2,6},{3,7},{4,0},{5,1},{6,2},{7,3},{8,12},{9,13},{10,... | collective-permute-start | bytes 110600 | tf_op jit(solution)/shard_map/ppermute | solution.py:306
  56.3 2.5 %collective-permute-start.10 = (bf16[144,128]{1,0:T(8,128)(2,1)S(1)}, bf16[144,128]{1,0:T(8,128)(2,1)S(1)}, u32[]{:S(2)}, u32[]{:S(2)}) collective-permute-start(bf16[144,128]{1,0:T(8,128)(2,1)S(1)} %get-tuple-element.38), channel_id=1, source_target_pairs={{0,6},{1,7},{2,4},{3,5},{4,2},{5,3},{6,0},{7,1},{8,14},{9,15},{10,... | collective-permute-start | bytes 110600 | tf_op jit(solution)/shard_map/ppermute | solution.py:306
  58.8 0.0 copy-done.5
  58.8 2.1 %collective-permute-done.8.refs_1_ = bf16[144,128]{1,0:T(8,128)(2,1)S(1)} collective-permute-done((bf16[144,128]{1,0:T(8,128)(2,1)S(1)}, bf16[144,128]{1,0:T(8,128)(2,1)S(1)}, u32[]{:S(2)}, u32[]{:S(2)}) %collective-permute-start.8) | collective-permute-done | bytes 36896 | tf_op jit(solution)/shard_map/ppermute | solution.py:306
  60.9 0.0 collective-permute-done.9.refs_2_
  60.9 3.1 %collective-permute-done.10.refs_3_ = bf16[144,128]{1,0:T(8,128)(2,1)S(1)} collective-permute-done((bf16[144,128]{1,0:T(8,128)(2,1)S(1)}, bf16[144,128]{1,0:T(8,128)(2,1)S(1)}, u32[]{:S(2)}, u32[]{:S(2)}) %collective-permute-start.10) | collective-permute-done | bytes 36896 | tf_op jit(solution)/shard_map/ppermute | solution.py:306
  64.0 0.2 shard_map.77.own_ref
  64.2 0.1 collective-permute-start.11
  64.3 0.1 pad_add_fusion.1.place_ref
  64.3 0.0 collective-permute-done.12.refs_1_
  64.4 1.1 %collective-permute-done.11.sibling_ref = bf16[128,128]{1,0:T(8,128)(2,1)S(1)} collective-permute-done((bf16[128,128]{1,0:T(8,128)(2,1)S(1)}, bf16[128,128]{1,0:T(8,128)(2,1)S(1)}, u32[]{:S(2)}, u32[]{:S(2)}) %collective-permute-start.11) | collective-permute-done | bytes 32800 | tf_op jit(solution)/shard_map/ppermute | solution.py:306
  65.5 0.0 collective-permute-done.14.refs_3_
  65.5 1.4 %shard_map.78 = (bf16[128,512]{1,0:T(8,128)(2,1)S(1)}, bf16[128,512]{1,0:T(8,128)(2,1)S(1)}, bf16[128,512]{1,0:T(8,128)(2,1)S(1)}, bf16[128,512]{1,0:T(8,128)(2,1)S(1)}) custom-call(s32[2]{0:T(128)S(1)} %pad_add_fusion.1.place_ref, bf16[128,128]{1,0:T(8,128)(2,1)S(1)} %shard_map.77.own_ref, bf16[128,128]{1,0:T(8,128)(2,1)S(1)} %collective-permute-done.11.sibling_ref, ...), custom_call_target="tpu_custom_call" | custom-call | tf_op jit(solution)/shard_map/pallas_call | solution.py:262
  66.9 1.6 %collective-permute-start.15 = (bf16[128,512]{1,0:T(8,128)(2,1)S(1)}, bf16[128,512]{1,0:T(8,128)(2,1)S(1)}, u32[]{:S(2)}, u32[]{:S(2)}) collective-permute-start(bf16[128,512]{1,0:T(8,128)(2,1)S(1)} %get-tuple-element.42), channel_id=1, source_target_pairs={{0,8},{8,0},{16,24},{24,16},{1,9},{9,1},{17,25},{25,17},{2,10},{10... | collective-permute-start | bytes 393224 | tf_op jit(solution)/shard_map/ppermute | solution.py:309
  68.4 1.5 %collective-permute-start.16 = (bf16[128,512]{1,0:T(8,128)(2,1)S(1)}, bf16[128,512]{1,0:T(8,128)(2,1)S(1)}, u32[]{:S(2)}, u32[]{:S(2)}) collective-permute-start(bf16[128,512]{1,0:T(8,128)(2,1)S(1)} %get-tuple-element.43), channel_id=1, source_target_pairs={{0,16},{8,24},{16,0},{24,8},{1,17},{9,25},{17,1},{25,9},{2,18},{10... | collective-permute-start | bytes 393224 | tf_op jit(solution)/shard_map/ppermute | solution.py:309
  70.0 0.5 collective-permute-start.17
  70.4 2.4 %collective-permute-done.15.refs_1_ = bf16[128,512]{1,0:T(8,128)(2,1)S(1)} collective-permute-done((bf16[128,512]{1,0:T(8,128)(2,1)S(1)}, bf16[128,512]{1,0:T(8,128)(2,1)S(1)}, u32[]{:S(2)}, u32[]{:S(2)}) %collective-permute-start.15) | collective-permute-done | bytes 131104 | tf_op jit(solution)/shard_map/ppermute | solution.py:309
  72.9 3.7 %collective-permute-done.16.refs_2_ = bf16[128,512]{1,0:T(8,128)(2,1)S(1)} collective-permute-done((bf16[128,512]{1,0:T(8,128)(2,1)S(1)}, bf16[128,512]{1,0:T(8,128)(2,1)S(1)}, u32[]{:S(2)}, u32[]{:S(2)}) %collective-permute-start.16) | collective-permute-done | bytes 131104 | tf_op jit(solution)/shard_map/ppermute | solution.py:309
  76.5 0.0 collective-permute-done.17.refs_3_
  76.5 0.1 shard_map.79
  76.6 0.1 collective-permute-start.18
  76.7 1.2 %collective-permute-done.18 = bf16[64,512]{1,0:T(8,128)(2,1)S(1)} collective-permute-done((bf16[64,512]{1,0:T(8,128)(2,1)S(1)}, bf16[64,512]{1,0:T(8,128)(2,1)S(1)}, u32[]{:S(2)}, u32[]{:S(2)}) %collective-permute-start.18) | collective-permute-done | bytes 65568 | tf_op jit(solution)/shard_map/ppermute | solution.py:306
  77.9 0.7 maximum_select_fusion
  (4 shorter events, 0.0 us)
Async XLA Ops:
  2.0 7.6 %collective-permute-start = (bf16[512,4096]{1,0:T(8,128)(2,1)}, bf16[512,4096]{1,0:T(8,128)(2,1)}, u32[]{:S(2)}, u32[]{:S(2)}) collective-permute-start(bf16[512,4096]{1,0:T(8,128)(2,1)} %refs_1_.3), channel_id=1, source_target_pairs={{0,1},{1,0},{2,3},{3,2},{4,5},{5,4},{6,7},{7,6},{8,9},{9,8},{10,11... | collective-permute-start | bytes 12582920 | tf_op jit(solution)/shard_map/ppermute | solution.py:306
  2.5 16.2 %collective-permute-start.1 = (bf16[544,256]{1,0:T(8,128)(2,1)}, bf16[544,256]{1,0:T(8,128)(2,1)S(1)}, u32[]{:S(2)}, u32[]{:S(2)}) collective-permute-start(bf16[544,256]{1,0:T(8,128)(2,1)} %get-tuple-element.26.refs_3_.refs_4_), channel_id=1, source_target_pairs={{0,2},{1,3},{2,0},{3,1},{4,6},{5,7},{6,4},{7,5},{8,10},{9,11},{10,... | collective-permute-start | bytes 835592 | tf_op jit(solution)/shard_map/ppermute | solution.py:306
  5.2 16.7 %collective-permute-start.3 = (bf16[544,256]{1,0:T(8,128)(2,1)}, bf16[544,256]{1,0:T(8,128)(2,1)S(1)}, u32[]{:S(2)}, u32[]{:S(2)}) collective-permute-start(bf16[544,256]{1,0:T(8,128)(2,1)} %get-tuple-element.26.refs_3_.refs_4_), channel_id=1, source_target_pairs={{0,4},{1,5},{2,6},{3,7},{4,0},{5,1},{6,2},{7,3},{8,12},{9,13},{10,... | collective-permute-start | bytes 835592 | tf_op jit(solution)/shard_map/ppermute | solution.py:306
  7.8 22.4 %collective-permute-start.2 = (bf16[544,256]{1,0:T(8,128)(2,1)}, bf16[544,256]{1,0:T(8,128)(2,1)S(1)}, u32[]{:S(2)}, u32[]{:S(2)}) collective-permute-start(bf16[544,256]{1,0:T(8,128)(2,1)} %get-tuple-element.29), channel_id=1, source_target_pairs={{0,3},{1,2},{2,1},{3,0},{4,7},{5,6},{6,5},{7,4},{8,11},{9,10},{10,... | collective-permute-start | bytes 835592 | tf_op jit(solution)/shard_map/ppermute | solution.py:306
  7.8 22.7 %collective-permute-start.4 = (bf16[544,256]{1,0:T(8,128)(2,1)}, bf16[544,256]{1,0:T(8,128)(2,1)S(1)}, u32[]{:S(2)}, u32[]{:S(2)}) collective-permute-start(bf16[544,256]{1,0:T(8,128)(2,1)} %get-tuple-element.29), channel_id=1, source_target_pairs={{0,5},{1,4},{2,7},{3,6},{4,1},{5,0},{6,3},{7,2},{8,13},{9,12},{10,... | collective-permute-start | bytes 835592 | tf_op jit(solution)/shard_map/ppermute | solution.py:306
  9.7 12.2 %collective-permute-start.5 = (bf16[544,256]{1,0:T(8,128)(2,1)}, bf16[544,256]{1,0:T(8,128)(2,1)S(1)}, u32[]{:S(2)}, u32[]{:S(2)}) collective-permute-start(bf16[544,256]{1,0:T(8,128)(2,1)} %get-tuple-element.29), channel_id=1, source_target_pairs={{0,1},{1,0},{2,3},{3,2},{4,5},{5,4},{6,7},{7,6},{8,9},{9,8},{10,11... | collective-permute-start | bytes 835592 | tf_op jit(solution)/shard_map/ppermute | solution.py:306
  21.9 20.0 %collective-permute-start.6 = (bf16[544,256]{1,0:T(8,128)(2,1)S(1)}, bf16[544,256]{1,0:T(8,128)(2,1)S(1)}, u32[]{:S(2)}, u32[]{:S(2)}) collective-permute-start(bf16[544,256]{1,0:T(8,128)(2,1)S(1)} %collective-permute-done.3.refs_5_.refs_8_), channel_id=1, source_target_pairs={{0,2},{1,3},{2,0},{3,1},{4,6},{5,7},{6,4},{7,5},{8,10},{9,11},{10,... | collective-permute-start | bytes 835592 | tf_op jit(solution)/shard_map/ppermute | solution.py:306
  21.9 2.2 %copy-start = (bf16[512,4096]{1,0:T(8,128)(2,1)S(1)}, bf16[512,4096]{1,0:T(8,128)(2,1)}, u32[]{:S(2)}) copy-start(bf16[512,4096]{1,0:T(8,128)(2,1)} %refs_1_.3) | copy-start | bytes 12582916
  24.1 1.0 %copy-start.2 = (bf16[544,256]{1,0:T(8,128)(2,1)S(1)}, bf16[544,256]{1,0:T(8,128)(2,1)}, u32[]{:S(2)}) copy-start(bf16[544,256]{1,0:T(8,128)(2,1)} %get-tuple-element.26.refs_3_.refs_4_) | copy-start | bytes 835588
  25.1 7.9 %copy-start.4 = (bf16[256,512]{1,0:T(8,128)(2,1)S(1)}, bf16[256,512]{1,0:T(8,128)(2,1)}, u32[]{:S(2)}) copy-start(bf16[256,512]{1,0:T(8,128)(2,1)} %refs_0_) | copy-start | bytes 786436
  30.5 17.9 %collective-permute-start.7 = (bf16[544,256]{1,0:T(8,128)(2,1)S(1)}, bf16[544,256]{1,0:T(8,128)(2,1)S(1)}, u32[]{:S(2)}, u32[]{:S(2)}) collective-permute-start(bf16[544,256]{1,0:T(8,128)(2,1)S(1)} %collective-permute-done.4.refs_6_.refs_9_), channel_id=1, source_target_pairs={{0,2},{1,3},{2,0},{3,1},{4,6},{5,7},{6,4},{7,5},{8,10},{9,11},{10,... | collective-permute-start | bytes 835592 | tf_op jit(solution)/shard_map/ppermute | solution.py:306
  33.0 14.9 %collective-permute-start.13 = (bf16[256,512]{1,0:T(8,128)(2,1)S(1)}, bf16[256,512]{1,0:T(8,128)(2,1)S(1)}, u32[]{:S(2)}, u32[]{:S(2)}) collective-permute-start(bf16[256,512]{1,0:T(8,128)(2,1)S(1)} %copy-done.4), channel_id=1, source_target_pairs={{0,4},{1,5},{2,6},{3,7},{4,0},{5,1},{6,2},{7,3},{8,12},{9,13},{10,... | collective-permute-start | bytes 786440 | tf_op jit(solution)/shard_map/ppermute | solution.py:306
  35.5 28.9 %collective-permute-start.12 = (bf16[256,512]{1,0:T(8,128)(2,1)S(1)}, bf16[256,512]{1,0:T(8,128)(2,1)}, u32[]{:S(2)}, u32[]{:S(2)}) collective-permute-start(bf16[256,512]{1,0:T(8,128)(2,1)S(1)} %copy-done.4), channel_id=1, source_target_pairs={{0,2},{1,3},{2,0},{3,1},{4,6},{5,7},{6,4},{7,5},{8,10},{9,11},{10,... | collective-permute-start | bytes 786440 | tf_op jit(solution)/shard_map/ppermute | solution.py:306
  35.5 2.2 %copy-start.1 = (bf16[512,4096]{1,0:T(8,128)(2,1)S(1)}, bf16[512,4096]{1,0:T(8,128)(2,1)}, u32[]{:S(2)}) copy-start(bf16[512,4096]{1,0:T(8,128)(2,1)} %refs_1_.3) | copy-start | bytes 12582916
  37.7 13.8 %copy-start.3 = (bf16[544,256]{1,0:T(8,128)(2,1)S(1)}, bf16[544,256]{1,0:T(8,128)(2,1)}, u32[]{:S(2)}) copy-start(bf16[544,256]{1,0:T(8,128)(2,1)} %get-tuple-element.26.refs_3_.refs_4_) | copy-start | bytes 835588
  41.9 16.9 %copy-start.5 = (bf16[256]{0:T(256)(128)(2,1)S(1)}, bf16[256]{0:T(256)(128)(2,1)}, u32[]{:S(2)}) copy-start(bf16[256]{0:T(256)(128)(2,1)} %param.12) | copy-start | bytes 1540
  48.4 17.1 %collective-permute-start.14 = (bf16[256,512]{1,0:T(8,128)(2,1)S(1)}, bf16[256,512]{1,0:T(8,128)(2,1)S(1)}, u32[]{:S(2)}, u32[]{:S(2)}) collective-permute-start(bf16[256,512]{1,0:T(8,128)(2,1)S(1)} %collective-permute-done.13.refs_2_), channel_id=1, source_target_pairs={{0,2},{1,3},{2,0},{3,1},{4,6},{5,7},{6,4},{7,5},{8,10},{9,11},{10,... | collective-permute-start | bytes 786440 | tf_op jit(solution)/shard_map/ppermute | solution.py:306
  54.3 6.6 %collective-permute-start.8 = (bf16[144,128]{1,0:T(8,128)(2,1)S(1)}, bf16[144,128]{1,0:T(8,128)(2,1)S(1)}, u32[]{:S(2)}, u32[]{:S(2)}) collective-permute-start(bf16[144,128]{1,0:T(8,128)(2,1)S(1)} %get-tuple-element.36), channel_id=1, source_target_pairs={{0,2},{1,3},{2,0},{3,1},{4,6},{5,7},{6,4},{7,5},{8,10},{9,11},{10,... | collective-permute-start | bytes 110600 | tf_op jit(solution)/shard_map/ppermute | solution.py:306
  54.4 6.5 %collective-permute-start.9 = (bf16[144,128]{1,0:T(8,128)(2,1)S(1)}, bf16[144,128]{1,0:T(8,128)(2,1)S(1)}, u32[]{:S(2)}, u32[]{:S(2)}) collective-permute-start(bf16[144,128]{1,0:T(8,128)(2,1)S(1)} %get-tuple-element.37), channel_id=1, source_target_pairs={{0,4},{1,5},{2,6},{3,7},{4,0},{5,1},{6,2},{7,3},{8,12},{9,13},{10,... | collective-permute-start | bytes 110600 | tf_op jit(solution)/shard_map/ppermute | solution.py:306
  56.3 7.7 %collective-permute-start.10 = (bf16[144,128]{1,0:T(8,128)(2,1)S(1)}, bf16[144,128]{1,0:T(8,128)(2,1)S(1)}, u32[]{:S(2)}, u32[]{:S(2)}) collective-permute-start(bf16[144,128]{1,0:T(8,128)(2,1)S(1)} %get-tuple-element.38), channel_id=1, source_target_pairs={{0,6},{1,7},{2,4},{3,5},{4,2},{5,3},{6,0},{7,1},{8,14},{9,15},{10,... | collective-permute-start | bytes 110600 | tf_op jit(solution)/shard_map/ppermute | solution.py:306
  64.2 1.3 %collective-permute-start.11 = (bf16[128,128]{1,0:T(8,128)(2,1)S(1)}, bf16[128,128]{1,0:T(8,128)(2,1)S(1)}, u32[]{:S(2)}, u32[]{:S(2)}) collective-permute-start(bf16[128,128]{1,0:T(8,128)(2,1)S(1)} %shard_map.77.own_ref), channel_id=1, source_target_pairs={{0,1},{1,0},{2,3},{3,2},{4,5},{5,4},{6,7},{7,6},{8,9},{9,8},{10,11... | collective-permute-start | bytes 98312 | tf_op jit(solution)/shard_map/ppermute | solution.py:306
  66.9 6.0 %collective-permute-start.15 = (bf16[128,512]{1,0:T(8,128)(2,1)S(1)}, bf16[128,512]{1,0:T(8,128)(2,1)S(1)}, u32[]{:S(2)}, u32[]{:S(2)}) collective-permute-start(bf16[128,512]{1,0:T(8,128)(2,1)S(1)} %get-tuple-element.42), channel_id=1, source_target_pairs={{0,8},{8,0},{16,24},{24,16},{1,9},{9,1},{17,25},{25,17},{2,10},{10... | collective-permute-start | bytes 393224 | tf_op jit(solution)/shard_map/ppermute | solution.py:309
  68.4 8.1 %collective-permute-start.16 = (bf16[128,512]{1,0:T(8,128)(2,1)S(1)}, bf16[128,512]{1,0:T(8,128)(2,1)S(1)}, u32[]{:S(2)}, u32[]{:S(2)}) collective-permute-start(bf16[128,512]{1,0:T(8,128)(2,1)S(1)} %get-tuple-element.43), channel_id=1, source_target_pairs={{0,16},{8,24},{16,0},{24,8},{1,17},{9,25},{17,1},{25,9},{2,18},{10... | collective-permute-start | bytes 393224 | tf_op jit(solution)/shard_map/ppermute | solution.py:309
  70.0 6.6 %collective-permute-start.17 = (bf16[128,512]{1,0:T(8,128)(2,1)S(1)}, bf16[128,512]{1,0:T(8,128)(2,1)S(1)}, u32[]{:S(2)}, u32[]{:S(2)}) collective-permute-start(bf16[128,512]{1,0:T(8,128)(2,1)S(1)} %get-tuple-element.44), channel_id=1, source_target_pairs={{0,24},{8,16},{16,8},{24,0},{1,25},{9,17},{17,9},{25,1},{2,26},{10... | collective-permute-start | bytes 393224 | tf_op jit(solution)/shard_map/ppermute | solution.py:309
  76.6 1.3 %collective-permute-start.18 = (bf16[64,512]{1,0:T(8,128)(2,1)S(1)}, bf16[64,512]{1,0:T(8,128)(2,1)S(1)}, u32[]{:S(2)}, u32[]{:S(2)}) collective-permute-start(bf16[64,512]{1,0:T(8,128)(2,1)S(1)} %get-tuple-element.46), channel_id=1, source_target_pairs={{0,1},{1,0},{2,3},{3,2},{4,5},{5,4},{6,7},{7,6},{8,9},{9,8},{10,11... | collective-permute-start | bytes 196616 | tf_op jit(solution)/shard_map/ppermute | solution.py:306

commit v14 on v12

--- a/solution.py
+++ b/solution.py
@@ -349,7 +349,7 @@
     for j in near_first:
         low = j & -j
         shard = shards[j ^ low]
-        shards[j] = across(shard if j == low else after(shard, messages[0]), CORES * low)
+        shards[j] = across(shard if j == low else after(shard, *arrived[1:]), CORES * low)
     normed = combine(core_only, arrived, head_gain.reshape(1, panel), heads)
 
     terms = output_terms(

time: 77.7 us -> 82.4 us (1.060)
  starting transfers between devices: 20.1 us -> 23.1 us
  waiting for transfers between devices: 38.9 us -> 40.6 us
    ppermute x16, starting transfers between devices: 16.6 us -> 19.6 us  [across(): return lax.ppermute(array, 'ctx', [(i, i ^ bits) for i in range(n_ctx)])]
    ppermute x16, waiting for transfers between devices: 32.8 us -> 34.7 us  [across(): return lax.ppermute(array, 'ctx', [(i, i ^ bits) for i in range(n_ctx)])]
  transfers between devices with their start and end apart: 19 -> 19, of which waited for: 11 -> 13; matrix products, arithmetic and copies ran while one was open for 2% -> 1% of each run, Pallas kernels for 13% -> 12%
where the time goes in v14:
time: 82.4 us; the launch traced here: 82.1 us
  waiting for transfers between devices  40.6 us (49%)
  starting transfers between devices  23.1 us (28%)
  Pallas kernels  13.3 us (16%)
  local copies, waits for them, and re-layouts  4.15 us (5%)
  other arithmetic  0.86 us (1%)
    ppermute x16, waiting for transfers between devices, across(): return lax.ppermute(array, 'ctx', [(i, i ^ bits) for i in range(n_ctx)])  34.7 us
    ppermute x16, starting transfers between devices, across(): return lax.ppermute(array, 'ctx', [(i, i ^ bits) for i in range(n_ctx)])  19.6 us
    pallas_call x2, Pallas kernels, project(): pl.pallas_call(functools.partial(project_kernel, count, extra, acc is not...  7.19 us
    ppermute x3, waiting for transfers between devices, over_dp(): return lax.ppermute(array, 'dp', [(d, d ^ bits) for d in range(n_dp)])  5.88 us
    ppermute x3, starting transfers between devices, over_dp(): return lax.ppermute(array, 'dp', [(d, d ^ bits) for d in range(n_dp)])  3.55 us
    unnamed x10, local copies, waits for them, and re-layouts  3.16 us
    pallas_call x1, Pallas kernels, attend(): pl.pallas_call(functools.partial(attend_kernel, count, heads, depth, grou...  2.82 us
    pallas_call x1, Pallas kernels, pack(): pl.pallas_call(pack_kernel, out_shape=[out, out], in_specs=[SMEM, ANY, AN...  2.02 us
  transfers between devices with their start and end apart: 19, of which 13 were waited for; matrix products, arithmetic and copies ran while one was open for 1% of the time, Pallas kernels for 12%

profile of v14, /device:TPU:0, one launch (start us, length us, event | category | flops | bytes accessed | tf_op | source)
XLA Modules:
  0.0 82.1 jit_solution(11244174101210128197)
XLA Ops:
  0.0 2.0 %shard_map.73 = (bf16[544,256]{1,0:T(8,128)(2,1)}, bf16[544,256]{1,0:T(8,128)(2,1)}) custom-call(s32[1]{0:T(128)} %bitcast.core_ref, bf16[512,256]{1,0:T(8,128)(2,1)} %key_ref.1, bf16[512,256]{1,0:T(8,128)(2,1)} %value_ref.1, bf16[64,256]{1,0:T(8,128)(2,1)} %query_ref.1), custom_call_target="tpu_custom_call" | custom-call | tf_op jit(solution)/shard_map/pallas_call | solution.py:235
  2.0 0.5 collective-permute-start
  2.5 2.7 %collective-permute-start.1 = (bf16[544,256]{1,0:T(8,128)(2,1)}, bf16[544,256]{1,0:T(8,128)(2,1)S(1)}, u32[]{:S(2)}, u32[]{:S(2)}) collective-permute-start(bf16[544,256]{1,0:T(8,128)(2,1)} %get-tuple-element.26.refs_3_.refs_4_), channel_id=1, source_target_pairs={{0,2},{1,3},{2,0},{3,1},{4,6},{5,7},{6,4},{7,5},{8,10},{9,11},{10,... | collective-permute-start | bytes 835592 | tf_op jit(solution)/shard_map/ppermute | solution.py:306
  5.2 2.6 %collective-permute-start.3 = (bf16[544,256]{1,0:T(8,128)(2,1)}, bf16[544,256]{1,0:T(8,128)(2,1)S(1)}, u32[]{:S(2)}, u32[]{:S(2)}) collective-permute-start(bf16[544,256]{1,0:T(8,128)(2,1)} %get-tuple-element.26.refs_3_.refs_4_), channel_id=1, source_target_pairs={{0,4},{1,5},{2,6},{3,7},{4,0},{5,1},{6,2},{7,3},{8,12},{9,13},{10,... | collective-permute-start | bytes 835592 | tf_op jit(solution)/shard_map/ppermute | solution.py:306
  7.8 0.0 collective-permute-start.2
  7.8 0.2 collective-permute-start.4
  8.0 0.1 stack.71.refs_2_
  8.1 0.1 slice.8.refs_0_
  8.1 1.5 %collective-permute-done.refs_2_ = bf16[512,4096]{1,0:T(8,128)(2,1)} collective-permute-done((bf16[512,4096]{1,0:T(8,128)(2,1)}, bf16[512,4096]{1,0:T(8,128)(2,1)}, u32[]{:S(2)}, u32[]{:S(2)}) %collective-permute-start) | collective-permute-done | bytes 4194336 | tf_op jit(solution)/shard_map/ppermute | solution.py:306
  9.7 0.4 collective-permute-start.5
  10.1 0.8 %slice_bitcast_fusion.3 = (s32[1,128]{1,0:T(1,128)S(1)}, s32[1,128]{1,0:T(1,128)S(1)}, s32[1,128]{1,0:T(1,128)S(1)}, s32[1,128]{1,0:T(1,128)S(1)}) fusion(s32[512]{0:T(512)} %param.11), kind=kLoop, calls=%fused_computation.7 | loop fusion | bytes 4096 | tf_op jit(solution)/shard_map/stack | solution.py:152
  10.9 7.9 %collective-permute-done.1.refs_3_.refs_6_ = bf16[544,256]{1,0:T(8,128)(2,1)S(1)} collective-permute-done((bf16[544,256]{1,0:T(8,128)(2,1)}, bf16[544,256]{1,0:T(8,128)(2,1)S(1)}, u32[]{:S(2)}, u32[]{:S(2)}) %collective-permute-start.1) | collective-permute-done | bytes 278560 | tf_op jit(solution)/shard_map/ppermute | solution.py:306
  18.8 3.2 %collective-permute-done.3.refs_5_.refs_8_ = bf16[544,256]{1,0:T(8,128)(2,1)S(1)} collective-permute-done((bf16[544,256]{1,0:T(8,128)(2,1)}, bf16[544,256]{1,0:T(8,128)(2,1)S(1)}, u32[]{:S(2)}, u32[]{:S(2)}) %collective-permute-start.3) | collective-permute-done | bytes 278560 | tf_op jit(solution)/shard_map/ppermute | solution.py:306
  21.9 0.0 collective-permute-start.6
  21.9 0.0 collective-permute-done.5.refs_4_.refs_5_
  21.9 0.0 copy-start
  21.9 2.2 %copy-done = bf16[512,4096]{1,0:T(8,128)(2,1)S(1)} copy-done((bf16[512,4096]{1,0:T(8,128)(2,1)S(1)}, bf16[512,4096]{1,0:T(8,128)(2,1)}, u32[]{:S(2)}) %copy-start) | copy-done | bytes 4194328
  24.1 0.0 copy-start.1
  24.1 1.0 %copy-done.1 = bf16[544,256]{1,0:T(8,128)(2,1)S(1)} copy-done((bf16[544,256]{1,0:T(8,128)(2,1)S(1)}, bf16[544,256]{1,0:T(8,128)(2,1)}, u32[]{:S(2)}) %copy-start.1) | copy-done | bytes 278552
  25.1 0.0 copy-start.3
  25.1 3.1 %shard_map.74 = (f32[1024,256]{1,0:T(8,128)S(1)}, bf16[2,16,512]{2,1,0:T(8,128)(2,1)}) custom-call(s32[2]{0:T(128)S(1)} %bitcast.21, bf16[512,4096]{1,0:T(8,128)(2,1)S(1)} %copy-done, bf16[512,4096]{1,0:T(8,128)(2,1)} %collective-permute-done.refs_2_, bf16[544,256]{1,0:T(8,128)(2,1)S(1)} %copy-done.1, bf16[544,256]{1,0:T(8,128)(2,1)S(1)} %collective-permute-done.5.refs_4_.refs_5_), custom_call_target="tpu_custom_call" | custom-call | flops 536870912 | bytes 2097152 | tf_op jit(solution)/shard_map/pallas_call | solution.py:81
  28.1 2.0 %collective-permute-done.2.refs_4_.refs_7_ = bf16[544,256]{1,0:T(8,128)(2,1)S(1)} collective-permute-done((bf16[544,256]{1,0:T(8,128)(2,1)}, bf16[544,256]{1,0:T(8,128)(2,1)S(1)}, u32[]{:S(2)}, u32[]{:S(2)}) %collective-permute-start.2) | collective-permute-done | bytes 278560 | tf_op jit(solution)/shard_map/ppermute | solution.py:306
  30.2 0.3 collective-permute-done.4.refs_6_.refs_9_
  30.5 2.5 %collective-permute-start.7 = (bf16[544,256]{1,0:T(8,128)(2,1)S(1)}, bf16[544,256]{1,0:T(8,128)(2,1)S(1)}, u32[]{:S(2)}, u32[]{:S(2)}) collective-permute-start(bf16[544,256]{1,0:T(8,128)(2,1)S(1)} %collective-permute-done.4.refs_6_.refs_9_), channel_id=1, source_target_pairs={{0,2},{1,3},{2,0},{3,1},{4,6},{5,7},{6,4},{7,5},{8,10},{9,11},{10,... | collective-permute-start | bytes 835592 | tf_op jit(solution)/shard_map/ppermute | solution.py:306
  33.0 0.0 copy-done.3
  33.0 2.4 %collective-permute-start.13 = (bf16[256,512]{1,0:T(8,128)(2,1)S(1)}, bf16[256,512]{1,0:T(8,128)(2,1)S(1)}, u32[]{:S(2)}, u32[]{:S(2)}) collective-permute-start(bf16[256,512]{1,0:T(8,128)(2,1)S(1)} %copy-done.3), channel_id=1, source_target_pairs={{0,4},{1,5},{2,6},{3,7},{4,0},{5,1},{6,2},{7,3},{8,12},{9,13},{10,... | collective-permute-start | bytes 786440 | tf_op jit(solution)/shard_map/ppermute | solution.py:306
  35.4 0.1 pad_add_fusion.2.refs_0_
  35.5 0.0 copy-start.2
  35.5 4.1 %shard_map.75 = (f32[1024,256]{1,0:T(8,128)S(1)}, bf16[4,512,512]{2,1,0:T(8,128)(2,1)S(1)}) custom-call(s32[6]{0:T(128)S(1)} %slice.8.refs_0_, bf16[512,4096]{1,0:T(8,128)(2,1)S(1)} %copy-done, bf16[512,4096]{1,0:T(8,128)(2,1)} %collective-permute-done.refs_2_, bf16[544,256]{1,0:T(8,128)(2,1)S(1)} %collective-permute-done.1.refs_3_.refs_6_, ...), custom_call_target="tpu_custom_call" | custom-call | flops 1073741824 | bytes 4194304 | tf_op jit(solution)/shard_map/pallas_call | solution.py:81
  39.6 0.0 copy-start.4
  39.6 0.0 collective-permute-done.6.refs_10_
  39.6 8.5 %collective-permute-done.7.refs_11_ = bf16[544,256]{1,0:T(8,128)(2,1)S(1)} collective-permute-done((bf16[544,256]{1,0:T(8,128)(2,1)S(1)}, bf16[544,256]{1,0:T(8,128)(2,1)S(1)}, u32[]{:S(2)}, u32[]{:S(2)}) %collective-permute-start.7) | collective-permute-done | bytes 278560 | tf_op jit(solution)/shard_map/ppermute | solution.py:306
  48.1 0.0 copy-done.2
  48.1 2.8 %shard_map.76 = (bf16[144,128]{1,0:T(8,128)(2,1)S(1)}, bf16[144,128]{1,0:T(8,128)(2,1)S(1)}, bf16[144,128]{1,0:T(8,128)(2,1)S(1)}, bf16[144,128]{1,0:T(8,128)(2,1)S(1)}) custom-call(s32[2]{0:T(128)S(1)} %pad_add_fusion.2.refs_0_, s32[4]{0:T(128)S(1)} %iota_xor_fusion.refs_1_, s32[8]{0:T(128)S(1)} %stack.71.refs_2_, ...), custom_call_target="tpu_custom_call" | custom-call | flops 536870912 | bytes 2097152 | tf_op jit(solution)/shard_map/pallas_call | solution.py:158
  50.9 3.9 %collective-permute-start.10 = (bf16[144,128]{1,0:T(8,128)(2,1)S(1)}, bf16[144,128]{1,0:T(8,128)(2,1)S(1)}, u32[]{:S(2)}, u32[]{:S(2)}) collective-permute-start(bf16[144,128]{1,0:T(8,128)(2,1)S(1)} %get-tuple-element.38), channel_id=1, source_target_pairs={{0,6},{1,7},{2,4},{3,5},{4,2},{5,3},{6,0},{7,1},{8,14},{9,15},{10,... | collective-permute-start | bytes 110600 | tf_op jit(solution)/shard_map/ppermute | solution.py:306
  54.8 0.0 collective-permute-start.8
  54.8 0.6 collective-permute-start.9
  55.4 1.4 %collective-permute-start.12 = (bf16[256,512]{1,0:T(8,128)(2,1)S(1)}, bf16[256,512]{1,0:T(8,128)(2,1)S(1)}, u32[]{:S(2)}, u32[]{:S(2)}) collective-permute-start(bf16[256,512]{1,0:T(8,128)(2,1)S(1)} %copy-done.3), channel_id=1, source_target_pairs={{0,2},{1,3},{2,0},{3,1},{4,6},{5,7},{6,4},{7,5},{8,10},{9,11},{10,... | collective-permute-start | bytes 786440 | tf_op jit(solution)/shard_map/ppermute | solution.py:306
  56.8 0.0 collective-permute-done.13.refs_2_
  56.8 0.0 collective-permute-done.10.refs_3_
  56.8 2.4 %collective-permute-done.8.refs_1_ = bf16[144,128]{1,0:T(8,128)(2,1)S(1)} collective-permute-done((bf16[144,128]{1,0:T(8,128)(2,1)S(1)}, bf16[144,128]{1,0:T(8,128)(2,1)S(1)}, u32[]{:S(2)}, u32[]{:S(2)}) %collective-permute-start.8) | collective-permute-done | bytes 36896 | tf_op jit(solution)/shard_map/ppermute | solution.py:306
  59.2 0.5 collective-permute-done.9.refs_2_
  59.8 2.4 %collective-permute-start.14 = (bf16[256,512]{1,0:T(8,128)(2,1)S(1)}, bf16[256,512]{1,0:T(8,128)(2,1)S(1)}, u32[]{:S(2)}, u32[]{:S(2)}) collective-permute-start(bf16[256,512]{1,0:T(8,128)(2,1)S(1)} %collective-permute-done.13.refs_2_), channel_id=1, source_target_pairs={{0,2},{1,3},{2,0},{3,1},{4,6},{5,7},{6,4},{7,5},{8,10},{9,11},{10,... | collective-permute-start | bytes 786440 | tf_op jit(solution)/shard_map/ppermute | solution.py:306
  62.1 0.0 copy-done.4
  62.1 0.2 shard_map.77.own_ref
  62.3 0.1 collective-permute-start.11
  62.4 0.1 pad_add_fusion.1.place_ref
  62.5 2.8 %collective-permute-done.12.refs_1_ = bf16[256,512]{1,0:T(8,128)(2,1)S(1)} collective-permute-done((bf16[256,512]{1,0:T(8,128)(2,1)S(1)}, bf16[256,512]{1,0:T(8,128)(2,1)S(1)}, u32[]{:S(2)}, u32[]{:S(2)}) %collective-permute-start.12) | collective-permute-done | bytes 262176 | tf_op jit(solution)/shard_map/ppermute | solution.py:306
  65.2 0.0 collective-permute-done.11.sibling_ref
  65.2 4.4 %collective-permute-done.14.refs_3_ = bf16[256,512]{1,0:T(8,128)(2,1)S(1)} collective-permute-done((bf16[256,512]{1,0:T(8,128)(2,1)S(1)}, bf16[256,512]{1,0:T(8,128)(2,1)S(1)}, u32[]{:S(2)}, u32[]{:S(2)}) %collective-permute-start.14) | collective-permute-done | bytes 262176 | tf_op jit(solution)/shard_map/ppermute | solution.py:306
  69.6 1.0 %shard_map.78 = (bf16[128,512]{1,0:T(8,128)(2,1)S(1)}, bf16[128,512]{1,0:T(8,128)(2,1)S(1)}, bf16[128,512]{1,0:T(8,128)(2,1)S(1)}, bf16[128,512]{1,0:T(8,128)(2,1)S(1)}) custom-call(s32[2]{0:T(128)S(1)} %pad_add_fusion.1.place_ref, bf16[128,128]{1,0:T(8,128)(2,1)S(1)} %shard_map.77.own_ref, bf16[128,128]{1,0:T(8,128)(2,1)S(1)} %collective-permute-done.11.sibling_ref, ...), custom_call_target="tpu_custom_call" | custom-call | tf_op jit(solution)/shard_map/pallas_call | solution.py:262
  70.6 1.7 %collective-permute-start.15 = (bf16[128,512]{1,0:T(8,128)(2,1)S(1)}, bf16[128,512]{1,0:T(8,128)(2,1)S(1)}, u32[]{:S(2)}, u32[]{:S(2)}) collective-permute-start(bf16[128,512]{1,0:T(8,128)(2,1)S(1)} %get-tuple-element.42), channel_id=1, source_target_pairs={{0,8},{8,0},{16,24},{24,16},{1,9},{9,1},{17,25},{25,17},{2,10},{10... | collective-permute-start | bytes 393224 | tf_op jit(solution)/shard_map/ppermute | solution.py:309
  72.3 1.5 %collective-permute-start.16 = (bf16[128,512]{1,0:T(8,128)(2,1)S(1)}, bf16[128,512]{1,0:T(8,128)(2,1)S(1)}, u32[]{:S(2)}, u32[]{:S(2)}) collective-permute-start(bf16[128,512]{1,0:T(8,128)(2,1)S(1)} %get-tuple-element.43), channel_id=1, source_target_pairs={{0,16},{8,24},{16,0},{24,8},{1,17},{9,25},{17,1},{25,9},{2,18},{10... | collective-permute-start | bytes 393224 | tf_op jit(solution)/shard_map/ppermute | solution.py:309
  73.8 0.3 collective-permute-start.17
  74.1 2.3 %collective-permute-done.15.refs_1_ = bf16[128,512]{1,0:T(8,128)(2,1)S(1)} collective-permute-done((bf16[128,512]{1,0:T(8,128)(2,1)S(1)}, bf16[128,512]{1,0:T(8,128)(2,1)S(1)}, u32[]{:S(2)}, u32[]{:S(2)}) %collective-permute-start.15) | collective-permute-done | bytes 131104 | tf_op jit(solution)/shard_map/ppermute | solution.py:309
  76.4 3.6 %collective-permute-done.16.refs_2_ = bf16[128,512]{1,0:T(8,128)(2,1)S(1)} collective-permute-done((bf16[128,512]{1,0:T(8,128)(2,1)S(1)}, bf16[128,512]{1,0:T(8,128)(2,1)S(1)}, u32[]{:S(2)}, u32[]{:S(2)}) %collective-permute-start.16) | collective-permute-done | bytes 131104 | tf_op jit(solution)/shard_map/ppermute | solution.py:309
  80.0 0.0 collective-permute-done.17.refs_3_
  80.0 0.1 shard_map.79
  80.1 0.1 collective-permute-start.18
  80.2 1.2 %collective-permute-done.18 = bf16[64,512]{1,0:T(8,128)(2,1)S(1)} collective-permute-done((bf16[64,512]{1,0:T(8,128)(2,1)S(1)}, bf16[64,512]{1,0:T(8,128)(2,1)S(1)}, u32[]{:S(2)}, u32[]{:S(2)}) %collective-permute-start.18) | collective-permute-done | bytes 65568 | tf_op jit(solution)/shard_map/ppermute | solution.py:306
  81.4 0.7 maximum_select_fusion
  (4 shorter events, 0.0 us)
Async XLA Ops:
  2.0 7.6 %collective-permute-start = (bf16[512,4096]{1,0:T(8,128)(2,1)}, bf16[512,4096]{1,0:T(8,128)(2,1)}, u32[]{:S(2)}, u32[]{:S(2)}) collective-permute-start(bf16[512,4096]{1,0:T(8,128)(2,1)} %refs_1_.3), channel_id=1, source_target_pairs={{0,1},{1,0},{2,3},{3,2},{4,5},{5,4},{6,7},{7,6},{8,9},{9,8},{10,11... | collective-permute-start | bytes 12582920 | tf_op jit(solution)/shard_map/ppermute | solution.py:306
  2.5 16.2 %collective-permute-start.1 = (bf16[544,256]{1,0:T(8,128)(2,1)}, bf16[544,256]{1,0:T(8,128)(2,1)S(1)}, u32[]{:S(2)}, u32[]{:S(2)}) collective-permute-start(bf16[544,256]{1,0:T(8,128)(2,1)} %get-tuple-element.26.refs_3_.refs_4_), channel_id=1, source_target_pairs={{0,2},{1,3},{2,0},{3,1},{4,6},{5,7},{6,4},{7,5},{8,10},{9,11},{10,... | collective-permute-start | bytes 835592 | tf_op jit(solution)/shard_map/ppermute | solution.py:306
  5.2 16.7 %collective-permute-start.3 = (bf16[544,256]{1,0:T(8,128)(2,1)}, bf16[544,256]{1,0:T(8,128)(2,1)S(1)}, u32[]{:S(2)}, u32[]{:S(2)}) collective-permute-start(bf16[544,256]{1,0:T(8,128)(2,1)} %get-tuple-element.26.refs_3_.refs_4_), channel_id=1, source_target_pairs={{0,4},{1,5},{2,6},{3,7},{4,0},{5,1},{6,2},{7,3},{8,12},{9,13},{10,... | collective-permute-start | bytes 835592 | tf_op jit(solution)/shard_map/ppermute | solution.py:306
  7.8 22.4 %collective-permute-start.2 = (bf16[544,256]{1,0:T(8,128)(2,1)}, bf16[544,256]{1,0:T(8,128)(2,1)S(1)}, u32[]{:S(2)}, u32[]{:S(2)}) collective-permute-start(bf16[544,256]{1,0:T(8,128)(2,1)} %get-tuple-element.29), channel_id=1, source_target_pairs={{0,3},{1,2},{2,1},{3,0},{4,7},{5,6},{6,5},{7,4},{8,11},{9,10},{10,... | collective-permute-start | bytes 835592 | tf_op jit(solution)/shard_map/ppermute | solution.py:306
  7.8 22.7 %collective-permute-start.4 = (bf16[544,256]{1,0:T(8,128)(2,1)}, bf16[544,256]{1,0:T(8,128)(2,1)S(1)}, u32[]{:S(2)}, u32[]{:S(2)}) collective-permute-start(bf16[544,256]{1,0:T(8,128)(2,1)} %get-tuple-element.29), channel_id=1, source_target_pairs={{0,5},{1,4},{2,7},{3,6},{4,1},{5,0},{6,3},{7,2},{8,13},{9,12},{10,... | collective-permute-start | bytes 835592 | tf_op jit(solution)/shard_map/ppermute | solution.py:306
  9.7 12.2 %collective-permute-start.5 = (bf16[544,256]{1,0:T(8,128)(2,1)}, bf16[544,256]{1,0:T(8,128)(2,1)S(1)}, u32[]{:S(2)}, u32[]{:S(2)}) collective-permute-start(bf16[544,256]{1,0:T(8,128)(2,1)} %get-tuple-element.29), channel_id=1, source_target_pairs={{0,1},{1,0},{2,3},{3,2},{4,5},{5,4},{6,7},{7,6},{8,9},{9,8},{10,11... | collective-permute-start | bytes 835592 | tf_op jit(solution)/shard_map/ppermute | solution.py:306
  21.9 17.7 %collective-permute-start.6 = (bf16[544,256]{1,0:T(8,128)(2,1)S(1)}, bf16[544,256]{1,0:T(8,128)(2,1)S(1)}, u32[]{:S(2)}, u32[]{:S(2)}) collective-permute-start(bf16[544,256]{1,0:T(8,128)(2,1)S(1)} %collective-permute-done.3.refs_5_.refs_8_), channel_id=1, source_target_pairs={{0,2},{1,3},{2,0},{3,1},{4,6},{5,7},{6,4},{7,5},{8,10},{9,11},{10,... | collective-permute-start | bytes 835592 | tf_op jit(solution)/shard_map/ppermute | solution.py:306
  21.9 2.2 %copy-start = (bf16[512,4096]{1,0:T(8,128)(2,1)S(1)}, bf16[512,4096]{1,0:T(8,128)(2,1)}, u32[]{:S(2)}) copy-start(bf16[512,4096]{1,0:T(8,128)(2,1)} %refs_1_.3) | copy-start | bytes 12582916
  24.1 1.0 %copy-start.1 = (bf16[544,256]{1,0:T(8,128)(2,1)S(1)}, bf16[544,256]{1,0:T(8,128)(2,1)}, u32[]{:S(2)}) copy-start(bf16[544,256]{1,0:T(8,128)(2,1)} %get-tuple-element.26.refs_3_.refs_4_) | copy-start | bytes 835588
  25.1 7.9 %copy-start.3 = (bf16[256,512]{1,0:T(8,128)(2,1)S(1)}, bf16[256,512]{1,0:T(8,128)(2,1)}, u32[]{:S(2)}) copy-start(bf16[256,512]{1,0:T(8,128)(2,1)} %refs_0_) | copy-start | bytes 786436
  30.5 17.6 %collective-permute-start.7 = (bf16[544,256]{1,0:T(8,128)(2,1)S(1)}, bf16[544,256]{1,0:T(8,128)(2,1)S(1)}, u32[]{:S(2)}, u32[]{:S(2)}) collective-permute-start(bf16[544,256]{1,0:T(8,128)(2,1)S(1)} %collective-permute-done.4.refs_6_.refs_9_), channel_id=1, source_target_pairs={{0,2},{1,3},{2,0},{3,1},{4,6},{5,7},{6,4},{7,5},{8,10},{9,11},{10,... | collective-permute-start | bytes 835592 | tf_op jit(solution)/shard_map/ppermute | solution.py:306
  33.0 23.8 %collective-permute-start.13 = (bf16[256,512]{1,0:T(8,128)(2,1)S(1)}, bf16[256,512]{1,0:T(8,128)(2,1)S(1)}, u32[]{:S(2)}, u32[]{:S(2)}) collective-permute-start(bf16[256,512]{1,0:T(8,128)(2,1)S(1)} %copy-done.3), channel_id=1, source_target_pairs={{0,4},{1,5},{2,6},{3,7},{4,0},{5,1},{6,2},{7,3},{8,12},{9,13},{10,... | collective-permute-start | bytes 786440 | tf_op jit(solution)/shard_map/ppermute | solution.py:306
  35.5 12.7 %copy-start.2 = (bf16[544,256]{1,0:T(8,128)(2,1)S(1)}, bf16[544,256]{1,0:T(8,128)(2,1)}, u32[]{:S(2)}) copy-start(bf16[544,256]{1,0:T(8,128)(2,1)} %get-tuple-element.26.refs_3_.refs_4_) | copy-start | bytes 835588
  39.6 22.5 %copy-start.4 = (bf16[256]{0:T(256)(128)(2,1)S(1)}, bf16[256]{0:T(256)(128)(2,1)}, u32[]{:S(2)}) copy-start(bf16[256]{0:T(256)(128)(2,1)} %param.12) | copy-start | bytes 1540
  50.9 5.9 %collective-permute-start.10 = (bf16[144,128]{1,0:T(8,128)(2,1)S(1)}, bf16[144,128]{1,0:T(8,128)(2,1)S(1)}, u32[]{:S(2)}, u32[]{:S(2)}) collective-permute-start(bf16[144,128]{1,0:T(8,128)(2,1)S(1)} %get-tuple-element.38), channel_id=1, source_target_pairs={{0,6},{1,7},{2,4},{3,5},{4,2},{5,3},{6,0},{7,1},{8,14},{9,15},{10,... | collective-permute-start | bytes 110600 | tf_op jit(solution)/shard_map/ppermute | solution.py:306
  54.8 4.4 %collective-permute-start.8 = (bf16[144,128]{1,0:T(8,128)(2,1)S(1)}, bf16[144,128]{1,0:T(8,128)(2,1)S(1)}, u32[]{:S(2)}, u32[]{:S(2)}) collective-permute-start(bf16[144,128]{1,0:T(8,128)(2,1)S(1)} %get-tuple-element.36), channel_id=1, source_target_pairs={{0,2},{1,3},{2,0},{3,1},{4,6},{5,7},{6,4},{7,5},{8,10},{9,11},{10,... | collective-permute-start | bytes 110600 | tf_op jit(solution)/shard_map/ppermute | solution.py:306
  54.8 5.0 %collective-permute-start.9 = (bf16[144,128]{1,0:T(8,128)(2,1)S(1)}, bf16[144,128]{1,0:T(8,128)(2,1)S(1)}, u32[]{:S(2)}, u32[]{:S(2)}) collective-permute-start(bf16[144,128]{1,0:T(8,128)(2,1)S(1)} %get-tuple-element.37), channel_id=1, source_target_pairs={{0,4},{1,5},{2,6},{3,7},{4,0},{5,1},{6,2},{7,3},{8,12},{9,13},{10,... | collective-permute-start | bytes 110600 | tf_op jit(solution)/shard_map/ppermute | solution.py:306
  55.4 9.8 %collective-permute-start.12 = (bf16[256,512]{1,0:T(8,128)(2,1)S(1)}, bf16[256,512]{1,0:T(8,128)(2,1)S(1)}, u32[]{:S(2)}, u32[]{:S(2)}) collective-permute-start(bf16[256,512]{1,0:T(8,128)(2,1)S(1)} %copy-done.3), channel_id=1, source_target_pairs={{0,2},{1,3},{2,0},{3,1},{4,6},{5,7},{6,4},{7,5},{8,10},{9,11},{10,... | collective-permute-start | bytes 786440 | tf_op jit(solution)/shard_map/ppermute | solution.py:306
  59.8 9.8 %collective-permute-start.14 = (bf16[256,512]{1,0:T(8,128)(2,1)S(1)}, bf16[256,512]{1,0:T(8,128)(2,1)S(1)}, u32[]{:S(2)}, u32[]{:S(2)}) collective-permute-start(bf16[256,512]{1,0:T(8,128)(2,1)S(1)} %collective-permute-done.13.refs_2_), channel_id=1, source_target_pairs={{0,2},{1,3},{2,0},{3,1},{4,6},{5,7},{6,4},{7,5},{8,10},{9,11},{10,... | collective-permute-start | bytes 786440 | tf_op jit(solution)/shard_map/ppermute | solution.py:306
  62.3 2.9 %collective-permute-start.11 = (bf16[128,128]{1,0:T(8,128)(2,1)S(1)}, bf16[128,128]{1,0:T(8,128)(2,1)S(1)}, u32[]{:S(2)}, u32[]{:S(2)}) collective-permute-start(bf16[128,128]{1,0:T(8,128)(2,1)S(1)} %shard_map.77.own_ref), channel_id=1, source_target_pairs={{0,1},{1,0},{2,3},{3,2},{4,5},{5,4},{6,7},{7,6},{8,9},{9,8},{10,11... | collective-permute-start | bytes 98312 | tf_op jit(solution)/shard_map/ppermute | solution.py:306
  70.6 5.9 %collective-permute-start.15 = (bf16[128,512]{1,0:T(8,128)(2,1)S(1)}, bf16[128,512]{1,0:T(8,128)(2,1)S(1)}, u32[]{:S(2)}, u32[]{:S(2)}) collective-permute-start(bf16[128,512]{1,0:T(8,128)(2,1)S(1)} %get-tuple-element.42), channel_id=1, source_target_pairs={{0,8},{8,0},{16,24},{24,16},{1,9},{9,1},{17,25},{25,17},{2,10},{10... | collective-permute-start | bytes 393224 | tf_op jit(solution)/shard_map/ppermute | solution.py:309
  72.3 7.7 %collective-permute-start.16 = (bf16[128,512]{1,0:T(8,128)(2,1)S(1)}, bf16[128,512]{1,0:T(8,128)(2,1)S(1)}, u32[]{:S(2)}, u32[]{:S(2)}) collective-permute-start(bf16[128,512]{1,0:T(8,128)(2,1)S(1)} %get-tuple-element.43), channel_id=1, source_target_pairs={{0,16},{8,24},{16,0},{24,8},{1,17},{9,25},{17,1},{25,9},{2,18},{10... | collective-permute-start | bytes 393224 | tf_op jit(solution)/shard_map/ppermute | solution.py:309
  73.8 6.2 %collective-permute-start.17 = (bf16[128,512]{1,0:T(8,128)(2,1)S(1)}, bf16[128,512]{1,0:T(8,128)(2,1)S(1)}, u32[]{:S(2)}, u32[]{:S(2)}) collective-permute-start(bf16[128,512]{1,0:T(8,128)(2,1)S(1)} %get-tuple-element.44), channel_id=1, source_target_pairs={{0,24},{8,16},{16,8},{24,0},{1,25},{9,17},{17,9},{25,1},{2,26},{10... | collective-permute-start | bytes 393224 | tf_op jit(solution)/shard_map/ppermute | solution.py:309
  80.1 1.3 %collective-permute-start.18 = (bf16[64,512]{1,0:T(8,128)(2,1)S(1)}, bf16[64,512]{1,0:T(8,128)(2,1)S(1)}, u32[]{:S(2)}, u32[]{:S(2)}) collective-permute-start(bf16[64,512]{1,0:T(8,128)(2,1)S(1)} %get-tuple-element.46), channel_id=1, source_target_pairs={{0,1},{1,0},{2,3},{3,2},{4,5},{5,4},{6,7},{7,6},{8,9},{9,8},{10,11... | collective-permute-start | bytes 196616 | tf_op jit(solution)/shard_map/ppermute | solution.py:306

commit v15 on v14

--- a/solution.py
+++ b/solution.py
@@ -349,7 +349,7 @@
     for j in near_first:
         low = j & -j
         shard = shards[j ^ low]
-        shards[j] = across(shard if j == low else after(shard, *arrived[1:]), CORES * low)
+        shards[j] = across(shard if j == low else after(shard, shards[1], *arrived[1:]), CORES * low)
     normed = combine(core_only, arrived, head_gain.reshape(1, panel), heads)
 
     terms = output_terms(

time: 82.4 us -> 79.2 us (0.961)
  waiting for transfers between devices: 40.6 us -> 38.5 us
  starting transfers between devices: 23.1 us -> 22.1 us
    ppermute x16, waiting for transfers between devices: 34.7 us -> 33.1 us  [across(): return lax.ppermute(array, 'ctx', [(i, i ^ bits) for i in range(n_ctx)])]
    ppermute x16, starting transfers between devices: 19.6 us -> 18.5 us  [across(): return lax.ppermute(array, 'ctx', [(i, i ^ bits) for i in range(n_ctx)])]
  transfers between devices with their start and end apart: 19 -> 19, of which waited for: 13 -> 15; matrix products, arithmetic and copies ran while one was open for 1% -> 1% of each run, Pallas kernels for 12% -> 13%
where the time goes in v15:
time: 79.2 us; the launch traced here: 78.9 us
  waiting for transfers between devices  38.5 us (49%)
  starting transfers between devices  22.1 us (28%)
  Pallas kernels  13.3 us (17%)
  local copies, waits for them, and re-layouts  4.15 us (5%)
  other arithmetic  0.86 us (1%)
    ppermute x16, waiting for transfers between devices, across(): return lax.ppermute(array, 'ctx', [(i, i ^ bits) for i in range(n_ctx)])  33.1 us
    ppermute x16, starting transfers between devices, across(): return lax.ppermute(array, 'ctx', [(i, i ^ bits) for i in range(n_ctx)])  18.5 us
    pallas_call x2, Pallas kernels, project(): pl.pallas_call(functools.partial(project_kernel, count, extra, acc is not...  7.19 us
    ppermute x3, waiting for transfers between devices, over_dp(): return lax.ppermute(array, 'dp', [(d, d ^ bits) for d in range(n_dp)])  5.38 us
    ppermute x3, starting transfers between devices, over_dp(): return lax.ppermute(array, 'dp', [(d, d ^ bits) for d in range(n_dp)])  3.55 us
    unnamed x10, local copies, waits for them, and re-layouts  3.16 us
    pallas_call x1, Pallas kernels, attend(): pl.pallas_call(functools.partial(attend_kernel, count, heads, depth, grou...  2.81 us
    pallas_call x1, Pallas kernels, pack(): pl.pallas_call(pack_kernel, out_shape=[out, out], in_specs=[SMEM, ANY, AN...  2.02 us
  transfers between devices with their start and end apart: 19, of which 15 were waited for; matrix products, arithmetic and copies ran while one was open for 1% of the time, Pallas kernels for 13%

profile of v15, /device:TPU:0, one launch (start us, length us, event | category | flops | bytes accessed | tf_op | source)
XLA Modules:
  0.0 78.9 jit_solution(10750819407301358560)
XLA Ops:
  0.0 2.0 %shard_map.73 = (bf16[544,256]{1,0:T(8,128)(2,1)}, bf16[544,256]{1,0:T(8,128)(2,1)}) custom-call(s32[1]{0:T(128)} %bitcast.core_ref, bf16[512,256]{1,0:T(8,128)(2,1)} %key_ref.1, bf16[512,256]{1,0:T(8,128)(2,1)} %value_ref.1, bf16[64,256]{1,0:T(8,128)(2,1)} %query_ref.1), custom_call_target="tpu_custom_call" | custom-call | tf_op jit(solution)/shard_map/pallas_call | solution.py:235
  2.0 0.5 collective-permute-start
  2.5 2.7 %collective-permute-start.1 = (bf16[544,256]{1,0:T(8,128)(2,1)}, bf16[544,256]{1,0:T(8,128)(2,1)S(1)}, u32[]{:S(2)}, u32[]{:S(2)}) collective-permute-start(bf16[544,256]{1,0:T(8,128)(2,1)} %get-tuple-element.26.refs_3_.refs_4_), channel_id=1, source_target_pairs={{0,2},{1,3},{2,0},{3,1},{4,6},{5,7},{6,4},{7,5},{8,10},{9,11},{10,... | collective-permute-start | bytes 835592 | tf_op jit(solution)/shard_map/ppermute | solution.py:306
  5.2 2.6 %collective-permute-start.3 = (bf16[544,256]{1,0:T(8,128)(2,1)}, bf16[544,256]{1,0:T(8,128)(2,1)S(1)}, u32[]{:S(2)}, u32[]{:S(2)}) collective-permute-start(bf16[544,256]{1,0:T(8,128)(2,1)} %get-tuple-element.26.refs_3_.refs_4_), channel_id=1, source_target_pairs={{0,4},{1,5},{2,6},{3,7},{4,0},{5,1},{6,2},{7,3},{8,12},{9,13},{10,... | collective-permute-start | bytes 835592 | tf_op jit(solution)/shard_map/ppermute | solution.py:306
  7.8 0.0 collective-permute-start.2
  7.8 0.2 collective-permute-start.4
  8.0 0.1 stack.71.refs_2_
  8.1 0.1 slice.8.refs_0_
  8.1 1.5 %collective-permute-done.refs_2_ = bf16[512,4096]{1,0:T(8,128)(2,1)} collective-permute-done((bf16[512,4096]{1,0:T(8,128)(2,1)}, bf16[512,4096]{1,0:T(8,128)(2,1)}, u32[]{:S(2)}, u32[]{:S(2)}) %collective-permute-start) | collective-permute-done | bytes 4194336 | tf_op jit(solution)/shard_map/ppermute | solution.py:306
  9.7 0.4 collective-permute-start.5
  10.1 0.8 %slice_bitcast_fusion.3 = (s32[1,128]{1,0:T(1,128)S(1)}, s32[1,128]{1,0:T(1,128)S(1)}, s32[1,128]{1,0:T(1,128)S(1)}, s32[1,128]{1,0:T(1,128)S(1)}) fusion(s32[512]{0:T(512)} %param.11), kind=kLoop, calls=%fused_computation.7 | loop fusion | bytes 4096 | tf_op jit(solution)/shard_map/stack | solution.py:152
  10.9 7.9 %collective-permute-done.1.refs_3_.refs_6_ = bf16[544,256]{1,0:T(8,128)(2,1)S(1)} collective-permute-done((bf16[544,256]{1,0:T(8,128)(2,1)}, bf16[544,256]{1,0:T(8,128)(2,1)S(1)}, u32[]{:S(2)}, u32[]{:S(2)}) %collective-permute-start.1) | collective-permute-done | bytes 278560 | tf_op jit(solution)/shard_map/ppermute | solution.py:306
  18.8 3.2 %collective-permute-done.3.refs_5_.refs_8_ = bf16[544,256]{1,0:T(8,128)(2,1)S(1)} collective-permute-done((bf16[544,256]{1,0:T(8,128)(2,1)}, bf16[544,256]{1,0:T(8,128)(2,1)S(1)}, u32[]{:S(2)}, u32[]{:S(2)}) %collective-permute-start.3) | collective-permute-done | bytes 278560 | tf_op jit(solution)/shard_map/ppermute | solution.py:306
  21.9 0.0 collective-permute-start.6
  21.9 0.0 collective-permute-done.5.refs_4_.refs_5_
  21.9 0.0 copy-start
  21.9 2.2 %copy-done = bf16[512,4096]{1,0:T(8,128)(2,1)S(1)} copy-done((bf16[512,4096]{1,0:T(8,128)(2,1)S(1)}, bf16[512,4096]{1,0:T(8,128)(2,1)}, u32[]{:S(2)}) %copy-start) | copy-done | bytes 4194328
  24.1 0.0 copy-start.1
  24.1 1.0 %copy-done.1 = bf16[544,256]{1,0:T(8,128)(2,1)S(1)} copy-done((bf16[544,256]{1,0:T(8,128)(2,1)S(1)}, bf16[544,256]{1,0:T(8,128)(2,1)}, u32[]{:S(2)}) %copy-start.1) | copy-done | bytes 278552
  25.1 0.0 copy-start.3
  25.1 3.1 %shard_map.74 = (f32[1024,256]{1,0:T(8,128)S(1)}, bf16[2,16,512]{2,1,0:T(8,128)(2,1)}) custom-call(s32[2]{0:T(128)S(1)} %bitcast.21, bf16[512,4096]{1,0:T(8,128)(2,1)S(1)} %copy-done, bf16[512,4096]{1,0:T(8,128)(2,1)} %collective-permute-done.refs_2_, bf16[544,256]{1,0:T(8,128)(2,1)S(1)} %copy-done.1, bf16[544,256]{1,0:T(8,128)(2,1)S(1)} %collective-permute-done.5.refs_4_.refs_5_), custom_call_target="tpu_custom_call" | custom-call | flops 536870912 | bytes 2097152 | tf_op jit(solution)/shard_map/pallas_call | solution.py:81
  28.1 2.0 %collective-permute-done.2.refs_4_.refs_7_ = bf16[544,256]{1,0:T(8,128)(2,1)S(1)} collective-permute-done((bf16[544,256]{1,0:T(8,128)(2,1)}, bf16[544,256]{1,0:T(8,128)(2,1)S(1)}, u32[]{:S(2)}, u32[]{:S(2)}) %collective-permute-start.2) | collective-permute-done | bytes 278560 | tf_op jit(solution)/shard_map/ppermute | solution.py:306
  30.2 0.3 collective-permute-done.4.refs_6_.refs_9_
  30.5 2.5 %collective-permute-start.7 = (bf16[544,256]{1,0:T(8,128)(2,1)S(1)}, bf16[544,256]{1,0:T(8,128)(2,1)S(1)}, u32[]{:S(2)}, u32[]{:S(2)}) collective-permute-start(bf16[544,256]{1,0:T(8,128)(2,1)S(1)} %collective-permute-done.4.refs_6_.refs_9_), channel_id=1, source_target_pairs={{0,2},{1,3},{2,0},{3,1},{4,6},{5,7},{6,4},{7,5},{8,10},{9,11},{10,... | collective-permute-start | bytes 835592 | tf_op jit(solution)/shard_map/ppermute | solution.py:306
  33.0 0.0 copy-done.3
  33.0 0.1 collective-permute-start.12
  33.1 2.4 %collective-permute-start.13 = (bf16[256,512]{1,0:T(8,128)(2,1)S(1)}, bf16[256,512]{1,0:T(8,128)(2,1)S(1)}, u32[]{:S(2)}, u32[]{:S(2)}) collective-permute-start(bf16[256,512]{1,0:T(8,128)(2,1)S(1)} %copy-done.3), channel_id=1, source_target_pairs={{0,4},{1,5},{2,6},{3,7},{4,0},{5,1},{6,2},{7,3},{8,12},{9,13},{10,... | collective-permute-start | bytes 786440 | tf_op jit(solution)/shard_map/ppermute | solution.py:306
  35.5 0.1 pad_add_fusion.2.refs_0_
  35.5 0.0 copy-start.2
  35.5 4.1 %shard_map.75 = (f32[1024,256]{1,0:T(8,128)S(1)}, bf16[4,512,512]{2,1,0:T(8,128)(2,1)S(1)}) custom-call(s32[6]{0:T(128)S(1)} %slice.8.refs_0_, bf16[512,4096]{1,0:T(8,128)(2,1)S(1)} %copy-done, bf16[512,4096]{1,0:T(8,128)(2,1)} %collective-permute-done.refs_2_, bf16[544,256]{1,0:T(8,128)(2,1)S(1)} %collective-permute-done.1.refs_3_.refs_6_, ...), custom_call_target="tpu_custom_call" | custom-call | flops 1073741824 | bytes 4194304 | tf_op jit(solution)/shard_map/pallas_call | solution.py:81
  39.7 0.0 copy-start.4
  39.7 0.0 collective-permute-done.6.refs_10_
  39.7 8.7 %collective-permute-done.7.refs_11_ = bf16[544,256]{1,0:T(8,128)(2,1)S(1)} collective-permute-done((bf16[544,256]{1,0:T(8,128)(2,1)S(1)}, bf16[544,256]{1,0:T(8,128)(2,1)S(1)}, u32[]{:S(2)}, u32[]{:S(2)}) %collective-permute-start.7) | collective-permute-done | bytes 278560 | tf_op jit(solution)/shard_map/ppermute | solution.py:306
  48.4 0.0 copy-done.2
  48.4 2.8 %shard_map.76 = (bf16[144,128]{1,0:T(8,128)(2,1)S(1)}, bf16[144,128]{1,0:T(8,128)(2,1)S(1)}, bf16[144,128]{1,0:T(8,128)(2,1)S(1)}, bf16[144,128]{1,0:T(8,128)(2,1)S(1)}) custom-call(s32[2]{0:T(128)S(1)} %pad_add_fusion.2.refs_0_, s32[4]{0:T(128)S(1)} %iota_xor_fusion.refs_1_, s32[8]{0:T(128)S(1)} %stack.71.refs_2_, ...), custom_call_target="tpu_custom_call" | custom-call | flops 536870912 | bytes 2097152 | tf_op jit(solution)/shard_map/pallas_call | solution.py:158
  51.2 4.1 %collective-permute-start.10 = (bf16[144,128]{1,0:T(8,128)(2,1)S(1)}, bf16[144,128]{1,0:T(8,128)(2,1)S(1)}, u32[]{:S(2)}, u32[]{:S(2)}) collective-permute-start(bf16[144,128]{1,0:T(8,128)(2,1)S(1)} %get-tuple-element.38), channel_id=1, source_target_pairs={{0,6},{1,7},{2,4},{3,5},{4,2},{5,3},{6,0},{7,1},{8,14},{9,15},{10,... | collective-permute-start | bytes 110600 | tf_op jit(solution)/shard_map/ppermute | solution.py:306
  55.3 0.0 collective-permute-start.8
  55.3 0.6 collective-permute-start.9
  55.9 0.0 collective-permute-done.12.refs_1_
  55.9 0.0 collective-permute-done.13.refs_2_
  55.9 1.5 %collective-permute-done.10.refs_3_ = bf16[144,128]{1,0:T(8,128)(2,1)S(1)} collective-permute-done((bf16[144,128]{1,0:T(8,128)(2,1)S(1)}, bf16[144,128]{1,0:T(8,128)(2,1)S(1)}, u32[]{:S(2)}, u32[]{:S(2)}) %collective-permute-start.10) | collective-permute-done | bytes 36896 | tf_op jit(solution)/shard_map/ppermute | solution.py:306
  57.4 1.8 %collective-permute-done.8.refs_1_ = bf16[144,128]{1,0:T(8,128)(2,1)S(1)} collective-permute-done((bf16[144,128]{1,0:T(8,128)(2,1)S(1)}, bf16[144,128]{1,0:T(8,128)(2,1)S(1)}, u32[]{:S(2)}, u32[]{:S(2)}) %collective-permute-start.8) | collective-permute-done | bytes 36896 | tf_op jit(solution)/shard_map/ppermute | solution.py:306
  59.2 0.9 %collective-permute-done.9.refs_2_ = bf16[144,128]{1,0:T(8,128)(2,1)S(1)} collective-permute-done((bf16[144,128]{1,0:T(8,128)(2,1)S(1)}, bf16[144,128]{1,0:T(8,128)(2,1)S(1)}, u32[]{:S(2)}, u32[]{:S(2)}) %collective-permute-start.9) | collective-permute-done | bytes 36896 | tf_op jit(solution)/shard_map/ppermute | solution.py:306
  60.1 2.4 %collective-permute-start.14 = (bf16[256,512]{1,0:T(8,128)(2,1)S(1)}, bf16[256,512]{1,0:T(8,128)(2,1)S(1)}, u32[]{:S(2)}, u32[]{:S(2)}) collective-permute-start(bf16[256,512]{1,0:T(8,128)(2,1)S(1)} %collective-permute-done.13.refs_2_), channel_id=1, source_target_pairs={{0,2},{1,3},{2,0},{3,1},{4,6},{5,7},{6,4},{7,5},{8,10},{9,11},{10,... | collective-permute-start | bytes 786440 | tf_op jit(solution)/shard_map/ppermute | solution.py:306
  62.5 0.0 copy-done.4
  62.5 0.2 shard_map.77.own_ref
  62.7 0.1 collective-permute-start.11
  62.8 0.1 pad_add_fusion.1.place_ref
  62.9 1.1 %collective-permute-done.11.sibling_ref = bf16[128,128]{1,0:T(8,128)(2,1)S(1)} collective-permute-done((bf16[128,128]{1,0:T(8,128)(2,1)S(1)}, bf16[128,128]{1,0:T(8,128)(2,1)S(1)}, u32[]{:S(2)}, u32[]{:S(2)}) %collective-permute-start.11) | collective-permute-done | bytes 32800 | tf_op jit(solution)/shard_map/ppermute | solution.py:306
  64.0 2.9 %collective-permute-done.14.refs_3_ = bf16[256,512]{1,0:T(8,128)(2,1)S(1)} collective-permute-done((bf16[256,512]{1,0:T(8,128)(2,1)S(1)}, bf16[256,512]{1,0:T(8,128)(2,1)S(1)}, u32[]{:S(2)}, u32[]{:S(2)}) %collective-permute-start.14) | collective-permute-done | bytes 262176 | tf_op jit(solution)/shard_map/ppermute | solution.py:306
  66.9 1.0 %shard_map.78 = (bf16[128,512]{1,0:T(8,128)(2,1)S(1)}, bf16[128,512]{1,0:T(8,128)(2,1)S(1)}, bf16[128,512]{1,0:T(8,128)(2,1)S(1)}, bf16[128,512]{1,0:T(8,128)(2,1)S(1)}) custom-call(s32[2]{0:T(128)S(1)} %pad_add_fusion.1.place_ref, bf16[128,128]{1,0:T(8,128)(2,1)S(1)} %shard_map.77.own_ref, bf16[128,128]{1,0:T(8,128)(2,1)S(1)} %collective-permute-done.11.sibling_ref, ...), custom_call_target="tpu_custom_call" | custom-call | tf_op jit(solution)/shard_map/pallas_call | solution.py:262
  67.9 1.6 %collective-permute-start.15 = (bf16[128,512]{1,0:T(8,128)(2,1)S(1)}, bf16[128,512]{1,0:T(8,128)(2,1)S(1)}, u32[]{:S(2)}, u32[]{:S(2)}) collective-permute-start(bf16[128,512]{1,0:T(8,128)(2,1)S(1)} %get-tuple-element.42), channel_id=1, source_target_pairs={{0,8},{8,0},{16,24},{24,16},{1,9},{9,1},{17,25},{25,17},{2,10},{10... | collective-permute-start | bytes 393224 | tf_op jit(solution)/shard_map/ppermute | solution.py:309
  69.5 1.5 %collective-permute-start.16 = (bf16[128,512]{1,0:T(8,128)(2,1)S(1)}, bf16[128,512]{1,0:T(8,128)(2,1)S(1)}, u32[]{:S(2)}, u32[]{:S(2)}) collective-permute-start(bf16[128,512]{1,0:T(8,128)(2,1)S(1)} %get-tuple-element.43), channel_id=1, source_target_pairs={{0,16},{8,24},{16,0},{24,8},{1,17},{9,25},{17,1},{25,9},{2,18},{10... | collective-permute-start | bytes 393224 | tf_op jit(solution)/shard_map/ppermute | solution.py:309
  71.0 0.5 collective-permute-start.17
  71.5 1.6 %collective-permute-done.15.refs_1_ = bf16[128,512]{1,0:T(8,128)(2,1)S(1)} collective-permute-done((bf16[128,512]{1,0:T(8,128)(2,1)S(1)}, bf16[128,512]{1,0:T(8,128)(2,1)S(1)}, u32[]{:S(2)}, u32[]{:S(2)}) %collective-permute-start.15) | collective-permute-done | bytes 131104 | tf_op jit(solution)/shard_map/ppermute | solution.py:309
  73.1 1.3 %collective-permute-done.16.refs_2_ = bf16[128,512]{1,0:T(8,128)(2,1)S(1)} collective-permute-done((bf16[128,512]{1,0:T(8,128)(2,1)S(1)}, bf16[128,512]{1,0:T(8,128)(2,1)S(1)}, u32[]{:S(2)}, u32[]{:S(2)}) %collective-permute-start.16) | collective-permute-done | bytes 131104 | tf_op jit(solution)/shard_map/ppermute | solution.py:309
  74.4 2.4 %collective-permute-done.17.refs_3_ = bf16[128,512]{1,0:T(8,128)(2,1)S(1)} collective-permute-done((bf16[128,512]{1,0:T(8,128)(2,1)S(1)}, bf16[128,512]{1,0:T(8,128)(2,1)S(1)}, u32[]{:S(2)}, u32[]{:S(2)}) %collective-permute-start.17) | collective-permute-done | bytes 131104 | tf_op jit(solution)/shard_map/ppermute | solution.py:309
  76.8 0.1 shard_map.79
  76.9 0.1 collective-permute-start.18
  77.0 1.2 %collective-permute-done.18 = bf16[64,512]{1,0:T(8,128)(2,1)S(1)} collective-permute-done((bf16[64,512]{1,0:T(8,128)(2,1)S(1)}, bf16[64,512]{1,0:T(8,128)(2,1)S(1)}, u32[]{:S(2)}, u32[]{:S(2)}) %collective-permute-start.18) | collective-permute-done | bytes 65568 | tf_op jit(solution)/shard_map/ppermute | solution.py:306
  78.2 0.7 maximum_select_fusion
  (4 shorter events, 0.0 us)
Async XLA Ops:
  2.0 7.6 %collective-permute-start = (bf16[512,4096]{1,0:T(8,128)(2,1)}, bf16[512,4096]{1,0:T(8,128)(2,1)}, u32[]{:S(2)}, u32[]{:S(2)}) collective-permute-start(bf16[512,4096]{1,0:T(8,128)(2,1)} %refs_1_.3), channel_id=1, source_target_pairs={{0,1},{1,0},{2,3},{3,2},{4,5},{5,4},{6,7},{7,6},{8,9},{9,8},{10,11... | collective-permute-start | bytes 12582920 | tf_op jit(solution)/shard_map/ppermute | solution.py:306
  2.5 16.2 %collective-permute-start.1 = (bf16[544,256]{1,0:T(8,128)(2,1)}, bf16[544,256]{1,0:T(8,128)(2,1)S(1)}, u32[]{:S(2)}, u32[]{:S(2)}) collective-permute-start(bf16[544,256]{1,0:T(8,128)(2,1)} %get-tuple-element.26.refs_3_.refs_4_), channel_id=1, source_target_pairs={{0,2},{1,3},{2,0},{3,1},{4,6},{5,7},{6,4},{7,5},{8,10},{9,11},{10,... | collective-permute-start | bytes 835592 | tf_op jit(solution)/shard_map/ppermute | solution.py:306
  5.2 16.7 %collective-permute-start.3 = (bf16[544,256]{1,0:T(8,128)(2,1)}, bf16[544,256]{1,0:T(8,128)(2,1)S(1)}, u32[]{:S(2)}, u32[]{:S(2)}) collective-permute-start(bf16[544,256]{1,0:T(8,128)(2,1)} %get-tuple-element.26.refs_3_.refs_4_), channel_id=1, source_target_pairs={{0,4},{1,5},{2,6},{3,7},{4,0},{5,1},{6,2},{7,3},{8,12},{9,13},{10,... | collective-permute-start | bytes 835592 | tf_op jit(solution)/shard_map/ppermute | solution.py:306
  7.8 22.4 %collective-permute-start.2 = (bf16[544,256]{1,0:T(8,128)(2,1)}, bf16[544,256]{1,0:T(8,128)(2,1)S(1)}, u32[]{:S(2)}, u32[]{:S(2)}) collective-permute-start(bf16[544,256]{1,0:T(8,128)(2,1)} %get-tuple-element.29), channel_id=1, source_target_pairs={{0,3},{1,2},{2,1},{3,0},{4,7},{5,6},{6,5},{7,4},{8,11},{9,10},{10,... | collective-permute-start | bytes 835592 | tf_op jit(solution)/shard_map/ppermute | solution.py:306
  7.8 22.7 %collective-permute-start.4 = (bf16[544,256]{1,0:T(8,128)(2,1)}, bf16[544,256]{1,0:T(8,128)(2,1)S(1)}, u32[]{:S(2)}, u32[]{:S(2)}) collective-permute-start(bf16[544,256]{1,0:T(8,128)(2,1)} %get-tuple-element.29), channel_id=1, source_target_pairs={{0,5},{1,4},{2,7},{3,6},{4,1},{5,0},{6,3},{7,2},{8,13},{9,12},{10,... | collective-permute-start | bytes 835592 | tf_op jit(solution)/shard_map/ppermute | solution.py:306
  9.7 12.2 %collective-permute-start.5 = (bf16[544,256]{1,0:T(8,128)(2,1)}, bf16[544,256]{1,0:T(8,128)(2,1)S(1)}, u32[]{:S(2)}, u32[]{:S(2)}) collective-permute-start(bf16[544,256]{1,0:T(8,128)(2,1)} %get-tuple-element.29), channel_id=1, source_target_pairs={{0,1},{1,0},{2,3},{3,2},{4,5},{5,4},{6,7},{7,6},{8,9},{9,8},{10,11... | collective-permute-start | bytes 835592 | tf_op jit(solution)/shard_map/ppermute | solution.py:306
  21.9 17.8 %collective-permute-start.6 = (bf16[544,256]{1,0:T(8,128)(2,1)S(1)}, bf16[544,256]{1,0:T(8,128)(2,1)S(1)}, u32[]{:S(2)}, u32[]{:S(2)}) collective-permute-start(bf16[544,256]{1,0:T(8,128)(2,1)S(1)} %collective-permute-done.3.refs_5_.refs_8_), channel_id=1, source_target_pairs={{0,2},{1,3},{2,0},{3,1},{4,6},{5,7},{6,4},{7,5},{8,10},{9,11},{10,... | collective-permute-start | bytes 835592 | tf_op jit(solution)/shard_map/ppermute | solution.py:306
  21.9 2.2 %copy-start = (bf16[512,4096]{1,0:T(8,128)(2,1)S(1)}, bf16[512,4096]{1,0:T(8,128)(2,1)}, u32[]{:S(2)}) copy-start(bf16[512,4096]{1,0:T(8,128)(2,1)} %refs_1_.3) | copy-start | bytes 12582916
  24.1 1.0 %copy-start.1 = (bf16[544,256]{1,0:T(8,128)(2,1)S(1)}, bf16[544,256]{1,0:T(8,128)(2,1)}, u32[]{:S(2)}) copy-start(bf16[544,256]{1,0:T(8,128)(2,1)} %get-tuple-element.26.refs_3_.refs_4_) | copy-start | bytes 835588
  25.1 7.9 %copy-start.3 = (bf16[256,512]{1,0:T(8,128)(2,1)S(1)}, bf16[256,512]{1,0:T(8,128)(2,1)}, u32[]{:S(2)}) copy-start(bf16[256,512]{1,0:T(8,128)(2,1)} %refs_0_) | copy-start | bytes 786436
  30.5 17.9 %collective-permute-start.7 = (bf16[544,256]{1,0:T(8,128)(2,1)S(1)}, bf16[544,256]{1,0:T(8,128)(2,1)S(1)}, u32[]{:S(2)}, u32[]{:S(2)}) collective-permute-start(bf16[544,256]{1,0:T(8,128)(2,1)S(1)} %collective-permute-done.4.refs_6_.refs_9_), channel_id=1, source_target_pairs={{0,2},{1,3},{2,0},{3,1},{4,6},{5,7},{6,4},{7,5},{8,10},{9,11},{10,... | collective-permute-start | bytes 835592 | tf_op jit(solution)/shard_map/ppermute | solution.py:306
  33.0 22.9 %collective-permute-start.12 = (bf16[256,512]{1,0:T(8,128)(2,1)S(1)}, bf16[256,512]{1,0:T(8,128)(2,1)S(1)}, u32[]{:S(2)}, u32[]{:S(2)}) collective-permute-start(bf16[256,512]{1,0:T(8,128)(2,1)S(1)} %copy-done.3), channel_id=1, source_target_pairs={{0,2},{1,3},{2,0},{3,1},{4,6},{5,7},{6,4},{7,5},{8,10},{9,11},{10,... | collective-permute-start | bytes 786440 | tf_op jit(solution)/shard_map/ppermute | solution.py:306
  33.1 22.8 %collective-permute-start.13 = (bf16[256,512]{1,0:T(8,128)(2,1)S(1)}, bf16[256,512]{1,0:T(8,128)(2,1)S(1)}, u32[]{:S(2)}, u32[]{:S(2)}) collective-permute-start(bf16[256,512]{1,0:T(8,128)(2,1)S(1)} %copy-done.3), channel_id=1, source_target_pairs={{0,4},{1,5},{2,6},{3,7},{4,0},{5,1},{6,2},{7,3},{8,12},{9,13},{10,... | collective-permute-start | bytes 786440 | tf_op jit(solution)/shard_map/ppermute | solution.py:306
  35.5 12.8 %copy-start.2 = (bf16[544,256]{1,0:T(8,128)(2,1)S(1)}, bf16[544,256]{1,0:T(8,128)(2,1)}, u32[]{:S(2)}) copy-start(bf16[544,256]{1,0:T(8,128)(2,1)} %get-tuple-element.26.refs_3_.refs_4_) | copy-start | bytes 835588
  39.7 22.9 %copy-start.4 = (bf16[256]{0:T(256)(128)(2,1)S(1)}, bf16[256]{0:T(256)(128)(2,1)}, u32[]{:S(2)}) copy-start(bf16[256]{0:T(256)(128)(2,1)} %param.12) | copy-start | bytes 1540
  51.2 6.2 %collective-permute-start.10 = (bf16[144,128]{1,0:T(8,128)(2,1)S(1)}, bf16[144,128]{1,0:T(8,128)(2,1)S(1)}, u32[]{:S(2)}, u32[]{:S(2)}) collective-permute-start(bf16[144,128]{1,0:T(8,128)(2,1)S(1)} %get-tuple-element.38), channel_id=1, source_target_pairs={{0,6},{1,7},{2,4},{3,5},{4,2},{5,3},{6,0},{7,1},{8,14},{9,15},{10,... | collective-permute-start | bytes 110600 | tf_op jit(solution)/shard_map/ppermute | solution.py:306
  55.3 4.0 %collective-permute-start.8 = (bf16[144,128]{1,0:T(8,128)(2,1)S(1)}, bf16[144,128]{1,0:T(8,128)(2,1)S(1)}, u32[]{:S(2)}, u32[]{:S(2)}) collective-permute-start(bf16[144,128]{1,0:T(8,128)(2,1)S(1)} %get-tuple-element.36), channel_id=1, source_target_pairs={{0,2},{1,3},{2,0},{3,1},{4,6},{5,7},{6,4},{7,5},{8,10},{9,11},{10,... | collective-permute-start | bytes 110600 | tf_op jit(solution)/shard_map/ppermute | solution.py:306
  55.3 4.9 %collective-permute-start.9 = (bf16[144,128]{1,0:T(8,128)(2,1)S(1)}, bf16[144,128]{1,0:T(8,128)(2,1)S(1)}, u32[]{:S(2)}, u32[]{:S(2)}) collective-permute-start(bf16[144,128]{1,0:T(8,128)(2,1)S(1)} %get-tuple-element.37), channel_id=1, source_target_pairs={{0,4},{1,5},{2,6},{3,7},{4,0},{5,1},{6,2},{7,3},{8,12},{9,13},{10,... | collective-permute-start | bytes 110600 | tf_op jit(solution)/shard_map/ppermute | solution.py:306
  60.1 6.8 %collective-permute-start.14 = (bf16[256,512]{1,0:T(8,128)(2,1)S(1)}, bf16[256,512]{1,0:T(8,128)(2,1)S(1)}, u32[]{:S(2)}, u32[]{:S(2)}) collective-permute-start(bf16[256,512]{1,0:T(8,128)(2,1)S(1)} %collective-permute-done.13.refs_2_), channel_id=1, source_target_pairs={{0,2},{1,3},{2,0},{3,1},{4,6},{5,7},{6,4},{7,5},{8,10},{9,11},{10,... | collective-permute-start | bytes 786440 | tf_op jit(solution)/shard_map/ppermute | solution.py:306
  62.7 1.3 %collective-permute-start.11 = (bf16[128,128]{1,0:T(8,128)(2,1)S(1)}, bf16[128,128]{1,0:T(8,128)(2,1)S(1)}, u32[]{:S(2)}, u32[]{:S(2)}) collective-permute-start(bf16[128,128]{1,0:T(8,128)(2,1)S(1)} %shard_map.77.own_ref), channel_id=1, source_target_pairs={{0,1},{1,0},{2,3},{3,2},{4,5},{5,4},{6,7},{7,6},{8,9},{9,8},{10,11... | collective-permute-start | bytes 98312 | tf_op jit(solution)/shard_map/ppermute | solution.py:306
  67.9 5.2 %collective-permute-start.15 = (bf16[128,512]{1,0:T(8,128)(2,1)S(1)}, bf16[128,512]{1,0:T(8,128)(2,1)S(1)}, u32[]{:S(2)}, u32[]{:S(2)}) collective-permute-start(bf16[128,512]{1,0:T(8,128)(2,1)S(1)} %get-tuple-element.42), channel_id=1, source_target_pairs={{0,8},{8,0},{16,24},{24,16},{1,9},{9,1},{17,25},{25,17},{2,10},{10... | collective-permute-start | bytes 393224 | tf_op jit(solution)/shard_map/ppermute | solution.py:309
  69.5 5.0 %collective-permute-start.16 = (bf16[128,512]{1,0:T(8,128)(2,1)S(1)}, bf16[128,512]{1,0:T(8,128)(2,1)S(1)}, u32[]{:S(2)}, u32[]{:S(2)}) collective-permute-start(bf16[128,512]{1,0:T(8,128)(2,1)S(1)} %get-tuple-element.43), channel_id=1, source_target_pairs={{0,16},{8,24},{16,0},{24,8},{1,17},{9,25},{17,1},{25,9},{2,18},{10... | collective-permute-start | bytes 393224 | tf_op jit(solution)/shard_map/ppermute | solution.py:309
  71.0 5.9 %collective-permute-start.17 = (bf16[128,512]{1,0:T(8,128)(2,1)S(1)}, bf16[128,512]{1,0:T(8,128)(2,1)S(1)}, u32[]{:S(2)}, u32[]{:S(2)}) collective-permute-start(bf16[128,512]{1,0:T(8,128)(2,1)S(1)} %get-tuple-element.44), channel_id=1, source_target_pairs={{0,24},{8,16},{16,8},{24,0},{1,25},{9,17},{17,9},{25,1},{2,26},{10... | collective-permute-start | bytes 393224 | tf_op jit(solution)/shard_map/ppermute | solution.py:309
  76.9 1.3 %collective-permute-start.18 = (bf16[64,512]{1,0:T(8,128)(2,1)S(1)}, bf16[64,512]{1,0:T(8,128)(2,1)S(1)}, u32[]{:S(2)}, u32[]{:S(2)}) collective-permute-start(bf16[64,512]{1,0:T(8,128)(2,1)S(1)} %get-tuple-element.46), channel_id=1, source_target_pairs={{0,1},{1,0},{2,3},{3,2},{4,5},{5,4},{6,7},{7,6},{8,9},{9,8},{10,11... | collective-permute-start | bytes 196616 | tf_op jit(solution)/shard_map/ppermute | solution.py:306

commit v16 on v11

--- a/solution.py
+++ b/solution.py
@@ -44,18 +44,17 @@
     return copies
 
 
-def add_products(copies, buffer, blocks, acc_ref, rows, depth, fresh):
-    for b, block in enumerate(blocks):
-        for which in range(CORES):
+def add_products(copies, buffer, blocks, base_ref, acc_ref, rows, depth):
+    for which in range(CORES):
+        place = slice(which * rows, (which + 1) * rows)
+        total = None if base_ref is None else base_ref[place, :]
+        for b, block in enumerate(blocks):
             slot = b * CORES + which
             if copies is not None:
                 copies[slot].wait()
             product = jnp.dot(buffer[slot], block[:depth, :], preferred_element_type=jnp.float32)
-            place = slice(which * rows, (which + 1) * rows)
-            if fresh and b == 0:
-                acc_ref[place, :] = product
-            else:
-                acc_ref[place, :] += product
+            total = product if total is None else total + product
+        acc_ref[place, :] = total
 
 
 def project_kernel(count, extra, has_acc, depth, *refs):
@@ -66,9 +65,7 @@
     contexts = (own_ref, sibling_ref)
     copies = start_slices(starts_ref, 0, contexts, buffer, sems, count, depth)
     later = start_slices(starts_ref, count, contexts, later_ref, sems, extra, depth)
-    if has_acc:
-        acc_ref[...] = acc_in[...]
-    add_products(copies, buffer, blocks, acc_ref, own_ref.shape[0], depth, not has_acc)
+    add_products(copies, buffer, blocks, acc_in, acc_ref, own_ref.shape[0], depth)
     for copy in later:
         copy.wait()
 
@@ -108,11 +105,10 @@
     rows = slices_ref.shape[1]
     half = heads * DH
     lines = blocks[0].shape[0] - depth
-    acc_ref[...] = acc_in[...]
     for b, block in enumerate(blocks):
         query_ref[places_ref[b], :lines, :] = block[depth:, :half]
         query_ref[places_ref[b], lines:, :] = block[depth:, half:]
-    add_products(None, slices_ref, blocks[-CORES:], acc_ref, rows, depth, False)
+    add_products(None, slices_ref, blocks[-CORES:], acc_in, acc_ref, rows, depth)
     score_scale = 1.0 / math.sqrt(DH)
     line = lax.broadcasted_iota(jnp.int32, (CORES * rows, 1), 0)
     positions = jnp.where(line < rows, firsts_ref[0] + line, firsts_ref[1] + line - rows)

time: 77.4 us -> 77.4 us (level)
  waiting for transfers between devices: 39.3 us -> 40.1 us
  Pallas kernels: 13.3 us -> 12.5 us
  transfers between devices with their start and end apart: 19 -> 19, of which waited for: 12 -> 12; matrix products, arithmetic and copies ran while one was open for 2% -> 2% of each run, Pallas kernels for 13% -> 12%
where the time goes in v16:
time: 77.4 us; the launch traced here: 77.1 us
  waiting for transfers between devices  40.1 us (52%)
  starting transfers between devices  19.4 us (25%)
  Pallas kernels  12.5 us (16%)
  local copies, waits for them, and re-layouts  4.15 us (5%)
  other arithmetic  0.86 us (1%)
    ppermute x16, waiting for transfers between devices, across(): return lax.ppermute(array, 'ctx', [(i, i ^ bits) for i in range(n_ctx)])  34 us
    ppermute x16, starting transfers between devices, across(): return lax.ppermute(array, 'ctx', [(i, i ^ bits) for i in range(n_ctx)])  15.9 us
    pallas_call x2, Pallas kernels, project(): pl.pallas_call(functools.partial(project_kernel, count, extra, acc is not...  6.45 us
    ppermute x3, waiting for transfers between devices, over_dp(): return lax.ppermute(array, 'dp', [(d, d ^ bits) for d in range(n_dp)])  6.09 us
    ppermute x3, starting transfers between devices, over_dp(): return lax.ppermute(array, 'dp', [(d, d ^ bits) for d in range(n_dp)])  3.55 us
    unnamed x10, local copies, waits for them, and re-layouts  3.16 us
    pallas_call x1, Pallas kernels, attend(): pl.pallas_call(functools.partial(attend_kernel, count, heads, depth, grou...  2.81 us
    pallas_call x1, Pallas kernels, pack(): pl.pallas_call(pack_kernel, out_shape=[out, out], in_specs=[SMEM, ANY, AN...  2.02 us
  transfers between devices with their start and end apart: 19, of which 12 were waited for; matrix products, arithmetic and copies ran while one was open for 2% of the time, Pallas kernels for 12%

profile of v16, /device:TPU:0, one launch (start us, length us, event | category | flops | bytes accessed | tf_op | source)
XLA Modules:
  0.0 77.1 jit_solution(11185199117657500758)
XLA Ops:
  0.0 2.0 %shard_map.73 = (bf16[544,256]{1,0:T(8,128)(2,1)}, bf16[544,256]{1,0:T(8,128)(2,1)}) custom-call(s32[1]{0:T(128)} %bitcast.core_ref, bf16[512,256]{1,0:T(8,128)(2,1)} %key_ref.1, bf16[512,256]{1,0:T(8,128)(2,1)} %value_ref.1, bf16[64,256]{1,0:T(8,128)(2,1)} %query_ref.1), custom_call_target="tpu_custom_call" | custom-call | tf_op jit(solution)/shard_map/pallas_call | solution.py:231
  2.0 0.5 collective-permute-start
  2.5 2.7 %collective-permute-start.1 = (bf16[544,256]{1,0:T(8,128)(2,1)}, bf16[544,256]{1,0:T(8,128)(2,1)S(1)}, u32[]{:S(2)}, u32[]{:S(2)}) collective-permute-start(bf16[544,256]{1,0:T(8,128)(2,1)} %get-tuple-element.26.refs_3_.refs_4_), channel_id=1, source_target_pairs={{0,2},{1,3},{2,0},{3,1},{4,6},{5,7},{6,4},{7,5},{8,10},{9,11},{10,... | collective-permute-start | bytes 835592 | tf_op jit(solution)/shard_map/ppermute | solution.py:302
  5.2 2.6 %collective-permute-start.3 = (bf16[544,256]{1,0:T(8,128)(2,1)}, bf16[544,256]{1,0:T(8,128)(2,1)S(1)}, u32[]{:S(2)}, u32[]{:S(2)}) collective-permute-start(bf16[544,256]{1,0:T(8,128)(2,1)} %get-tuple-element.26.refs_3_.refs_4_), channel_id=1, source_target_pairs={{0,4},{1,5},{2,6},{3,7},{4,0},{5,1},{6,2},{7,3},{8,12},{9,13},{10,... | collective-permute-start | bytes 835592 | tf_op jit(solution)/shard_map/ppermute | solution.py:302
  7.8 0.0 collective-permute-start.2
  7.8 0.2 collective-permute-start.4
  8.0 0.1 stack.71.refs_2_
  8.1 1.6 %collective-permute-done.refs_2_ = bf16[512,4096]{1,0:T(8,128)(2,1)} collective-permute-done((bf16[512,4096]{1,0:T(8,128)(2,1)}, bf16[512,4096]{1,0:T(8,128)(2,1)}, u32[]{:S(2)}, u32[]{:S(2)}) %collective-permute-start) | collective-permute-done | bytes 4194336 | tf_op jit(solution)/shard_map/ppermute | solution.py:302
  9.7 0.4 collective-permute-start.5
  10.1 0.1 slice.8.refs_0_
  10.1 0.8 %slice_bitcast_fusion.3 = (s32[1,128]{1,0:T(1,128)S(1)}, s32[1,128]{1,0:T(1,128)S(1)}, s32[1,128]{1,0:T(1,128)S(1)}, s32[1,128]{1,0:T(1,128)S(1)}) fusion(s32[512]{0:T(512)} %param.11), kind=kLoop, calls=%fused_computation.7 | loop fusion | bytes 4096 | tf_op jit(solution)/shard_map/stack | solution.py:148
  11.0 7.8 %collective-permute-done.1.refs_3_.refs_6_ = bf16[544,256]{1,0:T(8,128)(2,1)S(1)} collective-permute-done((bf16[544,256]{1,0:T(8,128)(2,1)}, bf16[544,256]{1,0:T(8,128)(2,1)S(1)}, u32[]{:S(2)}, u32[]{:S(2)}) %collective-permute-start.1) | collective-permute-done | bytes 278560 | tf_op jit(solution)/shard_map/ppermute | solution.py:302
  18.8 3.2 %collective-permute-done.3.refs_5_.refs_8_ = bf16[544,256]{1,0:T(8,128)(2,1)S(1)} collective-permute-done((bf16[544,256]{1,0:T(8,128)(2,1)}, bf16[544,256]{1,0:T(8,128)(2,1)S(1)}, u32[]{:S(2)}, u32[]{:S(2)}) %collective-permute-start.3) | collective-permute-done | bytes 278560 | tf_op jit(solution)/shard_map/ppermute | solution.py:302
  21.9 0.0 collective-permute-start.6
  21.9 0.0 collective-permute-done.5.refs_4_.refs_5_
  21.9 0.0 copy-start
  21.9 2.2 %copy-done = bf16[512,4096]{1,0:T(8,128)(2,1)S(1)} copy-done((bf16[512,4096]{1,0:T(8,128)(2,1)S(1)}, bf16[512,4096]{1,0:T(8,128)(2,1)}, u32[]{:S(2)}) %copy-start) | copy-done | bytes 4194328
  24.1 0.0 copy-start.1
  24.1 1.0 %copy-done.1 = bf16[544,256]{1,0:T(8,128)(2,1)S(1)} copy-done((bf16[544,256]{1,0:T(8,128)(2,1)S(1)}, bf16[544,256]{1,0:T(8,128)(2,1)}, u32[]{:S(2)}) %copy-start.1) | copy-done | bytes 278552
  25.1 2.6 %shard_map.74 = (f32[1024,256]{1,0:T(8,128)S(1)}, bf16[2,16,512]{2,1,0:T(8,128)(2,1)}) custom-call(s32[2]{0:T(128)S(1)} %bitcast.21, bf16[512,4096]{1,0:T(8,128)(2,1)S(1)} %copy-done, bf16[512,4096]{1,0:T(8,128)(2,1)} %collective-permute-done.refs_2_, bf16[544,256]{1,0:T(8,128)(2,1)S(1)} %copy-done.1, bf16[544,256]{1,0:T(8,128)(2,1)S(1)} %collective-permute-done.5.refs_4_.refs_5_), custom_call_target="tpu_custom_call" | custom-call | flops 536870912 | bytes 2097152 | tf_op jit(solution)/shard_map/pallas_call | solution.py:78
  27.7 2.5 %collective-permute-done.2.refs_4_.refs_7_ = bf16[544,256]{1,0:T(8,128)(2,1)S(1)} collective-permute-done((bf16[544,256]{1,0:T(8,128)(2,1)}, bf16[544,256]{1,0:T(8,128)(2,1)S(1)}, u32[]{:S(2)}, u32[]{:S(2)}) %collective-permute-start.2) | collective-permute-done | bytes 278560 | tf_op jit(solution)/shard_map/ppermute | solution.py:302
  30.2 0.3 collective-permute-done.4.refs_6_.refs_9_
  30.5 0.0 copy-start.3
  30.5 0.0 copy-start.2
  30.5 2.5 %collective-permute-start.7 = (bf16[544,256]{1,0:T(8,128)(2,1)S(1)}, bf16[544,256]{1,0:T(8,128)(2,1)S(1)}, u32[]{:S(2)}, u32[]{:S(2)}) collective-permute-start(bf16[544,256]{1,0:T(8,128)(2,1)S(1)} %collective-permute-done.4.refs_6_.refs_9_), channel_id=1, source_target_pairs={{0,2},{1,3},{2,0},{3,1},{4,6},{5,7},{6,4},{7,5},{8,10},{9,11},{10,... | collective-permute-start | bytes 835592 | tf_op jit(solution)/shard_map/ppermute | solution.py:302
  33.0 3.9 %shard_map.75 = (f32[1024,256]{1,0:T(8,128)S(1)}, bf16[4,512,512]{2,1,0:T(8,128)(2,1)S(1)}) custom-call(s32[6]{0:T(128)S(1)} %slice.8.refs_0_, bf16[512,4096]{1,0:T(8,128)(2,1)S(1)} %copy-done, bf16[512,4096]{1,0:T(8,128)(2,1)} %collective-permute-done.refs_2_, bf16[544,256]{1,0:T(8,128)(2,1)S(1)} %collective-permute-done.1.refs_3_.refs_6_, ...), custom_call_target="tpu_custom_call" | custom-call | flops 1073741824 | bytes 4194304 | tf_op jit(solution)/shard_map/pallas_call | solution.py:78
  36.9 0.0 copy-start.4
  36.9 0.0 copy-done.3
  36.9 2.4 %collective-permute-start.13 = (bf16[256,512]{1,0:T(8,128)(2,1)S(1)}, bf16[256,512]{1,0:T(8,128)(2,1)S(1)}, u32[]{:S(2)}, u32[]{:S(2)}) collective-permute-start(bf16[256,512]{1,0:T(8,128)(2,1)S(1)} %copy-done.3), channel_id=1, source_target_pairs={{0,4},{1,5},{2,6},{3,7},{4,0},{5,1},{6,2},{7,3},{8,12},{9,13},{10,... | collective-permute-start | bytes 786440 | tf_op jit(solution)/shard_map/ppermute | solution.py:302
  39.4 0.1 pad_add_fusion.2.refs_0_
  39.4 0.1 collective-permute-start.12
  39.5 0.0 collective-permute-done.6.refs_10_
  39.5 7.2 %collective-permute-done.7.refs_11_ = bf16[544,256]{1,0:T(8,128)(2,1)S(1)} collective-permute-done((bf16[544,256]{1,0:T(8,128)(2,1)S(1)}, bf16[544,256]{1,0:T(8,128)(2,1)S(1)}, u32[]{:S(2)}, u32[]{:S(2)}) %collective-permute-start.7) | collective-permute-done | bytes 278560 | tf_op jit(solution)/shard_map/ppermute | solution.py:302
  46.7 0.0 copy-done.2
  46.7 2.8 %shard_map.76 = (bf16[144,128]{1,0:T(8,128)(2,1)S(1)}, bf16[144,128]{1,0:T(8,128)(2,1)S(1)}, bf16[144,128]{1,0:T(8,128)(2,1)S(1)}, bf16[144,128]{1,0:T(8,128)(2,1)S(1)}) custom-call(s32[2]{0:T(128)S(1)} %pad_add_fusion.2.refs_0_, s32[4]{0:T(128)S(1)} %iota_xor_fusion.refs_1_, s32[8]{0:T(128)S(1)} %stack.71.refs_2_, ...), custom_call_target="tpu_custom_call" | custom-call | flops 536870912 | bytes 2097152 | tf_op jit(solution)/shard_map/pallas_call | solution.py:154
  49.5 2.8 %collective-permute-done.13.refs_2_ = bf16[256,512]{1,0:T(8,128)(2,1)S(1)} collective-permute-done((bf16[256,512]{1,0:T(8,128)(2,1)S(1)}, bf16[256,512]{1,0:T(8,128)(2,1)S(1)}, u32[]{:S(2)}, u32[]{:S(2)}) %collective-permute-start.13) | collective-permute-done | bytes 262176 | tf_op jit(solution)/shard_map/ppermute | solution.py:302
  52.3 0.0 collective-permute-start.14
  52.3 2.0 %collective-permute-start.10 = (bf16[144,128]{1,0:T(8,128)(2,1)S(1)}, bf16[144,128]{1,0:T(8,128)(2,1)S(1)}, u32[]{:S(2)}, u32[]{:S(2)}) collective-permute-start(bf16[144,128]{1,0:T(8,128)(2,1)S(1)} %get-tuple-element.38), channel_id=1, source_target_pairs={{0,6},{1,7},{2,4},{3,5},{4,2},{5,3},{6,0},{7,1},{8,14},{9,15},{10,... | collective-permute-start | bytes 110600 | tf_op jit(solution)/shard_map/ppermute | solution.py:302
  54.3 1.1 %collective-permute-start.8 = (bf16[144,128]{1,0:T(8,128)(2,1)S(1)}, bf16[144,128]{1,0:T(8,128)(2,1)S(1)}, u32[]{:S(2)}, u32[]{:S(2)}) collective-permute-start(bf16[144,128]{1,0:T(8,128)(2,1)S(1)} %get-tuple-element.36), channel_id=1, source_target_pairs={{0,2},{1,3},{2,0},{3,1},{4,6},{5,7},{6,4},{7,5},{8,10},{9,11},{10,... | collective-permute-start | bytes 110600 | tf_op jit(solution)/shard_map/ppermute | solution.py:302
  55.4 1.3 %collective-permute-start.9 = (bf16[144,128]{1,0:T(8,128)(2,1)S(1)}, bf16[144,128]{1,0:T(8,128)(2,1)S(1)}, u32[]{:S(2)}, u32[]{:S(2)}) collective-permute-start(bf16[144,128]{1,0:T(8,128)(2,1)S(1)} %get-tuple-element.37), channel_id=1, source_target_pairs={{0,4},{1,5},{2,6},{3,7},{4,0},{5,1},{6,2},{7,3},{8,12},{9,13},{10,... | collective-permute-start | bytes 110600 | tf_op jit(solution)/shard_map/ppermute | solution.py:302
  56.7 0.0 copy-done.4
  56.7 6.3 %collective-permute-done.10.refs_3_ = bf16[144,128]{1,0:T(8,128)(2,1)S(1)} collective-permute-done((bf16[144,128]{1,0:T(8,128)(2,1)S(1)}, bf16[144,128]{1,0:T(8,128)(2,1)S(1)}, u32[]{:S(2)}, u32[]{:S(2)}) %collective-permute-start.10) | collective-permute-done | bytes 36896 | tf_op jit(solution)/shard_map/ppermute | solution.py:302
  62.9 0.0 collective-permute-done.8.refs_1_
  63.0 0.0 collective-permute-done.9.refs_2_
  63.0 0.2 shard_map.77.own_ref
  63.1 0.1 collective-permute-start.11
  63.2 0.1 pad_add_fusion.1.place_ref
  63.3 0.0 collective-permute-done.12.refs_1_
  63.3 1.1 %collective-permute-done.11.sibling_ref = bf16[128,128]{1,0:T(8,128)(2,1)S(1)} collective-permute-done((bf16[128,128]{1,0:T(8,128)(2,1)S(1)}, bf16[128,128]{1,0:T(8,128)(2,1)S(1)}, u32[]{:S(2)}, u32[]{:S(2)}) %collective-permute-start.11) | collective-permute-done | bytes 32800 | tf_op jit(solution)/shard_map/ppermute | solution.py:302
  64.4 0.0 collective-permute-done.14.refs_3_
  64.4 1.0 %shard_map.78 = (bf16[128,512]{1,0:T(8,128)(2,1)S(1)}, bf16[128,512]{1,0:T(8,128)(2,1)S(1)}, bf16[128,512]{1,0:T(8,128)(2,1)S(1)}, bf16[128,512]{1,0:T(8,128)(2,1)S(1)}) custom-call(s32[2]{0:T(128)S(1)} %pad_add_fusion.1.place_ref, bf16[128,128]{1,0:T(8,128)(2,1)S(1)} %shard_map.77.own_ref, bf16[128,128]{1,0:T(8,128)(2,1)S(1)} %collective-permute-done.11.sibling_ref, ...), custom_call_target="tpu_custom_call" | custom-call | tf_op jit(solution)/shard_map/pallas_call | solution.py:258
  65.4 1.6 %collective-permute-start.15 = (bf16[128,512]{1,0:T(8,128)(2,1)S(1)}, bf16[128,512]{1,0:T(8,128)(2,1)S(1)}, u32[]{:S(2)}, u32[]{:S(2)}) collective-permute-start(bf16[128,512]{1,0:T(8,128)(2,1)S(1)} %get-tuple-element.42), channel_id=1, source_target_pairs={{0,8},{8,0},{16,24},{24,16},{1,9},{9,1},{17,25},{25,17},{2,10},{10... | collective-permute-start | bytes 393224 | tf_op jit(solution)/shard_map/ppermute | solution.py:305
  67.0 1.5 %collective-permute-start.16 = (bf16[128,512]{1,0:T(8,128)(2,1)S(1)}, bf16[128,512]{1,0:T(8,128)(2,1)S(1)}, u32[]{:S(2)}, u32[]{:S(2)}) collective-permute-start(bf16[128,512]{1,0:T(8,128)(2,1)S(1)} %get-tuple-element.43), channel_id=1, source_target_pairs={{0,16},{8,24},{16,0},{24,8},{1,17},{9,25},{17,1},{25,9},{2,18},{10... | collective-permute-start | bytes 393224 | tf_op jit(solution)/shard_map/ppermute | solution.py:305
  68.5 0.5 collective-permute-start.17
  69.0 2.4 %collective-permute-done.15.refs_1_ = bf16[128,512]{1,0:T(8,128)(2,1)S(1)} collective-permute-done((bf16[128,512]{1,0:T(8,128)(2,1)S(1)}, bf16[128,512]{1,0:T(8,128)(2,1)S(1)}, u32[]{:S(2)}, u32[]{:S(2)}) %collective-permute-start.15) | collective-permute-done | bytes 131104 | tf_op jit(solution)/shard_map/ppermute | solution.py:305
  71.4 3.7 %collective-permute-done.16.refs_2_ = bf16[128,512]{1,0:T(8,128)(2,1)S(1)} collective-permute-done((bf16[128,512]{1,0:T(8,128)(2,1)S(1)}, bf16[128,512]{1,0:T(8,128)(2,1)S(1)}, u32[]{:S(2)}, u32[]{:S(2)}) %collective-permute-start.16) | collective-permute-done | bytes 131104 | tf_op jit(solution)/shard_map/ppermute | solution.py:305
  75.1 0.0 collective-permute-done.17.refs_3_
  75.1 0.1 shard_map.79
  75.1 0.1 collective-permute-start.18
  75.2 1.2 %collective-permute-done.18 = bf16[64,512]{1,0:T(8,128)(2,1)S(1)} collective-permute-done((bf16[64,512]{1,0:T(8,128)(2,1)S(1)}, bf16[64,512]{1,0:T(8,128)(2,1)S(1)}, u32[]{:S(2)}, u32[]{:S(2)}) %collective-permute-start.18) | collective-permute-done | bytes 65568 | tf_op jit(solution)/shard_map/ppermute | solution.py:302
  76.5 0.7 maximum_select_fusion
  (4 shorter events, 0.0 us)
Async XLA Ops:
  2.0 7.6 %collective-permute-start = (bf16[512,4096]{1,0:T(8,128)(2,1)}, bf16[512,4096]{1,0:T(8,128)(2,1)}, u32[]{:S(2)}, u32[]{:S(2)}) collective-permute-start(bf16[512,4096]{1,0:T(8,128)(2,1)} %refs_1_.3), channel_id=1, source_target_pairs={{0,1},{1,0},{2,3},{3,2},{4,5},{5,4},{6,7},{7,6},{8,9},{9,8},{10,11... | collective-permute-start | bytes 12582920 | tf_op jit(solution)/shard_map/ppermute | solution.py:302
  2.5 16.2 %collective-permute-start.1 = (bf16[544,256]{1,0:T(8,128)(2,1)}, bf16[544,256]{1,0:T(8,128)(2,1)S(1)}, u32[]{:S(2)}, u32[]{:S(2)}) collective-permute-start(bf16[544,256]{1,0:T(8,128)(2,1)} %get-tuple-element.26.refs_3_.refs_4_), channel_id=1, source_target_pairs={{0,2},{1,3},{2,0},{3,1},{4,6},{5,7},{6,4},{7,5},{8,10},{9,11},{10,... | collective-permute-start | bytes 835592 | tf_op jit(solution)/shard_map/ppermute | solution.py:302
  5.2 16.7 %collective-permute-start.3 = (bf16[544,256]{1,0:T(8,128)(2,1)}, bf16[544,256]{1,0:T(8,128)(2,1)S(1)}, u32[]{:S(2)}, u32[]{:S(2)}) collective-permute-start(bf16[544,256]{1,0:T(8,128)(2,1)} %get-tuple-element.26.refs_3_.refs_4_), channel_id=1, source_target_pairs={{0,4},{1,5},{2,6},{3,7},{4,0},{5,1},{6,2},{7,3},{8,12},{9,13},{10,... | collective-permute-start | bytes 835592 | tf_op jit(solution)/shard_map/ppermute | solution.py:302
  7.8 22.4 %collective-permute-start.2 = (bf16[544,256]{1,0:T(8,128)(2,1)}, bf16[544,256]{1,0:T(8,128)(2,1)S(1)}, u32[]{:S(2)}, u32[]{:S(2)}) collective-permute-start(bf16[544,256]{1,0:T(8,128)(2,1)} %get-tuple-element.29), channel_id=1, source_target_pairs={{0,3},{1,2},{2,1},{3,0},{4,7},{5,6},{6,5},{7,4},{8,11},{9,10},{10,... | collective-permute-start | bytes 835592 | tf_op jit(solution)/shard_map/ppermute | solution.py:302
  7.8 22.7 %collective-permute-start.4 = (bf16[544,256]{1,0:T(8,128)(2,1)}, bf16[544,256]{1,0:T(8,128)(2,1)S(1)}, u32[]{:S(2)}, u32[]{:S(2)}) collective-permute-start(bf16[544,256]{1,0:T(8,128)(2,1)} %get-tuple-element.29), channel_id=1, source_target_pairs={{0,5},{1,4},{2,7},{3,6},{4,1},{5,0},{6,3},{7,2},{8,13},{9,12},{10,... | collective-permute-start | bytes 835592 | tf_op jit(solution)/shard_map/ppermute | solution.py:302
  9.7 12.2 %collective-permute-start.5 = (bf16[544,256]{1,0:T(8,128)(2,1)}, bf16[544,256]{1,0:T(8,128)(2,1)S(1)}, u32[]{:S(2)}, u32[]{:S(2)}) collective-permute-start(bf16[544,256]{1,0:T(8,128)(2,1)} %get-tuple-element.29), channel_id=1, source_target_pairs={{0,1},{1,0},{2,3},{3,2},{4,5},{5,4},{6,7},{7,6},{8,9},{9,8},{10,11... | collective-permute-start | bytes 835592 | tf_op jit(solution)/shard_map/ppermute | solution.py:302
  21.9 17.6 %collective-permute-start.6 = (bf16[544,256]{1,0:T(8,128)(2,1)S(1)}, bf16[544,256]{1,0:T(8,128)(2,1)S(1)}, u32[]{:S(2)}, u32[]{:S(2)}) collective-permute-start(bf16[544,256]{1,0:T(8,128)(2,1)S(1)} %collective-permute-done.3.refs_5_.refs_8_), channel_id=1, source_target_pairs={{0,2},{1,3},{2,0},{3,1},{4,6},{5,7},{6,4},{7,5},{8,10},{9,11},{10,... | collective-permute-start | bytes 835592 | tf_op jit(solution)/shard_map/ppermute | solution.py:302
  21.9 2.2 %copy-start = (bf16[512,4096]{1,0:T(8,128)(2,1)S(1)}, bf16[512,4096]{1,0:T(8,128)(2,1)}, u32[]{:S(2)}) copy-start(bf16[512,4096]{1,0:T(8,128)(2,1)} %refs_1_.3) | copy-start | bytes 12582916
  24.1 1.0 %copy-start.1 = (bf16[544,256]{1,0:T(8,128)(2,1)S(1)}, bf16[544,256]{1,0:T(8,128)(2,1)}, u32[]{:S(2)}) copy-start(bf16[544,256]{1,0:T(8,128)(2,1)} %get-tuple-element.26.refs_3_.refs_4_) | copy-start | bytes 835588
  30.5 6.4 %copy-start.3 = (bf16[256,512]{1,0:T(8,128)(2,1)S(1)}, bf16[256,512]{1,0:T(8,128)(2,1)}, u32[]{:S(2)}) copy-start(bf16[256,512]{1,0:T(8,128)(2,1)} %refs_0_) | copy-start | bytes 786436
  30.5 16.2 %copy-start.2 = (bf16[544,256]{1,0:T(8,128)(2,1)S(1)}, bf16[544,256]{1,0:T(8,128)(2,1)}, u32[]{:S(2)}) copy-start(bf16[544,256]{1,0:T(8,128)(2,1)} %get-tuple-element.26.refs_3_.refs_4_) | copy-start | bytes 835588
  30.5 16.2 %collective-permute-start.7 = (bf16[544,256]{1,0:T(8,128)(2,1)S(1)}, bf16[544,256]{1,0:T(8,128)(2,1)S(1)}, u32[]{:S(2)}, u32[]{:S(2)}) collective-permute-start(bf16[544,256]{1,0:T(8,128)(2,1)S(1)} %collective-permute-done.4.refs_6_.refs_9_), channel_id=1, source_target_pairs={{0,2},{1,3},{2,0},{3,1},{4,6},{5,7},{6,4},{7,5},{8,10},{9,11},{10,... | collective-permute-start | bytes 835592 | tf_op jit(solution)/shard_map/ppermute | solution.py:302
  36.9 19.8 %copy-start.4 = (bf16[256]{0:T(256)(128)(2,1)S(1)}, bf16[256]{0:T(256)(128)(2,1)}, u32[]{:S(2)}) copy-start(bf16[256]{0:T(256)(128)(2,1)} %param.12) | copy-start | bytes 1540
  36.9 15.4 %collective-permute-start.13 = (bf16[256,512]{1,0:T(8,128)(2,1)S(1)}, bf16[256,512]{1,0:T(8,128)(2,1)S(1)}, u32[]{:S(2)}, u32[]{:S(2)}) collective-permute-start(bf16[256,512]{1,0:T(8,128)(2,1)S(1)} %copy-done.3), channel_id=1, source_target_pairs={{0,4},{1,5},{2,6},{3,7},{4,0},{5,1},{6,2},{7,3},{8,12},{9,13},{10,... | collective-permute-start | bytes 786440 | tf_op jit(solution)/shard_map/ppermute | solution.py:302
  39.4 23.8 %collective-permute-start.12 = (bf16[256,512]{1,0:T(8,128)(2,1)S(1)}, bf16[256,512]{1,0:T(8,128)(2,1)S(1)}, u32[]{:S(2)}, u32[]{:S(2)}) collective-permute-start(bf16[256,512]{1,0:T(8,128)(2,1)S(1)} %copy-done.3), channel_id=1, source_target_pairs={{0,2},{1,3},{2,0},{3,1},{4,6},{5,7},{6,4},{7,5},{8,10},{9,11},{10,... | collective-permute-start | bytes 786440 | tf_op jit(solution)/shard_map/ppermute | solution.py:302
  52.3 12.1 %collective-permute-start.14 = (bf16[256,512]{1,0:T(8,128)(2,1)S(1)}, bf16[256,512]{1,0:T(8,128)(2,1)S(1)}, u32[]{:S(2)}, u32[]{:S(2)}) collective-permute-start(bf16[256,512]{1,0:T(8,128)(2,1)S(1)} %collective-permute-done.13.refs_2_), channel_id=1, source_target_pairs={{0,2},{1,3},{2,0},{3,1},{4,6},{5,7},{6,4},{7,5},{8,10},{9,11},{10,... | collective-permute-start | bytes 786440 | tf_op jit(solution)/shard_map/ppermute | solution.py:302
  52.3 10.6 %collective-permute-start.10 = (bf16[144,128]{1,0:T(8,128)(2,1)S(1)}, bf16[144,128]{1,0:T(8,128)(2,1)S(1)}, u32[]{:S(2)}, u32[]{:S(2)}) collective-permute-start(bf16[144,128]{1,0:T(8,128)(2,1)S(1)} %get-tuple-element.38), channel_id=1, source_target_pairs={{0,6},{1,7},{2,4},{3,5},{4,2},{5,3},{6,0},{7,1},{8,14},{9,15},{10,... | collective-permute-start | bytes 110600 | tf_op jit(solution)/shard_map/ppermute | solution.py:302
  54.3 8.7 %collective-permute-start.8 = (bf16[144,128]{1,0:T(8,128)(2,1)S(1)}, bf16[144,128]{1,0:T(8,128)(2,1)S(1)}, u32[]{:S(2)}, u32[]{:S(2)}) collective-permute-start(bf16[144,128]{1,0:T(8,128)(2,1)S(1)} %get-tuple-element.36), channel_id=1, source_target_pairs={{0,2},{1,3},{2,0},{3,1},{4,6},{5,7},{6,4},{7,5},{8,10},{9,11},{10,... | collective-permute-start | bytes 110600 | tf_op jit(solution)/shard_map/ppermute | solution.py:302
  55.4 7.5 %collective-permute-start.9 = (bf16[144,128]{1,0:T(8,128)(2,1)S(1)}, bf16[144,128]{1,0:T(8,128)(2,1)S(1)}, u32[]{:S(2)}, u32[]{:S(2)}) collective-permute-start(bf16[144,128]{1,0:T(8,128)(2,1)S(1)} %get-tuple-element.37), channel_id=1, source_target_pairs={{0,4},{1,5},{2,6},{3,7},{4,0},{5,1},{6,2},{7,3},{8,12},{9,13},{10,... | collective-permute-start | bytes 110600 | tf_op jit(solution)/shard_map/ppermute | solution.py:302
  63.1 1.3 %collective-permute-start.11 = (bf16[128,128]{1,0:T(8,128)(2,1)S(1)}, bf16[128,128]{1,0:T(8,128)(2,1)S(1)}, u32[]{:S(2)}, u32[]{:S(2)}) collective-permute-start(bf16[128,128]{1,0:T(8,128)(2,1)S(1)} %shard_map.77.own_ref), channel_id=1, source_target_pairs={{0,1},{1,0},{2,3},{3,2},{4,5},{5,4},{6,7},{7,6},{8,9},{9,8},{10,11... | collective-permute-start | bytes 98312 | tf_op jit(solution)/shard_map/ppermute | solution.py:302
  65.4 6.0 %collective-permute-start.15 = (bf16[128,512]{1,0:T(8,128)(2,1)S(1)}, bf16[128,512]{1,0:T(8,128)(2,1)S(1)}, u32[]{:S(2)}, u32[]{:S(2)}) collective-permute-start(bf16[128,512]{1,0:T(8,128)(2,1)S(1)} %get-tuple-element.42), channel_id=1, source_target_pairs={{0,8},{8,0},{16,24},{24,16},{1,9},{9,1},{17,25},{25,17},{2,10},{10... | collective-permute-start | bytes 393224 | tf_op jit(solution)/shard_map/ppermute | solution.py:305
  67.0 8.1 %collective-permute-start.16 = (bf16[128,512]{1,0:T(8,128)(2,1)S(1)}, bf16[128,512]{1,0:T(8,128)(2,1)S(1)}, u32[]{:S(2)}, u32[]{:S(2)}) collective-permute-start(bf16[128,512]{1,0:T(8,128)(2,1)S(1)} %get-tuple-element.43), channel_id=1, source_target_pairs={{0,16},{8,24},{16,0},{24,8},{1,17},{9,25},{17,1},{25,9},{2,18},{10... | collective-permute-start | bytes 393224 | tf_op jit(solution)/shard_map/ppermute | solution.py:305
  68.5 6.6 %collective-permute-start.17 = (bf16[128,512]{1,0:T(8,128)(2,1)S(1)}, bf16[128,512]{1,0:T(8,128)(2,1)S(1)}, u32[]{:S(2)}, u32[]{:S(2)}) collective-permute-start(bf16[128,512]{1,0:T(8,128)(2,1)S(1)} %get-tuple-element.44), channel_id=1, source_target_pairs={{0,24},{8,16},{16,8},{24,0},{1,25},{9,17},{17,9},{25,1},{2,26},{10... | collective-permute-start | bytes 393224 | tf_op jit(solution)/shard_map/ppermute | solution.py:305
  75.1 1.3 %collective-permute-start.18 = (bf16[64,512]{1,0:T(8,128)(2,1)S(1)}, bf16[64,512]{1,0:T(8,128)(2,1)S(1)}, u32[]{:S(2)}, u32[]{:S(2)}) collective-permute-start(bf16[64,512]{1,0:T(8,128)(2,1)S(1)} %get-tuple-element.46), channel_id=1, source_target_pairs={{0,1},{1,0},{2,3},{3,2},{4,5},{5,4},{6,7},{7,6},{8,9},{9,8},{10,11... | collective-permute-start | bytes 196616 | tf_op jit(solution)/shard_map/ppermute | solution.py:302

commit v17 on v16

--- a/solution.py
+++ b/solution.py
@@ -241,13 +241,11 @@
 def output_kernel(place_ref, own_ref, sibling_ref, *refs):
     chips = (len(refs) - 1) // 2
     weights, terms, result = refs[:chips], refs[chips:-1], refs[-1]
-    half = own_ref.shape[1]
-    mine = pl.ds(pl.multiple_of(place_ref[1] * half, DH), half)
-    other = pl.ds(pl.multiple_of((1 - place_ref[1]) * half, DH), half)
     own, sibling = own_ref[...], sibling_ref[...]
+    first = place_ref[1] == 0
+    rows = jnp.concatenate([jnp.where(first, own, sibling), jnp.where(first, sibling, own)], axis=1)
     for j, w_ref in enumerate(weights):
-        total = jnp.dot(own, w_ref[mine, :], preferred_element_type=jnp.float32)
-        total += jnp.dot(sibling, w_ref[other, :], preferred_element_type=jnp.float32)
+        total = jnp.dot(rows, w_ref[...], preferred_element_type=jnp.float32)
         result[j] = total.astype(jnp.bfloat16)
     for i, term in enumerate(terms):
         term[...] = result[place_ref[0] ^ i]
@@ -286,6 +284,23 @@
         out_specs=[VMEM, VMEM],
         compiler_params=PARAMS,
     )(core, *terms)
+
+
+def place_kernel(core_ref, mine_ref, theirs_ref, out_ref):
+    width = mine_ref.shape[1]
+    for part_ref, who in ((mine_ref, core_ref[0]), (theirs_ref, 1 - core_ref[0])):
+        out_ref[:, pl.ds(pl.multiple_of(who * width, DH), width)] = part_ref[...]
+
+
+def place_lanes(core, mine, theirs):
+    rows, width = mine.shape
+    return pl.pallas_call(
+        place_kernel,
+        out_shape=jax.ShapeDtypeStruct((rows, CORES * width), mine.dtype),
+        in_specs=[SMEM, VMEM, VMEM],
+        out_specs=VMEM,
+        compiler_params=PARAMS,
+    )(core, mine, theirs)
 
 
 def on_device(n_dp, n_ctx, context, w_key, w_value, queries, offsets, head_gain, w_out):
@@ -354,9 +369,7 @@
     terms = [terms[0]] + [over_dp(terms[i], i) for i in range(1, n_dp)]
     mine, other = add_terms(core_only, terms)
     theirs = across(other, 1)
-    return jnp.where(
-        core == 0, jnp.concatenate([mine, theirs], axis=1), jnp.concatenate([theirs, mine], axis=1)
-    )
+    return place_lanes(core_only, mine, theirs)
 
 
 def solution(mesh):

time: 77.4 us -> 77.3 us (level)
  no operation moved by 1% of the time
where the time goes in v17:
time: 77.3 us; the launch traced here: 77 us
  waiting for transfers between devices  40.1 us (52%)
  starting transfers between devices  19.4 us (25%)
  Pallas kernels  13.1 us (17%)
  local copies, waits for them, and re-layouts  4.15 us (5%)
    ppermute x16, waiting for transfers between devices, across(): return lax.ppermute(array, 'ctx', [(i, i ^ bits) for i in range(n_ctx)])  34 us
    ppermute x16, starting transfers between devices, across(): return lax.ppermute(array, 'ctx', [(i, i ^ bits) for i in range(n_ctx)])  15.9 us
    pallas_call x2, Pallas kernels, project(): pl.pallas_call(functools.partial(project_kernel, count, extra, acc is not...  6.45 us
    ppermute x3, waiting for transfers between devices, over_dp(): return lax.ppermute(array, 'dp', [(d, d ^ bits) for d in range(n_dp)])  6.1 us
    ppermute x3, starting transfers between devices, over_dp(): return lax.ppermute(array, 'dp', [(d, d ^ bits) for d in range(n_dp)])  3.55 us
    unnamed x10, local copies, waits for them, and re-layouts  3.16 us
    pallas_call x1, Pallas kernels, attend(): pl.pallas_call(functools.partial(attend_kernel, count, heads, depth, grou...  2.81 us
    pallas_call x1, Pallas kernels, pack(): pl.pallas_call(pack_kernel, out_shape=[out, out], in_specs=[SMEM, ANY, AN...  2.02 us
  transfers between devices with their start and end apart: 19, of which 12 were waited for; matrix products, arithmetic and copies ran while one was open for 2% of the time, Pallas kernels for 12%

profile of v17, /device:TPU:0, one launch (start us, length us, event | category | flops | bytes accessed | tf_op | source)
XLA Modules:
  0.0 77.0 jit_solution(16453234702964515042)
XLA Ops:
  0.0 2.0 %shard_map.73 = (bf16[544,256]{1,0:T(8,128)(2,1)}, bf16[544,256]{1,0:T(8,128)(2,1)}) custom-call(s32[1]{0:T(128)} %bitcast.core_ref, bf16[512,256]{1,0:T(8,128)(2,1)} %key_ref.1, bf16[512,256]{1,0:T(8,128)(2,1)} %value_ref.1, bf16[64,256]{1,0:T(8,128)(2,1)} %query_ref.1), custom_call_target="tpu_custom_call" | custom-call | tf_op jit(solution)/shard_map/pallas_call | solution.py:231
  2.0 0.5 collective-permute-start
  2.5 2.7 %collective-permute-start.1 = (bf16[544,256]{1,0:T(8,128)(2,1)}, bf16[544,256]{1,0:T(8,128)(2,1)S(1)}, u32[]{:S(2)}, u32[]{:S(2)}) collective-permute-start(bf16[544,256]{1,0:T(8,128)(2,1)} %get-tuple-element.26.refs_3_.refs_4_), channel_id=1, source_target_pairs={{0,2},{1,3},{2,0},{3,1},{4,6},{5,7},{6,4},{7,5},{8,10},{9,11},{10,... | collective-permute-start | bytes 835592 | tf_op jit(solution)/shard_map/ppermute | solution.py:317
  5.2 2.6 %collective-permute-start.3 = (bf16[544,256]{1,0:T(8,128)(2,1)}, bf16[544,256]{1,0:T(8,128)(2,1)S(1)}, u32[]{:S(2)}, u32[]{:S(2)}) collective-permute-start(bf16[544,256]{1,0:T(8,128)(2,1)} %get-tuple-element.26.refs_3_.refs_4_), channel_id=1, source_target_pairs={{0,4},{1,5},{2,6},{3,7},{4,0},{5,1},{6,2},{7,3},{8,12},{9,13},{10,... | collective-permute-start | bytes 835592 | tf_op jit(solution)/shard_map/ppermute | solution.py:317
  7.8 0.0 collective-permute-start.2
  7.8 0.2 collective-permute-start.4
  8.0 0.1 stack.71.refs_2_
  8.1 1.6 %collective-permute-done.refs_2_ = bf16[512,4096]{1,0:T(8,128)(2,1)} collective-permute-done((bf16[512,4096]{1,0:T(8,128)(2,1)}, bf16[512,4096]{1,0:T(8,128)(2,1)}, u32[]{:S(2)}, u32[]{:S(2)}) %collective-permute-start) | collective-permute-done | bytes 4194336 | tf_op jit(solution)/shard_map/ppermute | solution.py:317
  9.7 0.4 collective-permute-start.5
  10.1 0.1 slice.8.refs_0_
  10.1 0.8 %slice_bitcast_fusion.3 = (s32[1,128]{1,0:T(1,128)S(1)}, s32[1,128]{1,0:T(1,128)S(1)}, s32[1,128]{1,0:T(1,128)S(1)}, s32[1,128]{1,0:T(1,128)S(1)}) fusion(s32[512]{0:T(512)} %param.11), kind=kLoop, calls=%fused_computation.6 | loop fusion | bytes 4096 | tf_op jit(solution)/shard_map/stack | solution.py:148
  11.0 7.8 %collective-permute-done.1.refs_3_.refs_6_ = bf16[544,256]{1,0:T(8,128)(2,1)S(1)} collective-permute-done((bf16[544,256]{1,0:T(8,128)(2,1)}, bf16[544,256]{1,0:T(8,128)(2,1)S(1)}, u32[]{:S(2)}, u32[]{:S(2)}) %collective-permute-start.1) | collective-permute-done | bytes 278560 | tf_op jit(solution)/shard_map/ppermute | solution.py:317
  18.8 3.2 %collective-permute-done.3.refs_5_.refs_8_ = bf16[544,256]{1,0:T(8,128)(2,1)S(1)} collective-permute-done((bf16[544,256]{1,0:T(8,128)(2,1)}, bf16[544,256]{1,0:T(8,128)(2,1)S(1)}, u32[]{:S(2)}, u32[]{:S(2)}) %collective-permute-start.3) | collective-permute-done | bytes 278560 | tf_op jit(solution)/shard_map/ppermute | solution.py:317
  21.9 0.0 collective-permute-start.6
  21.9 0.0 collective-permute-done.5.refs_4_.refs_5_
  21.9 0.0 copy-start
  21.9 2.2 %copy-done = bf16[512,4096]{1,0:T(8,128)(2,1)S(1)} copy-done((bf16[512,4096]{1,0:T(8,128)(2,1)S(1)}, bf16[512,4096]{1,0:T(8,128)(2,1)}, u32[]{:S(2)}) %copy-start) | copy-done | bytes 4194328
  24.1 0.0 copy-start.1
  24.1 1.0 %copy-done.1 = bf16[544,256]{1,0:T(8,128)(2,1)S(1)} copy-done((bf16[544,256]{1,0:T(8,128)(2,1)S(1)}, bf16[544,256]{1,0:T(8,128)(2,1)}, u32[]{:S(2)}) %copy-start.1) | copy-done | bytes 278552
  25.1 2.6 %shard_map.74 = (f32[1024,256]{1,0:T(8,128)S(1)}, bf16[2,16,512]{2,1,0:T(8,128)(2,1)}) custom-call(s32[2]{0:T(128)S(1)} %bitcast.21, bf16[512,4096]{1,0:T(8,128)(2,1)S(1)} %copy-done, bf16[512,4096]{1,0:T(8,128)(2,1)} %collective-permute-done.refs_2_, bf16[544,256]{1,0:T(8,128)(2,1)S(1)} %copy-done.1, bf16[544,256]{1,0:T(8,128)(2,1)S(1)} %collective-permute-done.5.refs_4_.refs_5_), custom_call_target="tpu_custom_call" | custom-call | flops 536870912 | bytes 2097152 | tf_op jit(solution)/shard_map/pallas_call | solution.py:78
  27.7 2.5 %collective-permute-done.2.refs_4_.refs_7_ = bf16[544,256]{1,0:T(8,128)(2,1)S(1)} collective-permute-done((bf16[544,256]{1,0:T(8,128)(2,1)}, bf16[544,256]{1,0:T(8,128)(2,1)S(1)}, u32[]{:S(2)}, u32[]{:S(2)}) %collective-permute-start.2) | collective-permute-done | bytes 278560 | tf_op jit(solution)/shard_map/ppermute | solution.py:317
  30.2 0.3 collective-permute-done.4.refs_6_.refs_9_
  30.5 0.0 copy-start.3
  30.5 0.0 copy-start.2
  30.5 2.5 %collective-permute-start.7 = (bf16[544,256]{1,0:T(8,128)(2,1)S(1)}, bf16[544,256]{1,0:T(8,128)(2,1)S(1)}, u32[]{:S(2)}, u32[]{:S(2)}) collective-permute-start(bf16[544,256]{1,0:T(8,128)(2,1)S(1)} %collective-permute-done.4.refs_6_.refs_9_), channel_id=1, source_target_pairs={{0,2},{1,3},{2,0},{3,1},{4,6},{5,7},{6,4},{7,5},{8,10},{9,11},{10,... | collective-permute-start | bytes 835592 | tf_op jit(solution)/shard_map/ppermute | solution.py:317
  33.0 3.9 %shard_map.75 = (f32[1024,256]{1,0:T(8,128)S(1)}, bf16[4,512,512]{2,1,0:T(8,128)(2,1)S(1)}) custom-call(s32[6]{0:T(128)S(1)} %slice.8.refs_0_, bf16[512,4096]{1,0:T(8,128)(2,1)S(1)} %copy-done, bf16[512,4096]{1,0:T(8,128)(2,1)} %collective-permute-done.refs_2_, bf16[544,256]{1,0:T(8,128)(2,1)S(1)} %collective-permute-done.1.refs_3_.refs_6_, ...), custom_call_target="tpu_custom_call" | custom-call | flops 1073741824 | bytes 4194304 | tf_op jit(solution)/shard_map/pallas_call | solution.py:78
  36.9 0.0 copy-start.4
  36.9 0.0 copy-done.3
  36.9 2.4 %collective-permute-start.13 = (bf16[256,512]{1,0:T(8,128)(2,1)S(1)}, bf16[256,512]{1,0:T(8,128)(2,1)S(1)}, u32[]{:S(2)}, u32[]{:S(2)}) collective-permute-start(bf16[256,512]{1,0:T(8,128)(2,1)S(1)} %copy-done.3), channel_id=1, source_target_pairs={{0,4},{1,5},{2,6},{3,7},{4,0},{5,1},{6,2},{7,3},{8,12},{9,13},{10,... | collective-permute-start | bytes 786440 | tf_op jit(solution)/shard_map/ppermute | solution.py:317
  39.4 0.1 pad_add_fusion.2.refs_0_
  39.4 0.1 collective-permute-start.12
  39.5 0.0 collective-permute-done.6.refs_10_
  39.5 7.2 %collective-permute-done.7.refs_11_ = bf16[544,256]{1,0:T(8,128)(2,1)S(1)} collective-permute-done((bf16[544,256]{1,0:T(8,128)(2,1)S(1)}, bf16[544,256]{1,0:T(8,128)(2,1)S(1)}, u32[]{:S(2)}, u32[]{:S(2)}) %collective-permute-start.7) | collective-permute-done | bytes 278560 | tf_op jit(solution)/shard_map/ppermute | solution.py:317
  46.7 0.0 copy-done.2
  46.7 2.8 %shard_map.76 = (bf16[144,128]{1,0:T(8,128)(2,1)S(1)}, bf16[144,128]{1,0:T(8,128)(2,1)S(1)}, bf16[144,128]{1,0:T(8,128)(2,1)S(1)}, bf16[144,128]{1,0:T(8,128)(2,1)S(1)}) custom-call(s32[2]{0:T(128)S(1)} %pad_add_fusion.2.refs_0_, s32[4]{0:T(128)S(1)} %iota_xor_fusion.refs_1_, s32[8]{0:T(128)S(1)} %stack.71.refs_2_, ...), custom_call_target="tpu_custom_call" | custom-call | flops 536870912 | bytes 2097152 | tf_op jit(solution)/shard_map/pallas_call | solution.py:154
  49.5 2.8 %collective-permute-done.13.refs_2_ = bf16[256,512]{1,0:T(8,128)(2,1)S(1)} collective-permute-done((bf16[256,512]{1,0:T(8,128)(2,1)S(1)}, bf16[256,512]{1,0:T(8,128)(2,1)S(1)}, u32[]{:S(2)}, u32[]{:S(2)}) %collective-permute-start.13) | collective-permute-done | bytes 262176 | tf_op jit(solution)/shard_map/ppermute | solution.py:317
  52.3 0.0 collective-permute-start.14
  52.3 2.0 %collective-permute-start.10 = (bf16[144,128]{1,0:T(8,128)(2,1)S(1)}, bf16[144,128]{1,0:T(8,128)(2,1)S(1)}, u32[]{:S(2)}, u32[]{:S(2)}) collective-permute-start(bf16[144,128]{1,0:T(8,128)(2,1)S(1)} %get-tuple-element.38), channel_id=1, source_target_pairs={{0,6},{1,7},{2,4},{3,5},{4,2},{5,3},{6,0},{7,1},{8,14},{9,15},{10,... | collective-permute-start | bytes 110600 | tf_op jit(solution)/shard_map/ppermute | solution.py:317
  54.3 1.1 %collective-permute-start.8 = (bf16[144,128]{1,0:T(8,128)(2,1)S(1)}, bf16[144,128]{1,0:T(8,128)(2,1)S(1)}, u32[]{:S(2)}, u32[]{:S(2)}) collective-permute-start(bf16[144,128]{1,0:T(8,128)(2,1)S(1)} %get-tuple-element.36), channel_id=1, source_target_pairs={{0,2},{1,3},{2,0},{3,1},{4,6},{5,7},{6,4},{7,5},{8,10},{9,11},{10,... | collective-permute-start | bytes 110600 | tf_op jit(solution)/shard_map/ppermute | solution.py:317
  55.4 1.3 %collective-permute-start.9 = (bf16[144,128]{1,0:T(8,128)(2,1)S(1)}, bf16[144,128]{1,0:T(8,128)(2,1)S(1)}, u32[]{:S(2)}, u32[]{:S(2)}) collective-permute-start(bf16[144,128]{1,0:T(8,128)(2,1)S(1)} %get-tuple-element.37), channel_id=1, source_target_pairs={{0,4},{1,5},{2,6},{3,7},{4,0},{5,1},{6,2},{7,3},{8,12},{9,13},{10,... | collective-permute-start | bytes 110600 | tf_op jit(solution)/shard_map/ppermute | solution.py:317
  56.7 0.0 copy-done.4
  56.7 6.3 %collective-permute-done.10.refs_3_ = bf16[144,128]{1,0:T(8,128)(2,1)S(1)} collective-permute-done((bf16[144,128]{1,0:T(8,128)(2,1)S(1)}, bf16[144,128]{1,0:T(8,128)(2,1)S(1)}, u32[]{:S(2)}, u32[]{:S(2)}) %collective-permute-start.10) | collective-permute-done | bytes 36896 | tf_op jit(solution)/shard_map/ppermute | solution.py:317
  62.9 0.0 collective-permute-done.8.refs_1_
  63.0 0.0 collective-permute-done.9.refs_2_
  63.0 0.2 shard_map.77.own_ref
  63.1 0.1 collective-permute-start.11
  63.2 0.1 pad_add_fusion.1.place_ref
  63.3 0.0 collective-permute-done.12.refs_1_
  63.3 1.1 %collective-permute-done.11.sibling_ref = bf16[128,128]{1,0:T(8,128)(2,1)S(1)} collective-permute-done((bf16[128,128]{1,0:T(8,128)(2,1)S(1)}, bf16[128,128]{1,0:T(8,128)(2,1)S(1)}, u32[]{:S(2)}, u32[]{:S(2)}) %collective-permute-start.11) | collective-permute-done | bytes 32800 | tf_op jit(solution)/shard_map/ppermute | solution.py:317
  64.4 0.0 collective-permute-done.14.refs_3_
  64.4 0.9 %shard_map.78 = (bf16[128,512]{1,0:T(8,128)(2,1)S(1)}, bf16[128,512]{1,0:T(8,128)(2,1)S(1)}, bf16[128,512]{1,0:T(8,128)(2,1)S(1)}, bf16[128,512]{1,0:T(8,128)(2,1)S(1)}) custom-call(s32[2]{0:T(128)S(1)} %pad_add_fusion.1.place_ref, bf16[128,128]{1,0:T(8,128)(2,1)S(1)} %shard_map.77.own_ref, bf16[128,128]{1,0:T(8,128)(2,1)S(1)} %collective-permute-done.11.sibling_ref, ...), custom_call_target="tpu_custom_call" | custom-call | tf_op jit(solution)/shard_map/pallas_call | solution.py:256
  65.3 1.6 %collective-permute-start.15 = (bf16[128,512]{1,0:T(8,128)(2,1)S(1)}, bf16[128,512]{1,0:T(8,128)(2,1)S(1)}, u32[]{:S(2)}, u32[]{:S(2)}) collective-permute-start(bf16[128,512]{1,0:T(8,128)(2,1)S(1)} %get-tuple-element.42), channel_id=1, source_target_pairs={{0,8},{8,0},{16,24},{24,16},{1,9},{9,1},{17,25},{25,17},{2,10},{10... | collective-permute-start | bytes 393224 | tf_op jit(solution)/shard_map/ppermute | solution.py:320
  66.9 1.5 %collective-permute-start.16 = (bf16[128,512]{1,0:T(8,128)(2,1)S(1)}, bf16[128,512]{1,0:T(8,128)(2,1)S(1)}, u32[]{:S(2)}, u32[]{:S(2)}) collective-permute-start(bf16[128,512]{1,0:T(8,128)(2,1)S(1)} %get-tuple-element.43), channel_id=1, source_target_pairs={{0,16},{8,24},{16,0},{24,8},{1,17},{9,25},{17,1},{25,9},{2,18},{10... | collective-permute-start | bytes 393224 | tf_op jit(solution)/shard_map/ppermute | solution.py:320
  68.4 0.5 collective-permute-start.17
  68.8 2.4 %collective-permute-done.15.refs_1_ = bf16[128,512]{1,0:T(8,128)(2,1)S(1)} collective-permute-done((bf16[128,512]{1,0:T(8,128)(2,1)S(1)}, bf16[128,512]{1,0:T(8,128)(2,1)S(1)}, u32[]{:S(2)}, u32[]{:S(2)}) %collective-permute-start.15) | collective-permute-done | bytes 131104 | tf_op jit(solution)/shard_map/ppermute | solution.py:320
  71.3 3.7 %collective-permute-done.16.refs_2_ = bf16[128,512]{1,0:T(8,128)(2,1)S(1)} collective-permute-done((bf16[128,512]{1,0:T(8,128)(2,1)S(1)}, bf16[128,512]{1,0:T(8,128)(2,1)S(1)}, u32[]{:S(2)}, u32[]{:S(2)}) %collective-permute-start.16) | collective-permute-done | bytes 131104 | tf_op jit(solution)/shard_map/ppermute | solution.py:320
  74.9 0.0 collective-permute-done.17.refs_3_
  74.9 0.1 shard_map.79
  75.0 0.1 collective-permute-start.18
  75.1 1.2 %collective-permute-done.18.theirs_ref = bf16[64,512]{1,0:T(8,128)(2,1)S(1)} collective-permute-done((bf16[64,512]{1,0:T(8,128)(2,1)S(1)}, bf16[64,512]{1,0:T(8,128)(2,1)S(1)}, u32[]{:S(2)}, u32[]{:S(2)}) %collective-permute-start.18) | collective-permute-done | bytes 65568 | tf_op jit(solution)/shard_map/ppermute | solution.py:317
  76.3 0.7 shard_map.80
  (4 shorter events, 0.0 us)
Async XLA Ops:
  2.0 7.6 %collective-permute-start = (bf16[512,4096]{1,0:T(8,128)(2,1)}, bf16[512,4096]{1,0:T(8,128)(2,1)}, u32[]{:S(2)}, u32[]{:S(2)}) collective-permute-start(bf16[512,4096]{1,0:T(8,128)(2,1)} %refs_1_.3), channel_id=1, source_target_pairs={{0,1},{1,0},{2,3},{3,2},{4,5},{5,4},{6,7},{7,6},{8,9},{9,8},{10,11... | collective-permute-start | bytes 12582920 | tf_op jit(solution)/shard_map/ppermute | solution.py:317
  2.5 16.2 %collective-permute-start.1 = (bf16[544,256]{1,0:T(8,128)(2,1)}, bf16[544,256]{1,0:T(8,128)(2,1)S(1)}, u32[]{:S(2)}, u32[]{:S(2)}) collective-permute-start(bf16[544,256]{1,0:T(8,128)(2,1)} %get-tuple-element.26.refs_3_.refs_4_), channel_id=1, source_target_pairs={{0,2},{1,3},{2,0},{3,1},{4,6},{5,7},{6,4},{7,5},{8,10},{9,11},{10,... | collective-permute-start | bytes 835592 | tf_op jit(solution)/shard_map/ppermute | solution.py:317
  5.2 16.7 %collective-permute-start.3 = (bf16[544,256]{1,0:T(8,128)(2,1)}, bf16[544,256]{1,0:T(8,128)(2,1)S(1)}, u32[]{:S(2)}, u32[]{:S(2)}) collective-permute-start(bf16[544,256]{1,0:T(8,128)(2,1)} %get-tuple-element.26.refs_3_.refs_4_), channel_id=1, source_target_pairs={{0,4},{1,5},{2,6},{3,7},{4,0},{5,1},{6,2},{7,3},{8,12},{9,13},{10,... | collective-permute-start | bytes 835592 | tf_op jit(solution)/shard_map/ppermute | solution.py:317
  7.8 22.4 %collective-permute-start.2 = (bf16[544,256]{1,0:T(8,128)(2,1)}, bf16[544,256]{1,0:T(8,128)(2,1)S(1)}, u32[]{:S(2)}, u32[]{:S(2)}) collective-permute-start(bf16[544,256]{1,0:T(8,128)(2,1)} %get-tuple-element.29), channel_id=1, source_target_pairs={{0,3},{1,2},{2,1},{3,0},{4,7},{5,6},{6,5},{7,4},{8,11},{9,10},{10,... | collective-permute-start | bytes 835592 | tf_op jit(solution)/shard_map/ppermute | solution.py:317
  7.8 22.7 %collective-permute-start.4 = (bf16[544,256]{1,0:T(8,128)(2,1)}, bf16[544,256]{1,0:T(8,128)(2,1)S(1)}, u32[]{:S(2)}, u32[]{:S(2)}) collective-permute-start(bf16[544,256]{1,0:T(8,128)(2,1)} %get-tuple-element.29), channel_id=1, source_target_pairs={{0,5},{1,4},{2,7},{3,6},{4,1},{5,0},{6,3},{7,2},{8,13},{9,12},{10,... | collective-permute-start | bytes 835592 | tf_op jit(solution)/shard_map/ppermute | solution.py:317
  9.7 12.2 %collective-permute-start.5 = (bf16[544,256]{1,0:T(8,128)(2,1)}, bf16[544,256]{1,0:T(8,128)(2,1)S(1)}, u32[]{:S(2)}, u32[]{:S(2)}) collective-permute-start(bf16[544,256]{1,0:T(8,128)(2,1)} %get-tuple-element.29), channel_id=1, source_target_pairs={{0,1},{1,0},{2,3},{3,2},{4,5},{5,4},{6,7},{7,6},{8,9},{9,8},{10,11... | collective-permute-start | bytes 835592 | tf_op jit(solution)/shard_map/ppermute | solution.py:317
  21.9 17.6 %collective-permute-start.6 = (bf16[544,256]{1,0:T(8,128)(2,1)S(1)}, bf16[544,256]{1,0:T(8,128)(2,1)S(1)}, u32[]{:S(2)}, u32[]{:S(2)}) collective-permute-start(bf16[544,256]{1,0:T(8,128)(2,1)S(1)} %collective-permute-done.3.refs_5_.refs_8_), channel_id=1, source_target_pairs={{0,2},{1,3},{2,0},{3,1},{4,6},{5,7},{6,4},{7,5},{8,10},{9,11},{10,... | collective-permute-start | bytes 835592 | tf_op jit(solution)/shard_map/ppermute | solution.py:317
  21.9 2.2 %copy-start = (bf16[512,4096]{1,0:T(8,128)(2,1)S(1)}, bf16[512,4096]{1,0:T(8,128)(2,1)}, u32[]{:S(2)}) copy-start(bf16[512,4096]{1,0:T(8,128)(2,1)} %refs_1_.3) | copy-start | bytes 12582916
  24.1 1.0 %copy-start.1 = (bf16[544,256]{1,0:T(8,128)(2,1)S(1)}, bf16[544,256]{1,0:T(8,128)(2,1)}, u32[]{:S(2)}) copy-start(bf16[544,256]{1,0:T(8,128)(2,1)} %get-tuple-element.26.refs_3_.refs_4_) | copy-start | bytes 835588
  30.5 6.4 %copy-start.3 = (bf16[256,512]{1,0:T(8,128)(2,1)S(1)}, bf16[256,512]{1,0:T(8,128)(2,1)}, u32[]{:S(2)}) copy-start(bf16[256,512]{1,0:T(8,128)(2,1)} %refs_0_) | copy-start | bytes 786436
  30.5 16.2 %copy-start.2 = (bf16[544,256]{1,0:T(8,128)(2,1)S(1)}, bf16[544,256]{1,0:T(8,128)(2,1)}, u32[]{:S(2)}) copy-start(bf16[544,256]{1,0:T(8,128)(2,1)} %get-tuple-element.26.refs_3_.refs_4_) | copy-start | bytes 835588
  30.5 16.2 %collective-permute-start.7 = (bf16[544,256]{1,0:T(8,128)(2,1)S(1)}, bf16[544,256]{1,0:T(8,128)(2,1)S(1)}, u32[]{:S(2)}, u32[]{:S(2)}) collective-permute-start(bf16[544,256]{1,0:T(8,128)(2,1)S(1)} %collective-permute-done.4.refs_6_.refs_9_), channel_id=1, source_target_pairs={{0,2},{1,3},{2,0},{3,1},{4,6},{5,7},{6,4},{7,5},{8,10},{9,11},{10,... | collective-permute-start | bytes 835592 | tf_op jit(solution)/shard_map/ppermute | solution.py:317
  36.9 19.8 %copy-start.4 = (bf16[256]{0:T(256)(128)(2,1)S(1)}, bf16[256]{0:T(256)(128)(2,1)}, u32[]{:S(2)}) copy-start(bf16[256]{0:T(256)(128)(2,1)} %param.12) | copy-start | bytes 1540
  36.9 15.4 %collective-permute-start.13 = (bf16[256,512]{1,0:T(8,128)(2,1)S(1)}, bf16[256,512]{1,0:T(8,128)(2,1)S(1)}, u32[]{:S(2)}, u32[]{:S(2)}) collective-permute-start(bf16[256,512]{1,0:T(8,128)(2,1)S(1)} %copy-done.3), channel_id=1, source_target_pairs={{0,4},{1,5},{2,6},{3,7},{4,0},{5,1},{6,2},{7,3},{8,12},{9,13},{10,... | collective-permute-start | bytes 786440 | tf_op jit(solution)/shard_map/ppermute | solution.py:317
  39.4 23.8 %collective-permute-start.12 = (bf16[256,512]{1,0:T(8,128)(2,1)S(1)}, bf16[256,512]{1,0:T(8,128)(2,1)S(1)}, u32[]{:S(2)}, u32[]{:S(2)}) collective-permute-start(bf16[256,512]{1,0:T(8,128)(2,1)S(1)} %copy-done.3), channel_id=1, source_target_pairs={{0,2},{1,3},{2,0},{3,1},{4,6},{5,7},{6,4},{7,5},{8,10},{9,11},{10,... | collective-permute-start | bytes 786440 | tf_op jit(solution)/shard_map/ppermute | solution.py:317
  52.3 12.1 %collective-permute-start.14 = (bf16[256,512]{1,0:T(8,128)(2,1)S(1)}, bf16[256,512]{1,0:T(8,128)(2,1)S(1)}, u32[]{:S(2)}, u32[]{:S(2)}) collective-permute-start(bf16[256,512]{1,0:T(8,128)(2,1)S(1)} %collective-permute-done.13.refs_2_), channel_id=1, source_target_pairs={{0,2},{1,3},{2,0},{3,1},{4,6},{5,7},{6,4},{7,5},{8,10},{9,11},{10,... | collective-permute-start | bytes 786440 | tf_op jit(solution)/shard_map/ppermute | solution.py:317
  52.3 10.6 %collective-permute-start.10 = (bf16[144,128]{1,0:T(8,128)(2,1)S(1)}, bf16[144,128]{1,0:T(8,128)(2,1)S(1)}, u32[]{:S(2)}, u32[]{:S(2)}) collective-permute-start(bf16[144,128]{1,0:T(8,128)(2,1)S(1)} %get-tuple-element.38), channel_id=1, source_target_pairs={{0,6},{1,7},{2,4},{3,5},{4,2},{5,3},{6,0},{7,1},{8,14},{9,15},{10,... | collective-permute-start | bytes 110600 | tf_op jit(solution)/shard_map/ppermute | solution.py:317
  54.3 8.7 %collective-permute-start.8 = (bf16[144,128]{1,0:T(8,128)(2,1)S(1)}, bf16[144,128]{1,0:T(8,128)(2,1)S(1)}, u32[]{:S(2)}, u32[]{:S(2)}) collective-permute-start(bf16[144,128]{1,0:T(8,128)(2,1)S(1)} %get-tuple-element.36), channel_id=1, source_target_pairs={{0,2},{1,3},{2,0},{3,1},{4,6},{5,7},{6,4},{7,5},{8,10},{9,11},{10,... | collective-permute-start | bytes 110600 | tf_op jit(solution)/shard_map/ppermute | solution.py:317
  55.4 7.5 %collective-permute-start.9 = (bf16[144,128]{1,0:T(8,128)(2,1)S(1)}, bf16[144,128]{1,0:T(8,128)(2,1)S(1)}, u32[]{:S(2)}, u32[]{:S(2)}) collective-permute-start(bf16[144,128]{1,0:T(8,128)(2,1)S(1)} %get-tuple-element.37), channel_id=1, source_target_pairs={{0,4},{1,5},{2,6},{3,7},{4,0},{5,1},{6,2},{7,3},{8,12},{9,13},{10,... | collective-permute-start | bytes 110600 | tf_op jit(solution)/shard_map/ppermute | solution.py:317
  63.1 1.3 %collective-permute-start.11 = (bf16[128,128]{1,0:T(8,128)(2,1)S(1)}, bf16[128,128]{1,0:T(8,128)(2,1)S(1)}, u32[]{:S(2)}, u32[]{:S(2)}) collective-permute-start(bf16[128,128]{1,0:T(8,128)(2,1)S(1)} %shard_map.77.own_ref), channel_id=1, source_target_pairs={{0,1},{1,0},{2,3},{3,2},{4,5},{5,4},{6,7},{7,6},{8,9},{9,8},{10,11... | collective-permute-start | bytes 98312 | tf_op jit(solution)/shard_map/ppermute | solution.py:317
  65.3 6.0 %collective-permute-start.15 = (bf16[128,512]{1,0:T(8,128)(2,1)S(1)}, bf16[128,512]{1,0:T(8,128)(2,1)S(1)}, u32[]{:S(2)}, u32[]{:S(2)}) collective-permute-start(bf16[128,512]{1,0:T(8,128)(2,1)S(1)} %get-tuple-element.42), channel_id=1, source_target_pairs={{0,8},{8,0},{16,24},{24,16},{1,9},{9,1},{17,25},{25,17},{2,10},{10... | collective-permute-start | bytes 393224 | tf_op jit(solution)/shard_map/ppermute | solution.py:320
  66.9 8.1 %collective-permute-start.16 = (bf16[128,512]{1,0:T(8,128)(2,1)S(1)}, bf16[128,512]{1,0:T(8,128)(2,1)S(1)}, u32[]{:S(2)}, u32[]{:S(2)}) collective-permute-start(bf16[128,512]{1,0:T(8,128)(2,1)S(1)} %get-tuple-element.43), channel_id=1, source_target_pairs={{0,16},{8,24},{16,0},{24,8},{1,17},{9,25},{17,1},{25,9},{2,18},{10... | collective-permute-start | bytes 393224 | tf_op jit(solution)/shard_map/ppermute | solution.py:320
  68.4 6.6 %collective-permute-start.17 = (bf16[128,512]{1,0:T(8,128)(2,1)S(1)}, bf16[128,512]{1,0:T(8,128)(2,1)S(1)}, u32[]{:S(2)}, u32[]{:S(2)}) collective-permute-start(bf16[128,512]{1,0:T(8,128)(2,1)S(1)} %get-tuple-element.44), channel_id=1, source_target_pairs={{0,24},{8,16},{16,8},{24,0},{1,25},{9,17},{17,9},{25,1},{2,26},{10... | collective-permute-start | bytes 393224 | tf_op jit(solution)/shard_map/ppermute | solution.py:320
  75.0 1.3 %collective-permute-start.18 = (bf16[64,512]{1,0:T(8,128)(2,1)S(1)}, bf16[64,512]{1,0:T(8,128)(2,1)S(1)}, u32[]{:S(2)}, u32[]{:S(2)}) collective-permute-start(bf16[64,512]{1,0:T(8,128)(2,1)S(1)} %get-tuple-element.46), channel_id=1, source_target_pairs={{0,1},{1,0},{2,3},{3,2},{4,5},{5,4},{6,7},{7,6},{8,9},{9,8},{10,11... | collective-permute-start | bytes 196616 | tf_op jit(solution)/shard_map/ppermute | solution.py:317
